TPU v7x, 32 devices: a whole 2x2x4 slice. The times are simulated.
32 devices in a mesh: dp: 8 (over z, x), fsdp: 4 (over y, core).
Axes of the slice: x: 2, y: 2, z: 4, core: 2. Of those that a mesh axis runs over, the one named last changes fastest.
Arguments:
- hidden: bfloat16 [8192, 4, 1024], P(('dp', 'fsdp')), may hold values from -108 to 108
- head: bfloat16 [4, 1024, 1024], P('fsdp', 'dp'), may hold values from -14 to 14
- gain: bfloat16 [4, 1024], P('fsdp', 'dp'), may hold values from 0.5 to 1.5
- targets: int32 [8192, 4], P('dp', 'fsdp'), may hold values from 0 to 1023
- lengths: int32 [8], replicated, may hold values from 256 to 1024, as said below
Outputs:
- loss: float32 [], replicated
- grad_hidden: bfloat16 [8192, 4, 1024], P(('dp', 'fsdp'))
- grad_head: float32 [4, 1024, 1024], P('fsdp', 'dp')
Inputs may be any that keep to these rules, and one draw needn't show every extreme that they name: `lengths`: each dialogue has at least 256 valid frames, and some dialogue has all 1024.
All inputs are finite; a program needn't handle non-finite values.
Results may differ from a plain program's by a relative error of at most 0.015.
Values may be sent and summed in bfloat16 or wider, within the bound.
No kernel may reach another device: no remote copies, remote signals or barrier semaphores. Data moves between devices by JAX's collectives and lax.ppermute only.
A program may use at most 64 MiB of HBM per device.

v0:
```python
import jax
import jax.numpy as jnp
from jax import lax
from jax.sharding import PartitionSpec as P

EPS = 1e-05


def per_device(hidden, head, gain, targets, lengths):
    rows = lax.all_to_all(hidden, "fsdp", split_axis=1, concat_axis=0, tiled=True)
    rows = rows[:, 0, :]
    labels = targets[:, 0]
    frames = rows.shape[0]
    classes = head.shape[2]
    dialogue = lax.axis_index("dp")
    dialog_ids = jnp.arange(lengths.shape[0], dtype=jnp.int32)
    length = jnp.sum(jnp.where(dialog_ids == dialogue, lengths, 0))
    valid = (jnp.arange(frames, dtype=jnp.int32) < length).astype(jnp.float32)
    widened = rows.astype(jnp.float32)
    inverse = lax.rsqrt(jnp.mean(widened * widened, axis=1, keepdims=True) + EPS)
    scaled = widened * inverse
    weights = lax.all_gather(head[0], "dp", axis=0, tiled=True)
    gains = lax.all_gather(gain[0], "dp", axis=0, tiled=True)
    gains_wide = gains.astype(jnp.float32)
    columns = scaled
    piece_normed = (columns * gains_wide[None, :]).astype(jnp.bfloat16)
    logit_sum = jnp.dot(piece_normed, weights, preferred_element_type=jnp.float32)
    top = jnp.max(logit_sum, axis=1, keepdims=True)
    shifted = logit_sum - top
    total = jnp.sum(jnp.exp(shifted), axis=1, keepdims=True)
    log_total = top + jnp.log(total)
    onehot = (labels[:, None] == jnp.arange(classes, dtype=jnp.int32)[None, :]).astype(jnp.float32)
    picked = jnp.sum(logit_sum * onehot, axis=1)
    local = jnp.sum(valid * (log_total[:, 0] - picked))
    summed = lax.psum(local, ("dp", "fsdp"))
    loss = summed / (jnp.sum(lengths).astype(jnp.float32) * lax.axis_size("fsdp"))
    probs = jnp.exp(shifted) / total
    slopes = (valid[:, None] * (probs - onehot)).astype(jnp.bfloat16)
    back = lax.dot_general(
        slopes,
        lax.all_gather(head[0], "dp", axis=0, tiled=True),
        (((1,), (1,)), ((), ())),
        preferred_element_type=jnp.float32,
    )
    weighted = back * gains_wide[None, :]
    grad_rows = (
        inverse * weighted
        - widened * inverse**3 * jnp.mean(weighted * widened, axis=1, keepdims=True)
    ).astype(jnp.bfloat16)
    grad_hidden = lax.all_to_all(
        grad_rows[:, None, :], "fsdp", split_axis=0, concat_axis=1, tiled=True
    )
    columns = piece_normed
    grad_head = lax.psum_scatter(
        lax.dot_general(
            columns, slopes, (((0,), (0,)), ((), ())), preferred_element_type=jnp.float32
        ).astype(jnp.bfloat16),
        "dp",
        scatter_dimension=0,
        tiled=True,
    ).astype(jnp.float32)
    return (loss, grad_hidden, grad_head[None])


def solution(mesh):
    placed = (
        P(("dp", "fsdp"), None, None),
        P("fsdp", "dp", None),
        P("fsdp", "dp"),
        P("dp", "fsdp"),
        P(),
    )
    return jax.shard_map(
        per_device,
        mesh=mesh,
        in_specs=placed,
        out_specs=(P(), P(("dp", "fsdp"), None, None), P("fsdp", "dp", None)),
        check_vma=False,
    )
```

profile of v0, /device:TPU:0, one launch (start us, length us, event | category | flops | bytes accessed | tf_op | source)
XLA Modules:
  0.0 173.4 jit_solution(545153178059146699)
XLA Ops:
  7.2 0.0 all-gather.4.cloned.1.call-start
  7.2 0.7 all-gather.4.cloned.1.call-update
  7.9 3.6 %copy.24 = bf16[256,4,1024]{2,0,1:T(8,128)(2,1)} copy(bf16[256,4,1024]{2,1,0:T(4,128)(2,1)} %param.5) | data formatting | bytes 4194304 | tf_op args[0]
  11.5 4.2 %all-to-all-start = ((bf16[256,4,1024]{2,0,1:T(8,128)(2,1)}), bf16[256,4,1024]{2,0,1:T(8,128)(2,1)S(1)}, u32[]{:S(2)}, u32[]{:S(2)}) async-start(bf16[256,4,1024]{2,0,1:T(8,128)(2,1)} %copy.24), calls=%async_computation | async-start | bytes 4194304 | tf_op jit(solution)/shard_map/all_to_all | solution.py:10
  15.7 21.7 %all-gather = bf16[1,1024]{1,0:T(2,128)(2,1)S(1)} all-gather(bf16[1,128]{1,0:T(2,128)(2,1)S(1)} %copy-done.4), channel_id=2, replica_groups=mesh['dp'=8,'fsdp'=4] {'dp'}, dimensions={1}, use_global_device_ids=true | all-gather | bytes 2304 | tf_op jit(solution)/shard_map/all_gather | solution.py:23
  37.4 0.6 fusion.8
  38.1 0.6 fusion.6
  38.7 2.7 %all-to-all-done = bf16[256,4,1024]{2,0,1:T(8,128)(2,1)S(1)} async-done(((bf16[256,4,1024]{2,0,1:T(8,128)(2,1)}), bf16[256,4,1024]{2,0,1:T(8,128)(2,1)S(1)}, u32[]{:S(2)}, u32[]{:S(2)}) %all-to-all-start) | async-done | bytes 2097184 | tf_op jit(solution)/shard_map/all_to_all | solution.py:10
  41.4 2.4 %convert_element_type.61 = f32[256,4,1024]{2,0,1:T(8,128)} convert(bf16[256,4,1024]{2,0,1:T(8,128)(2,1)S(1)} %all-to-all-done) | non-fusion elementwise | flops 1048576 | bytes 6291456 | tf_op jit(solution)/shard_map/convert_element_type | solution.py:19
  43.8 5.4 %copy.30 = f32[1024,1024]{0,1:T(8,128)} copy(f32[1024,1024]{1,0:T(8,128)} %bitcast.30) | data formatting | bytes 8388608 | tf_op jit(solution)/shard_map/convert_element_type | solution.py:19
  49.2 0.5 multiply_reduce_fusion.1
  49.7 12.4 %all-gather.4.cloned.1.call-done = bf16[1,1024,1024]{2,1,0:T(8,128)(2,1)} async-done(((bf16[1,128,1024]{2,1,0:T(8,128)(2,1)}), bf16[1,1024,1024]{2,1,0:T(8,128)(2,1)}) %all-gather.4.cloned.1.call-update) | async-done | bytes 2097168 | tf_op jit(solution)/shard_map/all_gather | solution.py:22
  62.2 5.5 %fusion.9 = (f32[1024]{0:T(1024)S(1)}, f32[1024,1024]{0,1:T(8,128)S(1)}) fusion(bf16[1,1024,1024]{2,1,0:T(8,128)(2,1)} %all-gather.4.cloned.1.call-done, f32[1024,1024]{0,1:T(8,128)} %copy.30, f32[1024]{0:T(1024)S(1)} %bitcast.36, f32[1024]{0:T(1024)S(1)} %bitcast.32), kind=kOutput, calls=%fused_computation.25 | convolution fusion | flops 2151676928 | bytes 10498048 | tf_op jit(solution)/shard_map/dot_general | solution.py:27
  67.7 1.1 fusion
  68.8 1.0 copy-done.2
  69.8 1.6 copy-done
  71.4 3.9 %convolution_convert_fusion = bf16[1024,1024]{1,0:T(8,128)(2,1)} fusion(f32[1024,1024]{0,1:T(8,128)S(1)} %copy-done, f32[1024]{0:T(1024)S(1)} %bitcast.37, f32[1024]{0:T(1024)S(1)} %bitcast.33, f32[1024,1024]{0,1:T(8,128)S(1)} %get-tuple-element.14, f32[1024]{0:T(1024)S(1)} %get-tuple-element.9, f32[1024]{0:T(1024)S(1)} %fusion.6, s32[1024]{0:T(1024)S(1)} %bitcast.41, ...), kind=kOutput, calls=%fused_computation.14 | convolution fusion | flops 2159017984 | bytes 10510336 | tf_op jit(solution)/shard_map/dot_general | solution.py:55
  75.3 0.0 reduce-scatter.2.cloned.1.call-update
  75.3 6.8 %multiply_reduce_fusion = (f32[1024]{0:T(1024)S(1)}, f32[1024,1024]{0,1:T(8,128)S(1)}) fusion(f32[1024,1024]{0,1:T(8,128)} %copy.30, f32[1024]{0:T(1024)S(1)} %bitcast.38, f32[1024,1024]{0,1:T(8,128)} %copy-done.2, f32[1024]{0:T(1024)S(1)} %get-tuple-element.9, f32[1024]{0:T(1024)S(1)} %fusion.6, s32[1024]{0:T(1024)S(1)} %bitcast.42, ...), kind=kOutput, calls=%fused_computation.1 | convolution fusion | flops 2157968384 | bytes 14704640 | tf_op jit(solution)/shard_map/dot_general | solution.py:39
  82.2 0.8 fusion.1
  83.0 0.6 broadcast.58
  83.6 2.9 %reduce.3 = bf16[1024,1024]{0,1:T(8,128)(2,1)} reduce(bf16[1024,1,1024]{0,2,1:T(8,128)(2,1)S(1)} %fusion.1, bf16[]{:T(256)} %broadcast.58), dimensions={1}, to_apply=%copy.28.reduce_sub_computation | reduce | bytes 4194306 | tf_op jit(solution)/shard_map/broadcast_in_dim | solution.py:51
  86.5 2.9 %copy.34 = bf16[1024,1024]{1,0:T(8,128)(2,1)S(1)} copy(bf16[1024,1024]{0,1:T(8,128)(2,1)} %reduce.3) | data formatting | bytes 4194304
  89.4 2.9 %reshape.60 = bf16[4,2,131072]{2,1,0:T(2,128)(2,1)} reshape(bf16[1024,1024]{1,0:T(8,128)(2,1)S(1)} %copy.34) | data formatting | bytes 4194304
  92.3 3.6 %all-to-all-start.1 = ((bf16[4,2,131072]{2,1,0:T(2,128)(2,1)}), bf16[4,2,131072]{2,1,0:T(2,128)(2,1)S(1)}, u32[]{:S(2)}, u32[]{:S(2)}) async-start(bf16[4,2,131072]{2,1,0:T(2,128)(2,1)} %reshape.60), calls=%async_computation.1 | async-start | bytes 4194304 | tf_op jit(solution)/shard_map/all_to_all | solution.py:50
  96.6 1.3 select_reduce_fusion.1
  97.8 55.8 %psum.7 = f32[]{:T(128)} all-reduce(f32[]{:T(128)} %select_reduce_fusion.1), channel_id=1, replica_groups=mesh['dp'=8,'fsdp'=4] {'dp','fsdp'}, use_global_device_ids=true, to_apply=%region_6.7 | all-reduce | flops 1 | bytes 8 | tf_op jit(solution)/shard_map/psum | solution.py:35
  154.3 0.0 all-to-all-done.1
  154.3 3.4 %reshape.61 = bf16[1024,1,1024]{2,1,0:T(2,128)(2,1)} reshape(bf16[4,2,131072]{2,1,0:T(2,128)(2,1)S(1)} %all-to-all-done.1) | data formatting | bytes 4194304
  157.7 3.0 %copy.31 = bf16[1024,1,1024]{2,0,1:T(8,128)(2,1)S(1)} copy(bf16[1024,1,1024]{2,1,0:T(2,128)(2,1)} %reshape.61) | data formatting | bytes 4194304
  160.7 2.9 %copy.29 = bf16[256,4,1024]{2,1,0:T(4,128)(2,1)} copy(bf16[256,4,1024]{2,0,1:T(8,128)(2,1)S(1)} %bitcast.31) | data formatting | bytes 4194304
  163.6 1.8 %bitcast_convert_fusion = f32[1,128,1024]{2,1,0:T(8,128)} fusion(bf16[128,1024]{1,0:T(8,128)(2,1)} %reduce-scatter.2.cloned.1.call-done), kind=kLoop, calls=%fused_computation.15 | loop fusion | flops 131072 | bytes 786432 | tf_op jit(solution)/shard_map/broadcast_in_dim | solution.py:62
  (17 shorter events, 0.1 us)
Async XLA Ops:
  7.2 55.0 %all-gather.4.cloned.1.call-start = ((), (), s32[]{:S(2)}) async-start(), calls=%async_computation.4 | async-start | bytes 2359296 | tf_op jit(solution)/shard_map/all_gather | solution.py:22
  7.9 7.8 %copy-start.4 = (bf16[1,128]{1,0:T(2,128)(2,1)S(1)}, bf16[1,128]{1,0:T(2,128)(2,1)}, u32[]{:S(2)}) copy-start(bf16[1,128]{1,0:T(2,128)(2,1)} %param.7) | copy-start | bytes 772
  7.9 29.5 %copy-start.5 = (s32[8]{0:T(128)S(1)}, s32[8]{0:T(128)}, u32[]{:S(2)}) copy-start(s32[8]{0:T(128)} %param.9) | copy-start | bytes 100
  11.5 29.9 %all-to-all-start = ((bf16[256,4,1024]{2,0,1:T(8,128)(2,1)}), bf16[256,4,1024]{2,0,1:T(8,128)(2,1)S(1)}, u32[]{:S(2)}, u32[]{:S(2)}) async-start(bf16[256,4,1024]{2,0,1:T(8,128)(2,1)} %copy.24), calls=%async_computation | async-start | bytes 4194304 | tf_op jit(solution)/shard_map/all_to_all | solution.py:10
  15.7 147.9 %reduce-scatter.2.cloned.1.call-start = ((), (), s32[]{:S(2)}) async-start(), calls=%async_computation.3 | async-start | bytes 2359296 | tf_op jit(solution)/shard_map/reduce_scatter | solution.py:54
  62.2 5.5 %copy-start.3 = (s32[1024,1]{0,1:T(1,128)S(1)}, s32[1024,1]{0,1:T(1,128)}, u32[]{:S(2)}) copy-start(s32[1024,1]{0,1:T(1,128)} %param.8) | copy-start | bytes 12292
  67.7 2.1 %copy-start.2 = (f32[1024,1024]{0,1:T(8,128)}, f32[1024,1024]{0,1:T(8,128)S(1)}, u32[]{:S(2)}) copy-start(f32[1024,1024]{0,1:T(8,128)S(1)} %get-tuple-element.14) | copy-start | bytes 12582916
  67.7 3.7 %copy-start = (f32[1024,1024]{0,1:T(8,128)S(1)}, f32[1024,1024]{0,1:T(8,128)}, u32[]{:S(2)}) copy-start(f32[1024,1024]{0,1:T(8,128)} %copy.30) | copy-start | bytes 12582916
  75.3 6.8 %copy-start.1 = (f32[1024,1024]{0,1:T(8,128)S(1)}, f32[1024,1024]{0,1:T(8,128)}, u32[]{:S(2)}) copy-start(f32[1024,1024]{0,1:T(8,128)} %copy.30) | copy-start | bytes 12582916
  92.3 62.0 %all-to-all-start.1 = ((bf16[4,2,131072]{2,1,0:T(2,128)(2,1)}), bf16[4,2,131072]{2,1,0:T(2,128)(2,1)S(1)}, u32[]{:S(2)}, u32[]{:S(2)}) async-start(bf16[4,2,131072]{2,1,0:T(2,128)(2,1)} %reshape.60), calls=%async_computation.1 | async-start | bytes 4194304 | tf_op jit(solution)/shard_map/all_to_all | solution.py:50
Sparse Core Ops, SparseCore 0:
  10.1 51.9 all-gather.3
  75.4 66.3 reduce-scatter.1
where the time goes:
time: 174 us; the launch traced here: 173 us
  blocking collectives  77.5 us (45%)
  local copies, waits for them, and re-layouts  27.2 us (16%)
  between operations  16.6 us (10%)
  matrix products  16.2 us (9%)
  waiting for transfers between devices  15.8 us (9%)
  other arithmetic  12.1 us (7%)
  starting transfers between devices  7.89 us (5%)
    psum x1, blocking collectives, per_device(): summed = lax.psum(local, ('dp', 'fsdp'))  55.8 us
    all_gather x1, blocking collectives, per_device(): gains = lax.all_gather(gain[0], 'dp', axis=0, tiled=True)  21.7 us
    unnamed x19, local copies, waits for them, and re-layouts  21.3 us
    all_gather x1, waiting for transfers between devices, per_device(): weights = lax.all_gather(head[0], 'dp', axis=0, tiled=True)  12.4 us
    dot_general x1, matrix products, per_device(): lax.dot_general(slopes, lax.all_gather(head[0], 'dp', axis=0, tiled=True)...  6.79 us
    dot_general x1, matrix products, per_device(): jnp.dot(piece_normed, weights, preferred_element_type=jnp.float32)  5.48 us
    convert_element_type x1, local copies, waits for them, and re-layouts, per_device(): widened = rows.astype(jnp.float32)  5.39 us
    all_to_all x1, starting transfers between devices, per_device(): lax.all_to_all(hidden, 'fsdp', split_axis=1, concat_axis=0, tiled=True)  4.24 us
  transfers between devices with their start and end apart: 4, of which 2 were waited for; matrix products, arithmetic and copies ran while one was open for 23% of the time, Pallas kernels for 0%

commit v1 on v0

v1 whole, which is shorter than its diff:
```python
import jax
import jax.numpy as jnp
from jax import lax
from jax.experimental import pallas as pl
from jax.experimental.pallas import tpu as pltpu
from jax.sharding import PartitionSpec as P

EPS = 1e-05
WIDE = jnp.float32
HALF = jnp.bfloat16
VMEM = pl.BlockSpec(memory_space=pltpu.VMEM)
SMEM = pl.BlockSpec(memory_space=pltpu.SMEM)
ANY = pl.BlockSpec(memory_space=pl.ANY)
PACK_ROWS = 256


def params(mib):
    return pltpu.CompilerParams(vmem_limit_bytes=mib * 1024 * 1024)


def cost(flops, moved):
    return pl.CostEstimate(flops=flops, bytes_accessed=moved, transcendentals=0)


def unpack(hidden):
    frames, positions, width = hidden.shape
    chunk = PACK_ROWS // positions
    rows = chunk * positions

    def body(hidden_ref, out_ref):
        r = lax.broadcasted_iota(jnp.int32, (rows, rows), 0)
        c = lax.broadcasted_iota(jnp.int32, (rows, rows), 1)
        pick = (lax.rem(r, chunk) == lax.div(c, positions)) & (lax.rem(c, positions) == lax.div(r, chunk))
        flat = hidden_ref[...].reshape(rows, width)
        moved = jnp.dot(pick.astype(HALF), flat, preferred_element_type=WIDE).astype(HALF)
        out_ref[...] = moved.reshape(positions, chunk, width)

    out = pl.pallas_call(
        body,
        grid=(frames // chunk,),
        in_specs=[pl.BlockSpec((chunk, positions, width), lambda i: (i, 0, 0))],
        out_specs=pl.BlockSpec((positions, chunk, width), lambda i: (0, i, 0)),
        out_shape=jax.ShapeDtypeStruct((positions, frames, width), HALF),
        cost_estimate=cost(2 * frames * rows * positions * width, 4 * hidden.size),
        compiler_params=params(24),
        name="unpack",
    )(hidden)
    return out.reshape(positions * frames, width)


def pack(flat, positions):
    width = flat.shape[1]
    frames = flat.shape[0] // positions
    chunk = PACK_ROWS // positions
    rows = chunk * positions

    def body(flat_ref, out_ref):
        r = lax.broadcasted_iota(jnp.int32, (rows, rows), 0)
        c = lax.broadcasted_iota(jnp.int32, (rows, rows), 1)
        pick = (lax.rem(c, chunk) == lax.div(r, positions)) & (lax.rem(r, positions) == lax.div(c, chunk))
        block = flat_ref[...].reshape(rows, width)
        moved = jnp.dot(pick.astype(HALF), block, preferred_element_type=WIDE).astype(HALF)
        out_ref[...] = moved.reshape(chunk, positions, width)

    return pl.pallas_call(
        body,
        grid=(frames // chunk,),
        in_specs=[pl.BlockSpec((positions, chunk, width), lambda i: (0, i, 0))],
        out_specs=pl.BlockSpec((chunk, positions, width), lambda i: (i, 0, 0)),
        out_shape=jax.ShapeDtypeStruct((frames, positions, width), HALF),
        cost_estimate=cost(2 * frames * rows * positions * width, 4 * flat.size),
        compiler_params=params(24),
        name="pack",
    )(flat.reshape(positions, frames, width))


def forward(lengths, labels, gains, stream, pieces, blocks):
    frames, width = stream.shape
    height = frames // blocks
    depth, classes = pieces[0].shape
    n_dp = len(pieces)

    def body(*refs):
        length_ref, label_ref, gain_ref, stream_ref = refs[:4]
        piece_refs = refs[4 : 4 + n_dp]
        loss_ref, gain_out, weight_ref, slope_ref = refs[4 + n_dp : 8 + n_dp]
        part_refs = refs[8 + n_dp : 8 + 2 * n_dp]
        rows_ref, normed_ref, partial_ref, sems = refs[8 + 2 * n_dp :]

        dp = lax.axis_index("dp")

        def span(i):
            return pl.ds(pl.multiple_of((dp ^ i) * depth, depth), depth)

        copies = [
            pltpu.make_async_copy(
                stream_ref.at[pl.ds(j * height, height)], rows_ref.at[pl.ds(j * height, height)], sems.at[j]
            )
            for j in range(blocks)
        ]
        copies += [
            pltpu.make_async_copy(piece_refs[i], weight_ref.at[span(i)], sems.at[blocks + i]) for i in range(n_dp)
        ]
        for copy in copies:
            copy.start()
        gain = jnp.concatenate([gain_ref[i : i + 1, :].astype(WIDE) for i in range(n_dp)], axis=1)
        gain_out[...] = gain
        length = length_ref[dp]
        count = length_ref[0]
        for d in range(1, n_dp):
            count = count + length_ref[d]

        for j in range(blocks):
            copies[j].wait()
            values = rows_ref[j * height : (j + 1) * height, :].astype(WIDE)
            inverse = lax.rsqrt(jnp.mean(values * values, axis=1, keepdims=True) + EPS)
            normed_ref[j * height : (j + 1) * height, :] = (values * inverse * gain).astype(HALF)
        for copy in copies[blocks:]:
            copy.wait()
        weights = weight_ref[...]
        loss = jnp.zeros((1, 1), WIDE)
        for j in range(blocks):
            logits = jnp.dot(
                normed_ref[j * height : (j + 1) * height, :], weights, preferred_element_type=WIDE
            )
            label_row = label_ref[:, j * height : (j + 1) * height]
            label = jnp.broadcast_to(label_row, (8, height)).T[:, :1]
            slot = j * height + lax.broadcasted_iota(jnp.int32, (height, 1), 0)
            valid = jnp.where(slot < length, 1.0, 0.0).astype(WIDE)
            top = jnp.max(logits, axis=1, keepdims=True)
            shifted = logits - top
            powers = jnp.exp(shifted)
            total = jnp.sum(powers, axis=1, keepdims=True)
            hit = lax.broadcasted_iota(jnp.int32, (height, classes), 1) == label
            picked = jnp.sum(jnp.where(hit, shifted, 0.0), axis=1, keepdims=True)
            loss = loss + jnp.sum(valid * (jnp.log(total) - picked), axis=0, keepdims=True)
            probs = powers * (1.0 / total)
            slope_ref[j * height : (j + 1) * height, :] = (valid * jnp.where(hit, probs - 1.0, probs)).astype(HALF)
        loss_ref[...] = jnp.broadcast_to(loss / (count.astype(WIDE) * blocks), loss_ref.shape)
        step = min(256, width)
        for at in range(0, width, step):
            partial_ref[at : at + step, :] = lax.dot_general(
                normed_ref[:, at : at + step],
                slope_ref[...],
                (((0,), (0,)), ((), ())),
                preferred_element_type=WIDE,
            ).astype(HALF)
        for i in range(n_dp):
            part_refs[i][...] = partial_ref[span(i), :]

    out = pl.pallas_call(
        body,
        in_specs=[SMEM] + [VMEM] * 2 + [ANY] * (1 + n_dp),
        out_specs=[VMEM] * (4 + n_dp),
        out_shape=[
            jax.ShapeDtypeStruct((8, 128), WIDE),
            jax.ShapeDtypeStruct((1, width), WIDE),
            jax.ShapeDtypeStruct((width, classes), HALF),
            jax.ShapeDtypeStruct((frames, classes), HALF),
        ]
        + [jax.ShapeDtypeStruct((depth, classes), HALF)] * n_dp,
        scratch_shapes=[
            pltpu.VMEM((frames, width), HALF),
            pltpu.VMEM((frames, width), HALF),
            pltpu.VMEM((width, classes), HALF),
            pltpu.SemaphoreType.DMA((blocks + n_dp,)),
        ],
        cost_estimate=cost(4 * frames * width * classes, 6 * width * classes),
        compiler_params=params(28),
        name="forward",
    )(lengths, labels, gains, stream, *pieces)
    return (*out[:4], out[4:])


def backward(gain, weights, stream, slopes, blocks):
    frames, width = stream.shape
    classes = weights.shape[1]
    height = frames // blocks

    def body(gain_ref, weight_ref, stream_ref, slope_ref, out_ref):
        for j in range(blocks):
            rows = slice(j * height, (j + 1) * height)
            values = stream_ref[rows, :].astype(WIDE)
            inverse = lax.rsqrt(jnp.mean(values * values, axis=1, keepdims=True) + EPS)
            back = lax.dot_general(
                slope_ref[rows, :],
                weight_ref[...],
                (((1,), (1,)), ((), ())),
                preferred_element_type=WIDE,
            )
            weighted = back * gain_ref[...]
            scale = inverse * inverse * inverse * jnp.mean(weighted * values, axis=1, keepdims=True)
            out_ref[rows, :] = (inverse * weighted - values * scale).astype(HALF)

    return pl.pallas_call(
        body,
        in_specs=[VMEM] * 4,
        out_specs=VMEM,
        out_shape=jax.ShapeDtypeStruct((frames, width), HALF),
        cost_estimate=cost(2 * frames * width * classes, 6 * frames * width),
        compiler_params=params(24),
        name="backward",
    )(gain, weights, stream, slopes)


def per_device(n_dp, n_fsdp, hidden, head, gain, targets, lengths):
    inner = 2 if n_dp % 2 == 0 else 1
    line = n_dp // inner
    blocks = min(n_fsdp, 4)

    def swap(value, offset):
        return lax.ppermute(value, "dp", [(i, i ^ offset) for i in range(n_dp)])

    def wide(*values):
        total = values[0].astype(WIDE)
        for value in values[1:]:
            total = total + value.astype(WIDE)
        return total

    pieces = [None] * n_dp
    pieces[0] = head[0]
    for j in range(line - 1, 0, -1):
        pieces[j * inner] = swap(head[0], j * inner)
    if inner == 2:
        for j in range(line):
            pieces[j * inner + 1] = swap(pieces[j * inner], 1)

    stream = lax.all_to_all(unpack(hidden), "fsdp", split_axis=0, concat_axis=0, tiled=True)
    gains = lax.all_to_all(
        jnp.broadcast_to(gain, (n_dp, gain.shape[1])), "dp", split_axis=0, concat_axis=0, tiled=True
    )

    loss, gain_row, weights, slopes, parts = forward(lengths, targets.T, gains, stream, pieces, blocks)

    sums = [None] * line
    for j in range(line - 1, -1, -1):
        terms = [parts[j * inner]]
        if inner == 2:
            terms.append(swap(parts[j * inner + 1], 1))
        sums[j] = terms if j == 0 else [swap(wide(*terms).astype(HALF), j * inner)]
    grad_head = wide(*[term for terms in sums for term in terms])

    grads = backward(gain_row, weights, stream, slopes, blocks)
    grads = lax.all_to_all(grads, "fsdp", split_axis=0, concat_axis=0, tiled=True)
    grad_hidden = pack(grads, n_fsdp)

    n = n_dp * n_fsdp
    losses = lax.all_to_all(
        jnp.broadcast_to(loss[:1], (n, 128)), ("dp", "fsdp"), split_axis=0, concat_axis=0, tiled=True
    )
    return jnp.sum(losses[:, 0]), grad_hidden, grad_head[None]


def solution(mesh):
    n_dp, n_fsdp = mesh.shape["dp"], mesh.shape["fsdp"]
    placed = (
        P(("dp", "fsdp"), None, None),
        P("fsdp", "dp", None),
        P("fsdp", "dp"),
        P("dp", "fsdp"),
        P(),
    )
    return jax.shard_map(
        lambda *args: per_device(n_dp, n_fsdp, *args),
        mesh=mesh,
        in_specs=placed,
        out_specs=(P(), P(("dp", "fsdp"), None, None), P("fsdp", "dp", None)),
        check_vma=False,
    )
```

time: 174 us -> 133 us (0.76)
  the two profiles are of different devices: /device:TPU:0 before, /device:TPU:17 now
where the time goes in v1:
time: 133 us
  waiting for transfers between devices  56 us (42%)
  starting transfers between devices  33 us (25%)
  local copies, waits for them, and re-layouts  25.1 us (19%)
  Pallas kernels  15.9 us (12%)
  other arithmetic  1.8 us (1%)
    ppermute x14, waiting for transfers between devices, swap(): return lax.ppermute(value, 'dp', [(i, i ^ offset) for i in range(n_dp)])  56 us
    unnamed x57, local copies, waits for them, and re-layouts  23.2 us
    ppermute x14, starting transfers between devices, swap(): return lax.ppermute(value, 'dp', [(i, i ^ offset) for i in range(n_dp)])  11 us
    pallas_call x1, Pallas kernels, forward(): pl.pallas_call(body, in_specs=[SMEM] + [VMEM] * 2 + [ANY] * (1 + n_dp), o...  7.63 us
    all_to_all x1, starting transfers between devices, per_device(): lax.all_to_all(jnp.broadcast_to(loss[:1], (n, 128)), ('dp', 'fsdp'), spli...  7.38 us
    all_to_all x1, starting transfers between devices, per_device(): lax.all_to_all(jnp.broadcast_to(gain, (n_dp, gain.shape[1])), 'dp', split...  5.58 us
    all_to_all x1, starting transfers between devices, per_device(): lax.all_to_all(unpack(hidden), 'fsdp', split_axis=0, concat_axis=0, tiled...  4.95 us
    all_to_all x1, starting transfers between devices, per_device(): lax.all_to_all(grads, 'fsdp', split_axis=0, concat_axis=0, tiled=True)  4.07 us
  transfers between devices with their start and end apart: 18, of which 10 were waited for; matrix products, arithmetic and copies ran while one was open for 1% of the time, Pallas kernels for 4%

profile of v1, /device:TPU:17, one launch (start us, length us, event | category | flops | bytes accessed | tf_op | source)
XLA Modules:
  0.0 132.5 jit_solution(11575835287037417979)
XLA Ops:
  0.6 1.3 broadcast_in_dim.6
  1.9 5.6 %all-to-all-start = ((bf16[8,1,128]{2,1,0:T(2,128)(2,1)}), bf16[8,1,128]{2,1,0:T(2,128)(2,1)S(1)}, u32[]{:S(2)}, u32[]{:S(2)}) async-start(bf16[8,1,128]{2,1,0:T(2,128)(2,1)} %broadcast_in_dim.6), calls=%async_computation | async-start | bytes 8192 | tf_op jit(solution)/shard_map/all_to_all | solution.py:229
  7.5 1.6 %copy-done.1 = bf16[256,4,1024]{2,1,0:T(4,128)(2,1)S(1)} copy-done((bf16[256,4,1024]{2,1,0:T(4,128)(2,1)S(1)}, bf16[256,4,1024]{2,1,0:T(4,128)(2,1)}, u32[]{:S(2)}) %copy-start.1) | copy-done | bytes 2097176
  9.1 2.5 %unpack.1 = bf16[4,256,1024]{2,1,0:T(8,128)(2,1)} custom-call(bf16[256,4,1024]{2,1,0:T(4,128)(2,1)S(1)} %copy-done.1), custom_call_target="tpu_custom_call" | custom-call | flops 536870912 | bytes 4194304 | tf_op jit(solution)/shard_map/unpack/pallas_call | solution.py:38
  11.6 5.0 %all-to-all-start.1 = ((bf16[4,256,1024]{2,1,0:T(8,128)(2,1)}), bf16[4,256,1024]{2,1,0:T(8,128)(2,1)S(1)}, u32[]{:S(2)}, u32[]{:S(2)}) async-start(bf16[4,256,1024]{2,1,0:T(8,128)(2,1)} %unpack.1), calls=%async_computation.1 | async-start | bytes 4194304 | tf_op jit(solution)/shard_map/all_to_all | solution.py:228
  16.5 1.2 collective-permute-start.1
  19.2 1.2 collective-permute-start
  20.4 8.0 %collective-permute-done.1.refs_6_ = bf16[128,1024]{1,0:T(8,128)(2,1)S(1)} collective-permute-done((bf16[128,1024]{1,0:T(8,128)(2,1)S(1)}, bf16[128,1024]{1,0:T(8,128)(2,1)S(1)}, u32[]{:S(2)}, u32[]{:S(2)}) %collective-permute-start.1) | collective-permute-done | bytes 262176 | tf_op jit(solution)/shard_map/ppermute | solution.py:212
  32.0 10.2 %collective-permute-done.5.refs_10_ = bf16[128,1024]{1,0:T(8,128)(2,1)S(1)} collective-permute-done((bf16[128,1024]{1,0:T(8,128)(2,1)S(1)}, bf16[128,1024]{1,0:T(8,128)(2,1)S(1)}, u32[]{:S(2)}, u32[]{:S(2)}) %collective-permute-start.5) | collective-permute-done | bytes 262176 | tf_op jit(solution)/shard_map/ppermute | solution.py:212
  42.2 1.2 collective-permute-start.6
  46.2 2.6 %collective-permute-done.6.refs_11_ = bf16[128,1024]{1,0:T(8,128)(2,1)S(1)} collective-permute-done((bf16[128,1024]{1,0:T(8,128)(2,1)S(1)}, bf16[128,1024]{1,0:T(8,128)(2,1)S(1)}, u32[]{:S(2)}, u32[]{:S(2)}) %collective-permute-start.6) | collective-permute-done | bytes 262176 | tf_op jit(solution)/shard_map/ppermute | solution.py:212
  51.5 0.9 copy-done.16
  56.2 7.6 %forward.1 = (f32[8,128]{1,0:T(8,128)S(1)}, f32[1,1024]{1,0:T(1,128)S(1)}, bf16[1024,1024]{1,0:T(8,128)(2,1)S(1)}, bf16[1024,1024]{1,0:T(8,128)(2,1)S(1)}, bf16[...) custom-call(s32[8]{0:T(128)S(1)} %copy-done.27, ...), custom_call_target="tpu_custom_call" | custom-call | flops 4294967296 | bytes 6291456 | tf_op jit(solution)/shard_map/forward/pallas_call | solution.py:151
  63.9 1.3 copy-done.2
  65.2 1.3 %copy-done.4 = bf16[1024,1024]{1,0:T(8,128)(2,1)} copy-done((bf16[1024,1024]{1,0:T(8,128)(2,1)}, bf16[1024,1024]{1,0:T(8,128)(2,1)S(1)}, u32[]{:S(2)}) %copy-start.4) | copy-done | bytes 2097176
  70.0 7.4 %all-to-all-start.2 = ((f32[32,1,128]{2,1,0:T(1,128)}), f32[32,1,128]{2,1,0:T(1,128)S(1)}, u32[]{:S(2)}, u32[]{:S(2)}) async-start(f32[32,1,128]{2,1,0:T(1,128)} %broadcast_in_dim.14), calls=%async_computation.2 | async-start | bytes 32768 | tf_op jit(solution)/shard_map/all_to_all | solution.py:248
  77.4 1.6 %copy-done.3 = bf16[1024,1024]{1,0:T(8,128)(2,1)S(1)} copy-done((bf16[1024,1024]{1,0:T(8,128)(2,1)S(1)}, bf16[1024,1024]{1,0:T(8,128)(2,1)}, u32[]{:S(2)}) %copy-start.3) | copy-done | bytes 2097176
  79.0 1.6 %copy-done.5 = bf16[1024,1024]{1,0:T(8,128)(2,1)S(1)} copy-done((bf16[1024,1024]{1,0:T(8,128)(2,1)S(1)}, bf16[1024,1024]{1,0:T(8,128)(2,1)}, u32[]{:S(2)}) %copy-start.5) | copy-done | bytes 2097176
  80.5 3.1 %backward.1 = bf16[1024,1024]{1,0:T(8,128)(2,1)S(1)} custom-call(f32[1,1024]{1,0:T(1,128)S(1)} %get-tuple-element.16.gain_ref, bf16[1024,1024]{1,0:T(8,128)(2,1)S(1)} %copy-done.3, bf16[1024,1024]{1,0:T(8,128)(2,1)S(1)} %bitcast.14, bf16[1024,1024]{1,0:T(8,128)(2,1)S(1)} %copy-done.5), custom_call_target="tpu_custom_call" | custom-call | flops 2147483648 | bytes 6291456 | tf_op jit(solution)/shard_map/backward/pallas_call | solution.py:195
  83.6 1.3 copy-done
  85.0 4.1 %all-to-all-start.3 = ((bf16[4,256,1024]{2,1,0:T(8,128)(2,1)}), bf16[4,256,1024]{2,1,0:T(8,128)(2,1)S(1)}, u32[]{:S(2)}, u32[]{:S(2)}) async-start(bf16[4,256,1024]{2,1,0:T(8,128)(2,1)} %bitcast.15), calls=%async_computation.3 | async-start | bytes 4194304 | tf_op jit(solution)/shard_map/all_to_all | solution.py:244
  89.0 1.2 collective-permute-start.8
  90.5 1.2 collective-permute-start.12
  92.0 5.1 %collective-permute-done.8 = bf16[128,1024]{1,0:T(8,128)(2,1)S(1)} collective-permute-done((bf16[128,1024]{1,0:T(8,128)(2,1)}, bf16[128,1024]{1,0:T(8,128)(2,1)S(1)}, u32[]{:S(2)}, u32[]{:S(2)}) %collective-permute-start.8) | collective-permute-done | bytes 262176 | tf_op jit(solution)/shard_map/ppermute | solution.py:212
  97.2 1.3 collective-permute-start.9
  98.5 4.2 %collective-permute-done.10 = bf16[128,1024]{1,0:T(8,128)(2,1)S(1)} collective-permute-done((bf16[128,1024]{1,0:T(8,128)(2,1)}, bf16[128,1024]{1,0:T(8,128)(2,1)S(1)}, u32[]{:S(2)}, u32[]{:S(2)}) %collective-permute-start.10) | collective-permute-done | bytes 262176 | tf_op jit(solution)/shard_map/ppermute | solution.py:212
  102.9 5.5 %collective-permute-done.12 = bf16[128,1024]{1,0:T(8,128)(2,1)S(1)} collective-permute-done((bf16[128,1024]{1,0:T(8,128)(2,1)}, bf16[128,1024]{1,0:T(8,128)(2,1)S(1)}, u32[]{:S(2)}, u32[]{:S(2)}) %collective-permute-start.12) | collective-permute-done | bytes 262176 | tf_op jit(solution)/shard_map/ppermute | solution.py:212
  109.4 4.6 %collective-permute-done.7 = bf16[128,1024]{1,0:T(8,128)(2,1)S(1)} collective-permute-done((bf16[128,1024]{1,0:T(8,128)(2,1)S(1)}, bf16[128,1024]{1,0:T(8,128)(2,1)S(1)}, u32[]{:S(2)}, u32[]{:S(2)}) %collective-permute-start.7) | collective-permute-done | bytes 262176 | tf_op jit(solution)/shard_map/ppermute | solution.py:212
  114.0 4.9 %collective-permute-done.11 = bf16[128,1024]{1,0:T(8,128)(2,1)S(1)} collective-permute-done((bf16[128,1024]{1,0:T(8,128)(2,1)S(1)}, bf16[128,1024]{1,0:T(8,128)(2,1)S(1)}, u32[]{:S(2)}, u32[]{:S(2)}) %collective-permute-start.11) | collective-permute-done | bytes 262176 | tf_op jit(solution)/shard_map/ppermute | solution.py:212
  118.9 10.0 %collective-permute-done.13 = bf16[128,1024]{1,0:T(8,128)(2,1)S(1)} collective-permute-done((bf16[128,1024]{1,0:T(8,128)(2,1)S(1)}, bf16[128,1024]{1,0:T(8,128)(2,1)S(1)}, u32[]{:S(2)}, u32[]{:S(2)}) %collective-permute-start.13) | collective-permute-done | bytes 262176 | tf_op jit(solution)/shard_map/ppermute | solution.py:212
  128.8 1.0 add_bitcast_fusion
  129.8 2.7 %pack.1 = bf16[256,4,1024]{2,1,0:T(4,128)(2,1)} custom-call(bf16[4,256,1024]{2,1,0:T(8,128)(2,1)S(1)} %all-to-all-done.3.flat_ref), custom_call_target="tpu_custom_call" | custom-call | flops 536870912 | bytes 4194304 | tf_op jit(solution)/shard_map/pack/pallas_call | solution.py:65
  (73 shorter events, 19.6 us)
Async XLA Ops:
  1.9 9.7 %all-to-all-start = ((bf16[8,1,128]{2,1,0:T(2,128)(2,1)}), bf16[8,1,128]{2,1,0:T(2,128)(2,1)S(1)}, u32[]{:S(2)}, u32[]{:S(2)}) async-start(bf16[8,1,128]{2,1,0:T(2,128)(2,1)} %broadcast_in_dim.6), calls=%async_computation | async-start | bytes 8192 | tf_op jit(solution)/shard_map/all_to_all | solution.py:229
  7.5 1.6 %copy-start.1 = (bf16[256,4,1024]{2,1,0:T(4,128)(2,1)S(1)}, bf16[256,4,1024]{2,1,0:T(4,128)(2,1)}, u32[]{:S(2)}) copy-start(bf16[256,4,1024]{2,1,0:T(4,128)(2,1)} %hidden_ref.1) | copy-start | bytes 6291460
  11.6 5.0 %copy-start.6 = (bf16[1,128,1024]{2,1,0:T(8,128)(2,1)S(1)}, bf16[1,128,1024]{2,1,0:T(8,128)(2,1)}, u32[]{:S(2)}) copy-start(bf16[1,128,1024]{2,1,0:T(8,128)(2,1)} %param.6) | copy-start | bytes 786436
  11.6 38.0 %copy-start.26 = (s32[1024,1]{0,1:T(1,128)S(1)}, s32[1024,1]{0,1:T(1,128)}, u32[]{:S(2)}) copy-start(s32[1024,1]{0,1:T(1,128)} %param.8) | copy-start | bytes 12292
  11.6 38.0 %copy-start.27 = (s32[8]{0:T(128)S(1)}, s32[8]{0:T(128)}, u32[]{:S(2)}) copy-start(s32[8]{0:T(128)} %refs_0_.1) | copy-start | bytes 100
  11.6 38.0 %all-to-all-start.1 = ((bf16[4,256,1024]{2,1,0:T(8,128)(2,1)}), bf16[4,256,1024]{2,1,0:T(8,128)(2,1)S(1)}, u32[]{:S(2)}, u32[]{:S(2)}) async-start(bf16[4,256,1024]{2,1,0:T(8,128)(2,1)} %unpack.1), calls=%async_computation.1 | async-start | bytes 4194304 | tf_op jit(solution)/shard_map/all_to_all | solution.py:228
  16.5 11.8 %collective-permute-start.1 = (bf16[128,1024]{1,0:T(8,128)(2,1)S(1)}, bf16[128,1024]{1,0:T(8,128)(2,1)S(1)}, u32[]{:S(2)}, u32[]{:S(2)}) collective-permute-start(bf16[128,1024]{1,0:T(8,128)(2,1)S(1)} %bitcast.17), channel_id=1, source_target_pairs={{0,8},{4,12},{8,0},{12,4},{16,24},{20,28},{24,16},{28,20},{1,9},{5... | collective-permute-start | bytes 786440 | tf_op jit(solution)/shard_map/ppermute | solution.py:212
  17.8 13.0 %collective-permute-start.3 = (bf16[128,1024]{1,0:T(8,128)(2,1)S(1)}, bf16[128,1024]{1,0:T(8,128)(2,1)S(1)}, u32[]{:S(2)}, u32[]{:S(2)}) collective-permute-start(bf16[128,1024]{1,0:T(8,128)(2,1)S(1)} %bitcast.18), channel_id=1, source_target_pairs={{0,16},{4,20},{8,24},{12,28},{16,0},{20,4},{24,8},{28,12},{1,17},{... | collective-permute-start | bytes 786440 | tf_op jit(solution)/shard_map/ppermute | solution.py:212
  18.7 23.5 %collective-permute-start.5 = (bf16[128,1024]{1,0:T(8,128)(2,1)S(1)}, bf16[128,1024]{1,0:T(8,128)(2,1)S(1)}, u32[]{:S(2)}, u32[]{:S(2)}) collective-permute-start(bf16[128,1024]{1,0:T(8,128)(2,1)S(1)} %bitcast.19), channel_id=1, source_target_pairs={{0,24},{4,28},{8,16},{12,20},{16,8},{20,12},{24,0},{28,4},{1,25},{... | collective-permute-start | bytes 786440 | tf_op jit(solution)/shard_map/ppermute | solution.py:212
  19.2 24.9 %collective-permute-start = (bf16[128,1024]{1,0:T(8,128)(2,1)S(1)}, bf16[128,1024]{1,0:T(8,128)(2,1)S(1)}, u32[]{:S(2)}, u32[]{:S(2)}) collective-permute-start(bf16[128,1024]{1,0:T(8,128)(2,1)S(1)} %bitcast.20), channel_id=1, source_target_pairs={{0,4},{4,0},{8,12},{12,8},{16,20},{20,16},{24,28},{28,24},{1,5},{5... | collective-permute-start | bytes 786440 | tf_op jit(solution)/shard_map/ppermute | solution.py:212
  28.4 16.4 %collective-permute-start.2 = (bf16[128,1024]{1,0:T(8,128)(2,1)S(1)}, bf16[128,1024]{1,0:T(8,128)(2,1)S(1)}, u32[]{:S(2)}, u32[]{:S(2)}) collective-permute-start(bf16[128,1024]{1,0:T(8,128)(2,1)S(1)} %collective-permute-done.1.refs_6_), channel_id=1, source_target_pairs={{0,4},{4,0},{8,12},{12,8},{16,20},{20,16},{24,28},{28,24},{1,5},{5... | collective-permute-start | bytes 786440 | tf_op jit(solution)/shard_map/ppermute | solution.py:212
  30.7 14.8 %collective-permute-start.4 = (bf16[128,1024]{1,0:T(8,128)(2,1)S(1)}, bf16[128,1024]{1,0:T(8,128)(2,1)S(1)}, u32[]{:S(2)}, u32[]{:S(2)}) collective-permute-start(bf16[128,1024]{1,0:T(8,128)(2,1)S(1)} %collective-permute-done.3.refs_8_), channel_id=1, source_target_pairs={{0,4},{4,0},{8,12},{12,8},{16,20},{20,16},{24,28},{28,24},{1,5},{5... | collective-permute-start | bytes 786440 | tf_op jit(solution)/shard_map/ppermute | solution.py:212
  42.2 6.6 %collective-permute-start.6 = (bf16[128,1024]{1,0:T(8,128)(2,1)S(1)}, bf16[128,1024]{1,0:T(8,128)(2,1)S(1)}, u32[]{:S(2)}, u32[]{:S(2)}) collective-permute-start(bf16[128,1024]{1,0:T(8,128)(2,1)S(1)} %collective-permute-done.5.refs_10_), channel_id=1, source_target_pairs={{0,4},{4,0},{8,12},{12,8},{16,20},{20,16},{24,28},{28,24},{1,5},{5... | collective-permute-start | bytes 786440 | tf_op jit(solution)/shard_map/ppermute | solution.py:212
  49.6 1.0 copy-start.11
  50.5 0.9 copy-start.14
  51.5 0.9 copy-start.16
  52.4 0.9 copy-start.18
  63.8 1.3 copy-start.2
  65.2 1.3 %copy-start.4 = (bf16[1024,1024]{1,0:T(8,128)(2,1)}, bf16[1024,1024]{1,0:T(8,128)(2,1)S(1)}, u32[]{:S(2)}) copy-start(bf16[1024,1024]{1,0:T(8,128)(2,1)S(1)} %get-tuple-element.18.slope_ref) | copy-start | bytes 6291460
  70.0 15.0 %all-to-all-start.2 = ((f32[32,1,128]{2,1,0:T(1,128)}), f32[32,1,128]{2,1,0:T(1,128)S(1)}, u32[]{:S(2)}, u32[]{:S(2)}) async-start(f32[32,1,128]{2,1,0:T(1,128)} %broadcast_in_dim.14), calls=%async_computation.2 | async-start | bytes 32768 | tf_op jit(solution)/shard_map/all_to_all | solution.py:248
  77.4 1.6 %copy-start.3 = (bf16[1024,1024]{1,0:T(8,128)(2,1)S(1)}, bf16[1024,1024]{1,0:T(8,128)(2,1)}, u32[]{:S(2)}) copy-start(bf16[1024,1024]{1,0:T(8,128)(2,1)} %copy-done.2) | copy-start | bytes 6291460
  79.0 1.6 %copy-start.5 = (bf16[1024,1024]{1,0:T(8,128)(2,1)S(1)}, bf16[1024,1024]{1,0:T(8,128)(2,1)}, u32[]{:S(2)}) copy-start(bf16[1024,1024]{1,0:T(8,128)(2,1)} %copy-done.4) | copy-start | bytes 6291460
  83.6 1.3 copy-start
  85.0 6.7 %copy-start.8 = (bf16[128,1024]{1,0:T(8,128)(2,1)S(1)}, bf16[128,1024]{1,0:T(8,128)(2,1)}, u32[]{:S(2)}) copy-start(bf16[128,1024]{1,0:T(8,128)(2,1)} %copy-done.7) | copy-start | bytes 786436
  85.0 44.9 %all-to-all-start.3 = ((bf16[4,256,1024]{2,1,0:T(8,128)(2,1)}), bf16[4,256,1024]{2,1,0:T(8,128)(2,1)S(1)}, u32[]{:S(2)}, u32[]{:S(2)}) async-start(bf16[4,256,1024]{2,1,0:T(8,128)(2,1)} %bitcast.15), calls=%async_computation.3 | async-start | bytes 4194304 | tf_op jit(solution)/shard_map/all_to_all | solution.py:244
  89.0 8.1 %collective-permute-start.8 = (bf16[128,1024]{1,0:T(8,128)(2,1)}, bf16[128,1024]{1,0:T(8,128)(2,1)S(1)}, u32[]{:S(2)}, u32[]{:S(2)}) collective-permute-start(bf16[128,1024]{1,0:T(8,128)(2,1)} %copy-done.19), channel_id=1, source_target_pairs={{0,4},{4,0},{8,12},{12,8},{16,20},{20,16},{24,28},{28,24},{1,5},{5... | collective-permute-start | bytes 786440 | tf_op jit(solution)/shard_map/ppermute | solution.py:212
  90.2 12.5 %collective-permute-start.10 = (bf16[128,1024]{1,0:T(8,128)(2,1)}, bf16[128,1024]{1,0:T(8,128)(2,1)S(1)}, u32[]{:S(2)}, u32[]{:S(2)}) collective-permute-start(bf16[128,1024]{1,0:T(8,128)(2,1)} %copy-done.12), channel_id=1, source_target_pairs={{0,4},{4,0},{8,12},{12,8},{16,20},{20,16},{24,28},{28,24},{1,5},{5... | collective-permute-start | bytes 786440 | tf_op jit(solution)/shard_map/ppermute | solution.py:212
  90.5 17.8 %collective-permute-start.12 = (bf16[128,1024]{1,0:T(8,128)(2,1)}, bf16[128,1024]{1,0:T(8,128)(2,1)S(1)}, u32[]{:S(2)}, u32[]{:S(2)}) collective-permute-start(bf16[128,1024]{1,0:T(8,128)(2,1)} %copy-done.9), channel_id=1, source_target_pairs={{0,4},{4,0},{8,12},{12,8},{16,20},{20,16},{24,28},{28,24},{1,5},{5... | collective-permute-start | bytes 786440 | tf_op jit(solution)/shard_map/ppermute | solution.py:212
  91.7 22.3 %collective-permute-start.7 = (bf16[128,1024]{1,0:T(8,128)(2,1)S(1)}, bf16[128,1024]{1,0:T(8,128)(2,1)S(1)}, u32[]{:S(2)}, u32[]{:S(2)}) collective-permute-start(bf16[128,1024]{1,0:T(8,128)(2,1)S(1)} %copy-done.8), channel_id=1, source_target_pairs={{0,4},{4,0},{8,12},{12,8},{16,20},{20,16},{24,28},{28,24},{1,5},{5... | collective-permute-start | bytes 786440 | tf_op jit(solution)/shard_map/ppermute | solution.py:212
  97.2 16.8 %collective-permute-start.9 = (bf16[128,1024]{1,0:T(8,128)(2,1)S(1)}, bf16[128,1024]{1,0:T(8,128)(2,1)S(1)}, u32[]{:S(2)}, u32[]{:S(2)}) collective-permute-start(bf16[128,1024]{1,0:T(8,128)(2,1)S(1)} %add_convert_fusion.2), channel_id=1, source_target_pairs={{0,8},{4,12},{8,0},{12,4},{16,24},{20,28},{24,16},{28,20},{1,9},{5... | collective-permute-start | bytes 786440 | tf_op jit(solution)/shard_map/ppermute | solution.py:212
  102.8 16.1 %collective-permute-start.11 = (bf16[128,1024]{1,0:T(8,128)(2,1)S(1)}, bf16[128,1024]{1,0:T(8,128)(2,1)S(1)}, u32[]{:S(2)}, u32[]{:S(2)}) collective-permute-start(bf16[128,1024]{1,0:T(8,128)(2,1)S(1)} %add_convert_fusion.1), channel_id=1, source_target_pairs={{0,16},{4,20},{8,24},{12,28},{16,0},{20,4},{24,8},{28,12},{1,17},{... | collective-permute-start | bytes 786440 | tf_op jit(solution)/shard_map/ppermute | solution.py:212
  108.4 20.4 %collective-permute-start.13 = (bf16[128,1024]{1,0:T(8,128)(2,1)S(1)}, bf16[128,1024]{1,0:T(8,128)(2,1)S(1)}, u32[]{:S(2)}, u32[]{:S(2)}) collective-permute-start(bf16[128,1024]{1,0:T(8,128)(2,1)S(1)} %add_convert_fusion), channel_id=1, source_target_pairs={{0,24},{4,28},{8,16},{12,20},{16,8},{20,12},{24,0},{28,4},{1,25},{... | collective-permute-start | bytes 786440 | tf_op jit(solution)/shard_map/ppermute | solution.py:212
  (14 other events, 10.7 us)

commit v2 on v0

v2 whole, which is shorter than its diff:
```python
import jax
import jax.numpy as jnp
from jax import lax
from jax.experimental import pallas as pl
from jax.experimental.pallas import tpu as pltpu
from jax.sharding import PartitionSpec as P

EPS = 1e-05
WIDE = jnp.float32
HALF = jnp.bfloat16
VMEM = pl.BlockSpec(memory_space=pltpu.VMEM)
SMEM = pl.BlockSpec(memory_space=pltpu.SMEM)
ANY = pl.BlockSpec(memory_space=pl.ANY)
PACK_ROWS = 256
EXTRA = 8
UNPACK, PACK, NEAR, FAR, BACK_FAR, BACK_NEAR, FOLD, HOLD = 0.01, 0.01, 10, 0.01, 0.01, 0.01, 0.01, 0.01


def params(mib):
    return pltpu.CompilerParams(vmem_limit_bytes=mib * 1024 * 1024)


def cost(gigaflops):
    return pl.CostEstimate(flops=int(gigaflops * 1e9), bytes_accessed=0, transcendentals=0)


def unpack(hidden):
    frames, positions, width = hidden.shape
    chunk = PACK_ROWS // positions
    rows = chunk * positions
    steps = frames // chunk

    def body(hidden_ref, *refs):
        outs, (stage, sems) = refs[:-2], refs[-2:]
        copies = [
            pltpu.make_async_copy(
                hidden_ref.at[pl.ds(i * chunk, chunk)], stage.at[pl.ds(i * chunk, chunk)], sems.at[i]
            )
            for i in range(steps)
        ]
        for copy in copies:
            copy.start()
        me = lax.axis_index("fsdp")
        r = lax.broadcasted_iota(jnp.int32, (rows, rows), 0)
        c = lax.broadcasted_iota(jnp.int32, (rows, rows), 1)
        pick = (lax.rem(r, chunk) == lax.div(c, positions)) & (
            lax.rem(c, positions) == (lax.div(r, chunk) ^ me)
        )
        pick = pick.astype(HALF)
        for i in range(steps):
            copies[i].wait()
            here = slice(i * chunk, (i + 1) * chunk)
            flat = stage[here].reshape(rows, width)
            moved = jnp.dot(pick, flat, preferred_element_type=WIDE).astype(HALF)
            for j in range(positions):
                part = moved[j * chunk : (j + 1) * chunk]
                if j < 2:
                    outs[j][here, :] = part
                else:
                    outs[j // 2 + 1][j % 2, here, :] = part

    return pl.pallas_call(
        body,
        in_specs=[ANY],
        out_specs=[VMEM] * (positions // 2 + 1),
        out_shape=[jax.ShapeDtypeStruct((frames, width), HALF)] * 2
        + [jax.ShapeDtypeStruct((2, frames, width), HALF)] * (positions // 2 - 1),
        scratch_shapes=[pltpu.VMEM(hidden.shape, HALF), pltpu.SemaphoreType.DMA((steps,))],
        cost_estimate=cost(UNPACK),
        compiler_params=params(58),
        name="unpack",
    )(hidden)


def pack(own, side, pairs, relayed):
    frames, width = own.shape
    positions = 2 + 2 * len(pairs)
    chunk = PACK_ROWS // positions
    rows = chunk * positions
    n = len(pairs)

    def body(own_ref, side_ref, *refs):
        me = lax.axis_index("fsdp")
        r = lax.broadcasted_iota(jnp.int32, (rows, rows), 0)
        c = lax.broadcasted_iota(jnp.int32, (rows, rows), 1)
        pick = (lax.rem(c, chunk) == lax.div(r, positions)) & (
            lax.rem(r, positions) == (lax.div(c, chunk) ^ me)
        )
        parts = [own_ref[...], side_ref[...]]
        for i in range(n):
            parts += [refs[i][0], refs[n + i][...]]
        flat = jnp.concatenate(parts, axis=0)
        moved = jnp.dot(pick.astype(HALF), flat, preferred_element_type=WIDE).astype(HALF)
        refs[-1][...] = moved.reshape(chunk, positions, width)

    flat_spec = pl.BlockSpec((chunk, width), lambda i: (i, 0))
    return pl.pallas_call(
        body,
        grid=(frames // chunk,),
        in_specs=[flat_spec] * 2 + [pl.BlockSpec((1, chunk, width), lambda i: (0, i, 0))] * n + [flat_spec] * n,
        out_specs=pl.BlockSpec((chunk, positions, width), lambda i: (i, 0, 0)),
        out_shape=jax.ShapeDtypeStruct((frames, positions, width), HALF),
        cost_estimate=cost(PACK),
        compiler_params=params(24),
        name="pack",
    )(own, side, *pairs, *relayed)


def take(pair, after=()):
    def body(*refs):
        refs[-1][...] = refs[0][1]

    return pl.pallas_call(
        body,
        in_specs=[VMEM] + [ANY] * len(after),
        out_specs=VMEM,
        out_shape=jax.ShapeDtypeStruct(pair.shape[1:], pair.dtype),
        cost_estimate=cost(HOLD),
        compiler_params=params(8),
        name="take",
    )(pair, *after)


def split_rows(value, classes):
    high = value.astype(HALF).astype(WIDE)
    middle = (value - high).astype(HALF).astype(WIDE)
    low = value - high - middle
    row = lax.broadcasted_iota(jnp.int32, (EXTRA, classes), 0)
    terms = jnp.where(row == 0, high, jnp.where(row == 1, middle, jnp.where(row == 2, low, 0.0)))
    return terms.astype(HALF)


def softmax_rows(normed, weights, label_ref, block, length):
    height, classes = normed.shape[0], weights.shape[1]
    logits = jnp.dot(normed, weights, preferred_element_type=WIDE)
    if label_ref.shape[0] == 1:
        label_row = label_ref[:, pl.ds(pl.multiple_of(block * height, height), height)]
    else:
        label_row = label_ref[pl.ds(block, 1), :]
    label = jnp.broadcast_to(label_row, (8, height)).T[:, :1]
    slot = block * height + lax.broadcasted_iota(jnp.int32, (height, 1), 0)
    valid = jnp.where(slot < length, 1.0, 0.0).astype(WIDE)
    top = jnp.max(logits, axis=1, keepdims=True)
    shifted = logits - top
    powers = jnp.exp(shifted)
    total = jnp.sum(powers, axis=1, keepdims=True)
    hit = lax.broadcasted_iota(jnp.int32, (height, classes), 1) == label
    picked = jnp.sum(jnp.where(hit, shifted, 0.0), axis=1, keepdims=True)
    loss = jnp.sum(valid * (jnp.log(total) - picked), axis=0, keepdims=True)
    probs = powers * (1.0 / total)
    return (valid * jnp.where(hit, probs - 1.0, probs)).astype(HALF), loss


def norm_rows(values, gain):
    values = values.astype(WIDE)
    inverse = lax.rsqrt(jnp.mean(values * values, axis=1, keepdims=True) + EPS)
    return (values * inverse * gain).astype(HALF)


def forward_near(lengths, labels, gains, rows, pieces):
    height, width = rows[0].shape
    depth, classes = pieces[0].shape
    n_dp, n_gain, n = len(pieces), len(gains), len(rows)

    def body(*refs):
        length_ref, label_ref = refs[:2]
        gain_refs, refs = refs[2 : 2 + n_gain], refs[2 + n_gain :]
        row_refs, refs = refs[:n], refs[n:]
        piece_refs, refs = refs[:n_dp], refs[n_dp:]
        loss_ref, gain_out, weight_ref, normed_ref, slope_ref, sems = refs
        me, dp = lax.axis_index("fsdp"), lax.axis_index("dp")

        def span(i):
            return pl.ds(pl.multiple_of((dp ^ i) * depth, depth), depth)

        copies = [pltpu.make_async_copy(piece_refs[i], weight_ref.at[span(i)], sems.at[i]) for i in range(n_dp)]
        for copy in copies:
            copy.start()
        if gains[0].shape[1] == width:
            gain_out[...] = gain_refs[0][...].astype(WIDE)
        else:
            lines = jnp.concatenate([ref[...].astype(WIDE) for ref in gain_refs], axis=0)
            for i in range(n_dp):
                gain_out[:, span(i)] = lines[i : i + 1]
        gain = gain_out[...]
        for j in range(n):
            normed_ref[j] = norm_rows(row_refs[j][...], gain)
        for copy in copies:
            copy.wait()
        weights = weight_ref[...]
        loss = jnp.zeros((1, 1), WIDE)
        for j in range(n):
            slopes, part = softmax_rows(normed_ref[j], weights, label_ref, me ^ j, length_ref[dp])
            slope_ref[j] = slopes
            loss = loss + part
        loss_ref[...] = jnp.broadcast_to(loss, loss_ref.shape)

    return pl.pallas_call(
        body,
        in_specs=[SMEM] + [VMEM] * (1 + n_gain + n) + [ANY] * n_dp,
        out_specs=[VMEM] * 5,
        out_shape=[
            jax.ShapeDtypeStruct((8, 128), WIDE),
            jax.ShapeDtypeStruct((1, width), WIDE),
            jax.ShapeDtypeStruct((width, classes), HALF),
            jax.ShapeDtypeStruct((n, height, width), HALF),
            jax.ShapeDtypeStruct((n, height, classes), HALF),
        ],
        scratch_shapes=[pltpu.SemaphoreType.DMA((n_dp,))],
        cost_estimate=cost(NEAR),
        compiler_params=params(20),
        name="forward_near",
    )(lengths, labels, *gains, *rows, *pieces)


def forward_far(lengths, labels, gain, weights, pairs, relayed, normed, slopes, loss, n_dp):
    n = len(pairs)
    n_near, height, width = normed.shape
    classes = weights.shape[1]
    depth = width // n_dp
    blocks = n_near + 2 * n

    def body(*refs):
        length_ref, label_ref, gain_ref, weight_ref = refs[:4]
        pair_refs, side_refs, refs = refs[4 : 4 + n], refs[4 + n : 4 + 2 * n], refs[4 + 2 * n :]
        near_normed, near_slopes, near_loss, loss_ref, slope_ref = refs[:5]
        part_refs, (normed_ref, slopes_ref, partial_ref) = refs[5:-3], refs[-3:]
        me, dp = lax.axis_index("fsdp"), lax.axis_index("dp")
        gain, weights = gain_ref[...], weight_ref[...]
        count = length_ref[0]
        for d in range(1, n_dp):
            count = count + length_ref[d]
        for j in range(n_near):
            normed_ref[j * height : (j + 1) * height, :] = near_normed[j]
            slopes_ref[j * height : (j + 1) * height, :] = near_slopes[j]
        loss = near_loss[:1, :1]
        for j in range(2 * n):
            at = slice((n_near + j) * height, (n_near + j + 1) * height)
            normed_ref[at, :] = norm_rows(side_refs[j // 2][...] if j % 2 else pair_refs[j // 2][0], gain)
        for j in range(2 * n):
            at = slice((n_near + j) * height, (n_near + j + 1) * height)
            new, part = softmax_rows(normed_ref[at, :], weights, label_ref, me ^ (n_near + j), length_ref[dp])
            slope_ref[j] = new
            slopes_ref[at, :] = new
            loss = loss + part
        loss = jnp.broadcast_to(loss / (count.astype(WIDE) * blocks), (1, classes))
        loss_ref[...] = jnp.broadcast_to(loss, loss_ref.shape)
        step = min(256, width)
        for at in range(0, width, step):
            partial_ref[at : at + step, :] = lax.dot_general(
                normed_ref[:, at : at + step],
                slopes_ref[...],
                (((0,), (0,)), ((), ())),
                preferred_element_type=WIDE,
            ).astype(HALF)
        for i in range(n_dp):
            start = pl.multiple_of((dp ^ i) * depth, depth)
            part_refs[i][:depth, :] = partial_ref[pl.ds(start, depth), :]
        part_refs[n_dp - 1][depth:, :] = split_rows(loss, classes)

    out = pl.pallas_call(
        body,
        in_specs=[SMEM] + [VMEM] * (6 + 2 * n),
        out_specs=[VMEM] * (2 + n_dp),
        out_shape=[
            jax.ShapeDtypeStruct((8, classes), WIDE),
            jax.ShapeDtypeStruct((2 * n, height, classes), HALF),
        ]
        + [jax.ShapeDtypeStruct((depth, classes), HALF)] * (n_dp - 1)
        + [jax.ShapeDtypeStruct((depth + EXTRA, classes), HALF)],
        scratch_shapes=[
            pltpu.VMEM((blocks * height, width), HALF),
            pltpu.VMEM((blocks * height, classes), HALF),
            pltpu.VMEM((width, classes), HALF),
        ],
        cost_estimate=cost(FAR),
        compiler_params=params(24),
        name="forward_far",
    )(lengths, labels, gain, weights, *pairs, *relayed, normed, slopes, loss)
    return out[0], out[1], out[2:]


def grad_rows(values, slopes, weights, gain):
    values = values.astype(WIDE)
    inverse = lax.rsqrt(jnp.mean(values * values, axis=1, keepdims=True) + EPS)
    back = lax.dot_general(slopes, weights, (((1,), (1,)), ((), ())), preferred_element_type=WIDE)
    weighted = back * gain
    scale = inverse * inverse * inverse * jnp.mean(weighted * values, axis=1, keepdims=True)
    return (inverse * weighted - values * scale).astype(HALF)


def backward_far(gain, weights, pairs, relayed, slopes):
    n = len(pairs)
    shape = pairs[0].shape

    def body(gain_ref, weight_ref, slope_ref, *refs):
        for j in range(2 * n):
            values = refs[n + j // 2][...] if j % 2 else refs[j // 2][0]
            refs[2 * n + j // 2][j % 2] = grad_rows(values, slope_ref[j], weight_ref[...], gain_ref[...])

    return pl.pallas_call(
        body,
        in_specs=[VMEM] * (3 + 2 * n),
        out_specs=[VMEM] * n,
        out_shape=[jax.ShapeDtypeStruct(shape, HALF)] * n,
        cost_estimate=cost(BACK_FAR),
        compiler_params=params(20),
        name="backward_far",
    )(gain, weights, slopes, *pairs, *relayed)


def backward_near(gain, weights, rows, slopes, after):
    n = len(rows)

    def body(gain_ref, weight_ref, slope_ref, *refs):
        for j in range(n):
            refs[n + len(after) + j][...] = grad_rows(refs[j][...], slope_ref[j], weight_ref[...], gain_ref[...])

    return pl.pallas_call(
        body,
        in_specs=[VMEM] * (3 + n) + [ANY] * len(after),
        out_specs=[VMEM] * n,
        out_shape=[jax.ShapeDtypeStruct(rows[0].shape, HALF)] * n,
        cost_estimate=cost(BACK_NEAR),
        compiler_params=params(20),
        name="backward_near",
    )(gain, weights, slopes, *rows, *after)


def fold(terms, loss=None, held=(), after=(), last=False):
    depth, classes = terms[0].shape
    n = len(terms)
    n_loss = 0 if loss is None else 1
    carries = n_loss and not last

    def body(*refs):
        ins, loss_in = refs[:n], refs[n : n + n_loss]
        outs = refs[n + n_loss + len(held) + len(after) :]
        total = ins[0][...].astype(WIDE)
        for ref in ins[1:]:
            total = total + ref[:depth, :].astype(WIDE)
        outs[0][:depth, :] = total.astype(outs[0].dtype)
        if n_loss:
            extra = ins[-1][depth:, :].astype(WIDE)
            value = loss_in[0][:1, :] + (extra[:1] + extra[1:2] + extra[2:3])
            outs[1][...] = jnp.broadcast_to(value[:, : outs[1].shape[1]], outs[1].shape)
            if carries:
                outs[0][depth:, :] = split_rows(value, classes)

    shapes = [jax.ShapeDtypeStruct((depth + (EXTRA if carries else 0), classes), WIDE if last else HALF)]
    if n_loss:
        shapes.append(jax.ShapeDtypeStruct((8, 128) if last else loss.shape, WIDE))
    out = pl.pallas_call(
        body,
        in_specs=[VMEM] * (n + n_loss) + [ANY] * (len(held) + len(after)),
        out_specs=[VMEM] * (1 + n_loss) + [ANY] * len(held),
        out_shape=shapes + [jax.ShapeDtypeStruct(h.shape, h.dtype) for h in held],
        input_output_aliases={n + n_loss + i: 1 + n_loss + i for i in range(len(held))},
        cost_estimate=cost(FOLD),
        compiler_params=params(8),
        name="fold",
    )(*terms, *([loss] if n_loss else []), *held, *after)
    return out[0], (out[1] if n_loss else None), out[1 + n_loss :]


def hold(gains, piece, after):
    rows = sum(g.shape[0] for g in gains)

    def body(*refs):
        if gains:
            refs[-2][...] = jnp.concatenate([ref[...] for ref in refs[: len(gains)]], axis=0)

    out = pl.pallas_call(
        body,
        in_specs=[VMEM] * len(gains) + [ANY] * (1 + len(after)),
        out_specs=[VMEM] * bool(gains) + [ANY],
        out_shape=[jax.ShapeDtypeStruct((rows, g.shape[1]), HALF) for g in gains[:1]]
        + [jax.ShapeDtypeStruct(piece.shape, HALF)],
        input_output_aliases={len(gains): len(gains[:1])},
        cost_estimate=cost(HOLD),
        compiler_params=params(8),
        name="hold",
    )(*gains, piece, *after)
    return out[0], out[-1]


def per_device(n_dp, n_fsdp, hidden, head, gain, targets, lengths):
    inner = 2
    line = n_dp // inner
    n_pairs = n_fsdp // 2 - 1

    def swap(value, axis, offset):
        size = n_dp if axis == "dp" else n_fsdp
        return lax.ppermute(value, axis, [(i, i ^ offset) for i in range(size)])

    small = gain.shape[1] % 128 == 0 and line == 4
    gains = [gain, swap(gain, "dp", 1)] if small else [gain]
    pieces = [None] * n_dp
    pieces[0] = head[0]
    for o in sorted(range(1, line), key=lambda o: (bin(o).count("1"), -o)):
        bit = o & -o
        if small and o == 3:
            break
        pieces[o * inner] = swap(pieces[(o ^ bit) * inner], "dp", bit * inner)
    own, side, *pairs = unpack(hidden)
    pairs = [swap(pair, "fsdp", 2 * i + 2) for i, pair in enumerate(pairs)]
    for o in range(line):
        if small and o == 1:
            gain, pieces[2] = hold(gains, pieces[2], [own, pieces[1]])
        if pieces[o * inner] is not None:
            pieces[o * inner + 1] = swap(pieces[o * inner], "dp", 1)
    if small:
        gains = [gain, swap(gain, "dp", 2)]
        gain, side = hold(gains, side, [pieces[4]])
        pieces[6] = hold([], swap(pieces[4], "dp", 2), [pieces[3], pieces[5]])[1]
        pieces[7] = swap(pieces[6], "dp", 1)
        gains = [gain, swap(gain, "dp", 4)]
    else:
        gains = [lax.all_gather(gain, "dp", axis=1, tiled=True)]
    side = swap(side, "fsdp", 1)
    relayed = [swap(take(pair), "fsdp", 1) for pair in pairs]

    height = targets.shape[0] // n_fsdp
    labels = targets.T if height % 128 == 0 else targets.reshape(n_fsdp, height)
    loss, gain_row, weights, normed, near_slopes = forward_near(lengths, labels, gains, [own, side], pieces)
    loss, far_slopes, parts = forward_far(
        lengths, labels, gain_row, weights, pairs, relayed, normed, near_slopes, loss, n_dp
    )

    far = backward_far(gain_row, weights, pairs, relayed, far_slopes)
    near = None
    across = [None] * line
    waiting = list(range(line - 1, -1, -1))
    for o in (waiting.pop(0), waiting.pop(0)):
        across[o] = swap(parts[o * inner + 1], "dp", 1)
    came = [[] for _ in range(line)]
    rides = line - 1
    order = far[-1:]
    for o in range(line - 1, 0, -1):
        held = [parts[waiting[0] * inner + 1]] if waiting else []
        if o == rides:
            piece, loss, held = fold([parts[o * inner], across[o], *came[o]], loss, held, order)
        else:
            piece, _, held = fold([parts[o * inner], *came[o], across[o]], None, held, order)
        if near is None:
            near = backward_near(gain_row, weights, [own, side], near_slopes, [loss])
        bit, order = o & -o, [piece]
        moved = swap(piece, "dp", bit * inner)
        if o == rides:
            rides = o ^ bit
            came[rides] = [*came[rides], moved]
        else:
            came[o ^ bit] = [moved, *came[o ^ bit]]
        if held:
            across[waiting.pop(0)] = swap(held[0], "dp", 1)
    grad_head, loss, _ = fold([parts[0], across[0], *came[0]], loss, last=True)

    far = [swap(pair, "fsdp", 2 * i + 2) for i, pair in enumerate(far)]
    relayed = [swap(take(pair, came[0][-1:]), "fsdp", 1) for pair in far]
    grad_hidden = pack(near[0], swap(near[1], "fsdp", 1), far, relayed)

    bit = n_fsdp // 2
    while bit:
        loss = loss + swap(loss, "fsdp", bit)
        bit //= 2
    return loss[0, 0], grad_hidden, grad_head[None]


def solution(mesh):
    n_dp, n_fsdp = mesh.shape["dp"], mesh.shape["fsdp"]
    placed = (
        P(("dp", "fsdp"), None, None),
        P("fsdp", "dp", None),
        P("fsdp", "dp"),
        P("dp", "fsdp"),
        P(),
    )
    return jax.shard_map(
        lambda *args: per_device(n_dp, n_fsdp, *args),
        mesh=mesh,
        in_specs=placed,
        out_specs=(P(), P(("dp", "fsdp"), None, None), P("fsdp", "dp", None)),
        check_vma=False,
    )
```

time: 174 us -> 98.8 us (0.57)
  blocking collectives: 77.5 us -> 0 us
  waiting for transfers between devices: 15.8 us -> 48.2 us
  local copies, waits for them, and re-layouts: 27.2 us -> 1.58 us
  starting transfers between devices: 7.89 us -> 29 us
  Pallas kernels: 0 us -> 19 us
  matrix products: 16.2 us -> 0 us
  between operations: 16.6 us -> 0.81 us
  other arithmetic: 12.1 us -> 0.01 us
    psum x1 -> x0, blocking collectives: 55.8 us -> none  [per_device(): summed = lax.psum(local, ('dp', 'fsdp'))]
    ppermute x0 -> x25, waiting for transfers between devices: none -> 48.2 us  [swap(): return lax.ppermute(value, axis, [(i, i ^ offset) for i in range(size)])]
    ppermute x0 -> x25, starting transfers between devices: none -> 29 us  [swap(): return lax.ppermute(value, axis, [(i, i ^ offset) for i in range(size)])]
    all_gather x1 -> x0, blocking collectives: 21.7 us -> none  [per_device(): gains = lax.all_gather(gain[0], 'dp', axis=0, tiled=True)]
    unnamed x19 -> x12, local copies, waits for them, and re-layouts: 21.3 us -> 1.06 us
    pallas_call x0 -> x15, Pallas kernels: none -> 19 us  [the longest x1 4.92 us: forward_far(): pl.pallas_call(body, in_specs=[SMEM] + [VMEM] * (6 + 2 * n), out_specs=[V...]
    dot_general x3 -> x0, matrix products: 16.2 us -> none  [the longest x1 6.79 us: per_device(): lax.dot_general(slopes, lax.all_gather(head[0], 'dp', axis=0, tiled=True)...]
    all_gather x1 -> x0, waiting for transfers between devices: 12.4 us -> none  [per_device(): weights = lax.all_gather(head[0], 'dp', axis=0, tiled=True)]
  transfers between devices with their start and end apart: 4 -> 25, of which waited for: 2 -> 14; matrix products, arithmetic and copies ran while one was open for 23% -> 1% of each run, Pallas kernels for 0% -> 6%
where the time goes in v2:
time: 98.8 us; the launch traced here: 98.6 us
  waiting for transfers between devices  48.2 us (49%)
  starting transfers between devices  29 us (29%)
  Pallas kernels  19 us (19%)
  local copies, waits for them, and re-layouts  1.58 us (2%)
    ppermute x25, waiting for transfers between devices, swap(): return lax.ppermute(value, axis, [(i, i ^ offset) for i in range(size)])  48.2 us
    ppermute x25, starting transfers between devices, swap(): return lax.ppermute(value, axis, [(i, i ^ offset) for i in range(size)])  29 us
    pallas_call x1, Pallas kernels, forward_far(): pl.pallas_call(body, in_specs=[SMEM] + [VMEM] * (6 + 2 * n), out_specs=[V...  4.92 us
    pallas_call x1, Pallas kernels, unpack(): pl.pallas_call(body, in_specs=[ANY], out_specs=[VMEM] * (positions // 2 +...  3.61 us
    pallas_call x1, Pallas kernels, forward_near(): pl.pallas_call(body, in_specs=[SMEM] + [VMEM] * (1 + n_gain + n) + [ANY]...  3.47 us
    pallas_call x1, Pallas kernels, pack(): pl.pallas_call(body, grid=(frames // chunk,), in_specs=[flat_spec] * 2 +...  2.53 us
  transfers between devices with their start and end apart: 25, of which 14 were waited for; matrix products, arithmetic and copies ran while one was open for 1% of the time, Pallas kernels for 6%

profile of v2, /device:TPU:0, one launch (start us, length us, event | category | flops | bytes accessed | tf_op | source)
XLA Modules:
  0.0 98.6 jit_solution(333377139612790118)
XLA Ops:
  0.7 3.6 %unpack.1 = (bf16[256,1024]{1,0:T(8,128)(2,1)}, bf16[256,1024]{1,0:T(8,128)(2,1)}, bf16[2,256,1024]{2,1,0:T(8,128)(2,1)}) custom-call(bf16[256,4,1024]{2,1,0:T(4,128)(2,1)} %hidden_ref.1), custom_call_target="tpu_custom_call" | custom-call | flops 10000000 | tf_op jit(solution)/shard_map/unpack/pallas_call | solution.py:62
  4.3 3.0 %collective-permute-start.11 = (bf16[2,256,1024]{2,1,0:T(8,128)(2,1)}, bf16[2,256,1024]{2,1,0:T(8,128)(2,1)S(1)}, u32[]{:S(2)}, u32[]{:S(2)}) collective-permute-start(bf16[2,256,1024]{2,1,0:T(8,128)(2,1)} %get-tuple-element.43), channel_id=1, source_target_pairs={{0,2},{1,3},{2,0},{3,1},{4,6},{5,7},{6,4},{7,5},{8,10},{9,11},{10,... | collective-permute-start | bytes 3145736 | tf_op jit(solution)/shard_map/ppermute | solution.py:394
  7.3 1.5 %collective-permute-start.2 = (bf16[128,1024]{1,0:T(8,128)(2,1)S(1)}, bf16[128,1024]{1,0:T(8,128)(2,1)S(1)}, u32[]{:S(2)}, u32[]{:S(2)}) collective-permute-start(bf16[128,1024]{1,0:T(8,128)(2,1)S(1)} %bitcast.6), channel_id=1, source_target_pairs={{0,4},{4,0},{8,12},{12,8},{16,20},{20,16},{24,28},{28,24},{1,5},{5... | collective-permute-start | bytes 786440 | tf_op jit(solution)/shard_map/ppermute | solution.py:394
  8.8 1.6 %collective-permute-start.1 = (bf16[128,1024]{1,0:T(8,128)(2,1)S(1)}, bf16[128,1024]{1,0:T(8,128)(2,1)S(1)}, u32[]{:S(2)}, u32[]{:S(2)}) collective-permute-start(bf16[128,1024]{1,0:T(8,128)(2,1)S(1)} %bitcast.7), channel_id=1, source_target_pairs={{0,8},{4,12},{8,0},{12,4},{16,24},{20,28},{24,16},{28,20},{1,9},{5... | collective-permute-start | bytes 786440 | tf_op jit(solution)/shard_map/ppermute | solution.py:394
  10.4 2.6 %collective-permute-start.4 = (bf16[128,1024]{1,0:T(8,128)(2,1)S(1)}, bf16[128,1024]{1,0:T(8,128)(2,1)S(1)}, u32[]{:S(2)}, u32[]{:S(2)}) collective-permute-start(bf16[128,1024]{1,0:T(8,128)(2,1)S(1)} %bitcast.8), channel_id=1, source_target_pairs={{0,16},{4,20},{8,24},{12,28},{16,0},{20,4},{24,8},{28,12},{1,17},{... | collective-permute-start | bytes 786440 | tf_op jit(solution)/shard_map/ppermute | solution.py:394
  13.5 3.0 %collective-permute-done.refs_1_ = bf16[1,128]{1,0:T(2,128)(2,1)S(1)} collective-permute-done((bf16[1,128]{1,0:T(2,128)(2,1)S(1)}, bf16[1,128]{1,0:T(2,128)(2,1)S(1)}, u32[]{:S(2)}, u32[]{:S(2)}) %collective-permute-start) | collective-permute-done | bytes 288 | tf_op jit(solution)/shard_map/ppermute | solution.py:394
  16.5 5.3 %collective-permute-done.1.refs_2_ = bf16[128,1024]{1,0:T(8,128)(2,1)S(1)} collective-permute-done((bf16[128,1024]{1,0:T(8,128)(2,1)S(1)}, bf16[128,1024]{1,0:T(8,128)(2,1)S(1)}, u32[]{:S(2)}, u32[]{:S(2)}) %collective-permute-start.1) | collective-permute-done | bytes 262176 | tf_op jit(solution)/shard_map/ppermute | solution.py:394
  21.8 1.0 %copy-done = bf16[256,1024]{1,0:T(8,128)(2,1)S(1)} copy-done((bf16[256,1024]{1,0:T(8,128)(2,1)S(1)}, bf16[256,1024]{1,0:T(8,128)(2,1)}, u32[]{:S(2)}) %copy-start) | copy-done | bytes 524312
  23.5 0.7 collective-permute-done.4.refs_3_.refs_10_
  24.2 1.2 %collective-permute-start.9 = (bf16[128,1024]{1,0:T(8,128)(2,1)S(1)}, bf16[128,1024]{1,0:T(8,128)(2,1)S(1)}, u32[]{:S(2)}, u32[]{:S(2)}) collective-permute-start(bf16[128,1024]{1,0:T(8,128)(2,1)S(1)} %collective-permute-done.4.refs_3_.refs_10_), channel_id=1, source_target_pairs={{0,8},{4,12},{8,0},{12,4},{16,24},{20,28},{24,16},{28,20},{1,9},{5... | collective-permute-start | bytes 786440 | tf_op jit(solution)/shard_map/ppermute | solution.py:394
  25.5 1.5 %collective-permute-start.8 = (bf16[128,1024]{1,0:T(8,128)(2,1)S(1)}, bf16[128,1024]{1,0:T(8,128)(2,1)S(1)}, u32[]{:S(2)}, u32[]{:S(2)}) collective-permute-start(bf16[128,1024]{1,0:T(8,128)(2,1)S(1)} %collective-permute-done.4.refs_3_.refs_10_), channel_id=1, source_target_pairs={{0,4},{4,0},{8,12},{12,8},{16,20},{20,16},{24,28},{28,24},{1,5},{5... | collective-permute-start | bytes 786440 | tf_op jit(solution)/shard_map/ppermute | solution.py:394
  27.1 3.6 %collective-permute-done.9.refs_0_ = bf16[128,1024]{1,0:T(8,128)(2,1)S(1)} collective-permute-done((bf16[128,1024]{1,0:T(8,128)(2,1)S(1)}, bf16[128,1024]{1,0:T(8,128)(2,1)S(1)}, u32[]{:S(2)}, u32[]{:S(2)}) %collective-permute-start.9) | collective-permute-done | bytes 262176 | tf_op jit(solution)/shard_map/ppermute | solution.py:394
  30.6 4.4 %collective-permute-done.8.refs_2_.refs_11_ = bf16[128,1024]{1,0:T(8,128)(2,1)S(1)} collective-permute-done((bf16[128,1024]{1,0:T(8,128)(2,1)S(1)}, bf16[128,1024]{1,0:T(8,128)(2,1)S(1)}, u32[]{:S(2)}, u32[]{:S(2)}) %collective-permute-start.8) | collective-permute-done | bytes 262176 | tf_op jit(solution)/shard_map/ppermute | solution.py:394
  35.6 3.3 %collective-permute-start.5 = (bf16[4,128]{1,0:T(4,128)(2,1)S(1)}, bf16[4,128]{1,0:T(4,128)(2,1)S(1)}, u32[]{:S(2)}, u32[]{:S(2)}) collective-permute-start(bf16[4,128]{1,0:T(4,128)(2,1)S(1)} %get-tuple-element.38.refs_2_), channel_id=1, source_target_pairs={{0,16},{4,20},{8,24},{12,28},{16,0},{20,4},{24,8},{28,12},{1,17},{... | collective-permute-start | bytes 3080 | tf_op jit(solution)/shard_map/ppermute | solution.py:394
  39.0 1.4 %collective-permute-done.5.refs_3_ = bf16[4,128]{1,0:T(4,128)(2,1)S(1)} collective-permute-done((bf16[4,128]{1,0:T(4,128)(2,1)S(1)}, bf16[4,128]{1,0:T(4,128)(2,1)S(1)}, u32[]{:S(2)}, u32[]{:S(2)}) %collective-permute-start.5) | collective-permute-done | bytes 1056 | tf_op jit(solution)/shard_map/ppermute | solution.py:394
  40.5 1.0 %collective-permute-done.10.refs_13_ = bf16[128,1024]{1,0:T(8,128)(2,1)S(1)} collective-permute-done((bf16[128,1024]{1,0:T(8,128)(2,1)S(1)}, bf16[128,1024]{1,0:T(8,128)(2,1)S(1)}, u32[]{:S(2)}, u32[]{:S(2)}) %collective-permute-start.10) | collective-permute-done | bytes 262176 | tf_op jit(solution)/shard_map/ppermute | solution.py:394
  41.5 3.5 %forward_near.1 = (f32[8,128]{1,0:T(8,128)S(1)}, f32[1,1024]{1,0:T(1,128)S(1)}, bf16[1024,1024]{1,0:T(8,128)(2,1)S(1)}, bf16[2,256,1024]{2,1,0:T(8,128)(2,1)S(1)}, bf16[2,256,1024]{2,1,0:T(8,128)(2,1)S(1)}) custom-call(s32[8]{0:T(128)S(1)} %copy-done.4, s32[1,1024]{1,0:T(1,128)S(1)} %bitcast.4, bf16[4,128]{1,0:T(4,128)(2,1)S(1)} %get-tuple-element.38.refs_2_, ...), custom_call_target="tpu_custom_call" | custom-call | flops 10000000000 | tf_op jit(solution)/shard_map/forward_near/pallas_call | solution.py:198
  45.0 4.9 %forward_far.1 = (f32[8,1024]{1,0:T(8,128)S(1)}, bf16[2,256,1024]{2,1,0:T(8,128)(2,1)S(1)}, bf16[128,1024]{1,0:T(8,128)(2,1)S(1)}, bf16[128,1024]{1,0:T(8,128)(2...) custom-call(s32[8]{0:T(128)S(1)} %copy-done.4, ...), custom_call_target="tpu_custom_call" | custom-call | flops 10000000 | tf_op jit(solution)/shard_map/forward_far/pallas_call | solution.py:261
  49.9 1.6 %backward_far.1.refs_4_ = bf16[2,256,1024]{2,1,0:T(8,128)(2,1)S(1)} custom-call(f32[1,1024]{1,0:T(1,128)S(1)} %get-tuple-element.41.refs_2_.gain_ref, bf16[1024,1024]{1,0:T(8,128)(2,1)S(1)} %get-tuple-element.42.refs_3_.weight_ref, bf16[2,256,1024]{2,1,0:T(8,128)(2,1)S(1)} %get-tuple-element.54.slope_ref, ...), custom_call_target="tpu_custom_call" | custom-call | flops 10000000 | tf_op jit(solution)/shard_map/backward_far/pallas_call | solution.py:301
  52.7 5.9 %collective-permute-done.14.refs_1_ = bf16[136,1024]{1,0:T(8,128)(2,1)S(1)} collective-permute-done((bf16[136,1024]{1,0:T(8,128)(2,1)S(1)}, bf16[136,1024]{1,0:T(8,128)(2,1)S(1)}, u32[]{:S(2)}, u32[]{:S(2)}) %collective-permute-start.14) | collective-permute-done | bytes 278560 | tf_op jit(solution)/shard_map/ppermute | solution.py:394
  58.7 2.1 %collective-permute-start.15 = (bf16[136,1024]{1,0:T(8,128)(2,1)S(1)}, bf16[136,1024]{1,0:T(8,128)(2,1)S(1)}, u32[]{:S(2)}, u32[]{:S(2)}) collective-permute-start(bf16[136,1024]{1,0:T(8,128)(2,1)S(1)} %get-tuple-element.55.refs_5_), channel_id=1, source_target_pairs={{0,8},{4,12},{8,0},{12,4},{16,24},{20,28},{24,16},{28,20},{1,9},{5... | collective-permute-start | bytes 835592 | tf_op jit(solution)/shard_map/ppermute | solution.py:394
  61.1 6.0 %collective-permute-done.13.refs_1_ = bf16[128,1024]{1,0:T(8,128)(2,1)S(1)} collective-permute-done((bf16[128,1024]{1,0:T(8,128)(2,1)S(1)}, bf16[128,1024]{1,0:T(8,128)(2,1)S(1)}, u32[]{:S(2)}, u32[]{:S(2)}) %collective-permute-start.13) | collective-permute-done | bytes 262176 | tf_op jit(solution)/shard_map/ppermute | solution.py:394
  67.3 6.1 %collective-permute-start.19 = (bf16[136,1024]{1,0:T(8,128)(2,1)S(1)}, bf16[136,1024]{1,0:T(8,128)(2,1)S(1)}, u32[]{:S(2)}, u32[]{:S(2)}) collective-permute-start(bf16[136,1024]{1,0:T(8,128)(2,1)S(1)} %get-tuple-element.61.refs_2_), channel_id=1, source_target_pairs={{0,16},{4,20},{8,24},{12,28},{16,0},{20,4},{24,8},{28,12},{1,17},{... | collective-permute-start | bytes 835592 | tf_op jit(solution)/shard_map/ppermute | solution.py:394
  73.4 1.6 %backward_near.1 = (bf16[256,1024]{1,0:T(8,128)(2,1)S(1)}, bf16[256,1024]{1,0:T(8,128)(2,1)S(1)}) custom-call(f32[1,1024]{1,0:T(1,128)S(1)} %get-tuple-element.41.refs_2_.gain_ref, bf16[1024,1024]{1,0:T(8,128)(2,1)S(1)} %get-tuple-element.42.refs_3_.weight_ref, bf16[2,256,1024]{2,1,0:T(8,128)(2,1)S(1)} %get-tuple-element.45.refs_7_.slope_ref, ...), custom_call_target="tpu_custom_call" | custom-call | flops 10000000 | tf_op jit(solution)/shard_map/backward_near/pallas_call | solution.py:319
  75.0 5.8 %collective-permute-done.19.refs_3_.refs_1_ = bf16[136,1024]{1,0:T(8,128)(2,1)S(1)} collective-permute-done((bf16[136,1024]{1,0:T(8,128)(2,1)S(1)}, bf16[136,1024]{1,0:T(8,128)(2,1)S(1)}, u32[]{:S(2)}, u32[]{:S(2)}) %collective-permute-start.19) | collective-permute-done | bytes 278560 | tf_op jit(solution)/shard_map/ppermute | solution.py:394
  81.2 1.0 %collective-permute-start.18 = (bf16[128,1024]{1,0:T(8,128)(2,1)S(1)}, bf16[128,1024]{1,0:T(8,128)(2,1)S(1)}, u32[]{:S(2)}, u32[]{:S(2)}) collective-permute-start(bf16[128,1024]{1,0:T(8,128)(2,1)S(1)} %fold.6), channel_id=1, source_target_pairs={{0,8},{4,12},{8,0},{12,4},{16,24},{20,28},{24,16},{28,20},{1,9},{5... | collective-permute-start | bytes 786440 | tf_op jit(solution)/shard_map/ppermute | solution.py:394
  82.2 7.6 %collective-permute-done.16.refs_1_ = bf16[128,1024]{1,0:T(8,128)(2,1)S(1)} collective-permute-done((bf16[128,1024]{1,0:T(8,128)(2,1)S(1)}, bf16[128,1024]{1,0:T(8,128)(2,1)S(1)}, u32[]{:S(2)}, u32[]{:S(2)}) %collective-permute-start.16) | collective-permute-done | bytes 262176 | tf_op jit(solution)/shard_map/ppermute | solution.py:394
  89.9 0.9 fold.7
  90.8 1.5 %collective-permute-start.20 = (f32[8,128]{1,0:T(8,128)S(1)}, f32[8,128]{1,0:T(8,128)S(1)}, u32[]{:S(2)}, u32[]{:S(2)}) collective-permute-start(f32[8,128]{1,0:T(8,128)S(1)} %get-tuple-element.63), channel_id=1, source_target_pairs={{0,2},{1,3},{2,0},{3,1},{4,6},{5,7},{6,4},{7,5},{8,10},{9,11},{10,... | collective-permute-start | bytes 12296 | tf_op jit(solution)/shard_map/ppermute | solution.py:394
  92.3 2.1 %collective-permute-done.20 = f32[8,128]{1,0:T(8,128)S(1)} collective-permute-done((f32[8,128]{1,0:T(8,128)S(1)}, f32[8,128]{1,0:T(8,128)S(1)}, u32[]{:S(2)}, u32[]{:S(2)}) %collective-permute-start.20) | collective-permute-done | bytes 4128 | tf_op jit(solution)/shard_map/ppermute | solution.py:394
  94.4 1.2 %collective-permute-done.21 = f32[8,128]{1,0:T(8,128)S(1)} collective-permute-done((f32[8,128]{1,0:T(8,128)S(1)}, f32[8,128]{1,0:T(8,128)S(1)}, u32[]{:S(2)}, u32[]{:S(2)}) %collective-permute-start.21) | collective-permute-done | bytes 4128 | tf_op jit(solution)/shard_map/ppermute | solution.py:394
  96.1 2.5 %pack.1 = bf16[256,4,1024]{2,1,0:T(4,128)(2,1)} custom-call(bf16[256,1024]{1,0:T(8,128)(2,1)S(1)} %get-tuple-element.64.own_ref, bf16[256,1024]{1,0:T(8,128)(2,1)S(1)} %collective-permute-done.22.side_ref, bf16[2,256,1024]{2,1,0:T(8,128)(2,1)S(1)} %collective-permute-done.23.refs_0_, bf16[256,1024]{1,0:T(8,128)(2,1)S(1)} %collective-permute-done.24.refs_1_), custom_call_target="tpu_custom_call" | custom-call | flops 10000000 | tf_op jit(solution)/shard_map/pack/pallas_call | solution.py:97
  (48 shorter events, 4.8 us)
Async XLA Ops:
  0.6 6.7 %copy-start.5 = (bf16[1,128,1024]{2,1,0:T(8,128)(2,1)S(1)}, bf16[1,128,1024]{2,1,0:T(8,128)(2,1)}, u32[]{:S(2)}) copy-start(bf16[1,128,1024]{2,1,0:T(8,128)(2,1)} %param.6) | copy-start | bytes 786436
  0.6 12.3 %copy-start.3 = (bf16[1,128]{1,0:T(2,128)(2,1)S(1)}, bf16[1,128]{1,0:T(2,128)(2,1)}, u32[]{:S(2)}) copy-start(bf16[1,128]{1,0:T(2,128)(2,1)} %refs_0_.3) | copy-start | bytes 772
  4.3 34.6 %collective-permute-start.11 = (bf16[2,256,1024]{2,1,0:T(8,128)(2,1)}, bf16[2,256,1024]{2,1,0:T(8,128)(2,1)S(1)}, u32[]{:S(2)}, u32[]{:S(2)}) collective-permute-start(bf16[2,256,1024]{2,1,0:T(8,128)(2,1)} %get-tuple-element.43), channel_id=1, source_target_pairs={{0,2},{1,3},{2,0},{3,1},{4,6},{5,7},{6,4},{7,5},{8,10},{9,11},{10,... | collective-permute-start | bytes 3145736 | tf_op jit(solution)/shard_map/ppermute | solution.py:394
  7.3 9.2 %collective-permute-start.2 = (bf16[128,1024]{1,0:T(8,128)(2,1)S(1)}, bf16[128,1024]{1,0:T(8,128)(2,1)S(1)}, u32[]{:S(2)}, u32[]{:S(2)}) collective-permute-start(bf16[128,1024]{1,0:T(8,128)(2,1)S(1)} %bitcast.6), channel_id=1, source_target_pairs={{0,4},{4,0},{8,12},{12,8},{16,20},{20,16},{24,28},{28,24},{1,5},{5... | collective-permute-start | bytes 786440 | tf_op jit(solution)/shard_map/ppermute | solution.py:394
  8.8 13.0 %collective-permute-start.1 = (bf16[128,1024]{1,0:T(8,128)(2,1)S(1)}, bf16[128,1024]{1,0:T(8,128)(2,1)S(1)}, u32[]{:S(2)}, u32[]{:S(2)}) collective-permute-start(bf16[128,1024]{1,0:T(8,128)(2,1)S(1)} %bitcast.7), channel_id=1, source_target_pairs={{0,8},{4,12},{8,0},{12,4},{16,24},{20,28},{24,16},{28,20},{1,9},{5... | collective-permute-start | bytes 786440 | tf_op jit(solution)/shard_map/ppermute | solution.py:394
  10.4 13.9 %collective-permute-start.4 = (bf16[128,1024]{1,0:T(8,128)(2,1)S(1)}, bf16[128,1024]{1,0:T(8,128)(2,1)S(1)}, u32[]{:S(2)}, u32[]{:S(2)}) collective-permute-start(bf16[128,1024]{1,0:T(8,128)(2,1)S(1)} %bitcast.8), channel_id=1, source_target_pairs={{0,16},{4,20},{8,24},{12,28},{16,0},{20,4},{24,8},{28,12},{1,17},{... | collective-permute-start | bytes 786440 | tf_op jit(solution)/shard_map/ppermute | solution.py:394
  13.0 3.5 %collective-permute-start = (bf16[1,128]{1,0:T(2,128)(2,1)S(1)}, bf16[1,128]{1,0:T(2,128)(2,1)S(1)}, u32[]{:S(2)}, u32[]{:S(2)}) collective-permute-start(bf16[1,128]{1,0:T(2,128)(2,1)S(1)} %copy-done.3), channel_id=1, source_target_pairs={{0,4},{4,0},{8,12},{12,8},{16,20},{20,16},{24,28},{28,24},{1,5},{5... | collective-permute-start | bytes 776 | tf_op jit(solution)/shard_map/ppermute | solution.py:394
  21.8 1.0 %copy-start = (bf16[256,1024]{1,0:T(8,128)(2,1)S(1)}, bf16[256,1024]{1,0:T(8,128)(2,1)}, u32[]{:S(2)}) copy-start(bf16[256,1024]{1,0:T(8,128)(2,1)} %get-tuple-element.35.refs_3_.refs_4_.refs_0_) | copy-start | bytes 1572868
  22.8 18.6 %copy-start.1 = (bf16[256,1024]{1,0:T(8,128)(2,1)S(1)}, bf16[256,1024]{1,0:T(8,128)(2,1)}, u32[]{:S(2)}) copy-start(bf16[256,1024]{1,0:T(8,128)(2,1)} %get-tuple-element.35.refs_3_.refs_4_.refs_0_) | copy-start | bytes 1572868
  22.8 18.6 %copy-start.2 = (s32[1024,1]{0,1:T(1,128)S(1)}, s32[1024,1]{0,1:T(1,128)}, u32[]{:S(2)}) copy-start(s32[1024,1]{0,1:T(1,128)} %param.8) | copy-start | bytes 12292
  22.8 18.6 %copy-start.4 = (s32[8]{0:T(128)S(1)}, s32[8]{0:T(128)}, u32[]{:S(2)}) copy-start(s32[8]{0:T(128)} %refs_0_.5) | copy-start | bytes 100
  22.8 4.1 %collective-permute-start.3 = (bf16[2,128]{1,0:T(2,128)(2,1)S(1)}, bf16[2,128]{1,0:T(2,128)(2,1)S(1)}, u32[]{:S(2)}, u32[]{:S(2)}) collective-permute-start(bf16[2,128]{1,0:T(2,128)(2,1)S(1)} %get-tuple-element.36.refs_0_), channel_id=1, source_target_pairs={{0,8},{4,12},{8,0},{12,4},{16,24},{20,28},{24,16},{28,20},{1,9},{5... | collective-permute-start | bytes 1544 | tf_op jit(solution)/shard_map/ppermute | solution.py:394
  22.9 12.2 %collective-permute-start.7 = (bf16[128,1024]{1,0:T(8,128)(2,1)S(1)}, bf16[128,1024]{1,0:T(8,128)(2,1)S(1)}, u32[]{:S(2)}, u32[]{:S(2)}) collective-permute-start(bf16[128,1024]{1,0:T(8,128)(2,1)S(1)} %get-tuple-element.40.refs_8_), channel_id=1, source_target_pairs={{0,4},{4,0},{8,12},{12,8},{16,20},{20,16},{24,28},{28,24},{1,5},{5... | collective-permute-start | bytes 786440 | tf_op jit(solution)/shard_map/ppermute | solution.py:394
  24.2 6.4 %collective-permute-start.9 = (bf16[128,1024]{1,0:T(8,128)(2,1)S(1)}, bf16[128,1024]{1,0:T(8,128)(2,1)S(1)}, u32[]{:S(2)}, u32[]{:S(2)}) collective-permute-start(bf16[128,1024]{1,0:T(8,128)(2,1)S(1)} %collective-permute-done.4.refs_3_.refs_10_), channel_id=1, source_target_pairs={{0,8},{4,12},{8,0},{12,4},{16,24},{20,28},{24,16},{28,20},{1,9},{5... | collective-permute-start | bytes 786440 | tf_op jit(solution)/shard_map/ppermute | solution.py:394
  25.5 9.6 %collective-permute-start.8 = (bf16[128,1024]{1,0:T(8,128)(2,1)S(1)}, bf16[128,1024]{1,0:T(8,128)(2,1)S(1)}, u32[]{:S(2)}, u32[]{:S(2)}) collective-permute-start(bf16[128,1024]{1,0:T(8,128)(2,1)S(1)} %collective-permute-done.4.refs_3_.refs_10_), channel_id=1, source_target_pairs={{0,4},{4,0},{8,12},{12,8},{16,20},{20,16},{24,28},{28,24},{1,5},{5... | collective-permute-start | bytes 786440 | tf_op jit(solution)/shard_map/ppermute | solution.py:394
  27.0 14.5 %collective-permute-start.6 = (bf16[256,1024]{1,0:T(8,128)(2,1)}, bf16[256,1024]{1,0:T(8,128)(2,1)S(1)}, u32[]{:S(2)}, u32[]{:S(2)}) collective-permute-start(bf16[256,1024]{1,0:T(8,128)(2,1)} %get-tuple-element.39), channel_id=1, source_target_pairs={{0,1},{1,0},{2,3},{3,2},{4,5},{5,4},{6,7},{7,6},{8,9},{9,8},{10,11... | collective-permute-start | bytes 1572872 | tf_op jit(solution)/shard_map/ppermute | solution.py:394
  35.1 6.4 %collective-permute-start.10 = (bf16[128,1024]{1,0:T(8,128)(2,1)S(1)}, bf16[128,1024]{1,0:T(8,128)(2,1)S(1)}, u32[]{:S(2)}, u32[]{:S(2)}) collective-permute-start(bf16[128,1024]{1,0:T(8,128)(2,1)S(1)} %hold.5.refs_12_), channel_id=1, source_target_pairs={{0,4},{4,0},{8,12},{12,8},{16,20},{20,16},{24,28},{28,24},{1,5},{5... | collective-permute-start | bytes 786440 | tf_op jit(solution)/shard_map/ppermute | solution.py:394
  35.6 4.8 %collective-permute-start.5 = (bf16[4,128]{1,0:T(4,128)(2,1)S(1)}, bf16[4,128]{1,0:T(4,128)(2,1)S(1)}, u32[]{:S(2)}, u32[]{:S(2)}) collective-permute-start(bf16[4,128]{1,0:T(4,128)(2,1)S(1)} %get-tuple-element.38.refs_2_), channel_id=1, source_target_pairs={{0,16},{4,20},{8,24},{12,28},{16,0},{20,4},{24,8},{28,12},{1,17},{... | collective-permute-start | bytes 3080 | tf_op jit(solution)/shard_map/ppermute | solution.py:394
  38.9 6.0 %collective-permute-start.12 = (bf16[256,1024]{1,0:T(8,128)(2,1)S(1)}, bf16[256,1024]{1,0:T(8,128)(2,1)S(1)}, u32[]{:S(2)}, u32[]{:S(2)}) collective-permute-start(bf16[256,1024]{1,0:T(8,128)(2,1)S(1)} %take.2), channel_id=1, source_target_pairs={{0,1},{1,0},{2,3},{3,2},{4,5},{5,4},{6,7},{7,6},{8,9},{9,8},{10,11... | collective-permute-start | bytes 1572872 | tf_op jit(solution)/shard_map/ppermute | solution.py:394
  51.5 29.4 %collective-permute-start.23 = (bf16[2,256,1024]{2,1,0:T(8,128)(2,1)S(1)}, bf16[2,256,1024]{2,1,0:T(8,128)(2,1)S(1)}, u32[]{:S(2)}, u32[]{:S(2)}) collective-permute-start(bf16[2,256,1024]{2,1,0:T(8,128)(2,1)S(1)} %backward_far.1.refs_4_), channel_id=1, source_target_pairs={{0,2},{1,3},{2,0},{3,1},{4,6},{5,7},{6,4},{7,5},{8,10},{9,11},{10,... | collective-permute-start | bytes 3145736 | tf_op jit(solution)/shard_map/ppermute | solution.py:394
  52.1 6.5 %collective-permute-start.14 = (bf16[136,1024]{1,0:T(8,128)(2,1)S(1)}, bf16[136,1024]{1,0:T(8,128)(2,1)S(1)}, u32[]{:S(2)}, u32[]{:S(2)}) collective-permute-start(bf16[136,1024]{1,0:T(8,128)(2,1)S(1)} %get-tuple-element.51), channel_id=1, source_target_pairs={{0,4},{4,0},{8,12},{12,8},{16,20},{20,16},{24,28},{28,24},{1,5},{5... | collective-permute-start | bytes 835592 | tf_op jit(solution)/shard_map/ppermute | solution.py:394
  58.7 8.4 %collective-permute-start.15 = (bf16[136,1024]{1,0:T(8,128)(2,1)S(1)}, bf16[136,1024]{1,0:T(8,128)(2,1)S(1)}, u32[]{:S(2)}, u32[]{:S(2)}) collective-permute-start(bf16[136,1024]{1,0:T(8,128)(2,1)S(1)} %get-tuple-element.55.refs_5_), channel_id=1, source_target_pairs={{0,8},{4,12},{8,0},{12,4},{16,24},{20,28},{24,16},{28,20},{1,9},{5... | collective-permute-start | bytes 835592 | tf_op jit(solution)/shard_map/ppermute | solution.py:394
  60.8 6.4 %collective-permute-start.13 = (bf16[128,1024]{1,0:T(8,128)(2,1)S(1)}, bf16[128,1024]{1,0:T(8,128)(2,1)S(1)}, u32[]{:S(2)}, u32[]{:S(2)}) collective-permute-start(bf16[128,1024]{1,0:T(8,128)(2,1)S(1)} %get-tuple-element.49), channel_id=1, source_target_pairs={{0,4},{4,0},{8,12},{12,8},{16,20},{20,16},{24,28},{28,24},{1,5},{5... | collective-permute-start | bytes 786440 | tf_op jit(solution)/shard_map/ppermute | solution.py:394
  67.3 13.6 %collective-permute-start.19 = (bf16[136,1024]{1,0:T(8,128)(2,1)S(1)}, bf16[136,1024]{1,0:T(8,128)(2,1)S(1)}, u32[]{:S(2)}, u32[]{:S(2)}) collective-permute-start(bf16[136,1024]{1,0:T(8,128)(2,1)S(1)} %get-tuple-element.61.refs_2_), channel_id=1, source_target_pairs={{0,16},{4,20},{8,24},{12,28},{16,0},{20,4},{24,8},{28,12},{1,17},{... | collective-permute-start | bytes 835592 | tf_op jit(solution)/shard_map/ppermute | solution.py:394
  73.4 7.7 %collective-permute-start.17 = (bf16[128,1024]{1,0:T(8,128)(2,1)S(1)}, bf16[128,1024]{1,0:T(8,128)(2,1)S(1)}, u32[]{:S(2)}, u32[]{:S(2)}) collective-permute-start(bf16[128,1024]{1,0:T(8,128)(2,1)S(1)} %get-tuple-element.60), channel_id=1, source_target_pairs={{0,4},{4,0},{8,12},{12,8},{16,20},{20,16},{24,28},{28,24},{1,5},{5... | collective-permute-start | bytes 786440 | tf_op jit(solution)/shard_map/ppermute | solution.py:394
  75.0 21.1 %collective-permute-start.22 = (bf16[256,1024]{1,0:T(8,128)(2,1)S(1)}, bf16[256,1024]{1,0:T(8,128)(2,1)S(1)}, u32[]{:S(2)}, u32[]{:S(2)}) collective-permute-start(bf16[256,1024]{1,0:T(8,128)(2,1)S(1)} %get-tuple-element.65), channel_id=1, source_target_pairs={{0,1},{1,0},{2,3},{3,2},{4,5},{5,4},{6,7},{7,6},{8,9},{9,8},{10,11... | collective-permute-start | bytes 1572872 | tf_op jit(solution)/shard_map/ppermute | solution.py:394
  80.9 15.2 %collective-permute-start.24 = (bf16[256,1024]{1,0:T(8,128)(2,1)S(1)}, bf16[256,1024]{1,0:T(8,128)(2,1)S(1)}, u32[]{:S(2)}, u32[]{:S(2)}) collective-permute-start(bf16[256,1024]{1,0:T(8,128)(2,1)S(1)} %take.3), channel_id=1, source_target_pairs={{0,1},{1,0},{2,3},{3,2},{4,5},{5,4},{6,7},{7,6},{8,9},{9,8},{10,11... | collective-permute-start | bytes 1572872 | tf_op jit(solution)/shard_map/ppermute | solution.py:394
  81.0 8.7 %collective-permute-start.16 = (bf16[128,1024]{1,0:T(8,128)(2,1)S(1)}, bf16[128,1024]{1,0:T(8,128)(2,1)S(1)}, u32[]{:S(2)}, u32[]{:S(2)}) collective-permute-start(bf16[128,1024]{1,0:T(8,128)(2,1)S(1)} %get-tuple-element.58), channel_id=1, source_target_pairs={{0,4},{4,0},{8,12},{12,8},{16,20},{20,16},{24,28},{28,24},{1,5},{5... | collective-permute-start | bytes 786440 | tf_op jit(solution)/shard_map/ppermute | solution.py:394
  81.2 8.7 %collective-permute-start.18 = (bf16[128,1024]{1,0:T(8,128)(2,1)S(1)}, bf16[128,1024]{1,0:T(8,128)(2,1)S(1)}, u32[]{:S(2)}, u32[]{:S(2)}) collective-permute-start(bf16[128,1024]{1,0:T(8,128)(2,1)S(1)} %fold.6), channel_id=1, source_target_pairs={{0,8},{4,12},{8,0},{12,4},{16,24},{20,28},{24,16},{28,20},{1,9},{5... | collective-permute-start | bytes 786440 | tf_op jit(solution)/shard_map/ppermute | solution.py:394
  90.8 3.6 %collective-permute-start.20 = (f32[8,128]{1,0:T(8,128)S(1)}, f32[8,128]{1,0:T(8,128)S(1)}, u32[]{:S(2)}, u32[]{:S(2)}) collective-permute-start(f32[8,128]{1,0:T(8,128)S(1)} %get-tuple-element.63), channel_id=1, source_target_pairs={{0,2},{1,3},{2,0},{3,1},{4,6},{5,7},{6,4},{7,5},{8,10},{9,11},{10,... | collective-permute-start | bytes 12296 | tf_op jit(solution)/shard_map/ppermute | solution.py:394
  94.4 1.2 %collective-permute-start.21 = (f32[8,128]{1,0:T(8,128)S(1)}, f32[8,128]{1,0:T(8,128)S(1)}, u32[]{:S(2)}, u32[]{:S(2)}) collective-permute-start(f32[8,128]{1,0:T(8,128)S(1)} %add.6), channel_id=1, source_target_pairs={{0,1},{1,0},{2,3},{3,2},{4,5},{5,4},{6,7},{7,6},{8,9},{9,8},{10,11... | collective-permute-start | bytes 12296 | tf_op jit(solution)/shard_map/ppermute | solution.py:394

commit v3 on v2

--- a/solution.py
+++ b/solution.py
@@ -13,7 +13,7 @@
 ANY = pl.BlockSpec(memory_space=pl.ANY)
 PACK_ROWS = 256
 EXTRA = 8
-UNPACK, PACK, NEAR, FAR, BACK_FAR, BACK_NEAR, FOLD, HOLD = 0.01, 0.01, 10, 0.01, 0.01, 0.01, 0.01, 0.01
+UNPACK, PACK, NEAR, FAR, BACKWARD, FOLD, HOLD, LAST, RELAY = 0.01, 0.01, 3, 0.01, 0.01, 0.01, 0.01, 3, 1.5
 
 
 def params(mib):
@@ -54,17 +54,13 @@
             moved = jnp.dot(pick, flat, preferred_element_type=WIDE).astype(HALF)
             for j in range(positions):
                 part = moved[j * chunk : (j + 1) * chunk]
-                if j < 2:
-                    outs[j][here, :] = part
-                else:
-                    outs[j // 2 + 1][j % 2, here, :] = part
+                outs[j][here, :] = part
 
     return pl.pallas_call(
         body,
         in_specs=[ANY],
-        out_specs=[VMEM] * (positions // 2 + 1),
-        out_shape=[jax.ShapeDtypeStruct((frames, width), HALF)] * 2
-        + [jax.ShapeDtypeStruct((2, frames, width), HALF)] * (positions // 2 - 1),
+        out_specs=[VMEM] * positions,
+        out_shape=[jax.ShapeDtypeStruct((frames, width), HALF)] * positions,
         scratch_shapes=[pltpu.VMEM(hidden.shape, HALF), pltpu.SemaphoreType.DMA((steps,))],
         cost_estimate=cost(UNPACK),
         compiler_params=params(58),
@@ -72,53 +68,33 @@
     )(hidden)
 
 
-def pack(own, side, pairs, relayed):
-    frames, width = own.shape
-    positions = 2 + 2 * len(pairs)
+def pack(parts):
+    frames, width = parts[0].shape
+    positions = len(parts)
     chunk = PACK_ROWS // positions
     rows = chunk * positions
-    n = len(pairs)
-
-    def body(own_ref, side_ref, *refs):
+
+    def body(*refs):
         me = lax.axis_index("fsdp")
         r = lax.broadcasted_iota(jnp.int32, (rows, rows), 0)
         c = lax.broadcasted_iota(jnp.int32, (rows, rows), 1)
         pick = (lax.rem(c, chunk) == lax.div(r, positions)) & (
             lax.rem(r, positions) == (lax.div(c, chunk) ^ me)
         )
-        parts = [own_ref[...], side_ref[...]]
-        for i in range(n):
-            parts += [refs[i][0], refs[n + i][...]]
-        flat = jnp.concatenate(parts, axis=0)
+        flat = jnp.concatenate([ref[...] for ref in refs[:-1]], axis=0)
         moved = jnp.dot(pick.astype(HALF), flat, preferred_element_type=WIDE).astype(HALF)
         refs[-1][...] = moved.reshape(chunk, positions, width)
 
-    flat_spec = pl.BlockSpec((chunk, width), lambda i: (i, 0))
     return pl.pallas_call(
         body,
         grid=(frames // chunk,),
-        in_specs=[flat_spec] * 2 + [pl.BlockSpec((1, chunk, width), lambda i: (0, i, 0))] * n + [flat_spec] * n,
+        in_specs=[pl.BlockSpec((chunk, width), lambda i: (i, 0))] * positions,
         out_specs=pl.BlockSpec((chunk, positions, width), lambda i: (i, 0, 0)),
         out_shape=jax.ShapeDtypeStruct((frames, positions, width), HALF),
         cost_estimate=cost(PACK),
         compiler_params=params(24),
         name="pack",
-    )(own, side, *pairs, *relayed)
-
-
-def take(pair, after=()):
-    def body(*refs):
-        refs[-1][...] = refs[0][1]
-
-    return pl.pallas_call(
-        body,
-        in_specs=[VMEM] + [ANY] * len(after),
-        out_specs=VMEM,
-        out_shape=jax.ShapeDtypeStruct(pair.shape[1:], pair.dtype),
-        cost_estimate=cost(HOLD),
-        compiler_params=params(8),
-        name="take",
-    )(pair, *after)
+    )(*parts)
 
 
 def split_rows(value, classes):
@@ -213,16 +189,16 @@
     )(lengths, labels, *gains, *rows, *pieces)
 
 
-def forward_far(lengths, labels, gain, weights, pairs, relayed, normed, slopes, loss, n_dp):
-    n = len(pairs)
+def forward_far(lengths, labels, gain, weights, rows, normed, slopes, loss, n_dp):
+    n = len(rows)
     n_near, height, width = normed.shape
     classes = weights.shape[1]
     depth = width // n_dp
-    blocks = n_near + 2 * n
+    blocks = n_near + n
 
     def body(*refs):
         length_ref, label_ref, gain_ref, weight_ref = refs[:4]
-        pair_refs, side_refs, refs = refs[4 : 4 + n], refs[4 + n : 4 + 2 * n], refs[4 + 2 * n :]
+        row_refs, refs = refs[4 : 4 + n], refs[4 + n :]
         near_normed, near_slopes, near_loss, loss_ref, slope_ref = refs[:5]
         part_refs, (normed_ref, slopes_ref, partial_ref) = refs[5:-3], refs[-3:]
         me, dp = lax.axis_index("fsdp"), lax.axis_index("dp")
@@ -234,10 +210,10 @@
             normed_ref[j * height : (j + 1) * height, :] = near_normed[j]
             slopes_ref[j * height : (j + 1) * height, :] = near_slopes[j]
         loss = near_loss[:1, :1]
-        for j in range(2 * n):
+        for j in range(n):
             at = slice((n_near + j) * height, (n_near + j + 1) * height)
-            normed_ref[at, :] = norm_rows(side_refs[j // 2][...] if j % 2 else pair_refs[j // 2][0], gain)
-        for j in range(2 * n):
+            normed_ref[at, :] = norm_rows(row_refs[j][...], gain)
+        for j in range(n):
             at = slice((n_near + j) * height, (n_near + j + 1) * height)
             new, part = softmax_rows(normed_ref[at, :], weights, label_ref, me ^ (n_near + j), length_ref[dp])
             slope_ref[j] = new
@@ -260,11 +236,11 @@
 
     out = pl.pallas_call(
         body,
-        in_specs=[SMEM] + [VMEM] * (6 + 2 * n),
+        in_specs=[SMEM] + [VMEM] * (6 + n),
         out_specs=[VMEM] * (2 + n_dp),
         out_shape=[
             jax.ShapeDtypeStruct((8, classes), WIDE),
-            jax.ShapeDtypeStruct((2 * n, height, classes), HALF),
+            jax.ShapeDtypeStruct((n, height, classes), HALF),
         ]
         + [jax.ShapeDtypeStruct((depth, classes), HALF)] * (n_dp - 1)
         + [jax.ShapeDtypeStruct((depth + EXTRA, classes), HALF)],
@@ -276,7 +252,7 @@
         cost_estimate=cost(FAR),
         compiler_params=params(24),
         name="forward_far",
-    )(lengths, labels, gain, weights, *pairs, *relayed, normed, slopes, loss)
+    )(lengths, labels, gain, weights, *rows, normed, slopes, loss)
     return out[0], out[1], out[2:]
 
 
@@ -289,27 +265,7 @@
     return (inverse * weighted - values * scale).astype(HALF)
 
 
-def backward_far(gain, weights, pairs, relayed, slopes):
-    n = len(pairs)
-    shape = pairs[0].shape
-
-    def body(gain_ref, weight_ref, slope_ref, *refs):
-        for j in range(2 * n):
-            values = refs[n + j // 2][...] if j % 2 else refs[j // 2][0]
-            refs[2 * n + j // 2][j % 2] = grad_rows(values, slope_ref[j], weight_ref[...], gain_ref[...])
-
-    return pl.pallas_call(
-        body,
-        in_specs=[VMEM] * (3 + 2 * n),
-        out_specs=[VMEM] * n,
-        out_shape=[jax.ShapeDtypeStruct(shape, HALF)] * n,
-        cost_estimate=cost(BACK_FAR),
-        compiler_params=params(20),
-        name="backward_far",
-    )(gain, weights, slopes, *pairs, *relayed)
-
-
-def backward_near(gain, weights, rows, slopes, after):
+def backward(gain, weights, rows, slopes, after=()):
     n = len(rows)
 
     def body(gain_ref, weight_ref, slope_ref, *refs):
@@ -321,9 +277,9 @@
         in_specs=[VMEM] * (3 + n) + [ANY] * len(after),
         out_specs=[VMEM] * n,
         out_shape=[jax.ShapeDtypeStruct(rows[0].shape, HALF)] * n,
-        cost_estimate=cost(BACK_NEAR),
+        cost_estimate=cost(BACKWARD),
         compiler_params=params(20),
-        name="backward_near",
+        name="backward",
     )(gain, weights, slopes, *rows, *after)
 
 
@@ -356,14 +312,14 @@
         out_specs=[VMEM] * (1 + n_loss) + [ANY] * len(held),
         out_shape=shapes + [jax.ShapeDtypeStruct(h.shape, h.dtype) for h in held],
         input_output_aliases={n + n_loss + i: 1 + n_loss + i for i in range(len(held))},
-        cost_estimate=cost(FOLD),
+        cost_estimate=cost(LAST if last else FOLD),
         compiler_params=params(8),
         name="fold",
     )(*terms, *([loss] if n_loss else []), *held, *after)
     return out[0], (out[1] if n_loss else None), out[1 + n_loss :]
 
 
-def hold(gains, piece, after):
+def hold(gains, piece, after, claim=None):
     rows = sum(g.shape[0] for g in gains)
 
     def body(*refs):
@@ -377,7 +333,7 @@
         out_shape=[jax.ShapeDtypeStruct((rows, g.shape[1]), HALF) for g in gains[:1]]
         + [jax.ShapeDtypeStruct(piece.shape, HALF)],
         input_output_aliases={len(gains): len(gains[:1])},
-        cost_estimate=cost(HOLD),
+        cost_estimate=cost(claim or HOLD),
         compiler_params=params(8),
         name="hold",
     )(*gains, piece, *after)
@@ -387,11 +343,17 @@
 def per_device(n_dp, n_fsdp, hidden, head, gain, targets, lengths):
     inner = 2
     line = n_dp // inner
-    n_pairs = n_fsdp // 2 - 1
 
     def swap(value, axis, offset):
         size = n_dp if axis == "dp" else n_fsdp
         return lax.ppermute(value, axis, [(i, i ^ offset) for i in range(size)])
+
+    def exchange(blocks, after, claim=None):
+        came = [swap(block, "fsdp", j + 2 & ~1) for j, block in reversed(list(enumerate(blocks)))][::-1]
+        return [
+            swap(hold([], block, [came[j - 1], *after], claim)[1], "fsdp", 1) if j % 2 else block
+            for j, block in enumerate(came)
+        ]
 
     small = gain.shape[1] % 128 == 0 and line == 4
     gains = [gain, swap(gain, "dp", 1)] if small else [gain]
@@ -402,9 +364,11 @@
         if small and o == 3:
             break
         pieces[o * inner] = swap(pieces[(o ^ bit) * inner], "dp", bit * inner)
-    own, side, *pairs = unpack(hidden)
-    pairs = [swap(pair, "fsdp", 2 * i + 2) for i, pair in enumerate(pairs)]
+    own, side, *away = unpack(hidden)
+    far = exchange(away, [], RELAY)
     for o in range(line):
+        if small and o == 2:
+            pieces[4] = hold([], pieces[4], [own])[1]
         if small and o == 1:
             gain, pieces[2] = hold(gains, pieces[2], [own, pieces[1]])
         if pieces[o * inner] is not None:
@@ -418,16 +382,15 @@
     else:
         gains = [lax.all_gather(gain, "dp", axis=1, tiled=True)]
     side = swap(side, "fsdp", 1)
-    relayed = [swap(take(pair), "fsdp", 1) for pair in pairs]
 
     height = targets.shape[0] // n_fsdp
     labels = targets.T if height % 128 == 0 else targets.reshape(n_fsdp, height)
     loss, gain_row, weights, normed, near_slopes = forward_near(lengths, labels, gains, [own, side], pieces)
     loss, far_slopes, parts = forward_far(
-        lengths, labels, gain_row, weights, pairs, relayed, normed, near_slopes, loss, n_dp
+        lengths, labels, gain_row, weights, far, normed, near_slopes, loss, n_dp
     )
 
-    far = backward_far(gain_row, weights, pairs, relayed, far_slopes)
+    far = backward(gain_row, weights, far, far_slopes)
     near = None
     across = [None] * line
     waiting = list(range(line - 1, -1, -1))
@@ -443,7 +406,7 @@
         else:
             piece, _, held = fold([parts[o * inner], *came[o], across[o]], None, held, order)
         if near is None:
-            near = backward_near(gain_row, weights, [own, side], near_slopes, [loss])
+            near = backward(gain_row, weights, [own, side], near_slopes, [loss])
         bit, order = o & -o, [piece]
         moved = swap(piece, "dp", bit * inner)
         if o == rides:
@@ -455,9 +418,7 @@
             across[waiting.pop(0)] = swap(held[0], "dp", 1)
     grad_head, loss, _ = fold([parts[0], across[0], *came[0]], loss, last=True)
 
-    far = [swap(pair, "fsdp", 2 * i + 2) for i, pair in enumerate(far)]
-    relayed = [swap(take(pair, came[0][-1:]), "fsdp", 1) for pair in far]
-    grad_hidden = pack(near[0], swap(near[1], "fsdp", 1), far, relayed)
+    grad_hidden = pack([near[0], swap(near[1], "fsdp", 1), *exchange(far, order)])
 
     bit = n_fsdp // 2
     while bit:

time: 98.8 us -> 89.2 us (0.903)
  waiting for transfers between devices: 48.2 us -> 42.3 us
  starting transfers between devices: 29 us -> 25.4 us
    ppermute x25 -> x27, waiting for transfers between devices: 48.2 us -> 42.3 us  [swap(): return lax.ppermute(value, axis, [(i, i ^ offset) for i in range(size)])]
    ppermute x25 -> x27, starting transfers between devices: 29 us -> 25.4 us  [swap(): return lax.ppermute(value, axis, [(i, i ^ offset) for i in range(size)])]
    pallas_call x7 -> x5, Pallas kernels: 14.3 us -> 14.2 us  [the longest x1 4.91 us: forward_far(): pl.pallas_call(body, in_specs=[SMEM] + [VMEM] * (6 + n), out_specs=[VMEM]...]
  transfers between devices with their start and end apart: 25 -> 27, of which waited for: 14 -> 14; matrix products, arithmetic and copies ran while one was open for 1% -> 1% of each run, Pallas kernels for 6% -> 13%
where the time goes in v3:
time: 89.2 us; the launch traced here: 89 us
  waiting for transfers between devices  42.3 us (47%)
  starting transfers between devices  25.4 us (28%)
  Pallas kernels  18.9 us (21%)
  local copies, waits for them, and re-layouts  1.58 us (2%)
    ppermute x27, waiting for transfers between devices, swap(): return lax.ppermute(value, axis, [(i, i ^ offset) for i in range(size)])  42.3 us
    ppermute x27, starting transfers between devices, swap(): return lax.ppermute(value, axis, [(i, i ^ offset) for i in range(size)])  25.4 us
    pallas_call x1, Pallas kernels, forward_far(): pl.pallas_call(body, in_specs=[SMEM] + [VMEM] * (6 + n), out_specs=[VMEM]...  4.91 us
    pallas_call x1, Pallas kernels, unpack(): pl.pallas_call(body, in_specs=[ANY], out_specs=[VMEM] * positions, out_sh...  3.59 us
    pallas_call x1, Pallas kernels, forward_near(): pl.pallas_call(body, in_specs=[SMEM] + [VMEM] * (1 + n_gain + n) + [ANY]...  3.47 us
    pallas_call x2, Pallas kernels, backward(): pl.pallas_call(body, in_specs=[VMEM] * (3 + n) + [ANY] * len(after), out_...  3.16 us
    pallas_call x1, Pallas kernels, pack(): pl.pallas_call(body, grid=(frames // chunk,), in_specs=[pl.BlockSpec((chu...  2.53 us
  transfers between devices with their start and end apart: 27, of which 14 were waited for; matrix products, arithmetic and copies ran while one was open for 1% of the time, Pallas kernels for 13%

profile of v3, /device:TPU:0, one launch (start us, length us, event | category | flops | bytes accessed | tf_op | source)
XLA Modules:
  0.0 89.0 jit_solution(1728746601412015784)
XLA Ops:
  0.6 3.0 %collective-permute-start.2 = (bf16[128,1024]{1,0:T(8,128)(2,1)}, bf16[128,1024]{1,0:T(8,128)(2,1)S(1)}, u32[]{:S(2)}, u32[]{:S(2)}) collective-permute-start(bf16[128,1024]{1,0:T(8,128)(2,1)} %bitcast.6), channel_id=1, source_target_pairs={{0,4},{4,0},{8,12},{12,8},{16,20},{20,16},{24,28},{28,24},{1,5},{5... | collective-permute-start | bytes 786440 | tf_op jit(solution)/shard_map/ppermute | solution.py:349
  3.6 1.6 %collective-permute-start.1 = (bf16[128,1024]{1,0:T(8,128)(2,1)}, bf16[128,1024]{1,0:T(8,128)(2,1)S(1)}, u32[]{:S(2)}, u32[]{:S(2)}) collective-permute-start(bf16[128,1024]{1,0:T(8,128)(2,1)} %bitcast.7), channel_id=1, source_target_pairs={{0,8},{4,12},{8,0},{12,4},{16,24},{20,28},{24,16},{28,20},{1,9},{5... | collective-permute-start | bytes 786440 | tf_op jit(solution)/shard_map/ppermute | solution.py:349
  5.2 2.6 %collective-permute-start.4 = (bf16[128,1024]{1,0:T(8,128)(2,1)}, bf16[128,1024]{1,0:T(8,128)(2,1)S(1)}, u32[]{:S(2)}, u32[]{:S(2)}) collective-permute-start(bf16[128,1024]{1,0:T(8,128)(2,1)} %bitcast.8), channel_id=1, source_target_pairs={{0,16},{4,20},{8,24},{12,28},{16,0},{20,4},{24,8},{28,12},{1,17},{... | collective-permute-start | bytes 786440 | tf_op jit(solution)/shard_map/ppermute | solution.py:349
  8.3 3.6 %unpack.1 = (bf16[256,1024]{1,0:T(8,128)(2,1)}, bf16[256,1024]{1,0:T(8,128)(2,1)}, bf16[256,1024]{1,0:T(8,128)(2,1)}, bf16[256,1024]{1,0:T(8,128)(2,1)}) custom-call(bf16[256,4,1024]{2,1,0:T(4,128)(2,1)} %hidden_ref.1), custom_call_target="tpu_custom_call" | custom-call | flops 10000000 | tf_op jit(solution)/shard_map/unpack/pallas_call | solution.py:59
  11.9 1.6 %collective-permute-start.11 = (bf16[256,1024]{1,0:T(8,128)(2,1)}, bf16[256,1024]{1,0:T(8,128)(2,1)S(1)}, u32[]{:S(2)}, u32[]{:S(2)}) collective-permute-start(bf16[256,1024]{1,0:T(8,128)(2,1)} %get-tuple-element.46), channel_id=1, source_target_pairs={{0,2},{1,3},{2,0},{3,1},{4,6},{5,7},{6,4},{7,5},{8,10},{9,11},{10,... | collective-permute-start | bytes 1572872 | tf_op jit(solution)/shard_map/ppermute | solution.py:349
  14.0 3.1 %collective-permute-done.1.refs_2_ = bf16[128,1024]{1,0:T(8,128)(2,1)S(1)} collective-permute-done((bf16[128,1024]{1,0:T(8,128)(2,1)}, bf16[128,1024]{1,0:T(8,128)(2,1)S(1)}, u32[]{:S(2)}, u32[]{:S(2)}) %collective-permute-start.1) | collective-permute-done | bytes 262176 | tf_op jit(solution)/shard_map/ppermute | solution.py:349
  17.1 1.0 %copy-done = bf16[256,1024]{1,0:T(8,128)(2,1)S(1)} copy-done((bf16[256,1024]{1,0:T(8,128)(2,1)S(1)}, bf16[256,1024]{1,0:T(8,128)(2,1)}, u32[]{:S(2)}) %copy-start) | copy-done | bytes 524312
  19.5 1.2 %collective-permute-start.9 = (bf16[128,1024]{1,0:T(8,128)(2,1)S(1)}, bf16[128,1024]{1,0:T(8,128)(2,1)S(1)}, u32[]{:S(2)}, u32[]{:S(2)}) collective-permute-start(bf16[128,1024]{1,0:T(8,128)(2,1)S(1)} %hold.7.refs_3_.refs_10_), channel_id=1, source_target_pairs={{0,8},{4,12},{8,0},{12,4},{16,24},{20,28},{24,16},{28,20},{1,9},{5... | collective-permute-start | bytes 786440 | tf_op jit(solution)/shard_map/ppermute | solution.py:349
  20.7 1.6 %collective-permute-done.3.refs_1_ = bf16[2,128]{1,0:T(2,128)(2,1)S(1)} collective-permute-done((bf16[2,128]{1,0:T(2,128)(2,1)S(1)}, bf16[2,128]{1,0:T(2,128)(2,1)S(1)}, u32[]{:S(2)}, u32[]{:S(2)}) %collective-permute-start.3) | collective-permute-done | bytes 544 | tf_op jit(solution)/shard_map/ppermute | solution.py:349
  22.2 1.6 %collective-permute-start.8 = (bf16[128,1024]{1,0:T(8,128)(2,1)S(1)}, bf16[128,1024]{1,0:T(8,128)(2,1)S(1)}, u32[]{:S(2)}, u32[]{:S(2)}) collective-permute-start(bf16[128,1024]{1,0:T(8,128)(2,1)S(1)} %hold.7.refs_3_.refs_10_), channel_id=1, source_target_pairs={{0,4},{4,0},{8,12},{12,8},{16,20},{20,16},{24,28},{28,24},{1,5},{5... | collective-permute-start | bytes 786440 | tf_op jit(solution)/shard_map/ppermute | solution.py:349
  23.9 3.6 %collective-permute-done.7.refs_1_.refs_9_ = bf16[128,1024]{1,0:T(8,128)(2,1)S(1)} collective-permute-done((bf16[128,1024]{1,0:T(8,128)(2,1)S(1)}, bf16[128,1024]{1,0:T(8,128)(2,1)S(1)}, u32[]{:S(2)}, u32[]{:S(2)}) %collective-permute-start.7) | collective-permute-done | bytes 262176 | tf_op jit(solution)/shard_map/ppermute | solution.py:349
  27.5 3.2 %collective-permute-done.8.refs_2_.refs_11_ = bf16[128,1024]{1,0:T(8,128)(2,1)S(1)} collective-permute-done((bf16[128,1024]{1,0:T(8,128)(2,1)S(1)}, bf16[128,1024]{1,0:T(8,128)(2,1)S(1)}, u32[]{:S(2)}, u32[]{:S(2)}) %collective-permute-start.8) | collective-permute-done | bytes 262176 | tf_op jit(solution)/shard_map/ppermute | solution.py:349
  31.5 4.5 %collective-permute-done.12.refs_0_ = bf16[256,1024]{1,0:T(8,128)(2,1)S(1)} collective-permute-done((bf16[256,1024]{1,0:T(8,128)(2,1)}, bf16[256,1024]{1,0:T(8,128)(2,1)S(1)}, u32[]{:S(2)}, u32[]{:S(2)}) %collective-permute-start.12) | collective-permute-done | bytes 524320 | tf_op jit(solution)/shard_map/ppermute | solution.py:349
  36.3 4.1 %collective-permute-done.5.refs_3_ = bf16[4,128]{1,0:T(4,128)(2,1)S(1)} collective-permute-done((bf16[4,128]{1,0:T(4,128)(2,1)S(1)}, bf16[4,128]{1,0:T(4,128)(2,1)S(1)}, u32[]{:S(2)}, u32[]{:S(2)}) %collective-permute-start.5) | collective-permute-done | bytes 1056 | tf_op jit(solution)/shard_map/ppermute | solution.py:349
  40.5 3.5 %forward_near.1 = (f32[8,128]{1,0:T(8,128)S(1)}, f32[1,1024]{1,0:T(1,128)S(1)}, bf16[1024,1024]{1,0:T(8,128)(2,1)S(1)}, bf16[2,256,1024]{2,1,0:T(8,128)(2,1)S(1)}, bf16[2,256,1024]{2,1,0:T(8,128)(2,1)S(1)}) custom-call(s32[8]{0:T(128)S(1)} %copy-done.5, s32[1,1024]{1,0:T(1,128)S(1)} %bitcast.4, bf16[4,128]{1,0:T(4,128)(2,1)S(1)} %get-tuple-element.41.refs_2_, ...), custom_call_target="tpu_custom_call" | custom-call | flops 3000000000 | tf_op jit(solution)/shard_map/forward_near/pallas_call | solution.py:174
  44.0 4.9 %forward_far.1 = (f32[8,1024]{1,0:T(8,128)S(1)}, bf16[2,256,1024]{2,1,0:T(8,128)(2,1)S(1)}, bf16[128,1024]{1,0:T(8,128)(2,1)S(1)}, bf16[128,1024]{1,0:T(8,128)(2...) custom-call(s32[8]{0:T(128)S(1)} %copy-done.5, ...), custom_call_target="tpu_custom_call" | custom-call | flops 10000000 | tf_op jit(solution)/shard_map/forward_far/pallas_call | solution.py:237
  48.9 1.6 %collective-permute-start.15 = (bf16[136,1024]{1,0:T(8,128)(2,1)S(1)}, bf16[136,1024]{1,0:T(8,128)(2,1)S(1)}, u32[]{:S(2)}, u32[]{:S(2)}) collective-permute-start(bf16[136,1024]{1,0:T(8,128)(2,1)S(1)} %get-tuple-element.55), channel_id=1, source_target_pairs={{0,4},{4,0},{8,12},{12,8},{16,20},{20,16},{24,28},{28,24},{1,5},{5... | collective-permute-start | bytes 835592 | tf_op jit(solution)/shard_map/ppermute | solution.py:349
  50.5 1.6 %backward.2 = (bf16[256,1024]{1,0:T(8,128)(2,1)S(1)}, bf16[256,1024]{1,0:T(8,128)(2,1)S(1)}) custom-call(f32[1,1024]{1,0:T(1,128)S(1)} %get-tuple-element.44.refs_2_.gain_ref, bf16[1024,1024]{1,0:T(8,128)(2,1)S(1)} %get-tuple-element.45.refs_3_.weight_ref, bf16[2,256,1024]{2,1,0:T(8,128)(2,1)S(1)} %get-tuple-element.58.slope_ref, ...), custom_call_target="tpu_custom_call" | custom-call | flops 10000000 | tf_op jit(solution)/shard_map/backward/pallas_call | solution.py:275
  52.1 1.6 %collective-permute-start.24 = (bf16[256,1024]{1,0:T(8,128)(2,1)S(1)}, bf16[256,1024]{1,0:T(8,128)(2,1)S(1)}, u32[]{:S(2)}, u32[]{:S(2)}) collective-permute-start(bf16[256,1024]{1,0:T(8,128)(2,1)S(1)} %get-tuple-element.71), channel_id=1, source_target_pairs={{0,2},{1,3},{2,0},{3,1},{4,6},{5,7},{6,4},{7,5},{8,10},{9,11},{10,... | collective-permute-start | bytes 1572872 | tf_op jit(solution)/shard_map/ppermute | solution.py:349
  54.2 2.7 %collective-permute-done.15.refs_1_ = bf16[136,1024]{1,0:T(8,128)(2,1)S(1)} collective-permute-done((bf16[136,1024]{1,0:T(8,128)(2,1)S(1)}, bf16[136,1024]{1,0:T(8,128)(2,1)S(1)}, u32[]{:S(2)}, u32[]{:S(2)}) %collective-permute-start.15) | collective-permute-done | bytes 278560 | tf_op jit(solution)/shard_map/ppermute | solution.py:349
  57.5 1.5 %collective-permute-start.14 = (bf16[128,1024]{1,0:T(8,128)(2,1)S(1)}, bf16[128,1024]{1,0:T(8,128)(2,1)S(1)}, u32[]{:S(2)}, u32[]{:S(2)}) collective-permute-start(bf16[128,1024]{1,0:T(8,128)(2,1)S(1)} %get-tuple-element.53), channel_id=1, source_target_pairs={{0,4},{4,0},{8,12},{12,8},{16,20},{20,16},{24,28},{28,24},{1,5},{5... | collective-permute-start | bytes 786440 | tf_op jit(solution)/shard_map/ppermute | solution.py:349
  59.6 7.2 %collective-permute-done.14.refs_1_ = bf16[128,1024]{1,0:T(8,128)(2,1)S(1)} collective-permute-done((bf16[128,1024]{1,0:T(8,128)(2,1)S(1)}, bf16[128,1024]{1,0:T(8,128)(2,1)S(1)}, u32[]{:S(2)}, u32[]{:S(2)}) %collective-permute-start.14) | collective-permute-done | bytes 262176 | tf_op jit(solution)/shard_map/ppermute | solution.py:349
  67.2 1.5 %collective-permute-start.17 = (bf16[128,1024]{1,0:T(8,128)(2,1)S(1)}, bf16[128,1024]{1,0:T(8,128)(2,1)S(1)}, u32[]{:S(2)}, u32[]{:S(2)}) collective-permute-start(bf16[128,1024]{1,0:T(8,128)(2,1)S(1)} %get-tuple-element.63), channel_id=1, source_target_pairs={{0,4},{4,0},{8,12},{12,8},{16,20},{20,16},{24,28},{28,24},{1,5},{5... | collective-permute-start | bytes 786440 | tf_op jit(solution)/shard_map/ppermute | solution.py:349
  68.8 3.6 %collective-permute-done.18.refs_1_ = bf16[128,1024]{1,0:T(8,128)(2,1)S(1)} collective-permute-done((bf16[128,1024]{1,0:T(8,128)(2,1)S(1)}, bf16[128,1024]{1,0:T(8,128)(2,1)S(1)}, u32[]{:S(2)}, u32[]{:S(2)}) %collective-permute-start.18) | collective-permute-done | bytes 262176 | tf_op jit(solution)/shard_map/ppermute | solution.py:349
  72.4 1.7 %collective-permute-start.19 = (bf16[128,1024]{1,0:T(8,128)(2,1)S(1)}, bf16[128,1024]{1,0:T(8,128)(2,1)S(1)}, u32[]{:S(2)}, u32[]{:S(2)}) collective-permute-start(bf16[128,1024]{1,0:T(8,128)(2,1)S(1)} %fold.6.refs_2_), channel_id=1, source_target_pairs={{0,8},{4,12},{8,0},{12,4},{16,24},{20,28},{24,16},{28,20},{1,9},{5... | collective-permute-start | bytes 786440 | tf_op jit(solution)/shard_map/ppermute | solution.py:349
  74.1 1.6 %backward.3 = (bf16[256,1024]{1,0:T(8,128)(2,1)S(1)}, bf16[256,1024]{1,0:T(8,128)(2,1)S(1)}) custom-call(f32[1,1024]{1,0:T(1,128)S(1)} %get-tuple-element.44.refs_2_.gain_ref, bf16[1024,1024]{1,0:T(8,128)(2,1)S(1)} %get-tuple-element.45.refs_3_.weight_ref, bf16[2,256,1024]{2,1,0:T(8,128)(2,1)S(1)} %get-tuple-element.49.refs_7_.slope_ref, ...), custom_call_target="tpu_custom_call" | custom-call | flops 10000000 | tf_op jit(solution)/shard_map/backward/pallas_call | solution.py:275
  76.3 4.0 %collective-permute-done.19.refs_2_ = bf16[128,1024]{1,0:T(8,128)(2,1)S(1)} collective-permute-done((bf16[128,1024]{1,0:T(8,128)(2,1)S(1)}, bf16[128,1024]{1,0:T(8,128)(2,1)S(1)}, u32[]{:S(2)}, u32[]{:S(2)}) %collective-permute-start.19) | collective-permute-done | bytes 262176 | tf_op jit(solution)/shard_map/ppermute | solution.py:349
  80.2 0.9 %fold.7 = (f32[128,1024]{1,0:T(8,128)}, f32[8,128]{1,0:T(8,128)S(1)}) custom-call(bf16[128,1024]{1,0:T(8,128)(2,1)S(1)} %get-tuple-element.51.refs_0_, bf16[128,1024]{1,0:T(8,128)(2,1)S(1)} %collective-permute-done.17.refs_1_, bf16[128,1024]{1,0:T(8,128)(2,1)S(1)} %collective-permute-done.19.refs_2_, bf16[136,1024]{1,0:T(8,128)(2,1)S(1)} %collective-permute-done.20.refs_3_, ...), custom_call_target="tpu_custom_call" | custom-call | flops 3000000000 | tf_op jit(solution)/shard_map/fold/pallas_call | solution.py:309
  81.2 1.5 %collective-permute-start.21 = (f32[8,128]{1,0:T(8,128)S(1)}, f32[8,128]{1,0:T(8,128)S(1)}, u32[]{:S(2)}, u32[]{:S(2)}) collective-permute-start(f32[8,128]{1,0:T(8,128)S(1)} %get-tuple-element.68), channel_id=1, source_target_pairs={{0,2},{1,3},{2,0},{3,1},{4,6},{5,7},{6,4},{7,5},{8,10},{9,11},{10,... | collective-permute-start | bytes 12296 | tf_op jit(solution)/shard_map/ppermute | solution.py:349
  82.7 2.1 %collective-permute-done.21 = f32[8,128]{1,0:T(8,128)S(1)} collective-permute-done((f32[8,128]{1,0:T(8,128)S(1)}, f32[8,128]{1,0:T(8,128)S(1)}, u32[]{:S(2)}, u32[]{:S(2)}) %collective-permute-start.21) | collective-permute-done | bytes 4128 | tf_op jit(solution)/shard_map/ppermute | solution.py:349
  84.8 1.2 %collective-permute-done.22 = f32[8,128]{1,0:T(8,128)S(1)} collective-permute-done((f32[8,128]{1,0:T(8,128)S(1)}, f32[8,128]{1,0:T(8,128)S(1)}, u32[]{:S(2)}, u32[]{:S(2)}) %collective-permute-start.22) | collective-permute-done | bytes 4128 | tf_op jit(solution)/shard_map/ppermute | solution.py:349
  86.5 2.5 %pack.1 = bf16[256,4,1024]{2,1,0:T(4,128)(2,1)} custom-call(bf16[256,1024]{1,0:T(8,128)(2,1)S(1)} %get-tuple-element.69.refs_0_, bf16[256,1024]{1,0:T(8,128)(2,1)S(1)} %collective-permute-done.23.refs_1_, bf16[256,1024]{1,0:T(8,128)(2,1)S(1)} %collective-permute-done.24.refs_1_.refs_2_, bf16[256,1024]{1,0:T(8,128)(2,1)S(1)} %collective-permute-done.26.refs_3_), custom_call_target="tpu_custom_call" | custom-call | flops 10000000 | tf_op jit(solution)/shard_map/pack/pallas_call | solution.py:88
  (55 shorter events, 6.9 us)
Async XLA Ops:
  0.6 16.5 %copy-start.4 = (bf16[1,128]{1,0:T(2,128)(2,1)S(1)}, bf16[1,128]{1,0:T(2,128)(2,1)}, u32[]{:S(2)}) copy-start(bf16[1,128]{1,0:T(2,128)(2,1)} %refs_0_.3) | copy-start | bytes 772
  0.6 13.4 %collective-permute-start.2 = (bf16[128,1024]{1,0:T(8,128)(2,1)}, bf16[128,1024]{1,0:T(8,128)(2,1)S(1)}, u32[]{:S(2)}, u32[]{:S(2)}) collective-permute-start(bf16[128,1024]{1,0:T(8,128)(2,1)} %bitcast.6), channel_id=1, source_target_pairs={{0,4},{4,0},{8,12},{12,8},{16,20},{20,16},{24,28},{28,24},{1,5},{5... | collective-permute-start | bytes 786440 | tf_op jit(solution)/shard_map/ppermute | solution.py:349
  3.6 13.5 %collective-permute-start.1 = (bf16[128,1024]{1,0:T(8,128)(2,1)}, bf16[128,1024]{1,0:T(8,128)(2,1)S(1)}, u32[]{:S(2)}, u32[]{:S(2)}) collective-permute-start(bf16[128,1024]{1,0:T(8,128)(2,1)} %bitcast.7), channel_id=1, source_target_pairs={{0,8},{4,12},{8,0},{12,4},{16,24},{20,28},{24,16},{28,20},{1,9},{5... | collective-permute-start | bytes 786440 | tf_op jit(solution)/shard_map/ppermute | solution.py:349
  5.2 14.3 %collective-permute-start.4 = (bf16[128,1024]{1,0:T(8,128)(2,1)}, bf16[128,1024]{1,0:T(8,128)(2,1)S(1)}, u32[]{:S(2)}, u32[]{:S(2)}) collective-permute-start(bf16[128,1024]{1,0:T(8,128)(2,1)} %bitcast.8), channel_id=1, source_target_pairs={{0,16},{4,20},{8,24},{12,28},{16,0},{20,4},{24,8},{28,12},{1,17},{... | collective-permute-start | bytes 786440 | tf_op jit(solution)/shard_map/ppermute | solution.py:349
  7.8 5.7 %collective-permute-start = (bf16[1,128]{1,0:T(2,128)(2,1)}, bf16[1,128]{1,0:T(2,128)(2,1)S(1)}, u32[]{:S(2)}, u32[]{:S(2)}) collective-permute-start(bf16[1,128]{1,0:T(2,128)(2,1)} %refs_0_.3), channel_id=1, source_target_pairs={{0,4},{4,0},{8,12},{12,8},{16,20},{20,16},{24,28},{28,24},{1,5},{5... | collective-permute-start | bytes 776 | tf_op jit(solution)/shard_map/ppermute | solution.py:349
  11.9 19.6 %collective-permute-start.11 = (bf16[256,1024]{1,0:T(8,128)(2,1)}, bf16[256,1024]{1,0:T(8,128)(2,1)S(1)}, u32[]{:S(2)}, u32[]{:S(2)}) collective-permute-start(bf16[256,1024]{1,0:T(8,128)(2,1)} %get-tuple-element.46), channel_id=1, source_target_pairs={{0,2},{1,3},{2,0},{3,1},{4,6},{5,7},{6,4},{7,5},{8,10},{9,11},{10,... | collective-permute-start | bytes 1572872 | tf_op jit(solution)/shard_map/ppermute | solution.py:349
  13.5 22.5 %collective-permute-start.12 = (bf16[256,1024]{1,0:T(8,128)(2,1)}, bf16[256,1024]{1,0:T(8,128)(2,1)S(1)}, u32[]{:S(2)}, u32[]{:S(2)}) collective-permute-start(bf16[256,1024]{1,0:T(8,128)(2,1)} %get-tuple-element.47), channel_id=1, source_target_pairs={{0,2},{1,3},{2,0},{3,1},{4,6},{5,7},{6,4},{7,5},{8,10},{9,11},{10,... | collective-permute-start | bytes 1572872 | tf_op jit(solution)/shard_map/ppermute | solution.py:349
  18.2 9.3 %collective-permute-start.7 = (bf16[128,1024]{1,0:T(8,128)(2,1)S(1)}, bf16[128,1024]{1,0:T(8,128)(2,1)S(1)}, u32[]{:S(2)}, u32[]{:S(2)}) collective-permute-start(bf16[128,1024]{1,0:T(8,128)(2,1)S(1)} %get-tuple-element.43.refs_8_), channel_id=1, source_target_pairs={{0,4},{4,0},{8,12},{12,8},{16,20},{20,16},{24,28},{28,24},{1,5},{5... | collective-permute-start | bytes 786440 | tf_op jit(solution)/shard_map/ppermute | solution.py:349
  18.6 3.6 %collective-permute-start.3 = (bf16[2,128]{1,0:T(2,128)(2,1)S(1)}, bf16[2,128]{1,0:T(2,128)(2,1)S(1)}, u32[]{:S(2)}, u32[]{:S(2)}) collective-permute-start(bf16[2,128]{1,0:T(2,128)(2,1)S(1)} %get-tuple-element.39.refs_0_), channel_id=1, source_target_pairs={{0,8},{4,12},{8,0},{12,4},{16,24},{20,28},{24,16},{28,20},{1,9},{5... | collective-permute-start | bytes 1544 | tf_op jit(solution)/shard_map/ppermute | solution.py:349
  19.5 8.0 %collective-permute-start.9 = (bf16[128,1024]{1,0:T(8,128)(2,1)S(1)}, bf16[128,1024]{1,0:T(8,128)(2,1)S(1)}, u32[]{:S(2)}, u32[]{:S(2)}) collective-permute-start(bf16[128,1024]{1,0:T(8,128)(2,1)S(1)} %hold.7.refs_3_.refs_10_), channel_id=1, source_target_pairs={{0,8},{4,12},{8,0},{12,4},{16,24},{20,28},{24,16},{28,20},{1,9},{5... | collective-permute-start | bytes 786440 | tf_op jit(solution)/shard_map/ppermute | solution.py:349
  22.2 8.5 %collective-permute-start.8 = (bf16[128,1024]{1,0:T(8,128)(2,1)S(1)}, bf16[128,1024]{1,0:T(8,128)(2,1)S(1)}, u32[]{:S(2)}, u32[]{:S(2)}) collective-permute-start(bf16[128,1024]{1,0:T(8,128)(2,1)S(1)} %hold.7.refs_3_.refs_10_), channel_id=1, source_target_pairs={{0,4},{4,0},{8,12},{12,8},{16,20},{20,16},{24,28},{28,24},{1,5},{5... | collective-permute-start | bytes 786440 | tf_op jit(solution)/shard_map/ppermute | solution.py:349
  27.5 13.0 %collective-permute-start.6 = (bf16[256,1024]{1,0:T(8,128)(2,1)S(1)}, bf16[256,1024]{1,0:T(8,128)(2,1)S(1)}, u32[]{:S(2)}, u32[]{:S(2)}) collective-permute-start(bf16[256,1024]{1,0:T(8,128)(2,1)S(1)} %get-tuple-element.42), channel_id=1, source_target_pairs={{0,1},{1,0},{2,3},{3,2},{4,5},{5,4},{6,7},{7,6},{8,9},{9,8},{10,11... | collective-permute-start | bytes 1572872 | tf_op jit(solution)/shard_map/ppermute | solution.py:349
  30.7 9.8 %copy-start.1 = (bf16[256,1024]{1,0:T(8,128)(2,1)S(1)}, bf16[256,1024]{1,0:T(8,128)(2,1)}, u32[]{:S(2)}) copy-start(bf16[256,1024]{1,0:T(8,128)(2,1)} %get-tuple-element.38.refs_3_.refs_1_.refs_4_.refs_0_) | copy-start | bytes 1572868
  30.7 9.8 %copy-start.3 = (s32[1024,1]{0,1:T(1,128)S(1)}, s32[1024,1]{0,1:T(1,128)}, u32[]{:S(2)}) copy-start(s32[1024,1]{0,1:T(1,128)} %param.8) | copy-start | bytes 12292
  30.7 9.8 %copy-start.5 = (s32[8]{0:T(128)S(1)}, s32[8]{0:T(128)}, u32[]{:S(2)}) copy-start(s32[8]{0:T(128)} %refs_0_.5) | copy-start | bytes 100
  30.7 9.8 %copy-start.6 = (bf16[1,128,1024]{2,1,0:T(8,128)(2,1)S(1)}, bf16[1,128,1024]{2,1,0:T(8,128)(2,1)}, u32[]{:S(2)}) copy-start(bf16[1,128,1024]{2,1,0:T(8,128)(2,1)} %param.6) | copy-start | bytes 786436
  30.7 9.8 %collective-permute-start.10 = (bf16[128,1024]{1,0:T(8,128)(2,1)S(1)}, bf16[128,1024]{1,0:T(8,128)(2,1)S(1)}, u32[]{:S(2)}, u32[]{:S(2)}) collective-permute-start(bf16[128,1024]{1,0:T(8,128)(2,1)S(1)} %hold.9.refs_12_), channel_id=1, source_target_pairs={{0,4},{4,0},{8,12},{12,8},{16,20},{20,16},{24,28},{28,24},{1,5},{5... | collective-permute-start | bytes 786440 | tf_op jit(solution)/shard_map/ppermute | solution.py:349
  36.0 8.0 %collective-permute-start.13 = (bf16[256,1024]{1,0:T(8,128)(2,1)S(1)}, bf16[256,1024]{1,0:T(8,128)(2,1)S(1)}, u32[]{:S(2)}, u32[]{:S(2)}) collective-permute-start(bf16[256,1024]{1,0:T(8,128)(2,1)S(1)} %hold.10), channel_id=1, source_target_pairs={{0,1},{1,0},{2,3},{3,2},{4,5},{5,4},{6,7},{7,6},{8,9},{9,8},{10,11... | collective-permute-start | bytes 1572872 | tf_op jit(solution)/shard_map/ppermute | solution.py:349
  36.0 4.5 %collective-permute-start.5 = (bf16[4,128]{1,0:T(4,128)(2,1)S(1)}, bf16[4,128]{1,0:T(4,128)(2,1)S(1)}, u32[]{:S(2)}, u32[]{:S(2)}) collective-permute-start(bf16[4,128]{1,0:T(4,128)(2,1)S(1)} %get-tuple-element.41.refs_2_), channel_id=1, source_target_pairs={{0,16},{4,20},{8,24},{12,28},{16,0},{20,4},{24,8},{28,12},{1,17},{... | collective-permute-start | bytes 3080 | tf_op jit(solution)/shard_map/ppermute | solution.py:349
  48.9 8.0 %collective-permute-start.15 = (bf16[136,1024]{1,0:T(8,128)(2,1)S(1)}, bf16[136,1024]{1,0:T(8,128)(2,1)S(1)}, u32[]{:S(2)}, u32[]{:S(2)}) collective-permute-start(bf16[136,1024]{1,0:T(8,128)(2,1)S(1)} %get-tuple-element.55), channel_id=1, source_target_pairs={{0,4},{4,0},{8,12},{12,8},{16,20},{20,16},{24,28},{28,24},{1,5},{5... | collective-permute-start | bytes 835592 | tf_op jit(solution)/shard_map/ppermute | solution.py:349
  52.1 23.6 %collective-permute-start.24 = (bf16[256,1024]{1,0:T(8,128)(2,1)S(1)}, bf16[256,1024]{1,0:T(8,128)(2,1)S(1)}, u32[]{:S(2)}, u32[]{:S(2)}) collective-permute-start(bf16[256,1024]{1,0:T(8,128)(2,1)S(1)} %get-tuple-element.71), channel_id=1, source_target_pairs={{0,2},{1,3},{2,0},{3,1},{4,6},{5,7},{6,4},{7,5},{8,10},{9,11},{10,... | collective-permute-start | bytes 1572872 | tf_op jit(solution)/shard_map/ppermute | solution.py:349
  53.6 22.6 %collective-permute-start.25 = (bf16[256,1024]{1,0:T(8,128)(2,1)S(1)}, bf16[256,1024]{1,0:T(8,128)(2,1)S(1)}, u32[]{:S(2)}, u32[]{:S(2)}) collective-permute-start(bf16[256,1024]{1,0:T(8,128)(2,1)S(1)} %get-tuple-element.59.refs_4_), channel_id=1, source_target_pairs={{0,2},{1,3},{2,0},{3,1},{4,6},{5,7},{6,4},{7,5},{8,10},{9,11},{10,... | collective-permute-start | bytes 1572872 | tf_op jit(solution)/shard_map/ppermute | solution.py:349
  57.0 9.8 %collective-permute-start.16 = (bf16[136,1024]{1,0:T(8,128)(2,1)S(1)}, bf16[136,1024]{1,0:T(8,128)(2,1)S(1)}, u32[]{:S(2)}, u32[]{:S(2)}) collective-permute-start(bf16[136,1024]{1,0:T(8,128)(2,1)S(1)} %get-tuple-element.60.refs_5_), channel_id=1, source_target_pairs={{0,8},{4,12},{8,0},{12,4},{16,24},{20,28},{24,16},{28,20},{1,9},{5... | collective-permute-start | bytes 835592 | tf_op jit(solution)/shard_map/ppermute | solution.py:349
  57.5 9.2 %collective-permute-start.14 = (bf16[128,1024]{1,0:T(8,128)(2,1)S(1)}, bf16[128,1024]{1,0:T(8,128)(2,1)S(1)}, u32[]{:S(2)}, u32[]{:S(2)}) collective-permute-start(bf16[128,1024]{1,0:T(8,128)(2,1)S(1)} %get-tuple-element.53), channel_id=1, source_target_pairs={{0,4},{4,0},{8,12},{12,8},{16,20},{20,16},{24,28},{28,24},{1,5},{5... | collective-permute-start | bytes 786440 | tf_op jit(solution)/shard_map/ppermute | solution.py:349
  59.0 13.3 %collective-permute-start.18 = (bf16[128,1024]{1,0:T(8,128)(2,1)S(1)}, bf16[128,1024]{1,0:T(8,128)(2,1)S(1)}, u32[]{:S(2)}, u32[]{:S(2)}) collective-permute-start(bf16[128,1024]{1,0:T(8,128)(2,1)S(1)} %get-tuple-element.65), channel_id=1, source_target_pairs={{0,4},{4,0},{8,12},{12,8},{16,20},{20,16},{24,28},{28,24},{1,5},{5... | collective-permute-start | bytes 786440 | tf_op jit(solution)/shard_map/ppermute | solution.py:349
  66.9 13.3 %collective-permute-start.20 = (bf16[136,1024]{1,0:T(8,128)(2,1)S(1)}, bf16[136,1024]{1,0:T(8,128)(2,1)S(1)}, u32[]{:S(2)}, u32[]{:S(2)}) collective-permute-start(bf16[136,1024]{1,0:T(8,128)(2,1)S(1)} %get-tuple-element.66.refs_2_), channel_id=1, source_target_pairs={{0,16},{4,20},{8,24},{12,28},{16,0},{20,4},{24,8},{28,12},{1,17},{... | collective-permute-start | bytes 835592 | tf_op jit(solution)/shard_map/ppermute | solution.py:349
  67.2 9.1 %collective-permute-start.17 = (bf16[128,1024]{1,0:T(8,128)(2,1)S(1)}, bf16[128,1024]{1,0:T(8,128)(2,1)S(1)}, u32[]{:S(2)}, u32[]{:S(2)}) collective-permute-start(bf16[128,1024]{1,0:T(8,128)(2,1)S(1)} %get-tuple-element.63), channel_id=1, source_target_pairs={{0,4},{4,0},{8,12},{12,8},{16,20},{20,16},{24,28},{28,24},{1,5},{5... | collective-permute-start | bytes 786440 | tf_op jit(solution)/shard_map/ppermute | solution.py:349
  72.4 7.8 %collective-permute-start.19 = (bf16[128,1024]{1,0:T(8,128)(2,1)S(1)}, bf16[128,1024]{1,0:T(8,128)(2,1)S(1)}, u32[]{:S(2)}, u32[]{:S(2)}) collective-permute-start(bf16[128,1024]{1,0:T(8,128)(2,1)S(1)} %fold.6.refs_2_), channel_id=1, source_target_pairs={{0,8},{4,12},{8,0},{12,4},{16,24},{20,28},{24,16},{28,20},{1,9},{5... | collective-permute-start | bytes 786440 | tf_op jit(solution)/shard_map/ppermute | solution.py:349
  75.7 10.8 %collective-permute-start.23 = (bf16[256,1024]{1,0:T(8,128)(2,1)S(1)}, bf16[256,1024]{1,0:T(8,128)(2,1)S(1)}, u32[]{:S(2)}, u32[]{:S(2)}) collective-permute-start(bf16[256,1024]{1,0:T(8,128)(2,1)S(1)} %get-tuple-element.70), channel_id=1, source_target_pairs={{0,1},{1,0},{2,3},{3,2},{4,5},{5,4},{6,7},{7,6},{8,9},{9,8},{10,11... | collective-permute-start | bytes 1572872 | tf_op jit(solution)/shard_map/ppermute | solution.py:349
  76.3 10.2 %collective-permute-start.26 = (bf16[256,1024]{1,0:T(8,128)(2,1)S(1)}, bf16[256,1024]{1,0:T(8,128)(2,1)S(1)}, u32[]{:S(2)}, u32[]{:S(2)}) collective-permute-start(bf16[256,1024]{1,0:T(8,128)(2,1)S(1)} %hold.11), channel_id=1, source_target_pairs={{0,1},{1,0},{2,3},{3,2},{4,5},{5,4},{6,7},{7,6},{8,9},{9,8},{10,11... | collective-permute-start | bytes 1572872 | tf_op jit(solution)/shard_map/ppermute | solution.py:349
  81.2 3.6 %collective-permute-start.21 = (f32[8,128]{1,0:T(8,128)S(1)}, f32[8,128]{1,0:T(8,128)S(1)}, u32[]{:S(2)}, u32[]{:S(2)}) collective-permute-start(f32[8,128]{1,0:T(8,128)S(1)} %get-tuple-element.68), channel_id=1, source_target_pairs={{0,2},{1,3},{2,0},{3,1},{4,6},{5,7},{6,4},{7,5},{8,10},{9,11},{10,... | collective-permute-start | bytes 12296 | tf_op jit(solution)/shard_map/ppermute | solution.py:349
  84.8 1.2 %collective-permute-start.22 = (f32[8,128]{1,0:T(8,128)S(1)}, f32[8,128]{1,0:T(8,128)S(1)}, u32[]{:S(2)}, u32[]{:S(2)}) collective-permute-start(f32[8,128]{1,0:T(8,128)S(1)} %add.6), channel_id=1, source_target_pairs={{0,1},{1,0},{2,3},{3,2},{4,5},{5,4},{6,7},{7,6},{8,9},{9,8},{10,11... | collective-permute-start | bytes 12296 | tf_op jit(solution)/shard_map/ppermute | solution.py:349
  (2 other events, 6.8 us)

commit v4 on v3

--- a/solution.py
+++ b/solution.py
@@ -13,7 +13,7 @@
 ANY = pl.BlockSpec(memory_space=pl.ANY)
 PACK_ROWS = 256
 EXTRA = 8
-UNPACK, PACK, NEAR, FAR, BACKWARD, FOLD, HOLD, LAST, RELAY = 0.01, 0.01, 3, 0.01, 0.01, 0.01, 0.01, 3, 1.5
+UNPACK, PACK, NEAR, FAR, BACKWARD, FOLD, HOLD, LAST, RELAY, FINISH = 0.01, 0.01, 3, 0.01, 0.01, 0.01, 0.01, 3, 1.5, 0.01
 
 
 def params(mib):
@@ -55,12 +55,14 @@
             for j in range(positions):
                 part = moved[j * chunk : (j + 1) * chunk]
                 outs[j][here, :] = part
+        outs[-1][...] = jnp.zeros_like(outs[-1])
 
     return pl.pallas_call(
         body,
         in_specs=[ANY],
-        out_specs=[VMEM] * positions,
-        out_shape=[jax.ShapeDtypeStruct((frames, width), HALF)] * positions,
+        out_specs=[VMEM] * (positions + 1),
+        out_shape=[jax.ShapeDtypeStruct((frames, width), HALF)] * positions
+        + [jax.ShapeDtypeStruct((8, 128), WIDE)],
         scratch_shapes=[pltpu.VMEM(hidden.shape, HALF), pltpu.SemaphoreType.DMA((steps,))],
         cost_estimate=cost(UNPACK),
         compiler_params=params(58),
@@ -81,16 +83,17 @@
         pick = (lax.rem(c, chunk) == lax.div(r, positions)) & (
             lax.rem(r, positions) == (lax.div(c, chunk) ^ me)
         )
-        flat = jnp.concatenate([ref[...] for ref in refs[:-1]], axis=0)
+        flat = jnp.concatenate([ref[...] for ref in refs[:-2]], axis=0)
         moved = jnp.dot(pick.astype(HALF), flat, preferred_element_type=WIDE).astype(HALF)
-        refs[-1][...] = moved.reshape(chunk, positions, width)
+        refs[-2][...] = moved.reshape(chunk, positions, width)
+        refs[-1][...] = jnp.zeros_like(refs[-1])
 
     return pl.pallas_call(
         body,
         grid=(frames // chunk,),
         in_specs=[pl.BlockSpec((chunk, width), lambda i: (i, 0))] * positions,
-        out_specs=pl.BlockSpec((chunk, positions, width), lambda i: (i, 0, 0)),
-        out_shape=jax.ShapeDtypeStruct((frames, positions, width), HALF),
+        out_specs=[pl.BlockSpec((chunk, positions, width), lambda i: (i, 0, 0)), pl.BlockSpec((8, 128), lambda i: (0, 0))],
+        out_shape=[jax.ShapeDtypeStruct((frames, positions, width), HALF), jax.ShapeDtypeStruct((8, 128), WIDE)],
         cost_estimate=cost(PACK),
         compiler_params=params(24),
         name="pack",
@@ -340,6 +343,24 @@
     return out[0], out[-1]
 
 
+def finish(parts, after):
+    def body(*refs):
+        total = refs[0][...]
+        for ref in refs[1 : len(parts)]:
+            total = total + ref[...]
+        refs[-1][...] = total[:1, :1]
+
+    return pl.pallas_call(
+        body,
+        in_specs=[VMEM] * len(parts) + [ANY] * len(after),
+        out_specs=VMEM,
+        out_shape=jax.ShapeDtypeStruct((1, 1), WIDE),
+        cost_estimate=cost(FINISH),
+        compiler_params=params(4),
+        name="finish",
+    )(*parts, *after)
+
+
 def per_device(n_dp, n_fsdp, hidden, head, gain, targets, lengths):
     inner = 2
     line = n_dp // inner
@@ -364,21 +385,21 @@
         if small and o == 3:
             break
         pieces[o * inner] = swap(pieces[(o ^ bit) * inner], "dp", bit * inner)
-    own, side, *away = unpack(hidden)
+    own, side, *away, unpacked = unpack(hidden)
     far = exchange(away, [], RELAY)
     for o in range(line):
         if small and o == 2:
-            pieces[4] = hold([], pieces[4], [own])[1]
+            pieces[4] = hold([], pieces[4], [unpacked])[1]
         if small and o == 1:
-            gain, pieces[2] = hold(gains, pieces[2], [own, pieces[1]])
+            gain, pieces[2] = hold(gains, pieces[2], [pieces[1]])
         if pieces[o * inner] is not None:
             pieces[o * inner + 1] = swap(pieces[o * inner], "dp", 1)
     if small:
         gains = [gain, swap(gain, "dp", 2)]
         gain, side = hold(gains, side, [pieces[4]])
-        pieces[6] = hold([], swap(pieces[4], "dp", 2), [pieces[3], pieces[5]])[1]
+        gains = [gain, swap(gain, "dp", 4)]
+        pieces[6] = hold([], swap(pieces[4], "dp", 2), [pieces[3], gains[1], pieces[5]])[1]
         pieces[7] = swap(pieces[6], "dp", 1)
-        gains = [gain, swap(gain, "dp", 4)]
     else:
         gains = [lax.all_gather(gain, "dp", axis=1, tiled=True)]
     side = swap(side, "fsdp", 1)
@@ -418,13 +439,10 @@
             across[waiting.pop(0)] = swap(held[0], "dp", 1)
     grad_head, loss, _ = fold([parts[0], across[0], *came[0]], loss, last=True)
 
-    grad_hidden = pack([near[0], swap(near[1], "fsdp", 1), *exchange(far, order)])
-
-    bit = n_fsdp // 2
-    while bit:
-        loss = loss + swap(loss, "fsdp", bit)
-        bit //= 2
-    return loss[0, 0], grad_hidden, grad_head[None]
+    grad_hidden, packed = pack([near[0], swap(near[1], "fsdp", 1), *exchange(far, order)])
+
+    parts = [loss] + [swap(loss, "fsdp", j) for j in range(1, n_fsdp)]
+    return finish(parts, [packed])[0, 0], grad_hidden, grad_head[None]
 
 
 def solution(mesh):

time: 89.2 us -> 86.7 us (0.972)
  waiting for transfers between devices: 42.3 us -> 29.9 us
  starting transfers between devices: 25.4 us -> 35.6 us
    ppermute x27 -> x28, waiting for transfers between devices: 42.3 us -> 29.9 us  [swap(): return lax.ppermute(value, axis, [(i, i ^ offset) for i in range(size)])]
    ppermute x27 -> x28, starting transfers between devices: 25.4 us -> 35.6 us  [swap(): return lax.ppermute(value, axis, [(i, i ^ offset) for i in range(size)])]
    pallas_call x1 -> x2, Pallas kernels: 3.59 us -> 4.1 us  [the longest x1 3.58 us: unpack(): pl.pallas_call(body, in_specs=[ANY], out_specs=[VMEM] * (positions + 1),...]
  transfers between devices with their start and end apart: 27 -> 28, of which waited for: 14 -> 11; matrix products, arithmetic and copies ran while one was open for 1% -> 0% of each run, Pallas kernels for 13% -> 16%
where the time goes in v4:
time: 86.7 us; the launch traced here: 86.5 us
  starting transfers between devices  35.6 us (41%)
  waiting for transfers between devices  29.9 us (34%)
  Pallas kernels  19.5 us (22%)
    ppermute x28, starting transfers between devices, swap(): return lax.ppermute(value, axis, [(i, i ^ offset) for i in range(size)])  35.6 us
    ppermute x28, waiting for transfers between devices, swap(): return lax.ppermute(value, axis, [(i, i ^ offset) for i in range(size)])  29.9 us
    pallas_call x1, Pallas kernels, forward_far(): pl.pallas_call(body, in_specs=[SMEM] + [VMEM] * (6 + n), out_specs=[VMEM]...  4.92 us
    pallas_call x1, Pallas kernels, unpack(): pl.pallas_call(body, in_specs=[ANY], out_specs=[VMEM] * (positions + 1),...  3.58 us
    pallas_call x1, Pallas kernels, forward_near(): pl.pallas_call(body, in_specs=[SMEM] + [VMEM] * (1 + n_gain + n) + [ANY]...  3.47 us
    pallas_call x2, Pallas kernels, backward(): pl.pallas_call(body, in_specs=[VMEM] * (3 + n) + [ANY] * len(after), out_...  3.18 us
    pallas_call x1, Pallas kernels, pack(): pl.pallas_call(body, grid=(frames // chunk,), in_specs=[pl.BlockSpec((chu...  2.53 us
  transfers between devices with their start and end apart: 28, of which 11 were waited for; matrix products, arithmetic and copies ran while one was open for 0% of the time, Pallas kernels for 16%

profile of v4, /device:TPU:0, one launch (start us, length us, event | category | flops | bytes accessed | tf_op | source)
XLA Modules:
  0.0 86.5 jit_solution(5796906573841240063)
XLA Ops:
  0.6 3.0 %collective-permute-start.2 = (bf16[128,1024]{1,0:T(8,128)(2,1)}, bf16[128,1024]{1,0:T(8,128)(2,1)S(1)}, u32[]{:S(2)}, u32[]{:S(2)}) collective-permute-start(bf16[128,1024]{1,0:T(8,128)(2,1)} %bitcast.6), channel_id=1, source_target_pairs={{0,4},{4,0},{8,12},{12,8},{16,20},{20,16},{24,28},{28,24},{1,5},{5... | collective-permute-start | bytes 786440 | tf_op jit(solution)/shard_map/ppermute | solution.py:370
  3.6 1.6 %collective-permute-start.1 = (bf16[128,1024]{1,0:T(8,128)(2,1)}, bf16[128,1024]{1,0:T(8,128)(2,1)S(1)}, u32[]{:S(2)}, u32[]{:S(2)}) collective-permute-start(bf16[128,1024]{1,0:T(8,128)(2,1)} %bitcast.7), channel_id=1, source_target_pairs={{0,8},{4,12},{8,0},{12,4},{16,24},{20,28},{24,16},{28,20},{1,9},{5... | collective-permute-start | bytes 786440 | tf_op jit(solution)/shard_map/ppermute | solution.py:370
  5.2 2.6 %collective-permute-start.4 = (bf16[128,1024]{1,0:T(8,128)(2,1)}, bf16[128,1024]{1,0:T(8,128)(2,1)S(1)}, u32[]{:S(2)}, u32[]{:S(2)}) collective-permute-start(bf16[128,1024]{1,0:T(8,128)(2,1)} %bitcast.8), channel_id=1, source_target_pairs={{0,16},{4,20},{8,24},{12,28},{16,0},{20,4},{24,8},{28,12},{1,17},{... | collective-permute-start | bytes 786440 | tf_op jit(solution)/shard_map/ppermute | solution.py:370
  8.3 3.6 %unpack.1 = (bf16[256,1024]{1,0:T(8,128)(2,1)}, bf16[256,1024]{1,0:T(8,128)(2,1)}, bf16[256,1024]{1,0:T(8,128)(2,1)}, bf16[256,1024]{1,0:T(8,128)(2,1)}, f32[8,128]{1,0:T(8,128)}) custom-call(bf16[256,4,1024]{2,1,0:T(4,128)(2,1)} %hidden_ref.1), custom_call_target="tpu_custom_call" | custom-call | flops 10000000 | tf_op jit(solution)/shard_map/unpack/pallas_call | solution.py:60
  11.9 1.6 %collective-permute-start.11 = (bf16[256,1024]{1,0:T(8,128)(2,1)}, bf16[256,1024]{1,0:T(8,128)(2,1)S(1)}, u32[]{:S(2)}, u32[]{:S(2)}) collective-permute-start(bf16[256,1024]{1,0:T(8,128)(2,1)} %get-tuple-element.50), channel_id=1, source_target_pairs={{0,2},{1,3},{2,0},{3,1},{4,6},{5,7},{6,4},{7,5},{8,10},{9,11},{10,... | collective-permute-start | bytes 1572872 | tf_op jit(solution)/shard_map/ppermute | solution.py:370
  14.0 3.1 %collective-permute-done.1.refs_2_ = bf16[128,1024]{1,0:T(8,128)(2,1)S(1)} collective-permute-done((bf16[128,1024]{1,0:T(8,128)(2,1)}, bf16[128,1024]{1,0:T(8,128)(2,1)S(1)}, u32[]{:S(2)}, u32[]{:S(2)}) %collective-permute-start.1) | collective-permute-done | bytes 262176 | tf_op jit(solution)/shard_map/ppermute | solution.py:370
  17.6 1.9 %collective-permute-done.4.refs_0_ = bf16[128,1024]{1,0:T(8,128)(2,1)S(1)} collective-permute-done((bf16[128,1024]{1,0:T(8,128)(2,1)}, bf16[128,1024]{1,0:T(8,128)(2,1)S(1)}, u32[]{:S(2)}, u32[]{:S(2)}) %collective-permute-start.4) | collective-permute-done | bytes 262176 | tf_op jit(solution)/shard_map/ppermute | solution.py:370
  20.2 1.0 %collective-permute-done.3.refs_1_ = bf16[2,128]{1,0:T(2,128)(2,1)S(1)} collective-permute-done((bf16[2,128]{1,0:T(2,128)(2,1)S(1)}, bf16[2,128]{1,0:T(2,128)(2,1)S(1)}, u32[]{:S(2)}, u32[]{:S(2)}) %collective-permute-start.3) | collective-permute-done | bytes 544 | tf_op jit(solution)/shard_map/ppermute | solution.py:370
  21.1 1.2 %collective-permute-start.5 = (bf16[4,128]{1,0:T(4,128)(2,1)S(1)}, bf16[4,128]{1,0:T(4,128)(2,1)S(1)}, u32[]{:S(2)}, u32[]{:S(2)}) collective-permute-start(bf16[4,128]{1,0:T(4,128)(2,1)S(1)} %get-tuple-element.44.refs_2_), channel_id=1, source_target_pairs={{0,16},{4,20},{8,24},{12,28},{16,0},{20,4},{24,8},{28,12},{1,17},{... | collective-permute-start | bytes 3080 | tf_op jit(solution)/shard_map/ppermute | solution.py:370
  22.3 2.0 %collective-permute-start.9 = (bf16[128,1024]{1,0:T(8,128)(2,1)S(1)}, bf16[128,1024]{1,0:T(8,128)(2,1)S(1)}, u32[]{:S(2)}, u32[]{:S(2)}) collective-permute-start(bf16[128,1024]{1,0:T(8,128)(2,1)S(1)} %hold.7.refs_3_.refs_10_), channel_id=1, source_target_pairs={{0,8},{4,12},{8,0},{12,4},{16,24},{20,28},{24,16},{28,20},{1,9},{5... | collective-permute-start | bytes 786440 | tf_op jit(solution)/shard_map/ppermute | solution.py:370
  24.3 1.3 %collective-permute-done.5.refs_2_.refs_3_ = bf16[4,128]{1,0:T(4,128)(2,1)S(1)} collective-permute-done((bf16[4,128]{1,0:T(4,128)(2,1)S(1)}, bf16[4,128]{1,0:T(4,128)(2,1)S(1)}, u32[]{:S(2)}, u32[]{:S(2)}) %collective-permute-start.5) | collective-permute-done | bytes 1056 | tf_op jit(solution)/shard_map/ppermute | solution.py:370
  25.6 1.6 %collective-permute-start.8 = (bf16[128,1024]{1,0:T(8,128)(2,1)S(1)}, bf16[128,1024]{1,0:T(8,128)(2,1)S(1)}, u32[]{:S(2)}, u32[]{:S(2)}) collective-permute-start(bf16[128,1024]{1,0:T(8,128)(2,1)S(1)} %hold.7.refs_3_.refs_10_), channel_id=1, source_target_pairs={{0,4},{4,0},{8,12},{12,8},{16,20},{20,16},{24,28},{28,24},{1,5},{5... | collective-permute-start | bytes 786440 | tf_op jit(solution)/shard_map/ppermute | solution.py:370
  27.2 1.4 %collective-permute-done.9.refs_0_ = bf16[128,1024]{1,0:T(8,128)(2,1)S(1)} collective-permute-done((bf16[128,1024]{1,0:T(8,128)(2,1)S(1)}, bf16[128,1024]{1,0:T(8,128)(2,1)S(1)}, u32[]{:S(2)}, u32[]{:S(2)}) %collective-permute-start.9) | collective-permute-done | bytes 262176 | tf_op jit(solution)/shard_map/ppermute | solution.py:370
  28.7 4.8 %collective-permute-done.8.refs_3_.refs_11_ = bf16[128,1024]{1,0:T(8,128)(2,1)S(1)} collective-permute-done((bf16[128,1024]{1,0:T(8,128)(2,1)S(1)}, bf16[128,1024]{1,0:T(8,128)(2,1)S(1)}, u32[]{:S(2)}, u32[]{:S(2)}) %collective-permute-start.8) | collective-permute-done | bytes 262176 | tf_op jit(solution)/shard_map/ppermute | solution.py:370
  33.4 2.1 %collective-permute-start.10 = (bf16[128,1024]{1,0:T(8,128)(2,1)S(1)}, bf16[128,1024]{1,0:T(8,128)(2,1)S(1)}, u32[]{:S(2)}, u32[]{:S(2)}) collective-permute-start(bf16[128,1024]{1,0:T(8,128)(2,1)S(1)} %hold.9.refs_12_), channel_id=1, source_target_pairs={{0,4},{4,0},{8,12},{12,8},{16,20},{20,16},{24,28},{28,24},{1,5},{5... | collective-permute-start | bytes 786440 | tf_op jit(solution)/shard_map/ppermute | solution.py:370
  36.0 3.9 %collective-permute-done.10.refs_13_ = bf16[128,1024]{1,0:T(8,128)(2,1)S(1)} collective-permute-done((bf16[128,1024]{1,0:T(8,128)(2,1)S(1)}, bf16[128,1024]{1,0:T(8,128)(2,1)S(1)}, u32[]{:S(2)}, u32[]{:S(2)}) %collective-permute-start.10) | collective-permute-done | bytes 262176 | tf_op jit(solution)/shard_map/ppermute | solution.py:370
  39.9 3.5 %forward_near.1 = (f32[8,128]{1,0:T(8,128)S(1)}, f32[1,1024]{1,0:T(1,128)S(1)}, bf16[1024,1024]{1,0:T(8,128)(2,1)S(1)}, bf16[2,256,1024]{2,1,0:T(8,128)(2,1)S(1)}, bf16[2,256,1024]{2,1,0:T(8,128)(2,1)S(1)}) custom-call(s32[8]{0:T(128)S(1)} %copy-done.3, s32[1,1024]{1,0:T(1,128)S(1)} %bitcast.4, bf16[4,128]{1,0:T(4,128)(2,1)S(1)} %get-tuple-element.44.refs_2_, ...), custom_call_target="tpu_custom_call" | custom-call | flops 3000000000 | tf_op jit(solution)/shard_map/forward_near/pallas_call | solution.py:177
  43.4 4.9 %forward_far.1 = (f32[8,1024]{1,0:T(8,128)S(1)}, bf16[2,256,1024]{2,1,0:T(8,128)(2,1)S(1)}, bf16[128,1024]{1,0:T(8,128)(2,1)S(1)}, bf16[128,1024]{1,0:T(8,128)(2...) custom-call(s32[8]{0:T(128)S(1)} %copy-done.3, ...), custom_call_target="tpu_custom_call" | custom-call | flops 10000000 | tf_op jit(solution)/shard_map/forward_far/pallas_call | solution.py:240
  48.3 2.1 %collective-permute-start.15 = (bf16[136,1024]{1,0:T(8,128)(2,1)S(1)}, bf16[136,1024]{1,0:T(8,128)(2,1)S(1)}, u32[]{:S(2)}, u32[]{:S(2)}) collective-permute-start(bf16[136,1024]{1,0:T(8,128)(2,1)S(1)} %get-tuple-element.59), channel_id=1, source_target_pairs={{0,4},{4,0},{8,12},{12,8},{16,20},{20,16},{24,28},{28,24},{1,5},{5... | collective-permute-start | bytes 835592 | tf_op jit(solution)/shard_map/ppermute | solution.py:370
  50.4 1.6 %backward.2 = (bf16[256,1024]{1,0:T(8,128)(2,1)S(1)}, bf16[256,1024]{1,0:T(8,128)(2,1)S(1)}) custom-call(f32[1,1024]{1,0:T(1,128)S(1)} %get-tuple-element.48.refs_2_.gain_ref, bf16[1024,1024]{1,0:T(8,128)(2,1)S(1)} %get-tuple-element.49.refs_3_.weight_ref, bf16[2,256,1024]{2,1,0:T(8,128)(2,1)S(1)} %get-tuple-element.62.slope_ref, ...), custom_call_target="tpu_custom_call" | custom-call | flops 10000000 | tf_op jit(solution)/shard_map/backward/pallas_call | solution.py:278
  52.0 1.6 %collective-permute-start.25 = (bf16[256,1024]{1,0:T(8,128)(2,1)S(1)}, bf16[256,1024]{1,0:T(8,128)(2,1)S(1)}, u32[]{:S(2)}, u32[]{:S(2)}) collective-permute-start(bf16[256,1024]{1,0:T(8,128)(2,1)S(1)} %get-tuple-element.75), channel_id=1, source_target_pairs={{0,2},{1,3},{2,0},{3,1},{4,6},{5,7},{6,4},{7,5},{8,10},{9,11},{10,... | collective-permute-start | bytes 1572872 | tf_op jit(solution)/shard_map/ppermute | solution.py:370
  54.1 2.5 %collective-permute-done.15.refs_1_ = bf16[136,1024]{1,0:T(8,128)(2,1)S(1)} collective-permute-done((bf16[136,1024]{1,0:T(8,128)(2,1)S(1)}, bf16[136,1024]{1,0:T(8,128)(2,1)S(1)}, u32[]{:S(2)}, u32[]{:S(2)}) %collective-permute-start.15) | collective-permute-done | bytes 278560 | tf_op jit(solution)/shard_map/ppermute | solution.py:370
  56.7 2.5 %collective-permute-start.14 = (bf16[128,1024]{1,0:T(8,128)(2,1)S(1)}, bf16[128,1024]{1,0:T(8,128)(2,1)S(1)}, u32[]{:S(2)}, u32[]{:S(2)}) collective-permute-start(bf16[128,1024]{1,0:T(8,128)(2,1)S(1)} %get-tuple-element.57), channel_id=1, source_target_pairs={{0,4},{4,0},{8,12},{12,8},{16,20},{20,16},{24,28},{28,24},{1,5},{5... | collective-permute-start | bytes 786440 | tf_op jit(solution)/shard_map/ppermute | solution.py:370
  59.4 6.5 %collective-permute-done.14.refs_1_ = bf16[128,1024]{1,0:T(8,128)(2,1)S(1)} collective-permute-done((bf16[128,1024]{1,0:T(8,128)(2,1)S(1)}, bf16[128,1024]{1,0:T(8,128)(2,1)S(1)}, u32[]{:S(2)}, u32[]{:S(2)}) %collective-permute-start.14) | collective-permute-done | bytes 262176 | tf_op jit(solution)/shard_map/ppermute | solution.py:370
  66.0 4.1 %collective-permute-start.20 = (bf16[136,1024]{1,0:T(8,128)(2,1)S(1)}, bf16[136,1024]{1,0:T(8,128)(2,1)S(1)}, u32[]{:S(2)}, u32[]{:S(2)}) collective-permute-start(bf16[136,1024]{1,0:T(8,128)(2,1)S(1)} %get-tuple-element.70.refs_2_), channel_id=1, source_target_pairs={{0,16},{4,20},{8,24},{12,28},{16,0},{20,4},{24,8},{28,12},{1,17},{... | collective-permute-start | bytes 835592 | tf_op jit(solution)/shard_map/ppermute | solution.py:370
  70.1 1.9 %collective-permute-start.17 = (bf16[128,1024]{1,0:T(8,128)(2,1)S(1)}, bf16[128,1024]{1,0:T(8,128)(2,1)S(1)}, u32[]{:S(2)}, u32[]{:S(2)}) collective-permute-start(bf16[128,1024]{1,0:T(8,128)(2,1)S(1)} %get-tuple-element.67), channel_id=1, source_target_pairs={{0,4},{4,0},{8,12},{12,8},{16,20},{20,16},{24,28},{28,24},{1,5},{5... | collective-permute-start | bytes 786440 | tf_op jit(solution)/shard_map/ppermute | solution.py:370
  72.1 2.5 %collective-permute-start.19 = (bf16[128,1024]{1,0:T(8,128)(2,1)S(1)}, bf16[128,1024]{1,0:T(8,128)(2,1)S(1)}, u32[]{:S(2)}, u32[]{:S(2)}) collective-permute-start(bf16[128,1024]{1,0:T(8,128)(2,1)S(1)} %fold.6.refs_2_), channel_id=1, source_target_pairs={{0,8},{4,12},{8,0},{12,4},{16,24},{20,28},{24,16},{28,20},{1,9},{5... | collective-permute-start | bytes 786440 | tf_op jit(solution)/shard_map/ppermute | solution.py:370
  74.6 1.6 %backward.3 = (bf16[256,1024]{1,0:T(8,128)(2,1)S(1)}, bf16[256,1024]{1,0:T(8,128)(2,1)S(1)}) custom-call(f32[1,1024]{1,0:T(1,128)S(1)} %get-tuple-element.48.refs_2_.gain_ref, bf16[1024,1024]{1,0:T(8,128)(2,1)S(1)} %get-tuple-element.49.refs_3_.weight_ref, bf16[2,256,1024]{2,1,0:T(8,128)(2,1)S(1)} %get-tuple-element.53.refs_7_.slope_ref, ...), custom_call_target="tpu_custom_call" | custom-call | flops 10000000 | tf_op jit(solution)/shard_map/backward/pallas_call | solution.py:278
  76.8 3.1 %collective-permute-done.19.refs_2_ = bf16[128,1024]{1,0:T(8,128)(2,1)S(1)} collective-permute-done((bf16[128,1024]{1,0:T(8,128)(2,1)S(1)}, bf16[128,1024]{1,0:T(8,128)(2,1)S(1)}, u32[]{:S(2)}, u32[]{:S(2)}) %collective-permute-start.19) | collective-permute-done | bytes 262176 | tf_op jit(solution)/shard_map/ppermute | solution.py:370
  80.0 0.9 %fold.7 = (f32[128,1024]{1,0:T(8,128)}, f32[8,128]{1,0:T(8,128)S(1)}) custom-call(bf16[128,1024]{1,0:T(8,128)(2,1)S(1)} %get-tuple-element.55.refs_0_, bf16[128,1024]{1,0:T(8,128)(2,1)S(1)} %collective-permute-done.17.refs_1_, bf16[128,1024]{1,0:T(8,128)(2,1)S(1)} %collective-permute-done.19.refs_2_, bf16[136,1024]{1,0:T(8,128)(2,1)S(1)} %collective-permute-done.20.refs_3_, ...), custom_call_target="tpu_custom_call" | custom-call | flops 3000000000 | tf_op jit(solution)/shard_map/fold/pallas_call | solution.py:312
  80.9 2.4 %collective-permute-start.22 = (f32[8,128]{1,0:T(8,128)S(1)}, f32[8,128]{1,0:T(8,128)S(1)}, u32[]{:S(2)}, u32[]{:S(2)}) collective-permute-start(f32[8,128]{1,0:T(8,128)S(1)} %get-tuple-element.72.refs_0_), channel_id=1, source_target_pairs={{0,2},{1,3},{2,0},{3,1},{4,6},{5,7},{6,4},{7,5},{8,10},{9,11},{10,... | collective-permute-start | bytes 12296 | tf_op jit(solution)/shard_map/ppermute | solution.py:370
  83.4 2.5 %pack.1 = (bf16[256,4,1024]{2,1,0:T(4,128)(2,1)}, f32[8,128]{1,0:T(8,128)S(1)}) custom-call(bf16[256,1024]{1,0:T(8,128)(2,1)S(1)} %get-tuple-element.73.refs_0_, bf16[256,1024]{1,0:T(8,128)(2,1)S(1)} %collective-permute-done.24.refs_1_, bf16[256,1024]{1,0:T(8,128)(2,1)S(1)} %collective-permute-done.25.refs_1_.refs_2_, ...), custom_call_target="tpu_custom_call" | custom-call | flops 10000000 | tf_op jit(solution)/shard_map/pack/pallas_call | solution.py:91
  (53 shorter events, 4.9 us)
Async XLA Ops:
  0.6 16.5 %copy-start.4 = (bf16[1,128]{1,0:T(2,128)(2,1)S(1)}, bf16[1,128]{1,0:T(2,128)(2,1)}, u32[]{:S(2)}) copy-start(bf16[1,128]{1,0:T(2,128)(2,1)} %refs_0_.3) | copy-start | bytes 772
  0.6 13.4 %collective-permute-start.2 = (bf16[128,1024]{1,0:T(8,128)(2,1)}, bf16[128,1024]{1,0:T(8,128)(2,1)S(1)}, u32[]{:S(2)}, u32[]{:S(2)}) collective-permute-start(bf16[128,1024]{1,0:T(8,128)(2,1)} %bitcast.6), channel_id=1, source_target_pairs={{0,4},{4,0},{8,12},{12,8},{16,20},{20,16},{24,28},{28,24},{1,5},{5... | collective-permute-start | bytes 786440 | tf_op jit(solution)/shard_map/ppermute | solution.py:370
  3.6 13.5 %collective-permute-start.1 = (bf16[128,1024]{1,0:T(8,128)(2,1)}, bf16[128,1024]{1,0:T(8,128)(2,1)S(1)}, u32[]{:S(2)}, u32[]{:S(2)}) collective-permute-start(bf16[128,1024]{1,0:T(8,128)(2,1)} %bitcast.7), channel_id=1, source_target_pairs={{0,8},{4,12},{8,0},{12,4},{16,24},{20,28},{24,16},{28,20},{1,9},{5... | collective-permute-start | bytes 786440 | tf_op jit(solution)/shard_map/ppermute | solution.py:370
  5.2 14.3 %collective-permute-start.4 = (bf16[128,1024]{1,0:T(8,128)(2,1)}, bf16[128,1024]{1,0:T(8,128)(2,1)S(1)}, u32[]{:S(2)}, u32[]{:S(2)}) collective-permute-start(bf16[128,1024]{1,0:T(8,128)(2,1)} %bitcast.8), channel_id=1, source_target_pairs={{0,16},{4,20},{8,24},{12,28},{16,0},{20,4},{24,8},{28,12},{1,17},{... | collective-permute-start | bytes 786440 | tf_op jit(solution)/shard_map/ppermute | solution.py:370
  7.8 5.7 %collective-permute-start = (bf16[1,128]{1,0:T(2,128)(2,1)}, bf16[1,128]{1,0:T(2,128)(2,1)S(1)}, u32[]{:S(2)}, u32[]{:S(2)}) collective-permute-start(bf16[1,128]{1,0:T(2,128)(2,1)} %refs_0_.3), channel_id=1, source_target_pairs={{0,4},{4,0},{8,12},{12,8},{16,20},{20,16},{24,28},{28,24},{1,5},{5... | collective-permute-start | bytes 776 | tf_op jit(solution)/shard_map/ppermute | solution.py:370
  11.9 23.6 %collective-permute-start.11 = (bf16[256,1024]{1,0:T(8,128)(2,1)}, bf16[256,1024]{1,0:T(8,128)(2,1)S(1)}, u32[]{:S(2)}, u32[]{:S(2)}) collective-permute-start(bf16[256,1024]{1,0:T(8,128)(2,1)} %get-tuple-element.50), channel_id=1, source_target_pairs={{0,2},{1,3},{2,0},{3,1},{4,6},{5,7},{6,4},{7,5},{8,10},{9,11},{10,... | collective-permute-start | bytes 1572872 | tf_op jit(solution)/shard_map/ppermute | solution.py:370
  13.5 22.5 %collective-permute-start.12 = (bf16[256,1024]{1,0:T(8,128)(2,1)}, bf16[256,1024]{1,0:T(8,128)(2,1)S(1)}, u32[]{:S(2)}, u32[]{:S(2)}) collective-permute-start(bf16[256,1024]{1,0:T(8,128)(2,1)} %get-tuple-element.51), channel_id=1, source_target_pairs={{0,2},{1,3},{2,0},{3,1},{4,6},{5,7},{6,4},{7,5},{8,10},{9,11},{10,... | collective-permute-start | bytes 1572872 | tf_op jit(solution)/shard_map/ppermute | solution.py:370
  17.1 10.1 %collective-permute-start.7 = (bf16[128,1024]{1,0:T(8,128)(2,1)S(1)}, bf16[128,1024]{1,0:T(8,128)(2,1)S(1)}, u32[]{:S(2)}, u32[]{:S(2)}) collective-permute-start(bf16[128,1024]{1,0:T(8,128)(2,1)S(1)} %get-tuple-element.47.refs_8_), channel_id=1, source_target_pairs={{0,4},{4,0},{8,12},{12,8},{16,20},{20,16},{24,28},{28,24},{1,5},{5... | collective-permute-start | bytes 786440 | tf_op jit(solution)/shard_map/ppermute | solution.py:370
  17.6 3.5 %collective-permute-start.3 = (bf16[2,128]{1,0:T(2,128)(2,1)S(1)}, bf16[2,128]{1,0:T(2,128)(2,1)S(1)}, u32[]{:S(2)}, u32[]{:S(2)}) collective-permute-start(bf16[2,128]{1,0:T(2,128)(2,1)S(1)} %get-tuple-element.41.refs_0_), channel_id=1, source_target_pairs={{0,8},{4,12},{8,0},{12,4},{16,24},{20,28},{24,16},{28,20},{1,9},{5... | collective-permute-start | bytes 1544 | tf_op jit(solution)/shard_map/ppermute | solution.py:370
  21.1 4.5 %collective-permute-start.5 = (bf16[4,128]{1,0:T(4,128)(2,1)S(1)}, bf16[4,128]{1,0:T(4,128)(2,1)S(1)}, u32[]{:S(2)}, u32[]{:S(2)}) collective-permute-start(bf16[4,128]{1,0:T(4,128)(2,1)S(1)} %get-tuple-element.44.refs_2_), channel_id=1, source_target_pairs={{0,16},{4,20},{8,24},{12,28},{16,0},{20,4},{24,8},{28,12},{1,17},{... | collective-permute-start | bytes 3080 | tf_op jit(solution)/shard_map/ppermute | solution.py:370
  22.3 6.4 %collective-permute-start.9 = (bf16[128,1024]{1,0:T(8,128)(2,1)S(1)}, bf16[128,1024]{1,0:T(8,128)(2,1)S(1)}, u32[]{:S(2)}, u32[]{:S(2)}) collective-permute-start(bf16[128,1024]{1,0:T(8,128)(2,1)S(1)} %hold.7.refs_3_.refs_10_), channel_id=1, source_target_pairs={{0,8},{4,12},{8,0},{12,4},{16,24},{20,28},{24,16},{28,20},{1,9},{5... | collective-permute-start | bytes 786440 | tf_op jit(solution)/shard_map/ppermute | solution.py:370
  25.6 7.8 %collective-permute-start.8 = (bf16[128,1024]{1,0:T(8,128)(2,1)S(1)}, bf16[128,1024]{1,0:T(8,128)(2,1)S(1)}, u32[]{:S(2)}, u32[]{:S(2)}) collective-permute-start(bf16[128,1024]{1,0:T(8,128)(2,1)S(1)} %hold.7.refs_3_.refs_10_), channel_id=1, source_target_pairs={{0,4},{4,0},{8,12},{12,8},{16,20},{20,16},{24,28},{28,24},{1,5},{5... | collective-permute-start | bytes 786440 | tf_op jit(solution)/shard_map/ppermute | solution.py:370
  27.2 12.7 %collective-permute-start.6 = (bf16[256,1024]{1,0:T(8,128)(2,1)}, bf16[256,1024]{1,0:T(8,128)(2,1)S(1)}, u32[]{:S(2)}, u32[]{:S(2)}) collective-permute-start(bf16[256,1024]{1,0:T(8,128)(2,1)} %get-tuple-element.46), channel_id=1, source_target_pairs={{0,1},{1,0},{2,3},{3,2},{4,5},{5,4},{6,7},{7,6},{8,9},{9,8},{10,11... | collective-permute-start | bytes 1572872 | tf_op jit(solution)/shard_map/ppermute | solution.py:370
  33.4 6.5 %copy-start.1 = (s32[1024,1]{0,1:T(1,128)S(1)}, s32[1024,1]{0,1:T(1,128)}, u32[]{:S(2)}) copy-start(s32[1024,1]{0,1:T(1,128)} %param.8) | copy-start | bytes 12292
  33.4 6.5 %copy-start.3 = (s32[8]{0:T(128)S(1)}, s32[8]{0:T(128)}, u32[]{:S(2)}) copy-start(s32[8]{0:T(128)} %refs_0_.5) | copy-start | bytes 100
  33.4 6.5 %copy-start.5 = (bf16[1,128,1024]{2,1,0:T(8,128)(2,1)S(1)}, bf16[1,128,1024]{2,1,0:T(8,128)(2,1)}, u32[]{:S(2)}) copy-start(bf16[1,128,1024]{2,1,0:T(8,128)(2,1)} %param.6) | copy-start | bytes 786436
  33.4 6.4 %collective-permute-start.10 = (bf16[128,1024]{1,0:T(8,128)(2,1)S(1)}, bf16[128,1024]{1,0:T(8,128)(2,1)S(1)}, u32[]{:S(2)}, u32[]{:S(2)}) collective-permute-start(bf16[128,1024]{1,0:T(8,128)(2,1)S(1)} %hold.9.refs_12_), channel_id=1, source_target_pairs={{0,4},{4,0},{8,12},{12,8},{16,20},{20,16},{24,28},{28,24},{1,5},{5... | collective-permute-start | bytes 786440 | tf_op jit(solution)/shard_map/ppermute | solution.py:370
  36.0 7.4 %collective-permute-start.13 = (bf16[256,1024]{1,0:T(8,128)(2,1)S(1)}, bf16[256,1024]{1,0:T(8,128)(2,1)S(1)}, u32[]{:S(2)}, u32[]{:S(2)}) collective-permute-start(bf16[256,1024]{1,0:T(8,128)(2,1)S(1)} %hold.10), channel_id=1, source_target_pairs={{0,1},{1,0},{2,3},{3,2},{4,5},{5,4},{6,7},{7,6},{8,9},{9,8},{10,11... | collective-permute-start | bytes 1572872 | tf_op jit(solution)/shard_map/ppermute | solution.py:370
  48.3 8.2 %collective-permute-start.15 = (bf16[136,1024]{1,0:T(8,128)(2,1)S(1)}, bf16[136,1024]{1,0:T(8,128)(2,1)S(1)}, u32[]{:S(2)}, u32[]{:S(2)}) collective-permute-start(bf16[136,1024]{1,0:T(8,128)(2,1)S(1)} %get-tuple-element.59), channel_id=1, source_target_pairs={{0,4},{4,0},{8,12},{12,8},{16,20},{20,16},{24,28},{28,24},{1,5},{5... | collective-permute-start | bytes 835592 | tf_op jit(solution)/shard_map/ppermute | solution.py:370
  52.0 24.3 %collective-permute-start.25 = (bf16[256,1024]{1,0:T(8,128)(2,1)S(1)}, bf16[256,1024]{1,0:T(8,128)(2,1)S(1)}, u32[]{:S(2)}, u32[]{:S(2)}) collective-permute-start(bf16[256,1024]{1,0:T(8,128)(2,1)S(1)} %get-tuple-element.75), channel_id=1, source_target_pairs={{0,2},{1,3},{2,0},{3,1},{4,6},{5,7},{6,4},{7,5},{8,10},{9,11},{10,... | collective-permute-start | bytes 1572872 | tf_op jit(solution)/shard_map/ppermute | solution.py:370
  53.6 22.8 %collective-permute-start.26 = (bf16[256,1024]{1,0:T(8,128)(2,1)S(1)}, bf16[256,1024]{1,0:T(8,128)(2,1)S(1)}, u32[]{:S(2)}, u32[]{:S(2)}) collective-permute-start(bf16[256,1024]{1,0:T(8,128)(2,1)S(1)} %get-tuple-element.63.refs_4_), channel_id=1, source_target_pairs={{0,2},{1,3},{2,0},{3,1},{4,6},{5,7},{6,4},{7,5},{8,10},{9,11},{10,... | collective-permute-start | bytes 1572872 | tf_op jit(solution)/shard_map/ppermute | solution.py:370
  56.7 9.2 %collective-permute-start.16 = (bf16[136,1024]{1,0:T(8,128)(2,1)S(1)}, bf16[136,1024]{1,0:T(8,128)(2,1)S(1)}, u32[]{:S(2)}, u32[]{:S(2)}) collective-permute-start(bf16[136,1024]{1,0:T(8,128)(2,1)S(1)} %get-tuple-element.64.refs_5_), channel_id=1, source_target_pairs={{0,8},{4,12},{8,0},{12,4},{16,24},{20,28},{24,16},{28,20},{1,9},{5... | collective-permute-start | bytes 835592 | tf_op jit(solution)/shard_map/ppermute | solution.py:370
  56.7 9.1 %collective-permute-start.14 = (bf16[128,1024]{1,0:T(8,128)(2,1)S(1)}, bf16[128,1024]{1,0:T(8,128)(2,1)S(1)}, u32[]{:S(2)}, u32[]{:S(2)}) collective-permute-start(bf16[128,1024]{1,0:T(8,128)(2,1)S(1)} %get-tuple-element.57), channel_id=1, source_target_pairs={{0,4},{4,0},{8,12},{12,8},{16,20},{20,16},{24,28},{28,24},{1,5},{5... | collective-permute-start | bytes 786440 | tf_op jit(solution)/shard_map/ppermute | solution.py:370
  59.3 12.7 %collective-permute-start.18 = (bf16[128,1024]{1,0:T(8,128)(2,1)S(1)}, bf16[128,1024]{1,0:T(8,128)(2,1)S(1)}, u32[]{:S(2)}, u32[]{:S(2)}) collective-permute-start(bf16[128,1024]{1,0:T(8,128)(2,1)S(1)} %get-tuple-element.69), channel_id=1, source_target_pairs={{0,4},{4,0},{8,12},{12,8},{16,20},{20,16},{24,28},{28,24},{1,5},{5... | collective-permute-start | bytes 786440 | tf_op jit(solution)/shard_map/ppermute | solution.py:370
  66.0 14.0 %collective-permute-start.20 = (bf16[136,1024]{1,0:T(8,128)(2,1)S(1)}, bf16[136,1024]{1,0:T(8,128)(2,1)S(1)}, u32[]{:S(2)}, u32[]{:S(2)}) collective-permute-start(bf16[136,1024]{1,0:T(8,128)(2,1)S(1)} %get-tuple-element.70.refs_2_), channel_id=1, source_target_pairs={{0,16},{4,20},{8,24},{12,28},{16,0},{20,4},{24,8},{28,12},{1,17},{... | collective-permute-start | bytes 835592 | tf_op jit(solution)/shard_map/ppermute | solution.py:370
  70.1 6.8 %collective-permute-start.17 = (bf16[128,1024]{1,0:T(8,128)(2,1)S(1)}, bf16[128,1024]{1,0:T(8,128)(2,1)S(1)}, u32[]{:S(2)}, u32[]{:S(2)}) collective-permute-start(bf16[128,1024]{1,0:T(8,128)(2,1)S(1)} %get-tuple-element.67), channel_id=1, source_target_pairs={{0,4},{4,0},{8,12},{12,8},{16,20},{20,16},{24,28},{28,24},{1,5},{5... | collective-permute-start | bytes 786440 | tf_op jit(solution)/shard_map/ppermute | solution.py:370
  72.1 7.9 %collective-permute-start.19 = (bf16[128,1024]{1,0:T(8,128)(2,1)S(1)}, bf16[128,1024]{1,0:T(8,128)(2,1)S(1)}, u32[]{:S(2)}, u32[]{:S(2)}) collective-permute-start(bf16[128,1024]{1,0:T(8,128)(2,1)S(1)} %fold.6.refs_2_), channel_id=1, source_target_pairs={{0,8},{4,12},{8,0},{12,4},{16,24},{20,28},{24,16},{28,20},{1,9},{5... | collective-permute-start | bytes 786440 | tf_op jit(solution)/shard_map/ppermute | solution.py:370
  76.3 7.2 %collective-permute-start.24 = (bf16[256,1024]{1,0:T(8,128)(2,1)S(1)}, bf16[256,1024]{1,0:T(8,128)(2,1)S(1)}, u32[]{:S(2)}, u32[]{:S(2)}) collective-permute-start(bf16[256,1024]{1,0:T(8,128)(2,1)S(1)} %get-tuple-element.74), channel_id=1, source_target_pairs={{0,1},{1,0},{2,3},{3,2},{4,5},{5,4},{6,7},{7,6},{8,9},{9,8},{10,11... | collective-permute-start | bytes 1572872 | tf_op jit(solution)/shard_map/ppermute | solution.py:370
  76.4 7.1 %collective-permute-start.27 = (bf16[256,1024]{1,0:T(8,128)(2,1)S(1)}, bf16[256,1024]{1,0:T(8,128)(2,1)S(1)}, u32[]{:S(2)}, u32[]{:S(2)}) collective-permute-start(bf16[256,1024]{1,0:T(8,128)(2,1)S(1)} %hold.11), channel_id=1, source_target_pairs={{0,1},{1,0},{2,3},{3,2},{4,5},{5,4},{6,7},{7,6},{8,9},{9,8},{10,11... | collective-permute-start | bytes 1572872 | tf_op jit(solution)/shard_map/ppermute | solution.py:370
  80.9 5.1 %collective-permute-start.23 = (f32[8,128]{1,0:T(8,128)S(1)}, f32[8,128]{1,0:T(8,128)S(1)}, u32[]{:S(2)}, u32[]{:S(2)}) collective-permute-start(f32[8,128]{1,0:T(8,128)S(1)} %get-tuple-element.72.refs_0_), channel_id=1, source_target_pairs={{0,3},{1,2},{2,1},{3,0},{4,7},{5,6},{6,5},{7,4},{8,11},{9,10},{10,... | collective-permute-start | bytes 12296 | tf_op jit(solution)/shard_map/ppermute | solution.py:370
  80.9 5.1 %collective-permute-start.22 = (f32[8,128]{1,0:T(8,128)S(1)}, f32[8,128]{1,0:T(8,128)S(1)}, u32[]{:S(2)}, u32[]{:S(2)}) collective-permute-start(f32[8,128]{1,0:T(8,128)S(1)} %get-tuple-element.72.refs_0_), channel_id=1, source_target_pairs={{0,2},{1,3},{2,0},{3,1},{4,6},{5,7},{6,4},{7,5},{8,10},{9,11},{10,... | collective-permute-start | bytes 12296 | tf_op jit(solution)/shard_map/ppermute | solution.py:370
  83.3 2.6 %collective-permute-start.21 = (f32[8,128]{1,0:T(8,128)S(1)}, f32[8,128]{1,0:T(8,128)S(1)}, u32[]{:S(2)}, u32[]{:S(2)}) collective-permute-start(f32[8,128]{1,0:T(8,128)S(1)} %get-tuple-element.72.refs_0_), channel_id=1, source_target_pairs={{0,1},{1,0},{2,3},{3,2},{4,5},{5,4},{6,7},{7,6},{8,9},{9,8},{10,11... | collective-permute-start | bytes 12296 | tf_op jit(solution)/shard_map/ppermute | solution.py:370
  (2 other events, 7.1 us)

commit v5 on v4

--- a/solution.py
+++ b/solution.py
@@ -13,7 +13,7 @@
 ANY = pl.BlockSpec(memory_space=pl.ANY)
 PACK_ROWS = 256
 EXTRA = 8
-UNPACK, PACK, NEAR, FAR, BACKWARD, FOLD, HOLD, LAST, RELAY, FINISH = 0.01, 0.01, 3, 0.01, 0.01, 0.01, 0.01, 3, 1.5, 0.01
+UNPACK, PACK, NEAR, FAR, BACKWARD, FOLD, HOLD, LAST, RELAY, FINISH, RIDE = 0.01, 0.01, 3, 0.01, 0.01, 0.01, 0.01, 3, 1.5, 0.01, 0.01
 
 
 def params(mib):
@@ -268,22 +268,24 @@
     return (inverse * weighted - values * scale).astype(HALF)
 
 
-def backward(gain, weights, rows, slopes, after=()):
+def backward(gain, weights, rows, slopes, after=(), held=()):
     n = len(rows)
 
     def body(gain_ref, weight_ref, slope_ref, *refs):
         for j in range(n):
-            refs[n + len(after) + j][...] = grad_rows(refs[j][...], slope_ref[j], weight_ref[...], gain_ref[...])
+            refs[n + len(after) + len(held) + j][...] = grad_rows(refs[j][...], slope_ref[j], weight_ref[...], gain_ref[...])
 
     return pl.pallas_call(
         body,
-        in_specs=[VMEM] * (3 + n) + [ANY] * len(after),
-        out_specs=[VMEM] * n,
-        out_shape=[jax.ShapeDtypeStruct(rows[0].shape, HALF)] * n,
+        in_specs=[VMEM] * (3 + n) + [ANY] * (len(after) + len(held)),
+        out_specs=[VMEM] * n + [ANY] * len(held),
+        out_shape=[jax.ShapeDtypeStruct(rows[0].shape, HALF)] * n
+        + [jax.ShapeDtypeStruct(h.shape, h.dtype) for h in held],
+        input_output_aliases={3 + n + len(after) + i: n + i for i in range(len(held))},
         cost_estimate=cost(BACKWARD),
         compiler_params=params(20),
         name="backward",
-    )(gain, weights, slopes, *rows, *after)
+    )(gain, weights, slopes, *rows, *after, *held)
 
 
 def fold(terms, loss=None, held=(), after=(), last=False):
@@ -315,7 +317,7 @@
         out_specs=[VMEM] * (1 + n_loss) + [ANY] * len(held),
         out_shape=shapes + [jax.ShapeDtypeStruct(h.shape, h.dtype) for h in held],
         input_output_aliases={n + n_loss + i: 1 + n_loss + i for i in range(len(held))},
-        cost_estimate=cost(LAST if last else FOLD),
+        cost_estimate=cost(LAST if last else RIDE if n_loss else FOLD),
         compiler_params=params(8),
         name="fold",
     )(*terms, *([loss] if n_loss else []), *held, *after)
@@ -386,7 +388,6 @@
             break
         pieces[o * inner] = swap(pieces[(o ^ bit) * inner], "dp", bit * inner)
     own, side, *away, unpacked = unpack(hidden)
-    far = exchange(away, [], RELAY)
     for o in range(line):
         if small and o == 2:
             pieces[4] = hold([], pieces[4], [unpacked])[1]
@@ -398,11 +399,12 @@
         gains = [gain, swap(gain, "dp", 2)]
         gain, side = hold(gains, side, [pieces[4]])
         gains = [gain, swap(gain, "dp", 4)]
-        pieces[6] = hold([], swap(pieces[4], "dp", 2), [pieces[3], gains[1], pieces[5]])[1]
+        pieces[6] = hold([], swap(pieces[4], "dp", 2), [pieces[3], pieces[5]])[1]
         pieces[7] = swap(pieces[6], "dp", 1)
     else:
         gains = [lax.all_gather(gain, "dp", axis=1, tiled=True)]
     side = swap(side, "fsdp", 1)
+    far = exchange(away, gains[1:], RELAY)
 
     height = targets.shape[0] // n_fsdp
     labels = targets.T if height % 128 == 0 else targets.reshape(n_fsdp, height)
@@ -422,13 +424,17 @@
     order = far[-1:]
     for o in range(line - 1, 0, -1):
         held = [parts[waiting[0] * inner + 1]] if waiting else []
+        if near is None and line > 2:
+            held, later = [], held
         if o == rides:
             piece, loss, held = fold([parts[o * inner], across[o], *came[o]], loss, held, order)
         else:
             piece, _, held = fold([parts[o * inner], *came[o], across[o]], None, held, order)
+        bit, order = o & -o, [piece]
         if near is None:
-            near = backward(gain_row, weights, [own, side], near_slopes, [loss])
-        bit, order = o & -o, [piece]
+            near = backward(gain_row, weights, [own, side], near_slopes, [loss], later if line > 2 else [])
+            near, held = near[:2], near[2:] or held
+            beside = swap(near[1], "fsdp", 1)
         moved = swap(piece, "dp", bit * inner)
         if o == rides:
             rides = o ^ bit
@@ -439,7 +445,7 @@
             across[waiting.pop(0)] = swap(held[0], "dp", 1)
     grad_head, loss, _ = fold([parts[0], across[0], *came[0]], loss, last=True)
 
-    grad_hidden, packed = pack([near[0], swap(near[1], "fsdp", 1), *exchange(far, order)])
+    grad_hidden, packed = pack([near[0], beside, *exchange(far, order)])
 
     parts = [loss] + [swap(loss, "fsdp", j) for j in range(1, n_fsdp)]
     return finish(parts, [packed])[0, 0], grad_hidden, grad_head[None]

time: 86.7 us -> 85.1 us (0.982)
  starting transfers between devices: 35.6 us -> 25.8 us
  waiting for transfers between devices: 29.9 us -> 38.2 us
    ppermute x28, starting transfers between devices: 35.6 us -> 25.8 us  [swap(): return lax.ppermute(value, axis, [(i, i ^ offset) for i in range(size)])]
    ppermute x28, waiting for transfers between devices: 29.9 us -> 38.2 us  [swap(): return lax.ppermute(value, axis, [(i, i ^ offset) for i in range(size)])]
  transfers between devices with their start and end apart: 28 -> 28, of which waited for: 11 -> 14; matrix products, arithmetic and copies ran while one was open for 0% -> 0% of each run, Pallas kernels for 16% -> 17%
where the time goes in v5:
time: 85.1 us; the launch traced here: 84.9 us
  waiting for transfers between devices  38.2 us (45%)
  starting transfers between devices  25.8 us (30%)
  Pallas kernels  19.5 us (23%)
    ppermute x28, waiting for transfers between devices, swap(): return lax.ppermute(value, axis, [(i, i ^ offset) for i in range(size)])  38.2 us
    ppermute x28, starting transfers between devices, swap(): return lax.ppermute(value, axis, [(i, i ^ offset) for i in range(size)])  25.8 us
    pallas_call x1, Pallas kernels, forward_far(): pl.pallas_call(body, in_specs=[SMEM] + [VMEM] * (6 + n), out_specs=[VMEM]...  4.92 us
    pallas_call x1, Pallas kernels, unpack(): pl.pallas_call(body, in_specs=[ANY], out_specs=[VMEM] * (positions + 1),...  3.58 us
    pallas_call x1, Pallas kernels, forward_near(): pl.pallas_call(body, in_specs=[SMEM] + [VMEM] * (1 + n_gain + n) + [ANY]...  3.48 us
    pallas_call x2, Pallas kernels, backward(): pl.pallas_call(body, in_specs=[VMEM] * (3 + n) + [ANY] * (len(after) + le...  3.18 us
    pallas_call x1, Pallas kernels, pack(): pl.pallas_call(body, grid=(frames // chunk,), in_specs=[pl.BlockSpec((chu...  2.53 us
  transfers between devices with their start and end apart: 28, of which 14 were waited for; matrix products, arithmetic and copies ran while one was open for 0% of the time, Pallas kernels for 17%

profile of v5, /device:TPU:0, one launch (start us, length us, event | category | flops | bytes accessed | tf_op | source)
XLA Modules:
  0.0 84.9 jit_solution(12960677645910435213)
XLA Ops:
  0.6 3.0 %collective-permute-start.2 = (bf16[128,1024]{1,0:T(8,128)(2,1)}, bf16[128,1024]{1,0:T(8,128)(2,1)S(1)}, u32[]{:S(2)}, u32[]{:S(2)}) collective-permute-start(bf16[128,1024]{1,0:T(8,128)(2,1)} %bitcast.6), channel_id=1, source_target_pairs={{0,4},{4,0},{8,12},{12,8},{16,20},{20,16},{24,28},{28,24},{1,5},{5... | collective-permute-start | bytes 786440 | tf_op jit(solution)/shard_map/ppermute | solution.py:372
  3.6 1.6 %collective-permute-start.1 = (bf16[128,1024]{1,0:T(8,128)(2,1)}, bf16[128,1024]{1,0:T(8,128)(2,1)S(1)}, u32[]{:S(2)}, u32[]{:S(2)}) collective-permute-start(bf16[128,1024]{1,0:T(8,128)(2,1)} %bitcast.7), channel_id=1, source_target_pairs={{0,8},{4,12},{8,0},{12,4},{16,24},{20,28},{24,16},{28,20},{1,9},{5... | collective-permute-start | bytes 786440 | tf_op jit(solution)/shard_map/ppermute | solution.py:372
  5.2 2.6 %collective-permute-start.4 = (bf16[128,1024]{1,0:T(8,128)(2,1)}, bf16[128,1024]{1,0:T(8,128)(2,1)S(1)}, u32[]{:S(2)}, u32[]{:S(2)}) collective-permute-start(bf16[128,1024]{1,0:T(8,128)(2,1)} %bitcast.8), channel_id=1, source_target_pairs={{0,16},{4,20},{8,24},{12,28},{16,0},{20,4},{24,8},{28,12},{1,17},{... | collective-permute-start | bytes 786440 | tf_op jit(solution)/shard_map/ppermute | solution.py:372
  8.3 3.6 %unpack.1 = (bf16[256,1024]{1,0:T(8,128)(2,1)}, bf16[256,1024]{1,0:T(8,128)(2,1)}, bf16[256,1024]{1,0:T(8,128)(2,1)}, bf16[256,1024]{1,0:T(8,128)(2,1)}, f32[8,128]{1,0:T(8,128)}) custom-call(bf16[256,4,1024]{2,1,0:T(4,128)(2,1)} %hidden_ref.1), custom_call_target="tpu_custom_call" | custom-call | flops 10000000 | tf_op jit(solution)/shard_map/unpack/pallas_call | solution.py:60
  11.9 1.6 %collective-permute-start.11 = (bf16[256,1024]{1,0:T(8,128)(2,1)}, bf16[256,1024]{1,0:T(8,128)(2,1)S(1)}, u32[]{:S(2)}, u32[]{:S(2)}) collective-permute-start(bf16[256,1024]{1,0:T(8,128)(2,1)} %get-tuple-element.50), channel_id=1, source_target_pairs={{0,2},{1,3},{2,0},{3,1},{4,6},{5,7},{6,4},{7,5},{8,10},{9,11},{10,... | collective-permute-start | bytes 1572872 | tf_op jit(solution)/shard_map/ppermute | solution.py:372
  14.0 3.1 %collective-permute-done.1.refs_2_ = bf16[128,1024]{1,0:T(8,128)(2,1)S(1)} collective-permute-done((bf16[128,1024]{1,0:T(8,128)(2,1)}, bf16[128,1024]{1,0:T(8,128)(2,1)S(1)}, u32[]{:S(2)}, u32[]{:S(2)}) %collective-permute-start.1) | collective-permute-done | bytes 262176 | tf_op jit(solution)/shard_map/ppermute | solution.py:372
  17.6 1.9 %collective-permute-done.4.refs_0_ = bf16[128,1024]{1,0:T(8,128)(2,1)S(1)} collective-permute-done((bf16[128,1024]{1,0:T(8,128)(2,1)}, bf16[128,1024]{1,0:T(8,128)(2,1)S(1)}, u32[]{:S(2)}, u32[]{:S(2)}) %collective-permute-start.4) | collective-permute-done | bytes 262176 | tf_op jit(solution)/shard_map/ppermute | solution.py:372
  21.1 1.7 %collective-permute-start.8 = (bf16[128,1024]{1,0:T(8,128)(2,1)S(1)}, bf16[128,1024]{1,0:T(8,128)(2,1)S(1)}, u32[]{:S(2)}, u32[]{:S(2)}) collective-permute-start(bf16[128,1024]{1,0:T(8,128)(2,1)S(1)} %hold.7.refs_3_.refs_10_), channel_id=1, source_target_pairs={{0,4},{4,0},{8,12},{12,8},{16,20},{20,16},{24,28},{28,24},{1,5},{5... | collective-permute-start | bytes 786440 | tf_op jit(solution)/shard_map/ppermute | solution.py:372
  22.8 3.6 %collective-permute-done.7.refs_1_.refs_9_ = bf16[128,1024]{1,0:T(8,128)(2,1)S(1)} collective-permute-done((bf16[128,1024]{1,0:T(8,128)(2,1)S(1)}, bf16[128,1024]{1,0:T(8,128)(2,1)S(1)}, u32[]{:S(2)}, u32[]{:S(2)}) %collective-permute-start.7) | collective-permute-done | bytes 262176 | tf_op jit(solution)/shard_map/ppermute | solution.py:372
  26.5 1.5 %collective-permute-start.5 = (bf16[4,128]{1,0:T(4,128)(2,1)S(1)}, bf16[4,128]{1,0:T(4,128)(2,1)S(1)}, u32[]{:S(2)}, u32[]{:S(2)}) collective-permute-start(bf16[4,128]{1,0:T(4,128)(2,1)S(1)} %get-tuple-element.44.refs_2_), channel_id=1, source_target_pairs={{0,16},{4,20},{8,24},{12,28},{16,0},{20,4},{24,8},{28,12},{1,17},{... | collective-permute-start | bytes 3080 | tf_op jit(solution)/shard_map/ppermute | solution.py:372
  28.0 1.7 %collective-permute-done.8.refs_2_.refs_11_ = bf16[128,1024]{1,0:T(8,128)(2,1)S(1)} collective-permute-done((bf16[128,1024]{1,0:T(8,128)(2,1)S(1)}, bf16[128,1024]{1,0:T(8,128)(2,1)S(1)}, u32[]{:S(2)}, u32[]{:S(2)}) %collective-permute-start.8) | collective-permute-done | bytes 262176 | tf_op jit(solution)/shard_map/ppermute | solution.py:372
  29.7 0.8 collective-permute-start.10
  31.0 5.0 %collective-permute-done.12.refs_0_ = bf16[256,1024]{1,0:T(8,128)(2,1)S(1)} collective-permute-done((bf16[256,1024]{1,0:T(8,128)(2,1)}, bf16[256,1024]{1,0:T(8,128)(2,1)S(1)}, u32[]{:S(2)}, u32[]{:S(2)}) %collective-permute-start.12) | collective-permute-done | bytes 524320 | tf_op jit(solution)/shard_map/ppermute | solution.py:372
  36.1 3.5 %forward_near.1 = (f32[8,128]{1,0:T(8,128)S(1)}, f32[1,1024]{1,0:T(1,128)S(1)}, bf16[1024,1024]{1,0:T(8,128)(2,1)S(1)}, bf16[2,256,1024]{2,1,0:T(8,128)(2,1)S(1)}, bf16[2,256,1024]{2,1,0:T(8,128)(2,1)S(1)}) custom-call(s32[8]{0:T(128)S(1)} %copy-done.3, s32[1,1024]{1,0:T(1,128)S(1)} %bitcast.4, bf16[4,128]{1,0:T(4,128)(2,1)S(1)} %get-tuple-element.44.refs_2_, ...), custom_call_target="tpu_custom_call" | custom-call | flops 3000000000 | tf_op jit(solution)/shard_map/forward_near/pallas_call | solution.py:177
  39.6 4.9 %forward_far.1 = (f32[8,1024]{1,0:T(8,128)S(1)}, bf16[2,256,1024]{2,1,0:T(8,128)(2,1)S(1)}, bf16[128,1024]{1,0:T(8,128)(2,1)S(1)}, bf16[128,1024]{1,0:T(8,128)(2...) custom-call(s32[8]{0:T(128)S(1)} %copy-done.3, ...), custom_call_target="tpu_custom_call" | custom-call | flops 10000000 | tf_op jit(solution)/shard_map/forward_far/pallas_call | solution.py:240
  44.6 1.5 %collective-permute-start.15 = (bf16[136,1024]{1,0:T(8,128)(2,1)S(1)}, bf16[136,1024]{1,0:T(8,128)(2,1)S(1)}, u32[]{:S(2)}, u32[]{:S(2)}) collective-permute-start(bf16[136,1024]{1,0:T(8,128)(2,1)S(1)} %get-tuple-element.59), channel_id=1, source_target_pairs={{0,4},{4,0},{8,12},{12,8},{16,20},{20,16},{24,28},{28,24},{1,5},{5... | collective-permute-start | bytes 835592 | tf_op jit(solution)/shard_map/ppermute | solution.py:372
  46.0 1.6 %backward.2 = (bf16[256,1024]{1,0:T(8,128)(2,1)S(1)}, bf16[256,1024]{1,0:T(8,128)(2,1)S(1)}) custom-call(f32[1,1024]{1,0:T(1,128)S(1)} %get-tuple-element.48.refs_2_.gain_ref, bf16[1024,1024]{1,0:T(8,128)(2,1)S(1)} %get-tuple-element.49.refs_3_.weight_ref, bf16[2,256,1024]{2,1,0:T(8,128)(2,1)S(1)} %get-tuple-element.61.slope_ref, ...), custom_call_target="tpu_custom_call" | custom-call | flops 10000000 | tf_op jit(solution)/shard_map/backward/pallas_call | solution.py:278
  47.6 1.6 %collective-permute-start.25 = (bf16[256,1024]{1,0:T(8,128)(2,1)S(1)}, bf16[256,1024]{1,0:T(8,128)(2,1)S(1)}, u32[]{:S(2)}, u32[]{:S(2)}) collective-permute-start(bf16[256,1024]{1,0:T(8,128)(2,1)S(1)} %get-tuple-element.75), channel_id=1, source_target_pairs={{0,2},{1,3},{2,0},{3,1},{4,6},{5,7},{6,4},{7,5},{8,10},{9,11},{10,... | collective-permute-start | bytes 1572872 | tf_op jit(solution)/shard_map/ppermute | solution.py:372
  49.7 3.9 %collective-permute-done.15.refs_1_ = bf16[136,1024]{1,0:T(8,128)(2,1)S(1)} collective-permute-done((bf16[136,1024]{1,0:T(8,128)(2,1)S(1)}, bf16[136,1024]{1,0:T(8,128)(2,1)S(1)}, u32[]{:S(2)}, u32[]{:S(2)}) %collective-permute-start.15) | collective-permute-done | bytes 278560 | tf_op jit(solution)/shard_map/ppermute | solution.py:372
  53.7 0.9 %collective-permute-start.16 = (bf16[136,1024]{1,0:T(8,128)(2,1)S(1)}, bf16[136,1024]{1,0:T(8,128)(2,1)S(1)}, u32[]{:S(2)}, u32[]{:S(2)}) collective-permute-start(bf16[136,1024]{1,0:T(8,128)(2,1)S(1)} %get-tuple-element.63.refs_5_), channel_id=1, source_target_pairs={{0,8},{4,12},{8,0},{12,4},{16,24},{20,28},{24,16},{28,20},{1,9},{5... | collective-permute-start | bytes 835592 | tf_op jit(solution)/shard_map/ppermute | solution.py:372
  54.6 1.1 %collective-permute-start.14 = (bf16[128,1024]{1,0:T(8,128)(2,1)S(1)}, bf16[128,1024]{1,0:T(8,128)(2,1)S(1)}, u32[]{:S(2)}, u32[]{:S(2)}) collective-permute-start(bf16[128,1024]{1,0:T(8,128)(2,1)S(1)} %get-tuple-element.57), channel_id=1, source_target_pairs={{0,4},{4,0},{8,12},{12,8},{16,20},{20,16},{24,28},{28,24},{1,5},{5... | collective-permute-start | bytes 786440 | tf_op jit(solution)/shard_map/ppermute | solution.py:372
  55.7 1.6 %backward.3 = (bf16[256,1024]{1,0:T(8,128)(2,1)S(1)}, bf16[256,1024]{1,0:T(8,128)(2,1)S(1)}, bf16[128,1024]{1,0:T(8,128)(2,1)S(1)}) custom-call(f32[1,1024]{1,0:T(1,128)S(1)} %get-tuple-element.48.refs_2_.gain_ref, bf16[1024,1024]{1,0:T(8,128)(2,1)S(1)} %get-tuple-element.49.refs_3_.weight_ref, ...), custom_call_target="tpu_custom_call", output_to_operand_aliasing={{2}: (6, {})} | custom-call | flops 10000000 | tf_op jit(solution)/shard_map/backward/pallas_call | solution.py:278
  57.3 1.0 %collective-permute-start.18 = (bf16[128,1024]{1,0:T(8,128)(2,1)S(1)}, bf16[128,1024]{1,0:T(8,128)(2,1)S(1)}, u32[]{:S(2)}, u32[]{:S(2)}) collective-permute-start(bf16[128,1024]{1,0:T(8,128)(2,1)S(1)} %get-tuple-element.69), channel_id=1, source_target_pairs={{0,4},{4,0},{8,12},{12,8},{16,20},{20,16},{24,28},{28,24},{1,5},{5... | collective-permute-start | bytes 786440 | tf_op jit(solution)/shard_map/ppermute | solution.py:372
  58.3 5.6 %collective-permute-done.14.refs_1_ = bf16[128,1024]{1,0:T(8,128)(2,1)S(1)} collective-permute-done((bf16[128,1024]{1,0:T(8,128)(2,1)S(1)}, bf16[128,1024]{1,0:T(8,128)(2,1)S(1)}, u32[]{:S(2)}, u32[]{:S(2)}) %collective-permute-start.14) | collective-permute-done | bytes 262176 | tf_op jit(solution)/shard_map/ppermute | solution.py:372
  64.1 1.4 %collective-permute-start.17 = (bf16[128,1024]{1,0:T(8,128)(2,1)S(1)}, bf16[128,1024]{1,0:T(8,128)(2,1)S(1)}, u32[]{:S(2)}, u32[]{:S(2)}) collective-permute-start(bf16[128,1024]{1,0:T(8,128)(2,1)S(1)} %get-tuple-element.66), channel_id=1, source_target_pairs={{0,4},{4,0},{8,12},{12,8},{16,20},{20,16},{24,28},{28,24},{1,5},{5... | collective-permute-start | bytes 786440 | tf_op jit(solution)/shard_map/ppermute | solution.py:372
  65.5 4.0 %collective-permute-done.18.refs_1_ = bf16[128,1024]{1,0:T(8,128)(2,1)S(1)} collective-permute-done((bf16[128,1024]{1,0:T(8,128)(2,1)S(1)}, bf16[128,1024]{1,0:T(8,128)(2,1)S(1)}, u32[]{:S(2)}, u32[]{:S(2)}) %collective-permute-start.18) | collective-permute-done | bytes 262176 | tf_op jit(solution)/shard_map/ppermute | solution.py:372
  69.6 1.3 %collective-permute-start.19 = (bf16[128,1024]{1,0:T(8,128)(2,1)S(1)}, bf16[128,1024]{1,0:T(8,128)(2,1)S(1)}, u32[]{:S(2)}, u32[]{:S(2)}) collective-permute-start(bf16[128,1024]{1,0:T(8,128)(2,1)S(1)} %fold.6.refs_2_), channel_id=1, source_target_pairs={{0,8},{4,12},{8,0},{12,4},{16,24},{20,28},{24,16},{28,20},{1,9},{5... | collective-permute-start | bytes 786440 | tf_op jit(solution)/shard_map/ppermute | solution.py:372
  70.8 2.1 %collective-permute-done.26.refs_0_ = bf16[256,1024]{1,0:T(8,128)(2,1)S(1)} collective-permute-done((bf16[256,1024]{1,0:T(8,128)(2,1)S(1)}, bf16[256,1024]{1,0:T(8,128)(2,1)S(1)}, u32[]{:S(2)}, u32[]{:S(2)}) %collective-permute-start.26) | collective-permute-done | bytes 524320 | tf_op jit(solution)/shard_map/ppermute | solution.py:372
  73.0 6.0 %collective-permute-done.19.refs_2_ = bf16[128,1024]{1,0:T(8,128)(2,1)S(1)} collective-permute-done((bf16[128,1024]{1,0:T(8,128)(2,1)S(1)}, bf16[128,1024]{1,0:T(8,128)(2,1)S(1)}, u32[]{:S(2)}, u32[]{:S(2)}) %collective-permute-start.19) | collective-permute-done | bytes 262176 | tf_op jit(solution)/shard_map/ppermute | solution.py:372
  79.0 0.9 %fold.7 = (f32[128,1024]{1,0:T(8,128)}, f32[8,128]{1,0:T(8,128)S(1)}) custom-call(bf16[128,1024]{1,0:T(8,128)(2,1)S(1)} %get-tuple-element.55.refs_0_, bf16[128,1024]{1,0:T(8,128)(2,1)S(1)} %collective-permute-done.17.refs_1_, bf16[128,1024]{1,0:T(8,128)(2,1)S(1)} %collective-permute-done.19.refs_2_, bf16[136,1024]{1,0:T(8,128)(2,1)S(1)} %collective-permute-done.20.refs_3_, ...), custom_call_target="tpu_custom_call" | custom-call | flops 3000000000 | tf_op jit(solution)/shard_map/fold/pallas_call | solution.py:314
  80.0 1.5 %collective-permute-start.22 = (f32[8,128]{1,0:T(8,128)S(1)}, f32[8,128]{1,0:T(8,128)S(1)}, u32[]{:S(2)}, u32[]{:S(2)}) collective-permute-start(f32[8,128]{1,0:T(8,128)S(1)} %get-tuple-element.72.refs_0_), channel_id=1, source_target_pairs={{0,2},{1,3},{2,0},{3,1},{4,6},{5,7},{6,4},{7,5},{8,10},{9,11},{10,... | collective-permute-start | bytes 12296 | tf_op jit(solution)/shard_map/ppermute | solution.py:372
  81.8 2.5 %pack.1 = (bf16[256,4,1024]{2,1,0:T(4,128)(2,1)}, f32[8,128]{1,0:T(8,128)S(1)}) custom-call(bf16[256,1024]{1,0:T(8,128)(2,1)S(1)} %get-tuple-element.73.refs_0_, bf16[256,1024]{1,0:T(8,128)(2,1)S(1)} %collective-permute-done.24.refs_1_, bf16[256,1024]{1,0:T(8,128)(2,1)S(1)} %collective-permute-done.25.refs_1_.refs_2_, ...), custom_call_target="tpu_custom_call" | custom-call | flops 10000000 | tf_op jit(solution)/shard_map/pack/pallas_call | solution.py:91
  (53 shorter events, 5.8 us)
Async XLA Ops:
  0.6 16.5 %copy-start.4 = (bf16[1,128]{1,0:T(2,128)(2,1)S(1)}, bf16[1,128]{1,0:T(2,128)(2,1)}, u32[]{:S(2)}) copy-start(bf16[1,128]{1,0:T(2,128)(2,1)} %refs_0_.3) | copy-start | bytes 772
  0.6 13.4 %collective-permute-start.2 = (bf16[128,1024]{1,0:T(8,128)(2,1)}, bf16[128,1024]{1,0:T(8,128)(2,1)S(1)}, u32[]{:S(2)}, u32[]{:S(2)}) collective-permute-start(bf16[128,1024]{1,0:T(8,128)(2,1)} %bitcast.6), channel_id=1, source_target_pairs={{0,4},{4,0},{8,12},{12,8},{16,20},{20,16},{24,28},{28,24},{1,5},{5... | collective-permute-start | bytes 786440 | tf_op jit(solution)/shard_map/ppermute | solution.py:372
  3.6 13.5 %collective-permute-start.1 = (bf16[128,1024]{1,0:T(8,128)(2,1)}, bf16[128,1024]{1,0:T(8,128)(2,1)S(1)}, u32[]{:S(2)}, u32[]{:S(2)}) collective-permute-start(bf16[128,1024]{1,0:T(8,128)(2,1)} %bitcast.7), channel_id=1, source_target_pairs={{0,8},{4,12},{8,0},{12,4},{16,24},{20,28},{24,16},{28,20},{1,9},{5... | collective-permute-start | bytes 786440 | tf_op jit(solution)/shard_map/ppermute | solution.py:372
  5.2 14.3 %collective-permute-start.4 = (bf16[128,1024]{1,0:T(8,128)(2,1)}, bf16[128,1024]{1,0:T(8,128)(2,1)S(1)}, u32[]{:S(2)}, u32[]{:S(2)}) collective-permute-start(bf16[128,1024]{1,0:T(8,128)(2,1)} %bitcast.8), channel_id=1, source_target_pairs={{0,16},{4,20},{8,24},{12,28},{16,0},{20,4},{24,8},{28,12},{1,17},{... | collective-permute-start | bytes 786440 | tf_op jit(solution)/shard_map/ppermute | solution.py:372
  7.8 5.7 %collective-permute-start = (bf16[1,128]{1,0:T(2,128)(2,1)}, bf16[1,128]{1,0:T(2,128)(2,1)S(1)}, u32[]{:S(2)}, u32[]{:S(2)}) collective-permute-start(bf16[1,128]{1,0:T(2,128)(2,1)} %refs_0_.3), channel_id=1, source_target_pairs={{0,4},{4,0},{8,12},{12,8},{16,20},{20,16},{24,28},{28,24},{1,5},{5... | collective-permute-start | bytes 776 | tf_op jit(solution)/shard_map/ppermute | solution.py:372
  11.9 19.1 %collective-permute-start.11 = (bf16[256,1024]{1,0:T(8,128)(2,1)}, bf16[256,1024]{1,0:T(8,128)(2,1)S(1)}, u32[]{:S(2)}, u32[]{:S(2)}) collective-permute-start(bf16[256,1024]{1,0:T(8,128)(2,1)} %get-tuple-element.50), channel_id=1, source_target_pairs={{0,2},{1,3},{2,0},{3,1},{4,6},{5,7},{6,4},{7,5},{8,10},{9,11},{10,... | collective-permute-start | bytes 1572872 | tf_op jit(solution)/shard_map/ppermute | solution.py:372
  13.5 22.5 %collective-permute-start.12 = (bf16[256,1024]{1,0:T(8,128)(2,1)}, bf16[256,1024]{1,0:T(8,128)(2,1)S(1)}, u32[]{:S(2)}, u32[]{:S(2)}) collective-permute-start(bf16[256,1024]{1,0:T(8,128)(2,1)} %get-tuple-element.51), channel_id=1, source_target_pairs={{0,2},{1,3},{2,0},{3,1},{4,6},{5,7},{6,4},{7,5},{8,10},{9,11},{10,... | collective-permute-start | bytes 1572872 | tf_op jit(solution)/shard_map/ppermute | solution.py:372
  17.1 9.3 %collective-permute-start.7 = (bf16[128,1024]{1,0:T(8,128)(2,1)S(1)}, bf16[128,1024]{1,0:T(8,128)(2,1)S(1)}, u32[]{:S(2)}, u32[]{:S(2)}) collective-permute-start(bf16[128,1024]{1,0:T(8,128)(2,1)S(1)} %get-tuple-element.47.refs_8_), channel_id=1, source_target_pairs={{0,4},{4,0},{8,12},{12,8},{16,20},{20,16},{24,28},{28,24},{1,5},{5... | collective-permute-start | bytes 786440 | tf_op jit(solution)/shard_map/ppermute | solution.py:372
  17.6 3.6 %collective-permute-start.3 = (bf16[2,128]{1,0:T(2,128)(2,1)S(1)}, bf16[2,128]{1,0:T(2,128)(2,1)S(1)}, u32[]{:S(2)}, u32[]{:S(2)}) collective-permute-start(bf16[2,128]{1,0:T(2,128)(2,1)S(1)} %get-tuple-element.41.refs_0_), channel_id=1, source_target_pairs={{0,8},{4,12},{8,0},{12,4},{16,24},{20,28},{24,16},{28,20},{1,9},{5... | collective-permute-start | bytes 1544 | tf_op jit(solution)/shard_map/ppermute | solution.py:372
  20.2 6.4 %collective-permute-start.9 = (bf16[128,1024]{1,0:T(8,128)(2,1)S(1)}, bf16[128,1024]{1,0:T(8,128)(2,1)S(1)}, u32[]{:S(2)}, u32[]{:S(2)}) collective-permute-start(bf16[128,1024]{1,0:T(8,128)(2,1)S(1)} %hold.7.refs_3_.refs_10_), channel_id=1, source_target_pairs={{0,8},{4,12},{8,0},{12,4},{16,24},{20,28},{24,16},{28,20},{1,9},{5... | collective-permute-start | bytes 786440 | tf_op jit(solution)/shard_map/ppermute | solution.py:372
  21.1 8.5 %collective-permute-start.8 = (bf16[128,1024]{1,0:T(8,128)(2,1)S(1)}, bf16[128,1024]{1,0:T(8,128)(2,1)S(1)}, u32[]{:S(2)}, u32[]{:S(2)}) collective-permute-start(bf16[128,1024]{1,0:T(8,128)(2,1)S(1)} %hold.7.refs_3_.refs_10_), channel_id=1, source_target_pairs={{0,4},{4,0},{8,12},{12,8},{16,20},{20,16},{24,28},{28,24},{1,5},{5... | collective-permute-start | bytes 786440 | tf_op jit(solution)/shard_map/ppermute | solution.py:372
  26.4 9.7 %collective-permute-start.6 = (bf16[256,1024]{1,0:T(8,128)(2,1)}, bf16[256,1024]{1,0:T(8,128)(2,1)S(1)}, u32[]{:S(2)}, u32[]{:S(2)}) collective-permute-start(bf16[256,1024]{1,0:T(8,128)(2,1)} %get-tuple-element.46), channel_id=1, source_target_pairs={{0,1},{1,0},{2,3},{3,2},{4,5},{5,4},{6,7},{7,6},{8,9},{9,8},{10,11... | collective-permute-start | bytes 1572872 | tf_op jit(solution)/shard_map/ppermute | solution.py:372
  26.5 4.5 %collective-permute-start.5 = (bf16[4,128]{1,0:T(4,128)(2,1)S(1)}, bf16[4,128]{1,0:T(4,128)(2,1)S(1)}, u32[]{:S(2)}, u32[]{:S(2)}) collective-permute-start(bf16[4,128]{1,0:T(4,128)(2,1)S(1)} %get-tuple-element.44.refs_2_), channel_id=1, source_target_pairs={{0,16},{4,20},{8,24},{12,28},{16,0},{20,4},{24,8},{28,12},{1,17},{... | collective-permute-start | bytes 3080 | tf_op jit(solution)/shard_map/ppermute | solution.py:372
  29.7 6.5 %copy-start.1 = (s32[1024,1]{0,1:T(1,128)S(1)}, s32[1024,1]{0,1:T(1,128)}, u32[]{:S(2)}) copy-start(s32[1024,1]{0,1:T(1,128)} %param.8) | copy-start | bytes 12292
  29.7 6.5 %copy-start.3 = (s32[8]{0:T(128)S(1)}, s32[8]{0:T(128)}, u32[]{:S(2)}) copy-start(s32[8]{0:T(128)} %refs_0_.5) | copy-start | bytes 100
  29.7 6.5 %copy-start.5 = (bf16[1,128,1024]{2,1,0:T(8,128)(2,1)S(1)}, bf16[1,128,1024]{2,1,0:T(8,128)(2,1)}, u32[]{:S(2)}) copy-start(bf16[1,128,1024]{2,1,0:T(8,128)(2,1)} %param.6) | copy-start | bytes 786436
  29.7 6.4 %collective-permute-start.10 = (bf16[128,1024]{1,0:T(8,128)(2,1)S(1)}, bf16[128,1024]{1,0:T(8,128)(2,1)S(1)}, u32[]{:S(2)}, u32[]{:S(2)}) collective-permute-start(bf16[128,1024]{1,0:T(8,128)(2,1)S(1)} %hold.9.refs_12_), channel_id=1, source_target_pairs={{0,4},{4,0},{8,12},{12,8},{16,20},{20,16},{24,28},{28,24},{1,5},{5... | collective-permute-start | bytes 786440 | tf_op jit(solution)/shard_map/ppermute | solution.py:372
  36.0 3.6 %collective-permute-start.13 = (bf16[256,1024]{1,0:T(8,128)(2,1)S(1)}, bf16[256,1024]{1,0:T(8,128)(2,1)S(1)}, u32[]{:S(2)}, u32[]{:S(2)}) collective-permute-start(bf16[256,1024]{1,0:T(8,128)(2,1)S(1)} %hold.10), channel_id=1, source_target_pairs={{0,1},{1,0},{2,3},{3,2},{4,5},{5,4},{6,7},{7,6},{8,9},{9,8},{10,11... | collective-permute-start | bytes 1572872 | tf_op jit(solution)/shard_map/ppermute | solution.py:372
  44.6 9.1 %collective-permute-start.15 = (bf16[136,1024]{1,0:T(8,128)(2,1)S(1)}, bf16[136,1024]{1,0:T(8,128)(2,1)S(1)}, u32[]{:S(2)}, u32[]{:S(2)}) collective-permute-start(bf16[136,1024]{1,0:T(8,128)(2,1)S(1)} %get-tuple-element.59), channel_id=1, source_target_pairs={{0,4},{4,0},{8,12},{12,8},{16,20},{20,16},{24,28},{28,24},{1,5},{5... | collective-permute-start | bytes 835592 | tf_op jit(solution)/shard_map/ppermute | solution.py:372
  47.6 23.2 %collective-permute-start.25 = (bf16[256,1024]{1,0:T(8,128)(2,1)S(1)}, bf16[256,1024]{1,0:T(8,128)(2,1)S(1)}, u32[]{:S(2)}, u32[]{:S(2)}) collective-permute-start(bf16[256,1024]{1,0:T(8,128)(2,1)S(1)} %get-tuple-element.75), channel_id=1, source_target_pairs={{0,2},{1,3},{2,0},{3,1},{4,6},{5,7},{6,4},{7,5},{8,10},{9,11},{10,... | collective-permute-start | bytes 1572872 | tf_op jit(solution)/shard_map/ppermute | solution.py:372
  49.2 23.8 %collective-permute-start.26 = (bf16[256,1024]{1,0:T(8,128)(2,1)S(1)}, bf16[256,1024]{1,0:T(8,128)(2,1)S(1)}, u32[]{:S(2)}, u32[]{:S(2)}) collective-permute-start(bf16[256,1024]{1,0:T(8,128)(2,1)S(1)} %get-tuple-element.62.refs_3_), channel_id=1, source_target_pairs={{0,2},{1,3},{2,0},{3,1},{4,6},{5,7},{6,4},{7,5},{8,10},{9,11},{10,... | collective-permute-start | bytes 1572872 | tf_op jit(solution)/shard_map/ppermute | solution.py:372
  53.7 10.1 %collective-permute-start.16 = (bf16[136,1024]{1,0:T(8,128)(2,1)S(1)}, bf16[136,1024]{1,0:T(8,128)(2,1)S(1)}, u32[]{:S(2)}, u32[]{:S(2)}) collective-permute-start(bf16[136,1024]{1,0:T(8,128)(2,1)S(1)} %get-tuple-element.63.refs_5_), channel_id=1, source_target_pairs={{0,8},{4,12},{8,0},{12,4},{16,24},{20,28},{24,16},{28,20},{1,9},{5... | collective-permute-start | bytes 835592 | tf_op jit(solution)/shard_map/ppermute | solution.py:372
  54.6 9.2 %collective-permute-start.14 = (bf16[128,1024]{1,0:T(8,128)(2,1)S(1)}, bf16[128,1024]{1,0:T(8,128)(2,1)S(1)}, u32[]{:S(2)}, u32[]{:S(2)}) collective-permute-start(bf16[128,1024]{1,0:T(8,128)(2,1)S(1)} %get-tuple-element.57), channel_id=1, source_target_pairs={{0,4},{4,0},{8,12},{12,8},{16,20},{20,16},{24,28},{28,24},{1,5},{5... | collective-permute-start | bytes 786440 | tf_op jit(solution)/shard_map/ppermute | solution.py:372
  57.3 12.2 %collective-permute-start.18 = (bf16[128,1024]{1,0:T(8,128)(2,1)S(1)}, bf16[128,1024]{1,0:T(8,128)(2,1)S(1)}, u32[]{:S(2)}, u32[]{:S(2)}) collective-permute-start(bf16[128,1024]{1,0:T(8,128)(2,1)S(1)} %get-tuple-element.69), channel_id=1, source_target_pairs={{0,4},{4,0},{8,12},{12,8},{16,20},{20,16},{24,28},{28,24},{1,5},{5... | collective-permute-start | bytes 786440 | tf_op jit(solution)/shard_map/ppermute | solution.py:372
  64.0 15.0 %collective-permute-start.20 = (bf16[136,1024]{1,0:T(8,128)(2,1)S(1)}, bf16[136,1024]{1,0:T(8,128)(2,1)S(1)}, u32[]{:S(2)}, u32[]{:S(2)}) collective-permute-start(bf16[136,1024]{1,0:T(8,128)(2,1)S(1)} %get-tuple-element.70.refs_2_), channel_id=1, source_target_pairs={{0,16},{4,20},{8,24},{12,28},{16,0},{20,4},{24,8},{28,12},{1,17},{... | collective-permute-start | bytes 835592 | tf_op jit(solution)/shard_map/ppermute | solution.py:372
  64.1 8.9 %collective-permute-start.17 = (bf16[128,1024]{1,0:T(8,128)(2,1)S(1)}, bf16[128,1024]{1,0:T(8,128)(2,1)S(1)}, u32[]{:S(2)}, u32[]{:S(2)}) collective-permute-start(bf16[128,1024]{1,0:T(8,128)(2,1)S(1)} %get-tuple-element.66), channel_id=1, source_target_pairs={{0,4},{4,0},{8,12},{12,8},{16,20},{20,16},{24,28},{28,24},{1,5},{5... | collective-permute-start | bytes 786440 | tf_op jit(solution)/shard_map/ppermute | solution.py:372
  69.6 9.5 %collective-permute-start.19 = (bf16[128,1024]{1,0:T(8,128)(2,1)S(1)}, bf16[128,1024]{1,0:T(8,128)(2,1)S(1)}, u32[]{:S(2)}, u32[]{:S(2)}) collective-permute-start(bf16[128,1024]{1,0:T(8,128)(2,1)S(1)} %fold.6.refs_2_), channel_id=1, source_target_pairs={{0,8},{4,12},{8,0},{12,4},{16,24},{20,28},{24,16},{28,20},{1,9},{5... | collective-permute-start | bytes 786440 | tf_op jit(solution)/shard_map/ppermute | solution.py:372
  70.8 11.0 %collective-permute-start.24 = (bf16[256,1024]{1,0:T(8,128)(2,1)S(1)}, bf16[256,1024]{1,0:T(8,128)(2,1)S(1)}, u32[]{:S(2)}, u32[]{:S(2)}) collective-permute-start(bf16[256,1024]{1,0:T(8,128)(2,1)S(1)} %get-tuple-element.74), channel_id=1, source_target_pairs={{0,1},{1,0},{2,3},{3,2},{4,5},{5,4},{6,7},{7,6},{8,9},{9,8},{10,11... | collective-permute-start | bytes 1572872 | tf_op jit(solution)/shard_map/ppermute | solution.py:372
  73.0 8.9 %collective-permute-start.27 = (bf16[256,1024]{1,0:T(8,128)(2,1)S(1)}, bf16[256,1024]{1,0:T(8,128)(2,1)S(1)}, u32[]{:S(2)}, u32[]{:S(2)}) collective-permute-start(bf16[256,1024]{1,0:T(8,128)(2,1)S(1)} %hold.11), channel_id=1, source_target_pairs={{0,1},{1,0},{2,3},{3,2},{4,5},{5,4},{6,7},{7,6},{8,9},{9,8},{10,11... | collective-permute-start | bytes 1572872 | tf_op jit(solution)/shard_map/ppermute | solution.py:372
  80.0 4.4 %collective-permute-start.23 = (f32[8,128]{1,0:T(8,128)S(1)}, f32[8,128]{1,0:T(8,128)S(1)}, u32[]{:S(2)}, u32[]{:S(2)}) collective-permute-start(f32[8,128]{1,0:T(8,128)S(1)} %get-tuple-element.72.refs_0_), channel_id=1, source_target_pairs={{0,3},{1,2},{2,1},{3,0},{4,7},{5,6},{6,5},{7,4},{8,11},{9,10},{10,... | collective-permute-start | bytes 12296 | tf_op jit(solution)/shard_map/ppermute | solution.py:372
  80.0 4.4 %collective-permute-start.22 = (f32[8,128]{1,0:T(8,128)S(1)}, f32[8,128]{1,0:T(8,128)S(1)}, u32[]{:S(2)}, u32[]{:S(2)}) collective-permute-start(f32[8,128]{1,0:T(8,128)S(1)} %get-tuple-element.72.refs_0_), channel_id=1, source_target_pairs={{0,2},{1,3},{2,0},{3,1},{4,6},{5,7},{6,4},{7,5},{8,10},{9,11},{10,... | collective-permute-start | bytes 12296 | tf_op jit(solution)/shard_map/ppermute | solution.py:372
  81.5 2.9 %collective-permute-start.21 = (f32[8,128]{1,0:T(8,128)S(1)}, f32[8,128]{1,0:T(8,128)S(1)}, u32[]{:S(2)}, u32[]{:S(2)}) collective-permute-start(f32[8,128]{1,0:T(8,128)S(1)} %get-tuple-element.72.refs_0_), channel_id=1, source_target_pairs={{0,1},{1,0},{2,3},{3,2},{4,5},{5,4},{6,7},{7,6},{8,9},{9,8},{10,11... | collective-permute-start | bytes 12296 | tf_op jit(solution)/shard_map/ppermute | solution.py:372
  (2 other events, 7.1 us)

commit v6 on v5

--- a/solution.py
+++ b/solution.py
@@ -345,6 +345,22 @@
     return out[0], out[-1]
 
 
+def ride_end(loss, piece):
+    def body(loss_ref, piece_ref, out_ref):
+        extra = piece_ref[-EXTRA:, :128].astype(WIDE)
+        out_ref[...] = loss_ref[:, :128] + (extra[:1] + extra[1:2] + extra[2:3])
+
+    return pl.pallas_call(
+        body,
+        in_specs=[VMEM] * 2,
+        out_specs=VMEM,
+        out_shape=jax.ShapeDtypeStruct((8, 128), WIDE),
+        cost_estimate=cost(HOLD),
+        compiler_params=params(8),
+        name="ride_end",
+    )(loss, piece)
+
+
 def finish(parts, after):
     def body(*refs):
         total = refs[0][...]
@@ -423,7 +439,7 @@
     rides = line - 1
     order = far[-1:]
     for o in range(line - 1, 0, -1):
-        held = [parts[waiting[0] * inner + 1]] if waiting else []
+        held = [parts[waiting[0] * inner + 1]] if waiting and (o > 2 or o == 1) else []
         if near is None and line > 2:
             held, later = [], held
         if o == rides:
@@ -443,9 +459,11 @@
             came[o ^ bit] = [moved, *came[o ^ bit]]
         if held:
             across[waiting.pop(0)] = swap(held[0], "dp", 1)
-    grad_head, loss, _ = fold([parts[0], across[0], *came[0]], loss, last=True)
+    loss = ride_end(loss, came[0][-1])
 
     grad_hidden, packed = pack([near[0], beside, *exchange(far, order)])
+
+    grad_head = fold([parts[0], across[0], *came[0]], None, (), [], last=True)[0]
 
     parts = [loss] + [swap(loss, "fsdp", j) for j in range(1, n_fsdp)]
     return finish(parts, [packed])[0, 0], grad_hidden, grad_head[None]

time: 85.1 us -> 83.6 us (0.982)
  waiting for transfers between devices: 38.2 us -> 36.3 us
    ppermute x28, waiting for transfers between devices: 38.2 us -> 36.3 us  [swap(): return lax.ppermute(value, axis, [(i, i ^ offset) for i in range(size)])]
  transfers between devices with their start and end apart: 28 -> 28, of which waited for: 14 -> 15; matrix products, arithmetic and copies ran while one was open for 0% -> 0% of each run, Pallas kernels for 17% -> 17%
where the time goes in v6:
time: 83.6 us; the launch traced here: 83.4 us
  waiting for transfers between devices  36.3 us (43%)
  starting transfers between devices  26.1 us (31%)
  Pallas kernels  19.5 us (23%)
    ppermute x28, waiting for transfers between devices, swap(): return lax.ppermute(value, axis, [(i, i ^ offset) for i in range(size)])  36.3 us
    ppermute x28, starting transfers between devices, swap(): return lax.ppermute(value, axis, [(i, i ^ offset) for i in range(size)])  26.1 us
    pallas_call x1, Pallas kernels, forward_far(): pl.pallas_call(body, in_specs=[SMEM] + [VMEM] * (6 + n), out_specs=[VMEM]...  4.92 us
    pallas_call x1, Pallas kernels, unpack(): pl.pallas_call(body, in_specs=[ANY], out_specs=[VMEM] * (positions + 1),...  3.58 us
    pallas_call x1, Pallas kernels, forward_near(): pl.pallas_call(body, in_specs=[SMEM] + [VMEM] * (1 + n_gain + n) + [ANY]...  3.48 us
    pallas_call x2, Pallas kernels, backward(): pl.pallas_call(body, in_specs=[VMEM] * (3 + n) + [ANY] * (len(after) + le...  3.18 us
    pallas_call x1, Pallas kernels, pack(): pl.pallas_call(body, grid=(frames // chunk,), in_specs=[pl.BlockSpec((chu...  2.53 us
  transfers between devices with their start and end apart: 28, of which 15 were waited for; matrix products, arithmetic and copies ran while one was open for 0% of the time, Pallas kernels for 17%

profile of v6, /device:TPU:0, one launch (start us, length us, event | category | flops | bytes accessed | tf_op | source)
XLA Modules:
  0.0 83.4 jit_solution(5183130436678325565)
XLA Ops:
  0.6 3.0 %collective-permute-start.2 = (bf16[128,1024]{1,0:T(8,128)(2,1)}, bf16[128,1024]{1,0:T(8,128)(2,1)S(1)}, u32[]{:S(2)}, u32[]{:S(2)}) collective-permute-start(bf16[128,1024]{1,0:T(8,128)(2,1)} %bitcast.6), channel_id=1, source_target_pairs={{0,4},{4,0},{8,12},{12,8},{16,20},{20,16},{24,28},{28,24},{1,5},{5... | collective-permute-start | bytes 786440 | tf_op jit(solution)/shard_map/ppermute | solution.py:388
  3.6 1.6 %collective-permute-start.1 = (bf16[128,1024]{1,0:T(8,128)(2,1)}, bf16[128,1024]{1,0:T(8,128)(2,1)S(1)}, u32[]{:S(2)}, u32[]{:S(2)}) collective-permute-start(bf16[128,1024]{1,0:T(8,128)(2,1)} %bitcast.7), channel_id=1, source_target_pairs={{0,8},{4,12},{8,0},{12,4},{16,24},{20,28},{24,16},{28,20},{1,9},{5... | collective-permute-start | bytes 786440 | tf_op jit(solution)/shard_map/ppermute | solution.py:388
  5.2 2.6 %collective-permute-start.4 = (bf16[128,1024]{1,0:T(8,128)(2,1)}, bf16[128,1024]{1,0:T(8,128)(2,1)S(1)}, u32[]{:S(2)}, u32[]{:S(2)}) collective-permute-start(bf16[128,1024]{1,0:T(8,128)(2,1)} %bitcast.8), channel_id=1, source_target_pairs={{0,16},{4,20},{8,24},{12,28},{16,0},{20,4},{24,8},{28,12},{1,17},{... | collective-permute-start | bytes 786440 | tf_op jit(solution)/shard_map/ppermute | solution.py:388
  8.3 3.6 %unpack.1 = (bf16[256,1024]{1,0:T(8,128)(2,1)}, bf16[256,1024]{1,0:T(8,128)(2,1)}, bf16[256,1024]{1,0:T(8,128)(2,1)}, bf16[256,1024]{1,0:T(8,128)(2,1)}, f32[8,128]{1,0:T(8,128)}) custom-call(bf16[256,4,1024]{2,1,0:T(4,128)(2,1)} %hidden_ref.1), custom_call_target="tpu_custom_call" | custom-call | flops 10000000 | tf_op jit(solution)/shard_map/unpack/pallas_call | solution.py:60
  11.9 1.6 %collective-permute-start.11 = (bf16[256,1024]{1,0:T(8,128)(2,1)}, bf16[256,1024]{1,0:T(8,128)(2,1)S(1)}, u32[]{:S(2)}, u32[]{:S(2)}) collective-permute-start(bf16[256,1024]{1,0:T(8,128)(2,1)} %get-tuple-element.49), channel_id=1, source_target_pairs={{0,2},{1,3},{2,0},{3,1},{4,6},{5,7},{6,4},{7,5},{8,10},{9,11},{10,... | collective-permute-start | bytes 1572872 | tf_op jit(solution)/shard_map/ppermute | solution.py:388
  14.0 3.1 %collective-permute-done.1.refs_2_ = bf16[128,1024]{1,0:T(8,128)(2,1)S(1)} collective-permute-done((bf16[128,1024]{1,0:T(8,128)(2,1)}, bf16[128,1024]{1,0:T(8,128)(2,1)S(1)}, u32[]{:S(2)}, u32[]{:S(2)}) %collective-permute-start.1) | collective-permute-done | bytes 262176 | tf_op jit(solution)/shard_map/ppermute | solution.py:388
  17.6 1.9 %collective-permute-done.4.refs_0_ = bf16[128,1024]{1,0:T(8,128)(2,1)S(1)} collective-permute-done((bf16[128,1024]{1,0:T(8,128)(2,1)}, bf16[128,1024]{1,0:T(8,128)(2,1)S(1)}, u32[]{:S(2)}, u32[]{:S(2)}) %collective-permute-start.4) | collective-permute-done | bytes 262176 | tf_op jit(solution)/shard_map/ppermute | solution.py:388
  21.1 1.7 %collective-permute-start.8 = (bf16[128,1024]{1,0:T(8,128)(2,1)S(1)}, bf16[128,1024]{1,0:T(8,128)(2,1)S(1)}, u32[]{:S(2)}, u32[]{:S(2)}) collective-permute-start(bf16[128,1024]{1,0:T(8,128)(2,1)S(1)} %hold.7.refs_3_.refs_10_), channel_id=1, source_target_pairs={{0,4},{4,0},{8,12},{12,8},{16,20},{20,16},{24,28},{28,24},{1,5},{5... | collective-permute-start | bytes 786440 | tf_op jit(solution)/shard_map/ppermute | solution.py:388
  22.8 3.6 %collective-permute-done.7.refs_1_.refs_9_ = bf16[128,1024]{1,0:T(8,128)(2,1)S(1)} collective-permute-done((bf16[128,1024]{1,0:T(8,128)(2,1)S(1)}, bf16[128,1024]{1,0:T(8,128)(2,1)S(1)}, u32[]{:S(2)}, u32[]{:S(2)}) %collective-permute-start.7) | collective-permute-done | bytes 262176 | tf_op jit(solution)/shard_map/ppermute | solution.py:388
  26.5 1.5 %collective-permute-start.5 = (bf16[4,128]{1,0:T(4,128)(2,1)S(1)}, bf16[4,128]{1,0:T(4,128)(2,1)S(1)}, u32[]{:S(2)}, u32[]{:S(2)}) collective-permute-start(bf16[4,128]{1,0:T(4,128)(2,1)S(1)} %get-tuple-element.43.refs_2_), channel_id=1, source_target_pairs={{0,16},{4,20},{8,24},{12,28},{16,0},{20,4},{24,8},{28,12},{1,17},{... | collective-permute-start | bytes 3080 | tf_op jit(solution)/shard_map/ppermute | solution.py:388
  28.0 1.7 %collective-permute-done.8.refs_2_.refs_11_ = bf16[128,1024]{1,0:T(8,128)(2,1)S(1)} collective-permute-done((bf16[128,1024]{1,0:T(8,128)(2,1)S(1)}, bf16[128,1024]{1,0:T(8,128)(2,1)S(1)}, u32[]{:S(2)}, u32[]{:S(2)}) %collective-permute-start.8) | collective-permute-done | bytes 262176 | tf_op jit(solution)/shard_map/ppermute | solution.py:388
  31.0 5.0 %collective-permute-done.12.refs_0_ = bf16[256,1024]{1,0:T(8,128)(2,1)S(1)} collective-permute-done((bf16[256,1024]{1,0:T(8,128)(2,1)}, bf16[256,1024]{1,0:T(8,128)(2,1)S(1)}, u32[]{:S(2)}, u32[]{:S(2)}) %collective-permute-start.12) | collective-permute-done | bytes 524320 | tf_op jit(solution)/shard_map/ppermute | solution.py:388
  36.1 3.5 %forward_near.1 = (f32[8,128]{1,0:T(8,128)S(1)}, f32[1,1024]{1,0:T(1,128)S(1)}, bf16[1024,1024]{1,0:T(8,128)(2,1)S(1)}, bf16[2,256,1024]{2,1,0:T(8,128)(2,1)S(1)}, bf16[2,256,1024]{2,1,0:T(8,128)(2,1)S(1)}) custom-call(s32[8]{0:T(128)S(1)} %copy-done.3, s32[1,1024]{1,0:T(1,128)S(1)} %bitcast.4, bf16[4,128]{1,0:T(4,128)(2,1)S(1)} %get-tuple-element.43.refs_2_, ...), custom_call_target="tpu_custom_call" | custom-call | flops 3000000000 | tf_op jit(solution)/shard_map/forward_near/pallas_call | solution.py:177
  39.6 4.9 %forward_far.1 = (f32[8,1024]{1,0:T(8,128)S(1)}, bf16[2,256,1024]{2,1,0:T(8,128)(2,1)S(1)}, bf16[128,1024]{1,0:T(8,128)(2,1)S(1)}, bf16[128,1024]{1,0:T(8,128)(2...) custom-call(s32[8]{0:T(128)S(1)} %copy-done.3, ...), custom_call_target="tpu_custom_call" | custom-call | flops 10000000 | tf_op jit(solution)/shard_map/forward_far/pallas_call | solution.py:240
  44.6 1.5 %collective-permute-start.15 = (bf16[136,1024]{1,0:T(8,128)(2,1)S(1)}, bf16[136,1024]{1,0:T(8,128)(2,1)S(1)}, u32[]{:S(2)}, u32[]{:S(2)}) collective-permute-start(bf16[136,1024]{1,0:T(8,128)(2,1)S(1)} %get-tuple-element.57), channel_id=1, source_target_pairs={{0,4},{4,0},{8,12},{12,8},{16,20},{20,16},{24,28},{28,24},{1,5},{5... | collective-permute-start | bytes 835592 | tf_op jit(solution)/shard_map/ppermute | solution.py:388
  46.0 1.6 %backward.2 = (bf16[256,1024]{1,0:T(8,128)(2,1)S(1)}, bf16[256,1024]{1,0:T(8,128)(2,1)S(1)}) custom-call(f32[1,1024]{1,0:T(1,128)S(1)} %get-tuple-element.47.refs_2_.gain_ref, bf16[1024,1024]{1,0:T(8,128)(2,1)S(1)} %get-tuple-element.48.refs_3_.weight_ref, bf16[2,256,1024]{2,1,0:T(8,128)(2,1)S(1)} %get-tuple-element.59.slope_ref, ...), custom_call_target="tpu_custom_call" | custom-call | flops 10000000 | tf_op jit(solution)/shard_map/backward/pallas_call | solution.py:278
  47.6 1.6 %collective-permute-start.22 = (bf16[256,1024]{1,0:T(8,128)(2,1)S(1)}, bf16[256,1024]{1,0:T(8,128)(2,1)S(1)}, u32[]{:S(2)}, u32[]{:S(2)}) collective-permute-start(bf16[256,1024]{1,0:T(8,128)(2,1)S(1)} %get-tuple-element.68), channel_id=1, source_target_pairs={{0,2},{1,3},{2,0},{3,1},{4,6},{5,7},{6,4},{7,5},{8,10},{9,11},{10,... | collective-permute-start | bytes 1572872 | tf_op jit(solution)/shard_map/ppermute | solution.py:388
  49.7 3.9 %collective-permute-done.15.refs_1_ = bf16[136,1024]{1,0:T(8,128)(2,1)S(1)} collective-permute-done((bf16[136,1024]{1,0:T(8,128)(2,1)S(1)}, bf16[136,1024]{1,0:T(8,128)(2,1)S(1)}, u32[]{:S(2)}, u32[]{:S(2)}) %collective-permute-start.15) | collective-permute-done | bytes 278560 | tf_op jit(solution)/shard_map/ppermute | solution.py:388
  53.7 0.9 %collective-permute-start.16 = (bf16[136,1024]{1,0:T(8,128)(2,1)S(1)}, bf16[136,1024]{1,0:T(8,128)(2,1)S(1)}, u32[]{:S(2)}, u32[]{:S(2)}) collective-permute-start(bf16[136,1024]{1,0:T(8,128)(2,1)S(1)} %get-tuple-element.61.refs_4_), channel_id=1, source_target_pairs={{0,8},{4,12},{8,0},{12,4},{16,24},{20,28},{24,16},{28,20},{1,9},{5... | collective-permute-start | bytes 835592 | tf_op jit(solution)/shard_map/ppermute | solution.py:388
  54.6 1.1 %collective-permute-start.14 = (bf16[128,1024]{1,0:T(8,128)(2,1)S(1)}, bf16[128,1024]{1,0:T(8,128)(2,1)S(1)}, u32[]{:S(2)}, u32[]{:S(2)}) collective-permute-start(bf16[128,1024]{1,0:T(8,128)(2,1)S(1)} %get-tuple-element.55), channel_id=1, source_target_pairs={{0,4},{4,0},{8,12},{12,8},{16,20},{20,16},{24,28},{28,24},{1,5},{5... | collective-permute-start | bytes 786440 | tf_op jit(solution)/shard_map/ppermute | solution.py:388
  55.7 1.6 %backward.3 = (bf16[256,1024]{1,0:T(8,128)(2,1)S(1)}, bf16[256,1024]{1,0:T(8,128)(2,1)S(1)}, bf16[128,1024]{1,0:T(8,128)(2,1)S(1)}) custom-call(f32[1,1024]{1,0:T(1,128)S(1)} %get-tuple-element.47.refs_2_.gain_ref, bf16[1024,1024]{1,0:T(8,128)(2,1)S(1)} %get-tuple-element.48.refs_3_.weight_ref, ...), custom_call_target="tpu_custom_call", output_to_operand_aliasing={{2}: (6, {})} | custom-call | flops 10000000 | tf_op jit(solution)/shard_map/backward/pallas_call | solution.py:278
  57.3 1.0 %collective-permute-start.24 = (bf16[128,1024]{1,0:T(8,128)(2,1)S(1)}, bf16[128,1024]{1,0:T(8,128)(2,1)S(1)}, u32[]{:S(2)}, u32[]{:S(2)}) collective-permute-start(bf16[128,1024]{1,0:T(8,128)(2,1)S(1)} %get-tuple-element.70), channel_id=1, source_target_pairs={{0,4},{4,0},{8,12},{12,8},{16,20},{20,16},{24,28},{28,24},{1,5},{5... | collective-permute-start | bytes 786440 | tf_op jit(solution)/shard_map/ppermute | solution.py:388
  58.3 5.6 %collective-permute-done.14.refs_1_ = bf16[128,1024]{1,0:T(8,128)(2,1)S(1)} collective-permute-done((bf16[128,1024]{1,0:T(8,128)(2,1)S(1)}, bf16[128,1024]{1,0:T(8,128)(2,1)S(1)}, u32[]{:S(2)}, u32[]{:S(2)}) %collective-permute-start.14) | collective-permute-done | bytes 262176 | tf_op jit(solution)/shard_map/ppermute | solution.py:388
  64.1 3.2 %collective-permute-done.24.refs_1_ = bf16[128,1024]{1,0:T(8,128)(2,1)S(1)} collective-permute-done((bf16[128,1024]{1,0:T(8,128)(2,1)S(1)}, bf16[128,1024]{1,0:T(8,128)(2,1)S(1)}, u32[]{:S(2)}, u32[]{:S(2)}) %collective-permute-start.24) | collective-permute-done | bytes 262176 | tf_op jit(solution)/shard_map/ppermute | solution.py:388
  67.4 1.6 %collective-permute-start.26 = (bf16[128,1024]{1,0:T(8,128)(2,1)S(1)}, bf16[128,1024]{1,0:T(8,128)(2,1)S(1)}, u32[]{:S(2)}, u32[]{:S(2)}) collective-permute-start(bf16[128,1024]{1,0:T(8,128)(2,1)S(1)} %get-tuple-element.76), channel_id=1, source_target_pairs={{0,4},{4,0},{8,12},{12,8},{16,20},{20,16},{24,28},{28,24},{1,5},{5... | collective-permute-start | bytes 786440 | tf_op jit(solution)/shard_map/ppermute | solution.py:388
  69.0 1.7 %collective-permute-start.27 = (bf16[128,1024]{1,0:T(8,128)(2,1)S(1)}, bf16[128,1024]{1,0:T(8,128)(2,1)S(1)}, u32[]{:S(2)}, u32[]{:S(2)}) collective-permute-start(bf16[128,1024]{1,0:T(8,128)(2,1)S(1)} %get-tuple-element.72.refs_2_), channel_id=1, source_target_pairs={{0,8},{4,12},{8,0},{12,4},{16,24},{20,28},{24,16},{28,20},{1,9},{5... | collective-permute-start | bytes 786440 | tf_op jit(solution)/shard_map/ppermute | solution.py:388
  70.7 2.3 %collective-permute-done.23.refs_0_ = bf16[256,1024]{1,0:T(8,128)(2,1)S(1)} collective-permute-done((bf16[256,1024]{1,0:T(8,128)(2,1)S(1)}, bf16[256,1024]{1,0:T(8,128)(2,1)S(1)}, u32[]{:S(2)}, u32[]{:S(2)}) %collective-permute-start.23) | collective-permute-done | bytes 524320 | tf_op jit(solution)/shard_map/ppermute | solution.py:388
  73.0 3.5 %collective-permute-done.17.piece_ref.refs_3_ = bf16[136,1024]{1,0:T(8,128)(2,1)S(1)} collective-permute-done((bf16[136,1024]{1,0:T(8,128)(2,1)S(1)}, bf16[136,1024]{1,0:T(8,128)(2,1)S(1)}, u32[]{:S(2)}, u32[]{:S(2)}) %collective-permute-start.17) | collective-permute-done | bytes 278560 | tf_op jit(solution)/shard_map/ppermute | solution.py:388
  76.5 1.6 %collective-permute-start.19 = (f32[8,128]{1,0:T(8,128)S(1)}, f32[8,128]{1,0:T(8,128)S(1)}, u32[]{:S(2)}, u32[]{:S(2)}) collective-permute-start(f32[8,128]{1,0:T(8,128)S(1)} %ride_end.1.refs_0_), channel_id=1, source_target_pairs={{0,2},{1,3},{2,0},{3,1},{4,6},{5,7},{6,4},{7,5},{8,10},{9,11},{10,... | collective-permute-start | bytes 12296 | tf_op jit(solution)/shard_map/ppermute | solution.py:388
  78.1 1.3 %collective-permute-done.27.refs_2_ = bf16[128,1024]{1,0:T(8,128)(2,1)S(1)} collective-permute-done((bf16[128,1024]{1,0:T(8,128)(2,1)S(1)}, bf16[128,1024]{1,0:T(8,128)(2,1)S(1)}, u32[]{:S(2)}, u32[]{:S(2)}) %collective-permute-start.27) | collective-permute-done | bytes 262176 | tf_op jit(solution)/shard_map/ppermute | solution.py:388
  79.4 0.9 %fold.7 = f32[128,1024]{1,0:T(8,128)} custom-call(bf16[128,1024]{1,0:T(8,128)(2,1)S(1)} %get-tuple-element.75.refs_0_, bf16[128,1024]{1,0:T(8,128)(2,1)S(1)} %collective-permute-done.26.refs_1_, bf16[128,1024]{1,0:T(8,128)(2,1)S(1)} %collective-permute-done.27.refs_2_, bf16[136,1024]{1,0:T(8,128)(2,1)S(1)} %collective-permute-done.17.piece_ref.refs_3_), custom_call_target="tpu_custom_call" | custom-call | flops 3000000000 | tf_op jit(solution)/shard_map/fold/pallas_call | solution.py:314
  80.3 2.5 %pack.1 = (bf16[256,4,1024]{2,1,0:T(4,128)(2,1)}, f32[8,128]{1,0:T(8,128)S(1)}) custom-call(bf16[256,1024]{1,0:T(8,128)(2,1)S(1)} %get-tuple-element.66.refs_0_, bf16[256,1024]{1,0:T(8,128)(2,1)S(1)} %collective-permute-done.21.refs_1_, bf16[256,1024]{1,0:T(8,128)(2,1)S(1)} %collective-permute-done.22.refs_1_.refs_2_, ...), custom_call_target="tpu_custom_call" | custom-call | flops 10000000 | tf_op jit(solution)/shard_map/pack/pallas_call | solution.py:91
  (54 shorter events, 6.3 us)
Async XLA Ops:
  0.6 16.5 %copy-start.4 = (bf16[1,128]{1,0:T(2,128)(2,1)S(1)}, bf16[1,128]{1,0:T(2,128)(2,1)}, u32[]{:S(2)}) copy-start(bf16[1,128]{1,0:T(2,128)(2,1)} %refs_0_.3) | copy-start | bytes 772
  0.6 13.4 %collective-permute-start.2 = (bf16[128,1024]{1,0:T(8,128)(2,1)}, bf16[128,1024]{1,0:T(8,128)(2,1)S(1)}, u32[]{:S(2)}, u32[]{:S(2)}) collective-permute-start(bf16[128,1024]{1,0:T(8,128)(2,1)} %bitcast.6), channel_id=1, source_target_pairs={{0,4},{4,0},{8,12},{12,8},{16,20},{20,16},{24,28},{28,24},{1,5},{5... | collective-permute-start | bytes 786440 | tf_op jit(solution)/shard_map/ppermute | solution.py:388
  3.6 13.5 %collective-permute-start.1 = (bf16[128,1024]{1,0:T(8,128)(2,1)}, bf16[128,1024]{1,0:T(8,128)(2,1)S(1)}, u32[]{:S(2)}, u32[]{:S(2)}) collective-permute-start(bf16[128,1024]{1,0:T(8,128)(2,1)} %bitcast.7), channel_id=1, source_target_pairs={{0,8},{4,12},{8,0},{12,4},{16,24},{20,28},{24,16},{28,20},{1,9},{5... | collective-permute-start | bytes 786440 | tf_op jit(solution)/shard_map/ppermute | solution.py:388
  5.2 14.3 %collective-permute-start.4 = (bf16[128,1024]{1,0:T(8,128)(2,1)}, bf16[128,1024]{1,0:T(8,128)(2,1)S(1)}, u32[]{:S(2)}, u32[]{:S(2)}) collective-permute-start(bf16[128,1024]{1,0:T(8,128)(2,1)} %bitcast.8), channel_id=1, source_target_pairs={{0,16},{4,20},{8,24},{12,28},{16,0},{20,4},{24,8},{28,12},{1,17},{... | collective-permute-start | bytes 786440 | tf_op jit(solution)/shard_map/ppermute | solution.py:388
  7.8 5.7 %collective-permute-start = (bf16[1,128]{1,0:T(2,128)(2,1)}, bf16[1,128]{1,0:T(2,128)(2,1)S(1)}, u32[]{:S(2)}, u32[]{:S(2)}) collective-permute-start(bf16[1,128]{1,0:T(2,128)(2,1)} %refs_0_.3), channel_id=1, source_target_pairs={{0,4},{4,0},{8,12},{12,8},{16,20},{20,16},{24,28},{28,24},{1,5},{5... | collective-permute-start | bytes 776 | tf_op jit(solution)/shard_map/ppermute | solution.py:388
  11.9 19.1 %collective-permute-start.11 = (bf16[256,1024]{1,0:T(8,128)(2,1)}, bf16[256,1024]{1,0:T(8,128)(2,1)S(1)}, u32[]{:S(2)}, u32[]{:S(2)}) collective-permute-start(bf16[256,1024]{1,0:T(8,128)(2,1)} %get-tuple-element.49), channel_id=1, source_target_pairs={{0,2},{1,3},{2,0},{3,1},{4,6},{5,7},{6,4},{7,5},{8,10},{9,11},{10,... | collective-permute-start | bytes 1572872 | tf_op jit(solution)/shard_map/ppermute | solution.py:388
  13.5 22.5 %collective-permute-start.12 = (bf16[256,1024]{1,0:T(8,128)(2,1)}, bf16[256,1024]{1,0:T(8,128)(2,1)S(1)}, u32[]{:S(2)}, u32[]{:S(2)}) collective-permute-start(bf16[256,1024]{1,0:T(8,128)(2,1)} %get-tuple-element.50), channel_id=1, source_target_pairs={{0,2},{1,3},{2,0},{3,1},{4,6},{5,7},{6,4},{7,5},{8,10},{9,11},{10,... | collective-permute-start | bytes 1572872 | tf_op jit(solution)/shard_map/ppermute | solution.py:388
  17.1 9.3 %collective-permute-start.7 = (bf16[128,1024]{1,0:T(8,128)(2,1)S(1)}, bf16[128,1024]{1,0:T(8,128)(2,1)S(1)}, u32[]{:S(2)}, u32[]{:S(2)}) collective-permute-start(bf16[128,1024]{1,0:T(8,128)(2,1)S(1)} %get-tuple-element.46.refs_8_), channel_id=1, source_target_pairs={{0,4},{4,0},{8,12},{12,8},{16,20},{20,16},{24,28},{28,24},{1,5},{5... | collective-permute-start | bytes 786440 | tf_op jit(solution)/shard_map/ppermute | solution.py:388
  17.6 3.6 %collective-permute-start.3 = (bf16[2,128]{1,0:T(2,128)(2,1)S(1)}, bf16[2,128]{1,0:T(2,128)(2,1)S(1)}, u32[]{:S(2)}, u32[]{:S(2)}) collective-permute-start(bf16[2,128]{1,0:T(2,128)(2,1)S(1)} %get-tuple-element.40.refs_0_), channel_id=1, source_target_pairs={{0,8},{4,12},{8,0},{12,4},{16,24},{20,28},{24,16},{28,20},{1,9},{5... | collective-permute-start | bytes 1544 | tf_op jit(solution)/shard_map/ppermute | solution.py:388
  20.2 6.4 %collective-permute-start.9 = (bf16[128,1024]{1,0:T(8,128)(2,1)S(1)}, bf16[128,1024]{1,0:T(8,128)(2,1)S(1)}, u32[]{:S(2)}, u32[]{:S(2)}) collective-permute-start(bf16[128,1024]{1,0:T(8,128)(2,1)S(1)} %hold.7.refs_3_.refs_10_), channel_id=1, source_target_pairs={{0,8},{4,12},{8,0},{12,4},{16,24},{20,28},{24,16},{28,20},{1,9},{5... | collective-permute-start | bytes 786440 | tf_op jit(solution)/shard_map/ppermute | solution.py:388
  21.1 8.5 %collective-permute-start.8 = (bf16[128,1024]{1,0:T(8,128)(2,1)S(1)}, bf16[128,1024]{1,0:T(8,128)(2,1)S(1)}, u32[]{:S(2)}, u32[]{:S(2)}) collective-permute-start(bf16[128,1024]{1,0:T(8,128)(2,1)S(1)} %hold.7.refs_3_.refs_10_), channel_id=1, source_target_pairs={{0,4},{4,0},{8,12},{12,8},{16,20},{20,16},{24,28},{28,24},{1,5},{5... | collective-permute-start | bytes 786440 | tf_op jit(solution)/shard_map/ppermute | solution.py:388
  26.4 9.7 %collective-permute-start.6 = (bf16[256,1024]{1,0:T(8,128)(2,1)}, bf16[256,1024]{1,0:T(8,128)(2,1)S(1)}, u32[]{:S(2)}, u32[]{:S(2)}) collective-permute-start(bf16[256,1024]{1,0:T(8,128)(2,1)} %get-tuple-element.45), channel_id=1, source_target_pairs={{0,1},{1,0},{2,3},{3,2},{4,5},{5,4},{6,7},{7,6},{8,9},{9,8},{10,11... | collective-permute-start | bytes 1572872 | tf_op jit(solution)/shard_map/ppermute | solution.py:388
  26.5 4.5 %collective-permute-start.5 = (bf16[4,128]{1,0:T(4,128)(2,1)S(1)}, bf16[4,128]{1,0:T(4,128)(2,1)S(1)}, u32[]{:S(2)}, u32[]{:S(2)}) collective-permute-start(bf16[4,128]{1,0:T(4,128)(2,1)S(1)} %get-tuple-element.43.refs_2_), channel_id=1, source_target_pairs={{0,16},{4,20},{8,24},{12,28},{16,0},{20,4},{24,8},{28,12},{1,17},{... | collective-permute-start | bytes 3080 | tf_op jit(solution)/shard_map/ppermute | solution.py:388
  29.7 6.5 %copy-start.1 = (s32[1024,1]{0,1:T(1,128)S(1)}, s32[1024,1]{0,1:T(1,128)}, u32[]{:S(2)}) copy-start(s32[1024,1]{0,1:T(1,128)} %param.8) | copy-start | bytes 12292
  29.7 6.5 %copy-start.3 = (s32[8]{0:T(128)S(1)}, s32[8]{0:T(128)}, u32[]{:S(2)}) copy-start(s32[8]{0:T(128)} %refs_0_.5) | copy-start | bytes 100
  29.7 6.5 %copy-start.5 = (bf16[1,128,1024]{2,1,0:T(8,128)(2,1)S(1)}, bf16[1,128,1024]{2,1,0:T(8,128)(2,1)}, u32[]{:S(2)}) copy-start(bf16[1,128,1024]{2,1,0:T(8,128)(2,1)} %param.6) | copy-start | bytes 786436
  29.7 6.4 %collective-permute-start.10 = (bf16[128,1024]{1,0:T(8,128)(2,1)S(1)}, bf16[128,1024]{1,0:T(8,128)(2,1)S(1)}, u32[]{:S(2)}, u32[]{:S(2)}) collective-permute-start(bf16[128,1024]{1,0:T(8,128)(2,1)S(1)} %hold.9.refs_12_), channel_id=1, source_target_pairs={{0,4},{4,0},{8,12},{12,8},{16,20},{20,16},{24,28},{28,24},{1,5},{5... | collective-permute-start | bytes 786440 | tf_op jit(solution)/shard_map/ppermute | solution.py:388
  36.0 3.6 %collective-permute-start.13 = (bf16[256,1024]{1,0:T(8,128)(2,1)S(1)}, bf16[256,1024]{1,0:T(8,128)(2,1)S(1)}, u32[]{:S(2)}, u32[]{:S(2)}) collective-permute-start(bf16[256,1024]{1,0:T(8,128)(2,1)S(1)} %hold.10), channel_id=1, source_target_pairs={{0,1},{1,0},{2,3},{3,2},{4,5},{5,4},{6,7},{7,6},{8,9},{9,8},{10,11... | collective-permute-start | bytes 1572872 | tf_op jit(solution)/shard_map/ppermute | solution.py:388
  44.6 9.1 %collective-permute-start.15 = (bf16[136,1024]{1,0:T(8,128)(2,1)S(1)}, bf16[136,1024]{1,0:T(8,128)(2,1)S(1)}, u32[]{:S(2)}, u32[]{:S(2)}) collective-permute-start(bf16[136,1024]{1,0:T(8,128)(2,1)S(1)} %get-tuple-element.57), channel_id=1, source_target_pairs={{0,4},{4,0},{8,12},{12,8},{16,20},{20,16},{24,28},{28,24},{1,5},{5... | collective-permute-start | bytes 835592 | tf_op jit(solution)/shard_map/ppermute | solution.py:388
  47.6 23.1 %collective-permute-start.22 = (bf16[256,1024]{1,0:T(8,128)(2,1)S(1)}, bf16[256,1024]{1,0:T(8,128)(2,1)S(1)}, u32[]{:S(2)}, u32[]{:S(2)}) collective-permute-start(bf16[256,1024]{1,0:T(8,128)(2,1)S(1)} %get-tuple-element.68), channel_id=1, source_target_pairs={{0,2},{1,3},{2,0},{3,1},{4,6},{5,7},{6,4},{7,5},{8,10},{9,11},{10,... | collective-permute-start | bytes 1572872 | tf_op jit(solution)/shard_map/ppermute | solution.py:388
  49.2 23.8 %collective-permute-start.23 = (bf16[256,1024]{1,0:T(8,128)(2,1)S(1)}, bf16[256,1024]{1,0:T(8,128)(2,1)S(1)}, u32[]{:S(2)}, u32[]{:S(2)}) collective-permute-start(bf16[256,1024]{1,0:T(8,128)(2,1)S(1)} %get-tuple-element.60.refs_3_), channel_id=1, source_target_pairs={{0,2},{1,3},{2,0},{3,1},{4,6},{5,7},{6,4},{7,5},{8,10},{9,11},{10,... | collective-permute-start | bytes 1572872 | tf_op jit(solution)/shard_map/ppermute | solution.py:388
  53.7 10.1 %collective-permute-start.16 = (bf16[136,1024]{1,0:T(8,128)(2,1)S(1)}, bf16[136,1024]{1,0:T(8,128)(2,1)S(1)}, u32[]{:S(2)}, u32[]{:S(2)}) collective-permute-start(bf16[136,1024]{1,0:T(8,128)(2,1)S(1)} %get-tuple-element.61.refs_4_), channel_id=1, source_target_pairs={{0,8},{4,12},{8,0},{12,4},{16,24},{20,28},{24,16},{28,20},{1,9},{5... | collective-permute-start | bytes 835592 | tf_op jit(solution)/shard_map/ppermute | solution.py:388
  54.6 9.2 %collective-permute-start.14 = (bf16[128,1024]{1,0:T(8,128)(2,1)S(1)}, bf16[128,1024]{1,0:T(8,128)(2,1)S(1)}, u32[]{:S(2)}, u32[]{:S(2)}) collective-permute-start(bf16[128,1024]{1,0:T(8,128)(2,1)S(1)} %get-tuple-element.55), channel_id=1, source_target_pairs={{0,4},{4,0},{8,12},{12,8},{16,20},{20,16},{24,28},{28,24},{1,5},{5... | collective-permute-start | bytes 786440 | tf_op jit(solution)/shard_map/ppermute | solution.py:388
  57.3 10.0 %collective-permute-start.24 = (bf16[128,1024]{1,0:T(8,128)(2,1)S(1)}, bf16[128,1024]{1,0:T(8,128)(2,1)S(1)}, u32[]{:S(2)}, u32[]{:S(2)}) collective-permute-start(bf16[128,1024]{1,0:T(8,128)(2,1)S(1)} %get-tuple-element.70), channel_id=1, source_target_pairs={{0,4},{4,0},{8,12},{12,8},{16,20},{20,16},{24,28},{28,24},{1,5},{5... | collective-permute-start | bytes 786440 | tf_op jit(solution)/shard_map/ppermute | solution.py:388
  64.0 12.5 %collective-permute-start.17 = (bf16[136,1024]{1,0:T(8,128)(2,1)S(1)}, bf16[136,1024]{1,0:T(8,128)(2,1)S(1)}, u32[]{:S(2)}, u32[]{:S(2)}) collective-permute-start(bf16[136,1024]{1,0:T(8,128)(2,1)S(1)} %get-tuple-element.64.refs_3_), channel_id=1, source_target_pairs={{0,16},{4,20},{8,24},{12,28},{16,0},{20,4},{24,8},{28,12},{1,17},{... | collective-permute-start | bytes 835592 | tf_op jit(solution)/shard_map/ppermute | solution.py:388
  67.4 9.1 %collective-permute-start.26 = (bf16[128,1024]{1,0:T(8,128)(2,1)S(1)}, bf16[128,1024]{1,0:T(8,128)(2,1)S(1)}, u32[]{:S(2)}, u32[]{:S(2)}) collective-permute-start(bf16[128,1024]{1,0:T(8,128)(2,1)S(1)} %get-tuple-element.76), channel_id=1, source_target_pairs={{0,4},{4,0},{8,12},{12,8},{16,20},{20,16},{24,28},{28,24},{1,5},{5... | collective-permute-start | bytes 786440 | tf_op jit(solution)/shard_map/ppermute | solution.py:388
  69.0 10.3 %collective-permute-start.27 = (bf16[128,1024]{1,0:T(8,128)(2,1)S(1)}, bf16[128,1024]{1,0:T(8,128)(2,1)S(1)}, u32[]{:S(2)}, u32[]{:S(2)}) collective-permute-start(bf16[128,1024]{1,0:T(8,128)(2,1)S(1)} %get-tuple-element.72.refs_2_), channel_id=1, source_target_pairs={{0,8},{4,12},{8,0},{12,4},{16,24},{20,28},{24,16},{28,20},{1,9},{5... | collective-permute-start | bytes 786440 | tf_op jit(solution)/shard_map/ppermute | solution.py:388
  70.7 9.6 %collective-permute-start.21 = (bf16[256,1024]{1,0:T(8,128)(2,1)S(1)}, bf16[256,1024]{1,0:T(8,128)(2,1)S(1)}, u32[]{:S(2)}, u32[]{:S(2)}) collective-permute-start(bf16[256,1024]{1,0:T(8,128)(2,1)S(1)} %get-tuple-element.67), channel_id=1, source_target_pairs={{0,1},{1,0},{2,3},{3,2},{4,5},{5,4},{6,7},{7,6},{8,9},{9,8},{10,11... | collective-permute-start | bytes 1572872 | tf_op jit(solution)/shard_map/ppermute | solution.py:388
  73.0 7.3 %collective-permute-start.25 = (bf16[256,1024]{1,0:T(8,128)(2,1)S(1)}, bf16[256,1024]{1,0:T(8,128)(2,1)S(1)}, u32[]{:S(2)}, u32[]{:S(2)}) collective-permute-start(bf16[256,1024]{1,0:T(8,128)(2,1)S(1)} %hold.11), channel_id=1, source_target_pairs={{0,1},{1,0},{2,3},{3,2},{4,5},{5,4},{6,7},{7,6},{8,9},{9,8},{10,11... | collective-permute-start | bytes 1572872 | tf_op jit(solution)/shard_map/ppermute | solution.py:388
  76.5 6.3 %collective-permute-start.20 = (f32[8,128]{1,0:T(8,128)S(1)}, f32[8,128]{1,0:T(8,128)S(1)}, u32[]{:S(2)}, u32[]{:S(2)}) collective-permute-start(f32[8,128]{1,0:T(8,128)S(1)} %ride_end.1.refs_0_), channel_id=1, source_target_pairs={{0,3},{1,2},{2,1},{3,0},{4,7},{5,6},{6,5},{7,4},{8,11},{9,10},{10,... | collective-permute-start | bytes 12296 | tf_op jit(solution)/shard_map/ppermute | solution.py:388
  76.5 6.3 %collective-permute-start.19 = (f32[8,128]{1,0:T(8,128)S(1)}, f32[8,128]{1,0:T(8,128)S(1)}, u32[]{:S(2)}, u32[]{:S(2)}) collective-permute-start(f32[8,128]{1,0:T(8,128)S(1)} %ride_end.1.refs_0_), channel_id=1, source_target_pairs={{0,2},{1,3},{2,0},{3,1},{4,6},{5,7},{6,4},{7,5},{8,10},{9,11},{10,... | collective-permute-start | bytes 12296 | tf_op jit(solution)/shard_map/ppermute | solution.py:388
  79.3 3.5 %collective-permute-start.18 = (f32[8,128]{1,0:T(8,128)S(1)}, f32[8,128]{1,0:T(8,128)S(1)}, u32[]{:S(2)}, u32[]{:S(2)}) collective-permute-start(f32[8,128]{1,0:T(8,128)S(1)} %ride_end.1.refs_0_), channel_id=1, source_target_pairs={{0,1},{1,0},{2,3},{3,2},{4,5},{5,4},{6,7},{7,6},{8,9},{9,8},{10,11... | collective-permute-start | bytes 12296 | tf_op jit(solution)/shard_map/ppermute | solution.py:388
  (2 other events, 7.1 us)

commit v7 on v6

--- a/solution.py
+++ b/solution.py
@@ -404,14 +404,15 @@
             break
         pieces[o * inner] = swap(pieces[(o ^ bit) * inner], "dp", bit * inner)
     own, side, *away, unpacked = unpack(hidden)
-    for o in range(line):
-        if small and o == 2:
-            pieces[4] = hold([], pieces[4], [unpacked])[1]
-        if small and o == 1:
-            gain, pieces[2] = hold(gains, pieces[2], [pieces[1]])
-        if pieces[o * inner] is not None:
+    if not small:
+        for o in range(line):
             pieces[o * inner + 1] = swap(pieces[o * inner], "dp", 1)
     if small:
+        pieces[1] = swap(pieces[0], "dp", 1)
+        gain, pieces[1] = hold(gains, pieces[1], [pieces[2]])
+        pieces[3] = swap(pieces[1], "dp", 2)
+        pieces[4] = hold([], pieces[4], [unpacked])[1]
+        pieces[5] = swap(pieces[4], "dp", 1)
         gains = [gain, swap(gain, "dp", 2)]
         gain, side = hold(gains, side, [pieces[4]])
         gains = [gain, swap(gain, "dp", 4)]
@@ -431,25 +432,24 @@
 
     far = backward(gain_row, weights, far, far_slopes)
     near = None
+    first = [swap(parts[inner + 1], "dp", inner), swap(parts[inner], "dp", inner)]
     across = [None] * line
-    waiting = list(range(line - 1, -1, -1))
-    for o in (waiting.pop(0), waiting.pop(0)):
+    waiting = list(range(line - 1, 1, -1))
+    for o in waiting[:2]:
         across[o] = swap(parts[o * inner + 1], "dp", 1)
+    waiting = waiting[2:]
     came = [[] for _ in range(line)]
     rides = line - 1
-    order = far[-1:]
-    for o in range(line - 1, 0, -1):
-        held = [parts[waiting[0] * inner + 1]] if waiting and (o > 2 or o == 1) else []
-        if near is None and line > 2:
-            held, later = [], held
+    order = [*far[-1:], first[0]]
+    for o in range(line - 1, 1, -1):
+        held = [parts[waiting[0] * inner + 1]] if waiting else []
         if o == rides:
             piece, loss, held = fold([parts[o * inner], across[o], *came[o]], loss, held, order)
         else:
             piece, _, held = fold([parts[o * inner], *came[o], across[o]], None, held, order)
         bit, order = o & -o, [piece]
         if near is None:
-            near = backward(gain_row, weights, [own, side], near_slopes, [loss], later if line > 2 else [])
-            near, held = near[:2], near[2:] or held
+            near = backward(gain_row, weights, [own, side], near_slopes, [loss])
             beside = swap(near[1], "fsdp", 1)
         moved = swap(piece, "dp", bit * inner)
         if o == rides:
@@ -459,6 +459,9 @@
             came[o ^ bit] = [moved, *came[o ^ bit]]
         if held:
             across[waiting.pop(0)] = swap(held[0], "dp", 1)
+    both, _, _ = fold([parts[1], first[0]], None, (), near[-1:])
+    across[0] = swap(both, "dp", 1)
+    came[0] = [first[1], *came[0]]
     loss = ride_end(loss, came[0][-1])
 
     grad_hidden, packed = pack([near[0], beside, *exchange(far, order)])

time: 83.6 us -> 83.1 us (level)
  waiting for transfers between devices: 36.3 us -> 26 us
  starting transfers between devices: 26.1 us -> 35.9 us
    ppermute x28, waiting for transfers between devices: 36.3 us -> 26 us  [swap(): return lax.ppermute(value, axis, [(i, i ^ offset) for i in range(size)])]
    ppermute x28, starting transfers between devices: 26.1 us -> 35.9 us  [swap(): return lax.ppermute(value, axis, [(i, i ^ offset) for i in range(size)])]
  transfers between devices with their start and end apart: 28 -> 28, of which waited for: 15 -> 12; matrix products, arithmetic and copies ran while one was open for 0% -> 0% of each run, Pallas kernels for 17% -> 17%
where the time goes in v7:
time: 83.1 us; the launch traced here: 82.9 us
  starting transfers between devices  35.9 us (43%)
  waiting for transfers between devices  26 us (31%)
  Pallas kernels  19.5 us (23%)
    ppermute x28, starting transfers between devices, swap(): return lax.ppermute(value, axis, [(i, i ^ offset) for i in range(size)])  35.9 us
    ppermute x28, waiting for transfers between devices, swap(): return lax.ppermute(value, axis, [(i, i ^ offset) for i in range(size)])  26 us
    pallas_call x1, Pallas kernels, forward_far(): pl.pallas_call(body, in_specs=[SMEM] + [VMEM] * (6 + n), out_specs=[VMEM]...  4.92 us
    pallas_call x1, Pallas kernels, unpack(): pl.pallas_call(body, in_specs=[ANY], out_specs=[VMEM] * (positions + 1),...  3.59 us
    pallas_call x1, Pallas kernels, forward_near(): pl.pallas_call(body, in_specs=[SMEM] + [VMEM] * (1 + n_gain + n) + [ANY]...  3.47 us
    pallas_call x2, Pallas kernels, backward(): pl.pallas_call(body, in_specs=[VMEM] * (3 + n) + [ANY] * (len(after) + le...  3.18 us
    pallas_call x1, Pallas kernels, pack(): pl.pallas_call(body, grid=(frames // chunk,), in_specs=[pl.BlockSpec((chu...  2.53 us
  transfers between devices with their start and end apart: 28, of which 12 were waited for; matrix products, arithmetic and copies ran while one was open for 0% of the time, Pallas kernels for 17%

profile of v7, /device:TPU:0, one launch (start us, length us, event | category | flops | bytes accessed | tf_op | source)
XLA Modules:
  0.0 82.9 jit_solution(2487356667061272779)
XLA Ops:
  0.6 3.1 %collective-permute-start.2 = (bf16[128,1024]{1,0:T(8,128)(2,1)}, bf16[128,1024]{1,0:T(8,128)(2,1)S(1)}, u32[]{:S(2)}, u32[]{:S(2)}) collective-permute-start(bf16[128,1024]{1,0:T(8,128)(2,1)} %bitcast.6), channel_id=1, source_target_pairs={{0,8},{4,12},{8,0},{12,4},{16,24},{20,28},{24,16},{28,20},{1,9},{5... | collective-permute-start | bytes 786440 | tf_op jit(solution)/shard_map/ppermute | solution.py:388
  3.7 1.5 %collective-permute-start.1 = (bf16[128,1024]{1,0:T(8,128)(2,1)}, bf16[128,1024]{1,0:T(8,128)(2,1)S(1)}, u32[]{:S(2)}, u32[]{:S(2)}) collective-permute-start(bf16[128,1024]{1,0:T(8,128)(2,1)} %bitcast.7), channel_id=1, source_target_pairs={{0,4},{4,0},{8,12},{12,8},{16,20},{20,16},{24,28},{28,24},{1,5},{5... | collective-permute-start | bytes 786440 | tf_op jit(solution)/shard_map/ppermute | solution.py:388
  5.2 2.6 %collective-permute-start.4 = (bf16[128,1024]{1,0:T(8,128)(2,1)}, bf16[128,1024]{1,0:T(8,128)(2,1)S(1)}, u32[]{:S(2)}, u32[]{:S(2)}) collective-permute-start(bf16[128,1024]{1,0:T(8,128)(2,1)} %bitcast.8), channel_id=1, source_target_pairs={{0,16},{4,20},{8,24},{12,28},{16,0},{20,4},{24,8},{28,12},{1,17},{... | collective-permute-start | bytes 786440 | tf_op jit(solution)/shard_map/ppermute | solution.py:388
  8.3 3.6 %unpack.1 = (bf16[256,1024]{1,0:T(8,128)(2,1)}, bf16[256,1024]{1,0:T(8,128)(2,1)}, bf16[256,1024]{1,0:T(8,128)(2,1)}, bf16[256,1024]{1,0:T(8,128)(2,1)}, f32[8,128]{1,0:T(8,128)}) custom-call(bf16[256,4,1024]{2,1,0:T(4,128)(2,1)} %hidden_ref.1), custom_call_target="tpu_custom_call" | custom-call | flops 10000000 | tf_op jit(solution)/shard_map/unpack/pallas_call | solution.py:60
  11.9 1.6 %collective-permute-start.11 = (bf16[256,1024]{1,0:T(8,128)(2,1)}, bf16[256,1024]{1,0:T(8,128)(2,1)S(1)}, u32[]{:S(2)}, u32[]{:S(2)}) collective-permute-start(bf16[256,1024]{1,0:T(8,128)(2,1)} %get-tuple-element.46), channel_id=1, source_target_pairs={{0,2},{1,3},{2,0},{3,1},{4,6},{5,7},{6,4},{7,5},{8,10},{9,11},{10,... | collective-permute-start | bytes 1572872 | tf_op jit(solution)/shard_map/ppermute | solution.py:388
  14.6 2.0 %collective-permute-start.3 = (bf16[2,128]{1,0:T(2,128)(2,1)S(1)}, bf16[2,128]{1,0:T(2,128)(2,1)S(1)}, u32[]{:S(2)}, u32[]{:S(2)}) collective-permute-start(bf16[2,128]{1,0:T(2,128)(2,1)S(1)} %get-tuple-element.37.refs_0_), channel_id=1, source_target_pairs={{0,8},{4,12},{8,0},{12,4},{16,24},{20,28},{24,16},{28,20},{1,9},{5... | collective-permute-start | bytes 1544 | tf_op jit(solution)/shard_map/ppermute | solution.py:388
  16.6 3.0 %collective-permute-done.4.refs_0_ = bf16[128,1024]{1,0:T(8,128)(2,1)S(1)} collective-permute-done((bf16[128,1024]{1,0:T(8,128)(2,1)}, bf16[128,1024]{1,0:T(8,128)(2,1)S(1)}, u32[]{:S(2)}, u32[]{:S(2)}) %collective-permute-start.4) | collective-permute-done | bytes 262176 | tf_op jit(solution)/shard_map/ppermute | solution.py:388
  19.6 0.7 copy-done.2
  20.3 4.5 %collective-permute-done.3.refs_1_ = bf16[2,128]{1,0:T(2,128)(2,1)S(1)} collective-permute-done((bf16[2,128]{1,0:T(2,128)(2,1)S(1)}, bf16[2,128]{1,0:T(2,128)(2,1)S(1)}, u32[]{:S(2)}, u32[]{:S(2)}) %collective-permute-start.3) | collective-permute-done | bytes 544 | tf_op jit(solution)/shard_map/ppermute | solution.py:388
  24.8 1.7 %collective-permute-start.8 = (bf16[128,1024]{1,0:T(8,128)(2,1)S(1)}, bf16[128,1024]{1,0:T(8,128)(2,1)S(1)}, u32[]{:S(2)}, u32[]{:S(2)}) collective-permute-start(bf16[128,1024]{1,0:T(8,128)(2,1)S(1)} %hold.7.refs_3_.refs_10_), channel_id=1, source_target_pairs={{0,4},{4,0},{8,12},{12,8},{16,20},{20,16},{24,28},{28,24},{1,5},{5... | collective-permute-start | bytes 786440 | tf_op jit(solution)/shard_map/ppermute | solution.py:388
  26.6 2.4 %collective-permute-done.9.refs_0_ = bf16[128,1024]{1,0:T(8,128)(2,1)S(1)} collective-permute-done((bf16[128,1024]{1,0:T(8,128)(2,1)S(1)}, bf16[128,1024]{1,0:T(8,128)(2,1)S(1)}, u32[]{:S(2)}, u32[]{:S(2)}) %collective-permute-start.9) | collective-permute-done | bytes 262176 | tf_op jit(solution)/shard_map/ppermute | solution.py:388
  29.0 1.5 %collective-permute-start.5 = (bf16[4,128]{1,0:T(4,128)(2,1)S(1)}, bf16[4,128]{1,0:T(4,128)(2,1)S(1)}, u32[]{:S(2)}, u32[]{:S(2)}) collective-permute-start(bf16[4,128]{1,0:T(4,128)(2,1)S(1)} %get-tuple-element.40.refs_2_), channel_id=1, source_target_pairs={{0,16},{4,20},{8,24},{12,28},{16,0},{20,4},{24,8},{28,12},{1,17},{... | collective-permute-start | bytes 3080 | tf_op jit(solution)/shard_map/ppermute | solution.py:388
  31.2 1.8 %collective-permute-start.10 = (bf16[128,1024]{1,0:T(8,128)(2,1)S(1)}, bf16[128,1024]{1,0:T(8,128)(2,1)S(1)}, u32[]{:S(2)}, u32[]{:S(2)}) collective-permute-start(bf16[128,1024]{1,0:T(8,128)(2,1)S(1)} %hold.9.refs_12_), channel_id=1, source_target_pairs={{0,4},{4,0},{8,12},{12,8},{16,20},{20,16},{24,28},{28,24},{1,5},{5... | collective-permute-start | bytes 786440 | tf_op jit(solution)/shard_map/ppermute | solution.py:388
  33.4 2.6 %collective-permute-done.12.refs_0_ = bf16[256,1024]{1,0:T(8,128)(2,1)S(1)} collective-permute-done((bf16[256,1024]{1,0:T(8,128)(2,1)}, bf16[256,1024]{1,0:T(8,128)(2,1)S(1)}, u32[]{:S(2)}, u32[]{:S(2)}) %collective-permute-start.12) | collective-permute-done | bytes 524320 | tf_op jit(solution)/shard_map/ppermute | solution.py:388
  36.0 1.7 %collective-permute-done.10.refs_13_ = bf16[128,1024]{1,0:T(8,128)(2,1)S(1)} collective-permute-done((bf16[128,1024]{1,0:T(8,128)(2,1)S(1)}, bf16[128,1024]{1,0:T(8,128)(2,1)S(1)}, u32[]{:S(2)}, u32[]{:S(2)}) %collective-permute-start.10) | collective-permute-done | bytes 262176 | tf_op jit(solution)/shard_map/ppermute | solution.py:388
  37.7 3.5 %forward_near.1 = (f32[8,128]{1,0:T(8,128)S(1)}, f32[1,1024]{1,0:T(1,128)S(1)}, bf16[1024,1024]{1,0:T(8,128)(2,1)S(1)}, bf16[2,256,1024]{2,1,0:T(8,128)(2,1)S(1)}, bf16[2,256,1024]{2,1,0:T(8,128)(2,1)S(1)}) custom-call(s32[8]{0:T(128)S(1)} %copy-done.3, s32[1,1024]{1,0:T(1,128)S(1)} %bitcast.4, bf16[4,128]{1,0:T(4,128)(2,1)S(1)} %get-tuple-element.40.refs_2_, ...), custom_call_target="tpu_custom_call" | custom-call | flops 3000000000 | tf_op jit(solution)/shard_map/forward_near/pallas_call | solution.py:177
  41.2 4.9 %forward_far.1 = (f32[8,1024]{1,0:T(8,128)S(1)}, bf16[2,256,1024]{2,1,0:T(8,128)(2,1)S(1)}, bf16[128,1024]{1,0:T(8,128)(2,1)S(1)}, bf16[128,1024]{1,0:T(8,128)(2...) custom-call(s32[8]{0:T(128)S(1)} %copy-done.3, ...), custom_call_target="tpu_custom_call" | custom-call | flops 10000000 | tf_op jit(solution)/shard_map/forward_far/pallas_call | solution.py:240
  46.2 1.7 %collective-permute-start.15 = (bf16[136,1024]{1,0:T(8,128)(2,1)S(1)}, bf16[136,1024]{1,0:T(8,128)(2,1)S(1)}, u32[]{:S(2)}, u32[]{:S(2)}) collective-permute-start(bf16[136,1024]{1,0:T(8,128)(2,1)S(1)} %get-tuple-element.54), channel_id=1, source_target_pairs={{0,4},{4,0},{8,12},{12,8},{16,20},{20,16},{24,28},{28,24},{1,5},{5... | collective-permute-start | bytes 835592 | tf_op jit(solution)/shard_map/ppermute | solution.py:388
  47.9 2.3 %collective-permute-start.16 = (bf16[128,1024]{1,0:T(8,128)(2,1)S(1)}, bf16[128,1024]{1,0:T(8,128)(2,1)S(1)}, u32[]{:S(2)}, u32[]{:S(2)}) collective-permute-start(bf16[128,1024]{1,0:T(8,128)(2,1)S(1)} %get-tuple-element.58), channel_id=1, source_target_pairs={{0,8},{4,12},{8,0},{12,4},{16,24},{20,28},{24,16},{28,20},{1,9},{5... | collective-permute-start | bytes 786440 | tf_op jit(solution)/shard_map/ppermute | solution.py:388
  50.1 1.6 %backward.2 = (bf16[256,1024]{1,0:T(8,128)(2,1)S(1)}, bf16[256,1024]{1,0:T(8,128)(2,1)S(1)}) custom-call(f32[1,1024]{1,0:T(1,128)S(1)} %get-tuple-element.44.refs_2_.gain_ref, bf16[1024,1024]{1,0:T(8,128)(2,1)S(1)} %get-tuple-element.45.refs_3_.weight_ref, bf16[2,256,1024]{2,1,0:T(8,128)(2,1)S(1)} %get-tuple-element.56.slope_ref, ...), custom_call_target="tpu_custom_call" | custom-call | flops 10000000 | tf_op jit(solution)/shard_map/backward/pallas_call | solution.py:278
  51.7 1.6 %collective-permute-start.23 = (bf16[256,1024]{1,0:T(8,128)(2,1)S(1)}, bf16[256,1024]{1,0:T(8,128)(2,1)S(1)}, u32[]{:S(2)}, u32[]{:S(2)}) collective-permute-start(bf16[256,1024]{1,0:T(8,128)(2,1)S(1)} %get-tuple-element.65), channel_id=1, source_target_pairs={{0,2},{1,3},{2,0},{3,1},{4,6},{5,7},{6,4},{7,5},{8,10},{9,11},{10,... | collective-permute-start | bytes 1572872 | tf_op jit(solution)/shard_map/ppermute | solution.py:388
  54.6 2.3 %collective-permute-start.17 = (bf16[136,1024]{1,0:T(8,128)(2,1)S(1)}, bf16[136,1024]{1,0:T(8,128)(2,1)S(1)}, u32[]{:S(2)}, u32[]{:S(2)}) collective-permute-start(bf16[136,1024]{1,0:T(8,128)(2,1)S(1)} %get-tuple-element.59.refs_4_), channel_id=1, source_target_pairs={{0,8},{4,12},{8,0},{12,4},{16,24},{20,28},{24,16},{28,20},{1,9},{5... | collective-permute-start | bytes 835592 | tf_op jit(solution)/shard_map/ppermute | solution.py:388
  56.9 0.7 collective-permute-start.14
  57.6 5.7 %collective-permute-done.14.refs_1_ = bf16[128,1024]{1,0:T(8,128)(2,1)S(1)} collective-permute-done((bf16[128,1024]{1,0:T(8,128)(2,1)S(1)}, bf16[128,1024]{1,0:T(8,128)(2,1)S(1)}, u32[]{:S(2)}, u32[]{:S(2)}) %collective-permute-start.14) | collective-permute-done | bytes 262176 | tf_op jit(solution)/shard_map/ppermute | solution.py:388
  63.4 3.4 %collective-permute-start.18 = (bf16[136,1024]{1,0:T(8,128)(2,1)S(1)}, bf16[136,1024]{1,0:T(8,128)(2,1)S(1)}, u32[]{:S(2)}, u32[]{:S(2)}) collective-permute-start(bf16[136,1024]{1,0:T(8,128)(2,1)S(1)} %get-tuple-element.62.refs_2_), channel_id=1, source_target_pairs={{0,16},{4,20},{8,24},{12,28},{16,0},{20,4},{24,8},{28,12},{1,17},{... | collective-permute-start | bytes 835592 | tf_op jit(solution)/shard_map/ppermute | solution.py:388
  66.8 3.9 %collective-permute-start.27 = (bf16[128,1024]{1,0:T(8,128)(2,1)S(1)}, bf16[128,1024]{1,0:T(8,128)(2,1)S(1)}, u32[]{:S(2)}, u32[]{:S(2)}) collective-permute-start(bf16[128,1024]{1,0:T(8,128)(2,1)S(1)} %get-tuple-element.70), channel_id=1, source_target_pairs={{0,8},{4,12},{8,0},{12,4},{16,24},{20,28},{24,16},{28,20},{1,9},{5... | collective-permute-start | bytes 786440 | tf_op jit(solution)/shard_map/ppermute | solution.py:388
  70.8 1.6 %backward.3 = (bf16[256,1024]{1,0:T(8,128)(2,1)S(1)}, bf16[256,1024]{1,0:T(8,128)(2,1)S(1)}) custom-call(f32[1,1024]{1,0:T(1,128)S(1)} %get-tuple-element.44.refs_2_.gain_ref, bf16[1024,1024]{1,0:T(8,128)(2,1)S(1)} %get-tuple-element.45.refs_3_.weight_ref, bf16[2,256,1024]{2,1,0:T(8,128)(2,1)S(1)} %get-tuple-element.49.refs_7_.slope_ref, ...), custom_call_target="tpu_custom_call" | custom-call | flops 10000000 | tf_op jit(solution)/shard_map/backward/pallas_call | solution.py:278
  72.6 1.7 %collective-permute-done.24.refs_0_ = bf16[256,1024]{1,0:T(8,128)(2,1)S(1)} collective-permute-done((bf16[256,1024]{1,0:T(8,128)(2,1)S(1)}, bf16[256,1024]{1,0:T(8,128)(2,1)S(1)}, u32[]{:S(2)}, u32[]{:S(2)}) %collective-permute-start.24) | collective-permute-done | bytes 524320 | tf_op jit(solution)/shard_map/ppermute | solution.py:388
  74.4 1.7 %collective-permute-start.21 = (f32[8,128]{1,0:T(8,128)S(1)}, f32[8,128]{1,0:T(8,128)S(1)}, u32[]{:S(2)}, u32[]{:S(2)}) collective-permute-start(f32[8,128]{1,0:T(8,128)S(1)} %ride_end.1.refs_0_), channel_id=1, source_target_pairs={{0,3},{1,2},{2,1},{3,0},{4,7},{5,6},{6,5},{7,4},{8,11},{9,10},{10,... | collective-permute-start | bytes 12296 | tf_op jit(solution)/shard_map/ppermute | solution.py:388
  76.7 2.2 %collective-permute-done.26.refs_1_ = bf16[128,1024]{1,0:T(8,128)(2,1)S(1)} collective-permute-done((bf16[128,1024]{1,0:T(8,128)(2,1)S(1)}, bf16[128,1024]{1,0:T(8,128)(2,1)S(1)}, u32[]{:S(2)}, u32[]{:S(2)}) %collective-permute-start.26) | collective-permute-done | bytes 262176 | tf_op jit(solution)/shard_map/ppermute | solution.py:388
  78.9 0.9 %fold.7 = f32[128,1024]{1,0:T(8,128)} custom-call(bf16[128,1024]{1,0:T(8,128)(2,1)S(1)} %get-tuple-element.68.refs_0_, bf16[128,1024]{1,0:T(8,128)(2,1)S(1)} %collective-permute-done.26.refs_1_, bf16[128,1024]{1,0:T(8,128)(2,1)S(1)} %collective-permute-done.27.refs_2_, bf16[136,1024]{1,0:T(8,128)(2,1)S(1)} %collective-permute-done.18.piece_ref.refs_3_), custom_call_target="tpu_custom_call" | custom-call | flops 3000000000 | tf_op jit(solution)/shard_map/fold/pallas_call | solution.py:314
  79.8 2.5 %pack.1 = (bf16[256,4,1024]{2,1,0:T(4,128)(2,1)}, f32[8,128]{1,0:T(8,128)S(1)}) custom-call(bf16[256,1024]{1,0:T(8,128)(2,1)S(1)} %get-tuple-element.63.refs_0_, bf16[256,1024]{1,0:T(8,128)(2,1)S(1)} %collective-permute-done.22.refs_1_, bf16[256,1024]{1,0:T(8,128)(2,1)S(1)} %collective-permute-done.23.refs_1_.refs_2_, ...), custom_call_target="tpu_custom_call" | custom-call | flops 10000000 | tf_op jit(solution)/shard_map/pack/pallas_call | solution.py:91
  (54 shorter events, 5.7 us)
Async XLA Ops:
  0.6 13.9 %copy-start.4 = (bf16[1,128]{1,0:T(2,128)(2,1)S(1)}, bf16[1,128]{1,0:T(2,128)(2,1)}, u32[]{:S(2)}) copy-start(bf16[1,128]{1,0:T(2,128)(2,1)} %refs_0_.3) | copy-start | bytes 772
  0.6 13.9 %collective-permute-start.2 = (bf16[128,1024]{1,0:T(8,128)(2,1)}, bf16[128,1024]{1,0:T(8,128)(2,1)S(1)}, u32[]{:S(2)}, u32[]{:S(2)}) collective-permute-start(bf16[128,1024]{1,0:T(8,128)(2,1)} %bitcast.6), channel_id=1, source_target_pairs={{0,8},{4,12},{8,0},{12,4},{16,24},{20,28},{24,16},{28,20},{1,9},{5... | collective-permute-start | bytes 786440 | tf_op jit(solution)/shard_map/ppermute | solution.py:388
  3.7 10.8 %collective-permute-start.1 = (bf16[128,1024]{1,0:T(8,128)(2,1)}, bf16[128,1024]{1,0:T(8,128)(2,1)S(1)}, u32[]{:S(2)}, u32[]{:S(2)}) collective-permute-start(bf16[128,1024]{1,0:T(8,128)(2,1)} %bitcast.7), channel_id=1, source_target_pairs={{0,4},{4,0},{8,12},{12,8},{16,20},{20,16},{24,28},{28,24},{1,5},{5... | collective-permute-start | bytes 786440 | tf_op jit(solution)/shard_map/ppermute | solution.py:388
  5.2 14.4 %collective-permute-start.4 = (bf16[128,1024]{1,0:T(8,128)(2,1)}, bf16[128,1024]{1,0:T(8,128)(2,1)S(1)}, u32[]{:S(2)}, u32[]{:S(2)}) collective-permute-start(bf16[128,1024]{1,0:T(8,128)(2,1)} %bitcast.8), channel_id=1, source_target_pairs={{0,16},{4,20},{8,24},{12,28},{16,0},{20,4},{24,8},{28,12},{1,17},{... | collective-permute-start | bytes 786440 | tf_op jit(solution)/shard_map/ppermute | solution.py:388
  7.8 5.7 %collective-permute-start = (bf16[1,128]{1,0:T(2,128)(2,1)}, bf16[1,128]{1,0:T(2,128)(2,1)S(1)}, u32[]{:S(2)}, u32[]{:S(2)}) collective-permute-start(bf16[1,128]{1,0:T(2,128)(2,1)} %refs_0_.3), channel_id=1, source_target_pairs={{0,4},{4,0},{8,12},{12,8},{16,20},{20,16},{24,28},{28,24},{1,5},{5... | collective-permute-start | bytes 776 | tf_op jit(solution)/shard_map/ppermute | solution.py:388
  11.9 21.5 %collective-permute-start.11 = (bf16[256,1024]{1,0:T(8,128)(2,1)}, bf16[256,1024]{1,0:T(8,128)(2,1)S(1)}, u32[]{:S(2)}, u32[]{:S(2)}) collective-permute-start(bf16[256,1024]{1,0:T(8,128)(2,1)} %get-tuple-element.46), channel_id=1, source_target_pairs={{0,2},{1,3},{2,0},{3,1},{4,6},{5,7},{6,4},{7,5},{8,10},{9,11},{10,... | collective-permute-start | bytes 1572872 | tf_op jit(solution)/shard_map/ppermute | solution.py:388
  13.5 22.5 %collective-permute-start.12 = (bf16[256,1024]{1,0:T(8,128)(2,1)}, bf16[256,1024]{1,0:T(8,128)(2,1)S(1)}, u32[]{:S(2)}, u32[]{:S(2)}) collective-permute-start(bf16[256,1024]{1,0:T(8,128)(2,1)} %get-tuple-element.47), channel_id=1, source_target_pairs={{0,2},{1,3},{2,0},{3,1},{4,6},{5,7},{6,4},{7,5},{8,10},{9,11},{10,... | collective-permute-start | bytes 1572872 | tf_op jit(solution)/shard_map/ppermute | solution.py:388
  14.5 12.0 %collective-permute-start.7 = (bf16[128,1024]{1,0:T(8,128)(2,1)S(1)}, bf16[128,1024]{1,0:T(8,128)(2,1)S(1)}, u32[]{:S(2)}, u32[]{:S(2)}) collective-permute-start(bf16[128,1024]{1,0:T(8,128)(2,1)S(1)} %get-tuple-element.43.refs_7_), channel_id=1, source_target_pairs={{0,8},{4,12},{8,0},{12,4},{16,24},{20,28},{24,16},{28,20},{1,9},{5... | collective-permute-start | bytes 786440 | tf_op jit(solution)/shard_map/ppermute | solution.py:388
  14.6 10.2 %collective-permute-start.3 = (bf16[2,128]{1,0:T(2,128)(2,1)S(1)}, bf16[2,128]{1,0:T(2,128)(2,1)S(1)}, u32[]{:S(2)}, u32[]{:S(2)}) collective-permute-start(bf16[2,128]{1,0:T(2,128)(2,1)S(1)} %get-tuple-element.37.refs_0_), channel_id=1, source_target_pairs={{0,8},{4,12},{8,0},{12,4},{16,24},{20,28},{24,16},{28,20},{1,9},{5... | collective-permute-start | bytes 1544 | tf_op jit(solution)/shard_map/ppermute | solution.py:388
  20.3 8.7 %collective-permute-start.9 = (bf16[128,1024]{1,0:T(8,128)(2,1)S(1)}, bf16[128,1024]{1,0:T(8,128)(2,1)S(1)}, u32[]{:S(2)}, u32[]{:S(2)}) collective-permute-start(bf16[128,1024]{1,0:T(8,128)(2,1)S(1)} %hold.7.refs_3_.refs_10_), channel_id=1, source_target_pairs={{0,8},{4,12},{8,0},{12,4},{16,24},{20,28},{24,16},{28,20},{1,9},{5... | collective-permute-start | bytes 786440 | tf_op jit(solution)/shard_map/ppermute | solution.py:388
  24.8 6.4 %collective-permute-start.8 = (bf16[128,1024]{1,0:T(8,128)(2,1)S(1)}, bf16[128,1024]{1,0:T(8,128)(2,1)S(1)}, u32[]{:S(2)}, u32[]{:S(2)}) collective-permute-start(bf16[128,1024]{1,0:T(8,128)(2,1)S(1)} %hold.7.refs_3_.refs_10_), channel_id=1, source_target_pairs={{0,4},{4,0},{8,12},{12,8},{16,20},{20,16},{24,28},{28,24},{1,5},{5... | collective-permute-start | bytes 786440 | tf_op jit(solution)/shard_map/ppermute | solution.py:388
  26.5 11.2 %collective-permute-start.6 = (bf16[256,1024]{1,0:T(8,128)(2,1)}, bf16[256,1024]{1,0:T(8,128)(2,1)S(1)}, u32[]{:S(2)}, u32[]{:S(2)}) collective-permute-start(bf16[256,1024]{1,0:T(8,128)(2,1)} %get-tuple-element.42), channel_id=1, source_target_pairs={{0,1},{1,0},{2,3},{3,2},{4,5},{5,4},{6,7},{7,6},{8,9},{9,8},{10,11... | collective-permute-start | bytes 1572872 | tf_op jit(solution)/shard_map/ppermute | solution.py:388
  29.0 4.5 %collective-permute-start.5 = (bf16[4,128]{1,0:T(4,128)(2,1)S(1)}, bf16[4,128]{1,0:T(4,128)(2,1)S(1)}, u32[]{:S(2)}, u32[]{:S(2)}) collective-permute-start(bf16[4,128]{1,0:T(4,128)(2,1)S(1)} %get-tuple-element.40.refs_2_), channel_id=1, source_target_pairs={{0,16},{4,20},{8,24},{12,28},{16,0},{20,4},{24,8},{28,12},{1,17},{... | collective-permute-start | bytes 3080 | tf_op jit(solution)/shard_map/ppermute | solution.py:388
  31.2 6.5 %copy-start.1 = (s32[1024,1]{0,1:T(1,128)S(1)}, s32[1024,1]{0,1:T(1,128)}, u32[]{:S(2)}) copy-start(s32[1024,1]{0,1:T(1,128)} %param.8) | copy-start | bytes 12292
  31.2 6.5 %copy-start.3 = (s32[8]{0:T(128)S(1)}, s32[8]{0:T(128)}, u32[]{:S(2)}) copy-start(s32[8]{0:T(128)} %refs_0_.5) | copy-start | bytes 100
  31.2 6.6 %copy-start.5 = (bf16[1,128,1024]{2,1,0:T(8,128)(2,1)S(1)}, bf16[1,128,1024]{2,1,0:T(8,128)(2,1)}, u32[]{:S(2)}) copy-start(bf16[1,128,1024]{2,1,0:T(8,128)(2,1)} %param.6) | copy-start | bytes 786436
  31.2 6.5 %collective-permute-start.10 = (bf16[128,1024]{1,0:T(8,128)(2,1)S(1)}, bf16[128,1024]{1,0:T(8,128)(2,1)S(1)}, u32[]{:S(2)}, u32[]{:S(2)}) collective-permute-start(bf16[128,1024]{1,0:T(8,128)(2,1)S(1)} %hold.9.refs_12_), channel_id=1, source_target_pairs={{0,4},{4,0},{8,12},{12,8},{16,20},{20,16},{24,28},{28,24},{1,5},{5... | collective-permute-start | bytes 786440 | tf_op jit(solution)/shard_map/ppermute | solution.py:388
  36.0 5.2 %collective-permute-start.13 = (bf16[256,1024]{1,0:T(8,128)(2,1)S(1)}, bf16[256,1024]{1,0:T(8,128)(2,1)S(1)}, u32[]{:S(2)}, u32[]{:S(2)}) collective-permute-start(bf16[256,1024]{1,0:T(8,128)(2,1)S(1)} %hold.10), channel_id=1, source_target_pairs={{0,1},{1,0},{2,3},{3,2},{4,5},{5,4},{6,7},{7,6},{8,9},{9,8},{10,11... | collective-permute-start | bytes 1572872 | tf_op jit(solution)/shard_map/ppermute | solution.py:388
  46.2 8.3 %collective-permute-start.15 = (bf16[136,1024]{1,0:T(8,128)(2,1)S(1)}, bf16[136,1024]{1,0:T(8,128)(2,1)S(1)}, u32[]{:S(2)}, u32[]{:S(2)}) collective-permute-start(bf16[136,1024]{1,0:T(8,128)(2,1)S(1)} %get-tuple-element.54), channel_id=1, source_target_pairs={{0,4},{4,0},{8,12},{12,8},{16,20},{20,16},{24,28},{28,24},{1,5},{5... | collective-permute-start | bytes 835592 | tf_op jit(solution)/shard_map/ppermute | solution.py:388
  47.9 6.6 %collective-permute-start.16 = (bf16[128,1024]{1,0:T(8,128)(2,1)S(1)}, bf16[128,1024]{1,0:T(8,128)(2,1)S(1)}, u32[]{:S(2)}, u32[]{:S(2)}) collective-permute-start(bf16[128,1024]{1,0:T(8,128)(2,1)S(1)} %get-tuple-element.58), channel_id=1, source_target_pairs={{0,8},{4,12},{8,0},{12,4},{16,24},{20,28},{24,16},{28,20},{1,9},{5... | collective-permute-start | bytes 786440 | tf_op jit(solution)/shard_map/ppermute | solution.py:388
  51.7 20.8 %collective-permute-start.23 = (bf16[256,1024]{1,0:T(8,128)(2,1)S(1)}, bf16[256,1024]{1,0:T(8,128)(2,1)S(1)}, u32[]{:S(2)}, u32[]{:S(2)}) collective-permute-start(bf16[256,1024]{1,0:T(8,128)(2,1)S(1)} %get-tuple-element.65), channel_id=1, source_target_pairs={{0,2},{1,3},{2,0},{3,1},{4,6},{5,7},{6,4},{7,5},{8,10},{9,11},{10,... | collective-permute-start | bytes 1572872 | tf_op jit(solution)/shard_map/ppermute | solution.py:388
  53.3 21.1 %collective-permute-start.24 = (bf16[256,1024]{1,0:T(8,128)(2,1)S(1)}, bf16[256,1024]{1,0:T(8,128)(2,1)S(1)}, u32[]{:S(2)}, u32[]{:S(2)}) collective-permute-start(bf16[256,1024]{1,0:T(8,128)(2,1)S(1)} %get-tuple-element.57.refs_3_), channel_id=1, source_target_pairs={{0,2},{1,3},{2,0},{3,1},{4,6},{5,7},{6,4},{7,5},{8,10},{9,11},{10,... | collective-permute-start | bytes 1572872 | tf_op jit(solution)/shard_map/ppermute | solution.py:388
  54.6 8.7 %collective-permute-start.17 = (bf16[136,1024]{1,0:T(8,128)(2,1)S(1)}, bf16[136,1024]{1,0:T(8,128)(2,1)S(1)}, u32[]{:S(2)}, u32[]{:S(2)}) collective-permute-start(bf16[136,1024]{1,0:T(8,128)(2,1)S(1)} %get-tuple-element.59.refs_4_), channel_id=1, source_target_pairs={{0,8},{4,12},{8,0},{12,4},{16,24},{20,28},{24,16},{28,20},{1,9},{5... | collective-permute-start | bytes 835592 | tf_op jit(solution)/shard_map/ppermute | solution.py:388
  56.9 6.4 %collective-permute-start.14 = (bf16[128,1024]{1,0:T(8,128)(2,1)S(1)}, bf16[128,1024]{1,0:T(8,128)(2,1)S(1)}, u32[]{:S(2)}, u32[]{:S(2)}) collective-permute-start(bf16[128,1024]{1,0:T(8,128)(2,1)S(1)} %get-tuple-element.52), channel_id=1, source_target_pairs={{0,4},{4,0},{8,12},{12,8},{16,20},{20,16},{24,28},{28,24},{1,5},{5... | collective-permute-start | bytes 786440 | tf_op jit(solution)/shard_map/ppermute | solution.py:388
  63.4 10.9 %collective-permute-start.18 = (bf16[136,1024]{1,0:T(8,128)(2,1)S(1)}, bf16[136,1024]{1,0:T(8,128)(2,1)S(1)}, u32[]{:S(2)}, u32[]{:S(2)}) collective-permute-start(bf16[136,1024]{1,0:T(8,128)(2,1)S(1)} %get-tuple-element.62.refs_2_), channel_id=1, source_target_pairs={{0,16},{4,20},{8,24},{12,28},{16,0},{20,4},{24,8},{28,12},{1,17},{... | collective-permute-start | bytes 835592 | tf_op jit(solution)/shard_map/ppermute | solution.py:388
  66.8 9.2 %collective-permute-start.27 = (bf16[128,1024]{1,0:T(8,128)(2,1)S(1)}, bf16[128,1024]{1,0:T(8,128)(2,1)S(1)}, u32[]{:S(2)}, u32[]{:S(2)}) collective-permute-start(bf16[128,1024]{1,0:T(8,128)(2,1)S(1)} %get-tuple-element.70), channel_id=1, source_target_pairs={{0,8},{4,12},{8,0},{12,4},{16,24},{20,28},{24,16},{28,20},{1,9},{5... | collective-permute-start | bytes 786440 | tf_op jit(solution)/shard_map/ppermute | solution.py:388
  72.4 6.4 %collective-permute-start.26 = (bf16[128,1024]{1,0:T(8,128)(2,1)S(1)}, bf16[128,1024]{1,0:T(8,128)(2,1)S(1)}, u32[]{:S(2)}, u32[]{:S(2)}) collective-permute-start(bf16[128,1024]{1,0:T(8,128)(2,1)S(1)} %fold.6), channel_id=1, source_target_pairs={{0,4},{4,0},{8,12},{12,8},{16,20},{20,16},{24,28},{28,24},{1,5},{5... | collective-permute-start | bytes 786440 | tf_op jit(solution)/shard_map/ppermute | solution.py:388
  72.5 7.3 %collective-permute-start.22 = (bf16[256,1024]{1,0:T(8,128)(2,1)S(1)}, bf16[256,1024]{1,0:T(8,128)(2,1)S(1)}, u32[]{:S(2)}, u32[]{:S(2)}) collective-permute-start(bf16[256,1024]{1,0:T(8,128)(2,1)S(1)} %get-tuple-element.64.refs_2_), channel_id=1, source_target_pairs={{0,1},{1,0},{2,3},{3,2},{4,5},{5,4},{6,7},{7,6},{8,9},{9,8},{10,11... | collective-permute-start | bytes 1572872 | tf_op jit(solution)/shard_map/ppermute | solution.py:388
  74.4 5.5 %collective-permute-start.25 = (bf16[256,1024]{1,0:T(8,128)(2,1)S(1)}, bf16[256,1024]{1,0:T(8,128)(2,1)S(1)}, u32[]{:S(2)}, u32[]{:S(2)}) collective-permute-start(bf16[256,1024]{1,0:T(8,128)(2,1)S(1)} %hold.11), channel_id=1, source_target_pairs={{0,1},{1,0},{2,3},{3,2},{4,5},{5,4},{6,7},{7,6},{8,9},{9,8},{10,11... | collective-permute-start | bytes 1572872 | tf_op jit(solution)/shard_map/ppermute | solution.py:388
  74.4 8.0 %collective-permute-start.21 = (f32[8,128]{1,0:T(8,128)S(1)}, f32[8,128]{1,0:T(8,128)S(1)}, u32[]{:S(2)}, u32[]{:S(2)}) collective-permute-start(f32[8,128]{1,0:T(8,128)S(1)} %ride_end.1.refs_0_), channel_id=1, source_target_pairs={{0,3},{1,2},{2,1},{3,0},{4,7},{5,6},{6,5},{7,4},{8,11},{9,10},{10,... | collective-permute-start | bytes 12296 | tf_op jit(solution)/shard_map/ppermute | solution.py:388
  76.1 6.3 %collective-permute-start.20 = (f32[8,128]{1,0:T(8,128)S(1)}, f32[8,128]{1,0:T(8,128)S(1)}, u32[]{:S(2)}, u32[]{:S(2)}) collective-permute-start(f32[8,128]{1,0:T(8,128)S(1)} %ride_end.1.refs_0_), channel_id=1, source_target_pairs={{0,2},{1,3},{2,0},{3,1},{4,6},{5,7},{6,4},{7,5},{8,10},{9,11},{10,... | collective-permute-start | bytes 12296 | tf_op jit(solution)/shard_map/ppermute | solution.py:388
  78.9 3.5 %collective-permute-start.19 = (f32[8,128]{1,0:T(8,128)S(1)}, f32[8,128]{1,0:T(8,128)S(1)}, u32[]{:S(2)}, u32[]{:S(2)}) collective-permute-start(f32[8,128]{1,0:T(8,128)S(1)} %ride_end.1.refs_0_), channel_id=1, source_target_pairs={{0,1},{1,0},{2,3},{3,2},{4,5},{5,4},{6,7},{7,6},{8,9},{9,8},{10,11... | collective-permute-start | bytes 12296 | tf_op jit(solution)/shard_map/ppermute | solution.py:388
  (2 other events, 7.2 us)

commit v8 on v7

--- a/solution.py
+++ b/solution.py
@@ -414,7 +414,8 @@
         pieces[4] = hold([], pieces[4], [unpacked])[1]
         pieces[5] = swap(pieces[4], "dp", 1)
         gains = [gain, swap(gain, "dp", 2)]
-        gain, side = hold(gains, side, [pieces[4]])
+        gain, own = hold(gains, own, [pieces[4]])
+        side = hold([], side, [pieces[3]])[1]
         gains = [gain, swap(gain, "dp", 4)]
         pieces[6] = hold([], swap(pieces[4], "dp", 2), [pieces[3], pieces[5]])[1]
         pieces[7] = swap(pieces[6], "dp", 1)

time: 83.1 us -> 84.2 us (1.013)
  waiting for transfers between devices: 26 us -> 35.8 us
  starting transfers between devices: 35.9 us -> 26.2 us
  local copies, waits for them, and re-layouts: 0.7 us -> 1.73 us
    ppermute x28, waiting for transfers between devices: 26 us -> 35.8 us  [swap(): return lax.ppermute(value, axis, [(i, i ^ offset) for i in range(size)])]
    ppermute x28, starting transfers between devices: 35.9 us -> 26.2 us  [swap(): return lax.ppermute(value, axis, [(i, i ^ offset) for i in range(size)])]
    unnamed x12 -> x14, local copies, waits for them, and re-layouts: 0.7 us -> 1.73 us
  transfers between devices with their start and end apart: 28 -> 28, of which waited for: 12 -> 11; matrix products, arithmetic and copies ran while one was open for 0% -> 0% of each run, Pallas kernels for 17% -> 17%
where the time goes in v8:
time: 84.2 us; the launch traced here: 84 us
  waiting for transfers between devices  35.8 us (43%)
  starting transfers between devices  26.2 us (31%)
  Pallas kernels  19.5 us (23%)
  local copies, waits for them, and re-layouts  1.73 us (2%)
    ppermute x28, waiting for transfers between devices, swap(): return lax.ppermute(value, axis, [(i, i ^ offset) for i in range(size)])  35.8 us
    ppermute x28, starting transfers between devices, swap(): return lax.ppermute(value, axis, [(i, i ^ offset) for i in range(size)])  26.2 us
    pallas_call x1, Pallas kernels, forward_far(): pl.pallas_call(body, in_specs=[SMEM] + [VMEM] * (6 + n), out_specs=[VMEM]...  4.91 us
    pallas_call x1, Pallas kernels, unpack(): pl.pallas_call(body, in_specs=[ANY], out_specs=[VMEM] * (positions + 1),...  3.58 us
    pallas_call x1, Pallas kernels, forward_near(): pl.pallas_call(body, in_specs=[SMEM] + [VMEM] * (1 + n_gain + n) + [ANY]...  3.47 us
    pallas_call x2, Pallas kernels, backward(): pl.pallas_call(body, in_specs=[VMEM] * (3 + n) + [ANY] * (len(after) + le...  3.18 us
    pallas_call x1, Pallas kernels, pack(): pl.pallas_call(body, grid=(frames // chunk,), in_specs=[pl.BlockSpec((chu...  2.53 us
    unnamed x14, local copies, waits for them, and re-layouts  1.73 us
  transfers between devices with their start and end apart: 28, of which 11 were waited for; matrix products, arithmetic and copies ran while one was open for 0% of the time, Pallas kernels for 17%

profile of v8, /device:TPU:0, one launch (start us, length us, event | category | flops | bytes accessed | tf_op | source)
XLA Modules:
  0.0 84.0 jit_solution(16130900676151533766)
XLA Ops:
  0.6 3.1 %collective-permute-start.2 = (bf16[128,1024]{1,0:T(8,128)(2,1)}, bf16[128,1024]{1,0:T(8,128)(2,1)S(1)}, u32[]{:S(2)}, u32[]{:S(2)}) collective-permute-start(bf16[128,1024]{1,0:T(8,128)(2,1)} %bitcast.6), channel_id=1, source_target_pairs={{0,8},{4,12},{8,0},{12,4},{16,24},{20,28},{24,16},{28,20},{1,9},{5... | collective-permute-start | bytes 786440 | tf_op jit(solution)/shard_map/ppermute | solution.py:388
  3.7 1.5 %collective-permute-start.1 = (bf16[128,1024]{1,0:T(8,128)(2,1)}, bf16[128,1024]{1,0:T(8,128)(2,1)S(1)}, u32[]{:S(2)}, u32[]{:S(2)}) collective-permute-start(bf16[128,1024]{1,0:T(8,128)(2,1)} %bitcast.7), channel_id=1, source_target_pairs={{0,4},{4,0},{8,12},{12,8},{16,20},{20,16},{24,28},{28,24},{1,5},{5... | collective-permute-start | bytes 786440 | tf_op jit(solution)/shard_map/ppermute | solution.py:388
  5.2 2.6 %collective-permute-start.4 = (bf16[128,1024]{1,0:T(8,128)(2,1)}, bf16[128,1024]{1,0:T(8,128)(2,1)S(1)}, u32[]{:S(2)}, u32[]{:S(2)}) collective-permute-start(bf16[128,1024]{1,0:T(8,128)(2,1)} %bitcast.8), channel_id=1, source_target_pairs={{0,16},{4,20},{8,24},{12,28},{16,0},{20,4},{24,8},{28,12},{1,17},{... | collective-permute-start | bytes 786440 | tf_op jit(solution)/shard_map/ppermute | solution.py:388
  8.3 3.6 %unpack.1 = (bf16[256,1024]{1,0:T(8,128)(2,1)}, bf16[256,1024]{1,0:T(8,128)(2,1)}, bf16[256,1024]{1,0:T(8,128)(2,1)}, bf16[256,1024]{1,0:T(8,128)(2,1)}, f32[8,128]{1,0:T(8,128)}) custom-call(bf16[256,4,1024]{2,1,0:T(4,128)(2,1)} %hidden_ref.1), custom_call_target="tpu_custom_call" | custom-call | flops 10000000 | tf_op jit(solution)/shard_map/unpack/pallas_call | solution.py:60
  11.9 1.6 %collective-permute-start.11 = (bf16[256,1024]{1,0:T(8,128)(2,1)}, bf16[256,1024]{1,0:T(8,128)(2,1)S(1)}, u32[]{:S(2)}, u32[]{:S(2)}) collective-permute-start(bf16[256,1024]{1,0:T(8,128)(2,1)} %get-tuple-element.46), channel_id=1, source_target_pairs={{0,2},{1,3},{2,0},{3,1},{4,6},{5,7},{6,4},{7,5},{8,10},{9,11},{10,... | collective-permute-start | bytes 1572872 | tf_op jit(solution)/shard_map/ppermute | solution.py:388
  14.6 5.0 %collective-permute-done.4.refs_0_ = bf16[128,1024]{1,0:T(8,128)(2,1)S(1)} collective-permute-done((bf16[128,1024]{1,0:T(8,128)(2,1)}, bf16[128,1024]{1,0:T(8,128)(2,1)S(1)}, u32[]{:S(2)}, u32[]{:S(2)}) %collective-permute-start.4) | collective-permute-done | bytes 262176 | tf_op jit(solution)/shard_map/ppermute | solution.py:388
  20.9 3.9 %collective-permute-done.6.refs_1_.refs_9_ = bf16[128,1024]{1,0:T(8,128)(2,1)S(1)} collective-permute-done((bf16[128,1024]{1,0:T(8,128)(2,1)S(1)}, bf16[128,1024]{1,0:T(8,128)(2,1)S(1)}, u32[]{:S(2)}, u32[]{:S(2)}) %collective-permute-start.6) | collective-permute-done | bytes 262176 | tf_op jit(solution)/shard_map/ppermute | solution.py:388
  24.7 1.0 %copy-done.1 = bf16[256,1024]{1,0:T(8,128)(2,1)S(1)} copy-done((bf16[256,1024]{1,0:T(8,128)(2,1)S(1)}, bf16[256,1024]{1,0:T(8,128)(2,1)}, u32[]{:S(2)}) %copy-start.1) | copy-done | bytes 524312
  25.8 3.2 %collective-permute-done.3.refs_1_ = bf16[2,128]{1,0:T(2,128)(2,1)S(1)} collective-permute-done((bf16[2,128]{1,0:T(2,128)(2,1)S(1)}, bf16[2,128]{1,0:T(2,128)(2,1)S(1)}, u32[]{:S(2)}, u32[]{:S(2)}) %collective-permute-start.3) | collective-permute-done | bytes 544 | tf_op jit(solution)/shard_map/ppermute | solution.py:388
  29.1 1.6 %collective-permute-start.5 = (bf16[4,128]{1,0:T(4,128)(2,1)S(1)}, bf16[4,128]{1,0:T(4,128)(2,1)S(1)}, u32[]{:S(2)}, u32[]{:S(2)}) collective-permute-start(bf16[4,128]{1,0:T(4,128)(2,1)S(1)} %get-tuple-element.40.refs_2_), channel_id=1, source_target_pairs={{0,16},{4,20},{8,24},{12,28},{16,0},{20,4},{24,8},{28,12},{1,17},{... | collective-permute-start | bytes 3080 | tf_op jit(solution)/shard_map/ppermute | solution.py:388
  30.7 1.4 %collective-permute-start.10 = (bf16[128,1024]{1,0:T(8,128)(2,1)S(1)}, bf16[128,1024]{1,0:T(8,128)(2,1)S(1)}, u32[]{:S(2)}, u32[]{:S(2)}) collective-permute-start(bf16[128,1024]{1,0:T(8,128)(2,1)S(1)} %hold.11.refs_12_), channel_id=1, source_target_pairs={{0,4},{4,0},{8,12},{12,8},{16,20},{20,16},{24,28},{28,24},{1,5},{5... | collective-permute-start | bytes 786440 | tf_op jit(solution)/shard_map/ppermute | solution.py:388
  32.0 1.6 %collective-permute-done.5.refs_3_.refs_2_ = bf16[4,128]{1,0:T(4,128)(2,1)S(1)} collective-permute-done((bf16[4,128]{1,0:T(4,128)(2,1)S(1)}, bf16[4,128]{1,0:T(4,128)(2,1)S(1)}, u32[]{:S(2)}, u32[]{:S(2)}) %collective-permute-start.5) | collective-permute-done | bytes 1056 | tf_op jit(solution)/shard_map/ppermute | solution.py:388
  33.6 2.4 %collective-permute-done.12.refs_0_ = bf16[256,1024]{1,0:T(8,128)(2,1)S(1)} collective-permute-done((bf16[256,1024]{1,0:T(8,128)(2,1)}, bf16[256,1024]{1,0:T(8,128)(2,1)S(1)}, u32[]{:S(2)}, u32[]{:S(2)}) %collective-permute-start.12) | collective-permute-done | bytes 524320 | tf_op jit(solution)/shard_map/ppermute | solution.py:388
  36.0 3.2 %collective-permute-done.10.refs_13_ = bf16[128,1024]{1,0:T(8,128)(2,1)S(1)} collective-permute-done((bf16[128,1024]{1,0:T(8,128)(2,1)S(1)}, bf16[128,1024]{1,0:T(8,128)(2,1)S(1)}, u32[]{:S(2)}, u32[]{:S(2)}) %collective-permute-start.10) | collective-permute-done | bytes 262176 | tf_op jit(solution)/shard_map/ppermute | solution.py:388
  39.2 3.5 %forward_near.1 = (f32[8,128]{1,0:T(8,128)S(1)}, f32[1,1024]{1,0:T(1,128)S(1)}, bf16[1024,1024]{1,0:T(8,128)(2,1)S(1)}, bf16[2,256,1024]{2,1,0:T(8,128)(2,1)S(1)}, bf16[2,256,1024]{2,1,0:T(8,128)(2,1)S(1)}) custom-call(s32[8]{0:T(128)S(1)} %copy-done.4, s32[1,1024]{1,0:T(1,128)S(1)} %bitcast.4, bf16[4,128]{1,0:T(4,128)(2,1)S(1)} %get-tuple-element.40.refs_2_, ...), custom_call_target="tpu_custom_call" | custom-call | flops 3000000000 | tf_op jit(solution)/shard_map/forward_near/pallas_call | solution.py:177
  42.7 4.9 %forward_far.1 = (f32[8,1024]{1,0:T(8,128)S(1)}, bf16[2,256,1024]{2,1,0:T(8,128)(2,1)S(1)}, bf16[128,1024]{1,0:T(8,128)(2,1)S(1)}, bf16[128,1024]{1,0:T(8,128)(2...) custom-call(s32[8]{0:T(128)S(1)} %copy-done.4, ...), custom_call_target="tpu_custom_call" | custom-call | flops 10000000 | tf_op jit(solution)/shard_map/forward_far/pallas_call | solution.py:240
  47.6 1.4 %collective-permute-start.15 = (bf16[136,1024]{1,0:T(8,128)(2,1)S(1)}, bf16[136,1024]{1,0:T(8,128)(2,1)S(1)}, u32[]{:S(2)}, u32[]{:S(2)}) collective-permute-start(bf16[136,1024]{1,0:T(8,128)(2,1)S(1)} %get-tuple-element.54), channel_id=1, source_target_pairs={{0,4},{4,0},{8,12},{12,8},{16,20},{20,16},{24,28},{28,24},{1,5},{5... | collective-permute-start | bytes 835592 | tf_op jit(solution)/shard_map/ppermute | solution.py:388
  49.0 2.5 %collective-permute-start.16 = (bf16[128,1024]{1,0:T(8,128)(2,1)S(1)}, bf16[128,1024]{1,0:T(8,128)(2,1)S(1)}, u32[]{:S(2)}, u32[]{:S(2)}) collective-permute-start(bf16[128,1024]{1,0:T(8,128)(2,1)S(1)} %get-tuple-element.58), channel_id=1, source_target_pairs={{0,8},{4,12},{8,0},{12,4},{16,24},{20,28},{24,16},{28,20},{1,9},{5... | collective-permute-start | bytes 786440 | tf_op jit(solution)/shard_map/ppermute | solution.py:388
  51.5 1.6 %backward.2 = (bf16[256,1024]{1,0:T(8,128)(2,1)S(1)}, bf16[256,1024]{1,0:T(8,128)(2,1)S(1)}) custom-call(f32[1,1024]{1,0:T(1,128)S(1)} %get-tuple-element.44.refs_2_.gain_ref, bf16[1024,1024]{1,0:T(8,128)(2,1)S(1)} %get-tuple-element.45.refs_3_.weight_ref, bf16[2,256,1024]{2,1,0:T(8,128)(2,1)S(1)} %get-tuple-element.56.slope_ref, ...), custom_call_target="tpu_custom_call" | custom-call | flops 10000000 | tf_op jit(solution)/shard_map/backward/pallas_call | solution.py:278
  53.1 1.6 %collective-permute-start.23 = (bf16[256,1024]{1,0:T(8,128)(2,1)S(1)}, bf16[256,1024]{1,0:T(8,128)(2,1)S(1)}, u32[]{:S(2)}, u32[]{:S(2)}) collective-permute-start(bf16[256,1024]{1,0:T(8,128)(2,1)S(1)} %get-tuple-element.65), channel_id=1, source_target_pairs={{0,2},{1,3},{2,0},{3,1},{4,6},{5,7},{6,4},{7,5},{8,10},{9,11},{10,... | collective-permute-start | bytes 1572872 | tf_op jit(solution)/shard_map/ppermute | solution.py:388
  55.2 1.9 %collective-permute-done.16.refs_4_.refs_1_ = bf16[128,1024]{1,0:T(8,128)(2,1)S(1)} collective-permute-done((bf16[128,1024]{1,0:T(8,128)(2,1)S(1)}, bf16[128,1024]{1,0:T(8,128)(2,1)S(1)}, u32[]{:S(2)}, u32[]{:S(2)}) %collective-permute-start.16) | collective-permute-done | bytes 262176 | tf_op jit(solution)/shard_map/ppermute | solution.py:388
  57.2 1.8 %collective-permute-start.17 = (bf16[136,1024]{1,0:T(8,128)(2,1)S(1)}, bf16[136,1024]{1,0:T(8,128)(2,1)S(1)}, u32[]{:S(2)}, u32[]{:S(2)}) collective-permute-start(bf16[136,1024]{1,0:T(8,128)(2,1)S(1)} %get-tuple-element.59.refs_4_), channel_id=1, source_target_pairs={{0,8},{4,12},{8,0},{12,4},{16,24},{20,28},{24,16},{28,20},{1,9},{5... | collective-permute-start | bytes 835592 | tf_op jit(solution)/shard_map/ppermute | solution.py:388
  59.0 0.7 collective-permute-start.14
  59.7 5.7 %collective-permute-done.14.refs_1_ = bf16[128,1024]{1,0:T(8,128)(2,1)S(1)} collective-permute-done((bf16[128,1024]{1,0:T(8,128)(2,1)S(1)}, bf16[128,1024]{1,0:T(8,128)(2,1)S(1)}, u32[]{:S(2)}, u32[]{:S(2)}) %collective-permute-start.14) | collective-permute-done | bytes 262176 | tf_op jit(solution)/shard_map/ppermute | solution.py:388
  65.5 0.8 collective-permute-start.18
  66.9 1.6 %backward.3 = (bf16[256,1024]{1,0:T(8,128)(2,1)S(1)}, bf16[256,1024]{1,0:T(8,128)(2,1)S(1)}) custom-call(f32[1,1024]{1,0:T(1,128)S(1)} %get-tuple-element.44.refs_2_.gain_ref, bf16[1024,1024]{1,0:T(8,128)(2,1)S(1)} %get-tuple-element.45.refs_3_.weight_ref, bf16[2,256,1024]{2,1,0:T(8,128)(2,1)S(1)} %get-tuple-element.49.refs_7_.slope_ref, ...), custom_call_target="tpu_custom_call" | custom-call | flops 10000000 | tf_op jit(solution)/shard_map/backward/pallas_call | solution.py:278
  68.6 1.0 %collective-permute-start.26 = (bf16[128,1024]{1,0:T(8,128)(2,1)S(1)}, bf16[128,1024]{1,0:T(8,128)(2,1)S(1)}, u32[]{:S(2)}, u32[]{:S(2)}) collective-permute-start(bf16[128,1024]{1,0:T(8,128)(2,1)S(1)} %fold.6), channel_id=1, source_target_pairs={{0,4},{4,0},{8,12},{12,8},{16,20},{20,16},{24,28},{28,24},{1,5},{5... | collective-permute-start | bytes 786440 | tf_op jit(solution)/shard_map/ppermute | solution.py:388
  69.6 7.4 %collective-permute-done.24.refs_0_ = bf16[256,1024]{1,0:T(8,128)(2,1)S(1)} collective-permute-done((bf16[256,1024]{1,0:T(8,128)(2,1)S(1)}, bf16[256,1024]{1,0:T(8,128)(2,1)S(1)}, u32[]{:S(2)}, u32[]{:S(2)}) %collective-permute-start.24) | collective-permute-done | bytes 524320 | tf_op jit(solution)/shard_map/ppermute | solution.py:388
  77.1 1.0 %collective-permute-done.18.piece_ref.refs_3_ = bf16[136,1024]{1,0:T(8,128)(2,1)S(1)} collective-permute-done((bf16[136,1024]{1,0:T(8,128)(2,1)S(1)}, bf16[136,1024]{1,0:T(8,128)(2,1)S(1)}, u32[]{:S(2)}, u32[]{:S(2)}) %collective-permute-start.18) | collective-permute-done | bytes 278560 | tf_op jit(solution)/shard_map/ppermute | solution.py:388
  78.8 0.9 %collective-permute-start.20 = (f32[8,128]{1,0:T(8,128)S(1)}, f32[8,128]{1,0:T(8,128)S(1)}, u32[]{:S(2)}, u32[]{:S(2)}) collective-permute-start(f32[8,128]{1,0:T(8,128)S(1)} %ride_end.1.refs_0_), channel_id=1, source_target_pairs={{0,2},{1,3},{2,0},{3,1},{4,6},{5,7},{6,4},{7,5},{8,10},{9,11},{10,... | collective-permute-start | bytes 12296 | tf_op jit(solution)/shard_map/ppermute | solution.py:388
  80.0 0.9 %fold.7 = f32[128,1024]{1,0:T(8,128)} custom-call(bf16[128,1024]{1,0:T(8,128)(2,1)S(1)} %get-tuple-element.68.refs_0_, bf16[128,1024]{1,0:T(8,128)(2,1)S(1)} %collective-permute-done.26.refs_1_, bf16[128,1024]{1,0:T(8,128)(2,1)S(1)} %collective-permute-done.27.refs_2_, bf16[136,1024]{1,0:T(8,128)(2,1)S(1)} %collective-permute-done.18.piece_ref.refs_3_), custom_call_target="tpu_custom_call" | custom-call | flops 3000000000 | tf_op jit(solution)/shard_map/fold/pallas_call | solution.py:314
  80.9 2.5 %pack.1 = (bf16[256,4,1024]{2,1,0:T(4,128)(2,1)}, f32[8,128]{1,0:T(8,128)S(1)}) custom-call(bf16[256,1024]{1,0:T(8,128)(2,1)S(1)} %get-tuple-element.63.refs_0_, bf16[256,1024]{1,0:T(8,128)(2,1)S(1)} %collective-permute-done.22.refs_1_, bf16[256,1024]{1,0:T(8,128)(2,1)S(1)} %collective-permute-done.23.refs_1_.refs_2_, ...), custom_call_target="tpu_custom_call" | custom-call | flops 10000000 | tf_op jit(solution)/shard_map/pack/pallas_call | solution.py:91
  (57 shorter events, 5.9 us)
Async XLA Ops:
  0.6 13.9 %copy-start.5 = (bf16[1,128]{1,0:T(2,128)(2,1)S(1)}, bf16[1,128]{1,0:T(2,128)(2,1)}, u32[]{:S(2)}) copy-start(bf16[1,128]{1,0:T(2,128)(2,1)} %refs_0_.3) | copy-start | bytes 772
  0.6 13.9 %collective-permute-start.2 = (bf16[128,1024]{1,0:T(8,128)(2,1)}, bf16[128,1024]{1,0:T(8,128)(2,1)S(1)}, u32[]{:S(2)}, u32[]{:S(2)}) collective-permute-start(bf16[128,1024]{1,0:T(8,128)(2,1)} %bitcast.6), channel_id=1, source_target_pairs={{0,8},{4,12},{8,0},{12,4},{16,24},{20,28},{24,16},{28,20},{1,9},{5... | collective-permute-start | bytes 786440 | tf_op jit(solution)/shard_map/ppermute | solution.py:388
  3.7 10.8 %collective-permute-start.1 = (bf16[128,1024]{1,0:T(8,128)(2,1)}, bf16[128,1024]{1,0:T(8,128)(2,1)S(1)}, u32[]{:S(2)}, u32[]{:S(2)}) collective-permute-start(bf16[128,1024]{1,0:T(8,128)(2,1)} %bitcast.7), channel_id=1, source_target_pairs={{0,4},{4,0},{8,12},{12,8},{16,20},{20,16},{24,28},{28,24},{1,5},{5... | collective-permute-start | bytes 786440 | tf_op jit(solution)/shard_map/ppermute | solution.py:388
  5.2 14.4 %collective-permute-start.4 = (bf16[128,1024]{1,0:T(8,128)(2,1)}, bf16[128,1024]{1,0:T(8,128)(2,1)S(1)}, u32[]{:S(2)}, u32[]{:S(2)}) collective-permute-start(bf16[128,1024]{1,0:T(8,128)(2,1)} %bitcast.8), channel_id=1, source_target_pairs={{0,16},{4,20},{8,24},{12,28},{16,0},{20,4},{24,8},{28,12},{1,17},{... | collective-permute-start | bytes 786440 | tf_op jit(solution)/shard_map/ppermute | solution.py:388
  7.8 5.7 %collective-permute-start = (bf16[1,128]{1,0:T(2,128)(2,1)}, bf16[1,128]{1,0:T(2,128)(2,1)S(1)}, u32[]{:S(2)}, u32[]{:S(2)}) collective-permute-start(bf16[1,128]{1,0:T(2,128)(2,1)} %refs_0_.3), channel_id=1, source_target_pairs={{0,4},{4,0},{8,12},{12,8},{16,20},{20,16},{24,28},{28,24},{1,5},{5... | collective-permute-start | bytes 776 | tf_op jit(solution)/shard_map/ppermute | solution.py:388
  11.9 17.1 %copy-start = (bf16[256,1024]{1,0:T(8,128)(2,1)S(1)}, bf16[256,1024]{1,0:T(8,128)(2,1)}, u32[]{:S(2)}) copy-start(bf16[256,1024]{1,0:T(8,128)(2,1)} %get-tuple-element.38.refs_2_) | copy-start | bytes 1572868
  11.9 21.6 %collective-permute-start.11 = (bf16[256,1024]{1,0:T(8,128)(2,1)}, bf16[256,1024]{1,0:T(8,128)(2,1)S(1)}, u32[]{:S(2)}, u32[]{:S(2)}) collective-permute-start(bf16[256,1024]{1,0:T(8,128)(2,1)} %get-tuple-element.46), channel_id=1, source_target_pairs={{0,2},{1,3},{2,0},{3,1},{4,6},{5,7},{6,4},{7,5},{8,10},{9,11},{10,... | collective-permute-start | bytes 1572872 | tf_op jit(solution)/shard_map/ppermute | solution.py:388
  13.5 22.5 %collective-permute-start.12 = (bf16[256,1024]{1,0:T(8,128)(2,1)}, bf16[256,1024]{1,0:T(8,128)(2,1)S(1)}, u32[]{:S(2)}, u32[]{:S(2)}) collective-permute-start(bf16[256,1024]{1,0:T(8,128)(2,1)} %get-tuple-element.47), channel_id=1, source_target_pairs={{0,2},{1,3},{2,0},{3,1},{4,6},{5,7},{6,4},{7,5},{8,10},{9,11},{10,... | collective-permute-start | bytes 1572872 | tf_op jit(solution)/shard_map/ppermute | solution.py:388
  14.5 10.2 %collective-permute-start.6 = (bf16[128,1024]{1,0:T(8,128)(2,1)S(1)}, bf16[128,1024]{1,0:T(8,128)(2,1)S(1)}, u32[]{:S(2)}, u32[]{:S(2)}) collective-permute-start(bf16[128,1024]{1,0:T(8,128)(2,1)S(1)} %get-tuple-element.43.refs_7_), channel_id=1, source_target_pairs={{0,8},{4,12},{8,0},{12,4},{16,24},{20,28},{24,16},{28,20},{1,9},{5... | collective-permute-start | bytes 786440 | tf_op jit(solution)/shard_map/ppermute | solution.py:388
  20.3 8.8 %collective-permute-start.9 = (bf16[128,1024]{1,0:T(8,128)(2,1)S(1)}, bf16[128,1024]{1,0:T(8,128)(2,1)S(1)}, u32[]{:S(2)}, u32[]{:S(2)}) collective-permute-start(bf16[128,1024]{1,0:T(8,128)(2,1)S(1)} %hold.8.refs_3_.refs_10_), channel_id=1, source_target_pairs={{0,8},{4,12},{8,0},{12,4},{16,24},{20,28},{24,16},{28,20},{1,9},{5... | collective-permute-start | bytes 786440 | tf_op jit(solution)/shard_map/ppermute | solution.py:388
  20.3 10.4 %collective-permute-start.8 = (bf16[128,1024]{1,0:T(8,128)(2,1)S(1)}, bf16[128,1024]{1,0:T(8,128)(2,1)S(1)}, u32[]{:S(2)}, u32[]{:S(2)}) collective-permute-start(bf16[128,1024]{1,0:T(8,128)(2,1)S(1)} %hold.8.refs_3_.refs_10_), channel_id=1, source_target_pairs={{0,4},{4,0},{8,12},{12,8},{16,20},{20,16},{24,28},{28,24},{1,5},{5... | collective-permute-start | bytes 786440 | tf_op jit(solution)/shard_map/ppermute | solution.py:388
  24.7 4.3 %collective-permute-start.3 = (bf16[2,128]{1,0:T(2,128)(2,1)S(1)}, bf16[2,128]{1,0:T(2,128)(2,1)S(1)}, u32[]{:S(2)}, u32[]{:S(2)}) collective-permute-start(bf16[2,128]{1,0:T(2,128)(2,1)S(1)} %get-tuple-element.37.refs_0_), channel_id=1, source_target_pairs={{0,8},{4,12},{8,0},{12,4},{16,24},{20,28},{24,16},{28,20},{1,9},{5... | collective-permute-start | bytes 1544 | tf_op jit(solution)/shard_map/ppermute | solution.py:388
  29.0 10.1 %collective-permute-start.7 = (bf16[256,1024]{1,0:T(8,128)(2,1)S(1)}, bf16[256,1024]{1,0:T(8,128)(2,1)S(1)}, u32[]{:S(2)}, u32[]{:S(2)}) collective-permute-start(bf16[256,1024]{1,0:T(8,128)(2,1)S(1)} %hold.10), channel_id=1, source_target_pairs={{0,1},{1,0},{2,3},{3,2},{4,5},{5,4},{6,7},{7,6},{8,9},{9,8},{10,11... | collective-permute-start | bytes 1572872 | tf_op jit(solution)/shard_map/ppermute | solution.py:388
  29.1 4.5 %collective-permute-start.5 = (bf16[4,128]{1,0:T(4,128)(2,1)S(1)}, bf16[4,128]{1,0:T(4,128)(2,1)S(1)}, u32[]{:S(2)}, u32[]{:S(2)}) collective-permute-start(bf16[4,128]{1,0:T(4,128)(2,1)S(1)} %get-tuple-element.40.refs_2_), channel_id=1, source_target_pairs={{0,16},{4,20},{8,24},{12,28},{16,0},{20,4},{24,8},{28,12},{1,17},{... | collective-permute-start | bytes 3080 | tf_op jit(solution)/shard_map/ppermute | solution.py:388
  30.6 8.5 %copy-start.4 = (s32[8]{0:T(128)S(1)}, s32[8]{0:T(128)}, u32[]{:S(2)}) copy-start(s32[8]{0:T(128)} %refs_0_.5) | copy-start | bytes 100
  30.6 8.5 %copy-start.6 = (bf16[1,128,1024]{2,1,0:T(8,128)(2,1)S(1)}, bf16[1,128,1024]{2,1,0:T(8,128)(2,1)}, u32[]{:S(2)}) copy-start(bf16[1,128,1024]{2,1,0:T(8,128)(2,1)} %param.6) | copy-start | bytes 786436
  30.7 8.5 %collective-permute-start.10 = (bf16[128,1024]{1,0:T(8,128)(2,1)S(1)}, bf16[128,1024]{1,0:T(8,128)(2,1)S(1)}, u32[]{:S(2)}, u32[]{:S(2)}) collective-permute-start(bf16[128,1024]{1,0:T(8,128)(2,1)S(1)} %hold.11.refs_12_), channel_id=1, source_target_pairs={{0,4},{4,0},{8,12},{12,8},{16,20},{20,16},{24,28},{28,24},{1,5},{5... | collective-permute-start | bytes 786440 | tf_op jit(solution)/shard_map/ppermute | solution.py:388
  36.0 6.7 %collective-permute-start.13 = (bf16[256,1024]{1,0:T(8,128)(2,1)S(1)}, bf16[256,1024]{1,0:T(8,128)(2,1)S(1)}, u32[]{:S(2)}, u32[]{:S(2)}) collective-permute-start(bf16[256,1024]{1,0:T(8,128)(2,1)S(1)} %hold.12), channel_id=1, source_target_pairs={{0,1},{1,0},{2,3},{3,2},{4,5},{5,4},{6,7},{7,6},{8,9},{9,8},{10,11... | collective-permute-start | bytes 1572872 | tf_op jit(solution)/shard_map/ppermute | solution.py:388
  47.6 9.5 %collective-permute-start.15 = (bf16[136,1024]{1,0:T(8,128)(2,1)S(1)}, bf16[136,1024]{1,0:T(8,128)(2,1)S(1)}, u32[]{:S(2)}, u32[]{:S(2)}) collective-permute-start(bf16[136,1024]{1,0:T(8,128)(2,1)S(1)} %get-tuple-element.54), channel_id=1, source_target_pairs={{0,4},{4,0},{8,12},{12,8},{16,20},{20,16},{24,28},{28,24},{1,5},{5... | collective-permute-start | bytes 835592 | tf_op jit(solution)/shard_map/ppermute | solution.py:388
  49.0 8.1 %collective-permute-start.16 = (bf16[128,1024]{1,0:T(8,128)(2,1)S(1)}, bf16[128,1024]{1,0:T(8,128)(2,1)S(1)}, u32[]{:S(2)}, u32[]{:S(2)}) collective-permute-start(bf16[128,1024]{1,0:T(8,128)(2,1)S(1)} %get-tuple-element.58), channel_id=1, source_target_pairs={{0,8},{4,12},{8,0},{12,4},{16,24},{20,28},{24,16},{28,20},{1,9},{5... | collective-permute-start | bytes 786440 | tf_op jit(solution)/shard_map/ppermute | solution.py:388
  53.1 16.5 %collective-permute-start.23 = (bf16[256,1024]{1,0:T(8,128)(2,1)S(1)}, bf16[256,1024]{1,0:T(8,128)(2,1)S(1)}, u32[]{:S(2)}, u32[]{:S(2)}) collective-permute-start(bf16[256,1024]{1,0:T(8,128)(2,1)S(1)} %get-tuple-element.65), channel_id=1, source_target_pairs={{0,2},{1,3},{2,0},{3,1},{4,6},{5,7},{6,4},{7,5},{8,10},{9,11},{10,... | collective-permute-start | bytes 1572872 | tf_op jit(solution)/shard_map/ppermute | solution.py:388
  54.7 22.4 %collective-permute-start.24 = (bf16[256,1024]{1,0:T(8,128)(2,1)S(1)}, bf16[256,1024]{1,0:T(8,128)(2,1)S(1)}, u32[]{:S(2)}, u32[]{:S(2)}) collective-permute-start(bf16[256,1024]{1,0:T(8,128)(2,1)S(1)} %get-tuple-element.57.refs_3_), channel_id=1, source_target_pairs={{0,2},{1,3},{2,0},{3,1},{4,6},{5,7},{6,4},{7,5},{8,10},{9,11},{10,... | collective-permute-start | bytes 1572872 | tf_op jit(solution)/shard_map/ppermute | solution.py:388
  57.2 8.2 %collective-permute-start.17 = (bf16[136,1024]{1,0:T(8,128)(2,1)S(1)}, bf16[136,1024]{1,0:T(8,128)(2,1)S(1)}, u32[]{:S(2)}, u32[]{:S(2)}) collective-permute-start(bf16[136,1024]{1,0:T(8,128)(2,1)S(1)} %get-tuple-element.59.refs_4_), channel_id=1, source_target_pairs={{0,8},{4,12},{8,0},{12,4},{16,24},{20,28},{24,16},{28,20},{1,9},{5... | collective-permute-start | bytes 835592 | tf_op jit(solution)/shard_map/ppermute | solution.py:388
  59.0 6.4 %collective-permute-start.14 = (bf16[128,1024]{1,0:T(8,128)(2,1)S(1)}, bf16[128,1024]{1,0:T(8,128)(2,1)S(1)}, u32[]{:S(2)}, u32[]{:S(2)}) collective-permute-start(bf16[128,1024]{1,0:T(8,128)(2,1)S(1)} %get-tuple-element.52), channel_id=1, source_target_pairs={{0,4},{4,0},{8,12},{12,8},{16,20},{20,16},{24,28},{28,24},{1,5},{5... | collective-permute-start | bytes 786440 | tf_op jit(solution)/shard_map/ppermute | solution.py:388
  65.5 12.6 %collective-permute-start.18 = (bf16[136,1024]{1,0:T(8,128)(2,1)S(1)}, bf16[136,1024]{1,0:T(8,128)(2,1)S(1)}, u32[]{:S(2)}, u32[]{:S(2)}) collective-permute-start(bf16[136,1024]{1,0:T(8,128)(2,1)S(1)} %get-tuple-element.62.refs_2_), channel_id=1, source_target_pairs={{0,16},{4,20},{8,24},{12,28},{16,0},{20,4},{24,8},{28,12},{1,17},{... | collective-permute-start | bytes 835592 | tf_op jit(solution)/shard_map/ppermute | solution.py:388
  66.3 12.5 %collective-permute-start.27 = (bf16[128,1024]{1,0:T(8,128)(2,1)S(1)}, bf16[128,1024]{1,0:T(8,128)(2,1)S(1)}, u32[]{:S(2)}, u32[]{:S(2)}) collective-permute-start(bf16[128,1024]{1,0:T(8,128)(2,1)S(1)} %get-tuple-element.70), channel_id=1, source_target_pairs={{0,8},{4,12},{8,0},{12,4},{16,24},{20,28},{24,16},{28,20},{1,9},{5... | collective-permute-start | bytes 786440 | tf_op jit(solution)/shard_map/ppermute | solution.py:388
  68.6 11.1 %collective-permute-start.26 = (bf16[128,1024]{1,0:T(8,128)(2,1)S(1)}, bf16[128,1024]{1,0:T(8,128)(2,1)S(1)}, u32[]{:S(2)}, u32[]{:S(2)}) collective-permute-start(bf16[128,1024]{1,0:T(8,128)(2,1)S(1)} %fold.6), channel_id=1, source_target_pairs={{0,4},{4,0},{8,12},{12,8},{16,20},{20,16},{24,28},{28,24},{1,5},{5... | collective-permute-start | bytes 786440 | tf_op jit(solution)/shard_map/ppermute | solution.py:388
  69.6 11.3 %collective-permute-start.22 = (bf16[256,1024]{1,0:T(8,128)(2,1)S(1)}, bf16[256,1024]{1,0:T(8,128)(2,1)S(1)}, u32[]{:S(2)}, u32[]{:S(2)}) collective-permute-start(bf16[256,1024]{1,0:T(8,128)(2,1)S(1)} %get-tuple-element.64.refs_2_), channel_id=1, source_target_pairs={{0,1},{1,0},{2,3},{3,2},{4,5},{5,4},{6,7},{7,6},{8,9},{9,8},{10,11... | collective-permute-start | bytes 1572872 | tf_op jit(solution)/shard_map/ppermute | solution.py:388
  77.1 3.9 %collective-permute-start.25 = (bf16[256,1024]{1,0:T(8,128)(2,1)S(1)}, bf16[256,1024]{1,0:T(8,128)(2,1)S(1)}, u32[]{:S(2)}, u32[]{:S(2)}) collective-permute-start(bf16[256,1024]{1,0:T(8,128)(2,1)S(1)} %hold.13), channel_id=1, source_target_pairs={{0,1},{1,0},{2,3},{3,2},{4,5},{5,4},{6,7},{7,6},{8,9},{9,8},{10,11... | collective-permute-start | bytes 1572872 | tf_op jit(solution)/shard_map/ppermute | solution.py:388
  78.1 5.3 %collective-permute-start.21 = (f32[8,128]{1,0:T(8,128)S(1)}, f32[8,128]{1,0:T(8,128)S(1)}, u32[]{:S(2)}, u32[]{:S(2)}) collective-permute-start(f32[8,128]{1,0:T(8,128)S(1)} %ride_end.1.refs_0_), channel_id=1, source_target_pairs={{0,3},{1,2},{2,1},{3,0},{4,7},{5,6},{6,5},{7,4},{8,11},{9,10},{10,... | collective-permute-start | bytes 12296 | tf_op jit(solution)/shard_map/ppermute | solution.py:388
  78.8 4.7 %collective-permute-start.20 = (f32[8,128]{1,0:T(8,128)S(1)}, f32[8,128]{1,0:T(8,128)S(1)}, u32[]{:S(2)}, u32[]{:S(2)}) collective-permute-start(f32[8,128]{1,0:T(8,128)S(1)} %ride_end.1.refs_0_), channel_id=1, source_target_pairs={{0,2},{1,3},{2,0},{3,1},{4,6},{5,7},{6,4},{7,5},{8,10},{9,11},{10,... | collective-permute-start | bytes 12296 | tf_op jit(solution)/shard_map/ppermute | solution.py:388
  79.7 3.8 %collective-permute-start.19 = (f32[8,128]{1,0:T(8,128)S(1)}, f32[8,128]{1,0:T(8,128)S(1)}, u32[]{:S(2)}, u32[]{:S(2)}) collective-permute-start(f32[8,128]{1,0:T(8,128)S(1)} %ride_end.1.refs_0_), channel_id=1, source_target_pairs={{0,1},{1,0},{2,3},{3,2},{4,5},{5,4},{6,7},{7,6},{8,9},{9,8},{10,11... | collective-permute-start | bytes 12296 | tf_op jit(solution)/shard_map/ppermute | solution.py:388
  (3 other events, 10.2 us)

commit v9 on v7

--- a/solution.py
+++ b/solution.py
@@ -404,15 +404,14 @@
             break
         pieces[o * inner] = swap(pieces[(o ^ bit) * inner], "dp", bit * inner)
     own, side, *away, unpacked = unpack(hidden)
-    if not small:
-        for o in range(line):
+    for o in range(line):
+        if small and o == 2:
+            pieces[4] = hold([], pieces[4], [unpacked])[1]
+        if small and o == 1:
+            gain, pieces[2] = hold(gains, pieces[2], [pieces[1]])
+        if pieces[o * inner] is not None:
             pieces[o * inner + 1] = swap(pieces[o * inner], "dp", 1)
     if small:
-        pieces[1] = swap(pieces[0], "dp", 1)
-        gain, pieces[1] = hold(gains, pieces[1], [pieces[2]])
-        pieces[3] = swap(pieces[1], "dp", 2)
-        pieces[4] = hold([], pieces[4], [unpacked])[1]
-        pieces[5] = swap(pieces[4], "dp", 1)
         gains = [gain, swap(gain, "dp", 2)]
         gain, side = hold(gains, side, [pieces[4]])
         gains = [gain, swap(gain, "dp", 4)]

time: 83.1 us -> 82.8 us (level)
  starting transfers between devices: 35.9 us -> 24.9 us
  waiting for transfers between devices: 26 us -> 36.8 us
    ppermute x28, starting transfers between devices: 35.9 us -> 24.9 us  [swap(): return lax.ppermute(value, axis, [(i, i ^ offset) for i in range(size)])]
    ppermute x28, waiting for transfers between devices: 26 us -> 36.8 us  [swap(): return lax.ppermute(value, axis, [(i, i ^ offset) for i in range(size)])]
  transfers between devices with their start and end apart: 28 -> 28, of which waited for: 12 -> 14; matrix products, arithmetic and copies ran while one was open for 0% -> 0% of each run, Pallas kernels for 17% -> 17%
where the time goes in v9:
time: 82.8 us; the launch traced here: 82.6 us
  waiting for transfers between devices  36.8 us (44%)
  starting transfers between devices  24.9 us (30%)
  Pallas kernels  19.5 us (24%)
    ppermute x28, waiting for transfers between devices, swap(): return lax.ppermute(value, axis, [(i, i ^ offset) for i in range(size)])  36.8 us
    ppermute x28, starting transfers between devices, swap(): return lax.ppermute(value, axis, [(i, i ^ offset) for i in range(size)])  24.9 us
    pallas_call x1, Pallas kernels, forward_far(): pl.pallas_call(body, in_specs=[SMEM] + [VMEM] * (6 + n), out_specs=[VMEM]...  4.92 us
    pallas_call x1, Pallas kernels, unpack(): pl.pallas_call(body, in_specs=[ANY], out_specs=[VMEM] * (positions + 1),...  3.59 us
    pallas_call x1, Pallas kernels, forward_near(): pl.pallas_call(body, in_specs=[SMEM] + [VMEM] * (1 + n_gain + n) + [ANY]...  3.48 us
    pallas_call x2, Pallas kernels, backward(): pl.pallas_call(body, in_specs=[VMEM] * (3 + n) + [ANY] * (len(after) + le...  3.18 us
    pallas_call x1, Pallas kernels, pack(): pl.pallas_call(body, grid=(frames // chunk,), in_specs=[pl.BlockSpec((chu...  2.53 us
  transfers between devices with their start and end apart: 28, of which 14 were waited for; matrix products, arithmetic and copies ran while one was open for 0% of the time, Pallas kernels for 17%

profile of v9, /device:TPU:0, one launch (start us, length us, event | category | flops | bytes accessed | tf_op | source)
XLA Modules:
  0.0 82.6 jit_solution(10423382400495719288)
XLA Ops:
  0.6 3.0 %collective-permute-start.2 = (bf16[128,1024]{1,0:T(8,128)(2,1)}, bf16[128,1024]{1,0:T(8,128)(2,1)S(1)}, u32[]{:S(2)}, u32[]{:S(2)}) collective-permute-start(bf16[128,1024]{1,0:T(8,128)(2,1)} %bitcast.6), channel_id=1, source_target_pairs={{0,4},{4,0},{8,12},{12,8},{16,20},{20,16},{24,28},{28,24},{1,5},{5... | collective-permute-start | bytes 786440 | tf_op jit(solution)/shard_map/ppermute | solution.py:388
  3.6 1.6 %collective-permute-start.1 = (bf16[128,1024]{1,0:T(8,128)(2,1)}, bf16[128,1024]{1,0:T(8,128)(2,1)S(1)}, u32[]{:S(2)}, u32[]{:S(2)}) collective-permute-start(bf16[128,1024]{1,0:T(8,128)(2,1)} %bitcast.7), channel_id=1, source_target_pairs={{0,8},{4,12},{8,0},{12,4},{16,24},{20,28},{24,16},{28,20},{1,9},{5... | collective-permute-start | bytes 786440 | tf_op jit(solution)/shard_map/ppermute | solution.py:388
  5.2 2.6 %collective-permute-start.4 = (bf16[128,1024]{1,0:T(8,128)(2,1)}, bf16[128,1024]{1,0:T(8,128)(2,1)S(1)}, u32[]{:S(2)}, u32[]{:S(2)}) collective-permute-start(bf16[128,1024]{1,0:T(8,128)(2,1)} %bitcast.8), channel_id=1, source_target_pairs={{0,16},{4,20},{8,24},{12,28},{16,0},{20,4},{24,8},{28,12},{1,17},{... | collective-permute-start | bytes 786440 | tf_op jit(solution)/shard_map/ppermute | solution.py:388
  8.3 3.6 %unpack.1 = (bf16[256,1024]{1,0:T(8,128)(2,1)}, bf16[256,1024]{1,0:T(8,128)(2,1)}, bf16[256,1024]{1,0:T(8,128)(2,1)}, bf16[256,1024]{1,0:T(8,128)(2,1)}, f32[8,128]{1,0:T(8,128)}) custom-call(bf16[256,4,1024]{2,1,0:T(4,128)(2,1)} %hidden_ref.1), custom_call_target="tpu_custom_call" | custom-call | flops 10000000 | tf_op jit(solution)/shard_map/unpack/pallas_call | solution.py:60
  11.9 1.6 %collective-permute-start.11 = (bf16[256,1024]{1,0:T(8,128)(2,1)}, bf16[256,1024]{1,0:T(8,128)(2,1)S(1)}, u32[]{:S(2)}, u32[]{:S(2)}) collective-permute-start(bf16[256,1024]{1,0:T(8,128)(2,1)} %get-tuple-element.46), channel_id=1, source_target_pairs={{0,2},{1,3},{2,0},{3,1},{4,6},{5,7},{6,4},{7,5},{8,10},{9,11},{10,... | collective-permute-start | bytes 1572872 | tf_op jit(solution)/shard_map/ppermute | solution.py:388
  14.0 3.1 %collective-permute-done.1.refs_2_ = bf16[128,1024]{1,0:T(8,128)(2,1)S(1)} collective-permute-done((bf16[128,1024]{1,0:T(8,128)(2,1)}, bf16[128,1024]{1,0:T(8,128)(2,1)S(1)}, u32[]{:S(2)}, u32[]{:S(2)}) %collective-permute-start.1) | collective-permute-done | bytes 262176 | tf_op jit(solution)/shard_map/ppermute | solution.py:388
  17.6 1.9 %collective-permute-done.4.refs_0_ = bf16[128,1024]{1,0:T(8,128)(2,1)S(1)} collective-permute-done((bf16[128,1024]{1,0:T(8,128)(2,1)}, bf16[128,1024]{1,0:T(8,128)(2,1)S(1)}, u32[]{:S(2)}, u32[]{:S(2)}) %collective-permute-start.4) | collective-permute-done | bytes 262176 | tf_op jit(solution)/shard_map/ppermute | solution.py:388
  19.5 0.7 copy-done.2
  21.1 1.7 %collective-permute-start.8 = (bf16[128,1024]{1,0:T(8,128)(2,1)S(1)}, bf16[128,1024]{1,0:T(8,128)(2,1)S(1)}, u32[]{:S(2)}, u32[]{:S(2)}) collective-permute-start(bf16[128,1024]{1,0:T(8,128)(2,1)S(1)} %hold.7.refs_3_.refs_10_), channel_id=1, source_target_pairs={{0,4},{4,0},{8,12},{12,8},{16,20},{20,16},{24,28},{28,24},{1,5},{5... | collective-permute-start | bytes 786440 | tf_op jit(solution)/shard_map/ppermute | solution.py:388
  22.8 3.6 %collective-permute-done.7.refs_1_.refs_9_ = bf16[128,1024]{1,0:T(8,128)(2,1)S(1)} collective-permute-done((bf16[128,1024]{1,0:T(8,128)(2,1)S(1)}, bf16[128,1024]{1,0:T(8,128)(2,1)S(1)}, u32[]{:S(2)}, u32[]{:S(2)}) %collective-permute-start.7) | collective-permute-done | bytes 262176 | tf_op jit(solution)/shard_map/ppermute | solution.py:388
  26.6 1.5 %collective-permute-start.5 = (bf16[4,128]{1,0:T(4,128)(2,1)S(1)}, bf16[4,128]{1,0:T(4,128)(2,1)S(1)}, u32[]{:S(2)}, u32[]{:S(2)}) collective-permute-start(bf16[4,128]{1,0:T(4,128)(2,1)S(1)} %get-tuple-element.40.refs_2_), channel_id=1, source_target_pairs={{0,16},{4,20},{8,24},{12,28},{16,0},{20,4},{24,8},{28,12},{1,17},{... | collective-permute-start | bytes 3080 | tf_op jit(solution)/shard_map/ppermute | solution.py:388
  28.0 1.7 %collective-permute-done.8.refs_2_.refs_11_ = bf16[128,1024]{1,0:T(8,128)(2,1)S(1)} collective-permute-done((bf16[128,1024]{1,0:T(8,128)(2,1)S(1)}, bf16[128,1024]{1,0:T(8,128)(2,1)S(1)}, u32[]{:S(2)}, u32[]{:S(2)}) %collective-permute-start.8) | collective-permute-done | bytes 262176 | tf_op jit(solution)/shard_map/ppermute | solution.py:388
  29.7 0.8 collective-permute-start.10
  30.5 0.6 collective-permute-done.5.refs_3_.refs_2_
  31.1 4.9 %collective-permute-done.12.refs_0_ = bf16[256,1024]{1,0:T(8,128)(2,1)S(1)} collective-permute-done((bf16[256,1024]{1,0:T(8,128)(2,1)}, bf16[256,1024]{1,0:T(8,128)(2,1)S(1)}, u32[]{:S(2)}, u32[]{:S(2)}) %collective-permute-start.12) | collective-permute-done | bytes 524320 | tf_op jit(solution)/shard_map/ppermute | solution.py:388
  36.1 3.5 %forward_near.1 = (f32[8,128]{1,0:T(8,128)S(1)}, f32[1,1024]{1,0:T(1,128)S(1)}, bf16[1024,1024]{1,0:T(8,128)(2,1)S(1)}, bf16[2,256,1024]{2,1,0:T(8,128)(2,1)S(1)}, bf16[2,256,1024]{2,1,0:T(8,128)(2,1)S(1)}) custom-call(s32[8]{0:T(128)S(1)} %copy-done.3, s32[1,1024]{1,0:T(1,128)S(1)} %bitcast.4, bf16[4,128]{1,0:T(4,128)(2,1)S(1)} %get-tuple-element.40.refs_2_, ...), custom_call_target="tpu_custom_call" | custom-call | flops 3000000000 | tf_op jit(solution)/shard_map/forward_near/pallas_call | solution.py:177
  39.6 4.9 %forward_far.1 = (f32[8,1024]{1,0:T(8,128)S(1)}, bf16[2,256,1024]{2,1,0:T(8,128)(2,1)S(1)}, bf16[128,1024]{1,0:T(8,128)(2,1)S(1)}, bf16[128,1024]{1,0:T(8,128)(2...) custom-call(s32[8]{0:T(128)S(1)} %copy-done.3, ...), custom_call_target="tpu_custom_call" | custom-call | flops 10000000 | tf_op jit(solution)/shard_map/forward_far/pallas_call | solution.py:240
  44.6 1.5 %collective-permute-start.15 = (bf16[136,1024]{1,0:T(8,128)(2,1)S(1)}, bf16[136,1024]{1,0:T(8,128)(2,1)S(1)}, u32[]{:S(2)}, u32[]{:S(2)}) collective-permute-start(bf16[136,1024]{1,0:T(8,128)(2,1)S(1)} %get-tuple-element.54), channel_id=1, source_target_pairs={{0,4},{4,0},{8,12},{12,8},{16,20},{20,16},{24,28},{28,24},{1,5},{5... | collective-permute-start | bytes 835592 | tf_op jit(solution)/shard_map/ppermute | solution.py:388
  46.0 0.8 collective-permute-start.16
  46.8 1.6 %backward.2 = (bf16[256,1024]{1,0:T(8,128)(2,1)S(1)}, bf16[256,1024]{1,0:T(8,128)(2,1)S(1)}) custom-call(f32[1,1024]{1,0:T(1,128)S(1)} %get-tuple-element.44.refs_2_.gain_ref, bf16[1024,1024]{1,0:T(8,128)(2,1)S(1)} %get-tuple-element.45.refs_3_.weight_ref, bf16[2,256,1024]{2,1,0:T(8,128)(2,1)S(1)} %get-tuple-element.56.slope_ref, ...), custom_call_target="tpu_custom_call" | custom-call | flops 10000000 | tf_op jit(solution)/shard_map/backward/pallas_call | solution.py:278
  48.4 1.6 %collective-permute-start.23 = (bf16[256,1024]{1,0:T(8,128)(2,1)S(1)}, bf16[256,1024]{1,0:T(8,128)(2,1)S(1)}, u32[]{:S(2)}, u32[]{:S(2)}) collective-permute-start(bf16[256,1024]{1,0:T(8,128)(2,1)S(1)} %get-tuple-element.65), channel_id=1, source_target_pairs={{0,2},{1,3},{2,0},{3,1},{4,6},{5,7},{6,4},{7,5},{8,10},{9,11},{10,... | collective-permute-start | bytes 1572872 | tf_op jit(solution)/shard_map/ppermute | solution.py:388
  50.5 3.9 %collective-permute-done.16.refs_4_.refs_1_ = bf16[128,1024]{1,0:T(8,128)(2,1)S(1)} collective-permute-done((bf16[128,1024]{1,0:T(8,128)(2,1)S(1)}, bf16[128,1024]{1,0:T(8,128)(2,1)S(1)}, u32[]{:S(2)}, u32[]{:S(2)}) %collective-permute-start.16) | collective-permute-done | bytes 262176 | tf_op jit(solution)/shard_map/ppermute | solution.py:388
  55.1 0.9 %collective-permute-start.14 = (bf16[128,1024]{1,0:T(8,128)(2,1)S(1)}, bf16[128,1024]{1,0:T(8,128)(2,1)S(1)}, u32[]{:S(2)}, u32[]{:S(2)}) collective-permute-start(bf16[128,1024]{1,0:T(8,128)(2,1)S(1)} %get-tuple-element.52), channel_id=1, source_target_pairs={{0,4},{4,0},{8,12},{12,8},{16,20},{20,16},{24,28},{28,24},{1,5},{5... | collective-permute-start | bytes 786440 | tf_op jit(solution)/shard_map/ppermute | solution.py:388
  56.0 6.3 %collective-permute-done.14.refs_1_ = bf16[128,1024]{1,0:T(8,128)(2,1)S(1)} collective-permute-done((bf16[128,1024]{1,0:T(8,128)(2,1)S(1)}, bf16[128,1024]{1,0:T(8,128)(2,1)S(1)}, u32[]{:S(2)}, u32[]{:S(2)}) %collective-permute-start.14) | collective-permute-done | bytes 262176 | tf_op jit(solution)/shard_map/ppermute | solution.py:388
  62.8 1.5 %collective-permute-start.27 = (bf16[128,1024]{1,0:T(8,128)(2,1)S(1)}, bf16[128,1024]{1,0:T(8,128)(2,1)S(1)}, u32[]{:S(2)}, u32[]{:S(2)}) collective-permute-start(bf16[128,1024]{1,0:T(8,128)(2,1)S(1)} %get-tuple-element.70), channel_id=1, source_target_pairs={{0,8},{4,12},{8,0},{12,4},{16,24},{20,28},{24,16},{28,20},{1,9},{5... | collective-permute-start | bytes 786440 | tf_op jit(solution)/shard_map/ppermute | solution.py:388
  64.3 1.6 %backward.3 = (bf16[256,1024]{1,0:T(8,128)(2,1)S(1)}, bf16[256,1024]{1,0:T(8,128)(2,1)S(1)}) custom-call(f32[1,1024]{1,0:T(1,128)S(1)} %get-tuple-element.44.refs_2_.gain_ref, bf16[1024,1024]{1,0:T(8,128)(2,1)S(1)} %get-tuple-element.45.refs_3_.weight_ref, bf16[2,256,1024]{2,1,0:T(8,128)(2,1)S(1)} %get-tuple-element.49.refs_7_.slope_ref, ...), custom_call_target="tpu_custom_call" | custom-call | flops 10000000 | tf_op jit(solution)/shard_map/backward/pallas_call | solution.py:278
  66.0 1.0 %collective-permute-start.26 = (bf16[128,1024]{1,0:T(8,128)(2,1)S(1)}, bf16[128,1024]{1,0:T(8,128)(2,1)S(1)}, u32[]{:S(2)}, u32[]{:S(2)}) collective-permute-start(bf16[128,1024]{1,0:T(8,128)(2,1)S(1)} %fold.6), channel_id=1, source_target_pairs={{0,4},{4,0},{8,12},{12,8},{16,20},{20,16},{24,28},{28,24},{1,5},{5... | collective-permute-start | bytes 786440 | tf_op jit(solution)/shard_map/ppermute | solution.py:388
  67.0 6.1 %collective-permute-done.24.refs_0_ = bf16[256,1024]{1,0:T(8,128)(2,1)S(1)} collective-permute-done((bf16[256,1024]{1,0:T(8,128)(2,1)S(1)}, bf16[256,1024]{1,0:T(8,128)(2,1)S(1)}, u32[]{:S(2)}, u32[]{:S(2)}) %collective-permute-start.24) | collective-permute-done | bytes 524320 | tf_op jit(solution)/shard_map/ppermute | solution.py:388
  73.1 3.6 %collective-permute-done.18.piece_ref.refs_3_ = bf16[136,1024]{1,0:T(8,128)(2,1)S(1)} collective-permute-done((bf16[136,1024]{1,0:T(8,128)(2,1)S(1)}, bf16[136,1024]{1,0:T(8,128)(2,1)S(1)}, u32[]{:S(2)}, u32[]{:S(2)}) %collective-permute-start.18) | collective-permute-done | bytes 278560 | tf_op jit(solution)/shard_map/ppermute | solution.py:388
  77.3 1.1 %collective-permute-start.20 = (f32[8,128]{1,0:T(8,128)S(1)}, f32[8,128]{1,0:T(8,128)S(1)}, u32[]{:S(2)}, u32[]{:S(2)}) collective-permute-start(f32[8,128]{1,0:T(8,128)S(1)} %ride_end.1.refs_0_), channel_id=1, source_target_pairs={{0,2},{1,3},{2,0},{3,1},{4,6},{5,7},{6,4},{7,5},{8,10},{9,11},{10,... | collective-permute-start | bytes 12296 | tf_op jit(solution)/shard_map/ppermute | solution.py:388
  78.6 0.9 %fold.7 = f32[128,1024]{1,0:T(8,128)} custom-call(bf16[128,1024]{1,0:T(8,128)(2,1)S(1)} %get-tuple-element.68.refs_0_, bf16[128,1024]{1,0:T(8,128)(2,1)S(1)} %collective-permute-done.26.refs_1_, bf16[128,1024]{1,0:T(8,128)(2,1)S(1)} %collective-permute-done.27.refs_2_, bf16[136,1024]{1,0:T(8,128)(2,1)S(1)} %collective-permute-done.18.piece_ref.refs_3_), custom_call_target="tpu_custom_call" | custom-call | flops 3000000000 | tf_op jit(solution)/shard_map/fold/pallas_call | solution.py:314
  79.5 2.5 %pack.1 = (bf16[256,4,1024]{2,1,0:T(4,128)(2,1)}, f32[8,128]{1,0:T(8,128)S(1)}) custom-call(bf16[256,1024]{1,0:T(8,128)(2,1)S(1)} %get-tuple-element.63.refs_0_, bf16[256,1024]{1,0:T(8,128)(2,1)S(1)} %collective-permute-done.22.refs_1_, bf16[256,1024]{1,0:T(8,128)(2,1)S(1)} %collective-permute-done.23.refs_1_.refs_2_, ...), custom_call_target="tpu_custom_call" | custom-call | flops 10000000 | tf_op jit(solution)/shard_map/pack/pallas_call | solution.py:91
  (54 shorter events, 5.8 us)
Async XLA Ops:
  0.6 16.5 %copy-start.4 = (bf16[1,128]{1,0:T(2,128)(2,1)S(1)}, bf16[1,128]{1,0:T(2,128)(2,1)}, u32[]{:S(2)}) copy-start(bf16[1,128]{1,0:T(2,128)(2,1)} %refs_0_.3) | copy-start | bytes 772
  0.6 13.4 %collective-permute-start.2 = (bf16[128,1024]{1,0:T(8,128)(2,1)}, bf16[128,1024]{1,0:T(8,128)(2,1)S(1)}, u32[]{:S(2)}, u32[]{:S(2)}) collective-permute-start(bf16[128,1024]{1,0:T(8,128)(2,1)} %bitcast.6), channel_id=1, source_target_pairs={{0,4},{4,0},{8,12},{12,8},{16,20},{20,16},{24,28},{28,24},{1,5},{5... | collective-permute-start | bytes 786440 | tf_op jit(solution)/shard_map/ppermute | solution.py:388
  3.6 13.5 %collective-permute-start.1 = (bf16[128,1024]{1,0:T(8,128)(2,1)}, bf16[128,1024]{1,0:T(8,128)(2,1)S(1)}, u32[]{:S(2)}, u32[]{:S(2)}) collective-permute-start(bf16[128,1024]{1,0:T(8,128)(2,1)} %bitcast.7), channel_id=1, source_target_pairs={{0,8},{4,12},{8,0},{12,4},{16,24},{20,28},{24,16},{28,20},{1,9},{5... | collective-permute-start | bytes 786440 | tf_op jit(solution)/shard_map/ppermute | solution.py:388
  5.2 14.3 %collective-permute-start.4 = (bf16[128,1024]{1,0:T(8,128)(2,1)}, bf16[128,1024]{1,0:T(8,128)(2,1)S(1)}, u32[]{:S(2)}, u32[]{:S(2)}) collective-permute-start(bf16[128,1024]{1,0:T(8,128)(2,1)} %bitcast.8), channel_id=1, source_target_pairs={{0,16},{4,20},{8,24},{12,28},{16,0},{20,4},{24,8},{28,12},{1,17},{... | collective-permute-start | bytes 786440 | tf_op jit(solution)/shard_map/ppermute | solution.py:388
  7.8 5.7 %collective-permute-start = (bf16[1,128]{1,0:T(2,128)(2,1)}, bf16[1,128]{1,0:T(2,128)(2,1)S(1)}, u32[]{:S(2)}, u32[]{:S(2)}) collective-permute-start(bf16[1,128]{1,0:T(2,128)(2,1)} %refs_0_.3), channel_id=1, source_target_pairs={{0,4},{4,0},{8,12},{12,8},{16,20},{20,16},{24,28},{28,24},{1,5},{5... | collective-permute-start | bytes 776 | tf_op jit(solution)/shard_map/ppermute | solution.py:388
  11.9 19.1 %collective-permute-start.11 = (bf16[256,1024]{1,0:T(8,128)(2,1)}, bf16[256,1024]{1,0:T(8,128)(2,1)S(1)}, u32[]{:S(2)}, u32[]{:S(2)}) collective-permute-start(bf16[256,1024]{1,0:T(8,128)(2,1)} %get-tuple-element.46), channel_id=1, source_target_pairs={{0,2},{1,3},{2,0},{3,1},{4,6},{5,7},{6,4},{7,5},{8,10},{9,11},{10,... | collective-permute-start | bytes 1572872 | tf_op jit(solution)/shard_map/ppermute | solution.py:388
  13.5 22.5 %collective-permute-start.12 = (bf16[256,1024]{1,0:T(8,128)(2,1)}, bf16[256,1024]{1,0:T(8,128)(2,1)S(1)}, u32[]{:S(2)}, u32[]{:S(2)}) collective-permute-start(bf16[256,1024]{1,0:T(8,128)(2,1)} %get-tuple-element.47), channel_id=1, source_target_pairs={{0,2},{1,3},{2,0},{3,1},{4,6},{5,7},{6,4},{7,5},{8,10},{9,11},{10,... | collective-permute-start | bytes 1572872 | tf_op jit(solution)/shard_map/ppermute | solution.py:388
  17.1 9.3 %collective-permute-start.7 = (bf16[128,1024]{1,0:T(8,128)(2,1)S(1)}, bf16[128,1024]{1,0:T(8,128)(2,1)S(1)}, u32[]{:S(2)}, u32[]{:S(2)}) collective-permute-start(bf16[128,1024]{1,0:T(8,128)(2,1)S(1)} %get-tuple-element.43.refs_8_), channel_id=1, source_target_pairs={{0,4},{4,0},{8,12},{12,8},{16,20},{20,16},{24,28},{28,24},{1,5},{5... | collective-permute-start | bytes 786440 | tf_op jit(solution)/shard_map/ppermute | solution.py:388
  17.6 3.6 %collective-permute-start.3 = (bf16[2,128]{1,0:T(2,128)(2,1)S(1)}, bf16[2,128]{1,0:T(2,128)(2,1)S(1)}, u32[]{:S(2)}, u32[]{:S(2)}) collective-permute-start(bf16[2,128]{1,0:T(2,128)(2,1)S(1)} %get-tuple-element.37.refs_0_), channel_id=1, source_target_pairs={{0,8},{4,12},{8,0},{12,4},{16,24},{20,28},{24,16},{28,20},{1,9},{5... | collective-permute-start | bytes 1544 | tf_op jit(solution)/shard_map/ppermute | solution.py:388
  20.2 6.4 %collective-permute-start.9 = (bf16[128,1024]{1,0:T(8,128)(2,1)S(1)}, bf16[128,1024]{1,0:T(8,128)(2,1)S(1)}, u32[]{:S(2)}, u32[]{:S(2)}) collective-permute-start(bf16[128,1024]{1,0:T(8,128)(2,1)S(1)} %hold.7.refs_3_.refs_10_), channel_id=1, source_target_pairs={{0,8},{4,12},{8,0},{12,4},{16,24},{20,28},{24,16},{28,20},{1,9},{5... | collective-permute-start | bytes 786440 | tf_op jit(solution)/shard_map/ppermute | solution.py:388
  21.1 8.5 %collective-permute-start.8 = (bf16[128,1024]{1,0:T(8,128)(2,1)S(1)}, bf16[128,1024]{1,0:T(8,128)(2,1)S(1)}, u32[]{:S(2)}, u32[]{:S(2)}) collective-permute-start(bf16[128,1024]{1,0:T(8,128)(2,1)S(1)} %hold.7.refs_3_.refs_10_), channel_id=1, source_target_pairs={{0,4},{4,0},{8,12},{12,8},{16,20},{20,16},{24,28},{28,24},{1,5},{5... | collective-permute-start | bytes 786440 | tf_op jit(solution)/shard_map/ppermute | solution.py:388
  26.4 9.7 %collective-permute-start.6 = (bf16[256,1024]{1,0:T(8,128)(2,1)}, bf16[256,1024]{1,0:T(8,128)(2,1)S(1)}, u32[]{:S(2)}, u32[]{:S(2)}) collective-permute-start(bf16[256,1024]{1,0:T(8,128)(2,1)} %get-tuple-element.42), channel_id=1, source_target_pairs={{0,1},{1,0},{2,3},{3,2},{4,5},{5,4},{6,7},{7,6},{8,9},{9,8},{10,11... | collective-permute-start | bytes 1572872 | tf_op jit(solution)/shard_map/ppermute | solution.py:388
  26.6 4.5 %collective-permute-start.5 = (bf16[4,128]{1,0:T(4,128)(2,1)S(1)}, bf16[4,128]{1,0:T(4,128)(2,1)S(1)}, u32[]{:S(2)}, u32[]{:S(2)}) collective-permute-start(bf16[4,128]{1,0:T(4,128)(2,1)S(1)} %get-tuple-element.40.refs_2_), channel_id=1, source_target_pairs={{0,16},{4,20},{8,24},{12,28},{16,0},{20,4},{24,8},{28,12},{1,17},{... | collective-permute-start | bytes 3080 | tf_op jit(solution)/shard_map/ppermute | solution.py:388
  29.7 6.5 %copy-start.1 = (s32[1024,1]{0,1:T(1,128)S(1)}, s32[1024,1]{0,1:T(1,128)}, u32[]{:S(2)}) copy-start(s32[1024,1]{0,1:T(1,128)} %param.8) | copy-start | bytes 12292
  29.7 6.5 %copy-start.3 = (s32[8]{0:T(128)S(1)}, s32[8]{0:T(128)}, u32[]{:S(2)}) copy-start(s32[8]{0:T(128)} %refs_0_.5) | copy-start | bytes 100
  29.7 6.5 %copy-start.5 = (bf16[1,128,1024]{2,1,0:T(8,128)(2,1)S(1)}, bf16[1,128,1024]{2,1,0:T(8,128)(2,1)}, u32[]{:S(2)}) copy-start(bf16[1,128,1024]{2,1,0:T(8,128)(2,1)} %param.6) | copy-start | bytes 786436
  29.7 6.4 %collective-permute-start.10 = (bf16[128,1024]{1,0:T(8,128)(2,1)S(1)}, bf16[128,1024]{1,0:T(8,128)(2,1)S(1)}, u32[]{:S(2)}, u32[]{:S(2)}) collective-permute-start(bf16[128,1024]{1,0:T(8,128)(2,1)S(1)} %hold.9.refs_12_), channel_id=1, source_target_pairs={{0,4},{4,0},{8,12},{12,8},{16,20},{20,16},{24,28},{28,24},{1,5},{5... | collective-permute-start | bytes 786440 | tf_op jit(solution)/shard_map/ppermute | solution.py:388
  36.0 3.6 %collective-permute-start.13 = (bf16[256,1024]{1,0:T(8,128)(2,1)S(1)}, bf16[256,1024]{1,0:T(8,128)(2,1)S(1)}, u32[]{:S(2)}, u32[]{:S(2)}) collective-permute-start(bf16[256,1024]{1,0:T(8,128)(2,1)S(1)} %hold.10), channel_id=1, source_target_pairs={{0,1},{1,0},{2,3},{3,2},{4,5},{5,4},{6,7},{7,6},{8,9},{9,8},{10,11... | collective-permute-start | bytes 1572872 | tf_op jit(solution)/shard_map/ppermute | solution.py:388
  44.6 9.9 %collective-permute-start.15 = (bf16[136,1024]{1,0:T(8,128)(2,1)S(1)}, bf16[136,1024]{1,0:T(8,128)(2,1)S(1)}, u32[]{:S(2)}, u32[]{:S(2)}) collective-permute-start(bf16[136,1024]{1,0:T(8,128)(2,1)S(1)} %get-tuple-element.54), channel_id=1, source_target_pairs={{0,4},{4,0},{8,12},{12,8},{16,20},{20,16},{24,28},{28,24},{1,5},{5... | collective-permute-start | bytes 835592 | tf_op jit(solution)/shard_map/ppermute | solution.py:388
  46.0 8.4 %collective-permute-start.16 = (bf16[128,1024]{1,0:T(8,128)(2,1)S(1)}, bf16[128,1024]{1,0:T(8,128)(2,1)S(1)}, u32[]{:S(2)}, u32[]{:S(2)}) collective-permute-start(bf16[128,1024]{1,0:T(8,128)(2,1)S(1)} %get-tuple-element.58), channel_id=1, source_target_pairs={{0,8},{4,12},{8,0},{12,4},{16,24},{20,28},{24,16},{28,20},{1,9},{5... | collective-permute-start | bytes 786440 | tf_op jit(solution)/shard_map/ppermute | solution.py:388
  48.4 18.5 %collective-permute-start.23 = (bf16[256,1024]{1,0:T(8,128)(2,1)S(1)}, bf16[256,1024]{1,0:T(8,128)(2,1)S(1)}, u32[]{:S(2)}, u32[]{:S(2)}) collective-permute-start(bf16[256,1024]{1,0:T(8,128)(2,1)S(1)} %get-tuple-element.65), channel_id=1, source_target_pairs={{0,2},{1,3},{2,0},{3,1},{4,6},{5,7},{6,4},{7,5},{8,10},{9,11},{10,... | collective-permute-start | bytes 1572872 | tf_op jit(solution)/shard_map/ppermute | solution.py:388
  50.0 23.1 %collective-permute-start.24 = (bf16[256,1024]{1,0:T(8,128)(2,1)S(1)}, bf16[256,1024]{1,0:T(8,128)(2,1)S(1)}, u32[]{:S(2)}, u32[]{:S(2)}) collective-permute-start(bf16[256,1024]{1,0:T(8,128)(2,1)S(1)} %get-tuple-element.57.refs_3_), channel_id=1, source_target_pairs={{0,2},{1,3},{2,0},{3,1},{4,6},{5,7},{6,4},{7,5},{8,10},{9,11},{10,... | collective-permute-start | bytes 1572872 | tf_op jit(solution)/shard_map/ppermute | solution.py:388
  54.6 8.0 %collective-permute-start.17 = (bf16[136,1024]{1,0:T(8,128)(2,1)S(1)}, bf16[136,1024]{1,0:T(8,128)(2,1)S(1)}, u32[]{:S(2)}, u32[]{:S(2)}) collective-permute-start(bf16[136,1024]{1,0:T(8,128)(2,1)S(1)} %get-tuple-element.59.refs_4_), channel_id=1, source_target_pairs={{0,8},{4,12},{8,0},{12,4},{16,24},{20,28},{24,16},{28,20},{1,9},{5... | collective-permute-start | bytes 835592 | tf_op jit(solution)/shard_map/ppermute | solution.py:388
  55.1 7.2 %collective-permute-start.14 = (bf16[128,1024]{1,0:T(8,128)(2,1)S(1)}, bf16[128,1024]{1,0:T(8,128)(2,1)S(1)}, u32[]{:S(2)}, u32[]{:S(2)}) collective-permute-start(bf16[128,1024]{1,0:T(8,128)(2,1)S(1)} %get-tuple-element.52), channel_id=1, source_target_pairs={{0,4},{4,0},{8,12},{12,8},{16,20},{20,16},{24,28},{28,24},{1,5},{5... | collective-permute-start | bytes 786440 | tf_op jit(solution)/shard_map/ppermute | solution.py:388
  62.8 14.0 %collective-permute-start.18 = (bf16[136,1024]{1,0:T(8,128)(2,1)S(1)}, bf16[136,1024]{1,0:T(8,128)(2,1)S(1)}, u32[]{:S(2)}, u32[]{:S(2)}) collective-permute-start(bf16[136,1024]{1,0:T(8,128)(2,1)S(1)} %get-tuple-element.62.refs_2_), channel_id=1, source_target_pairs={{0,16},{4,20},{8,24},{12,28},{16,0},{20,4},{24,8},{28,12},{1,17},{... | collective-permute-start | bytes 835592 | tf_op jit(solution)/shard_map/ppermute | solution.py:388
  62.8 14.4 %collective-permute-start.27 = (bf16[128,1024]{1,0:T(8,128)(2,1)S(1)}, bf16[128,1024]{1,0:T(8,128)(2,1)S(1)}, u32[]{:S(2)}, u32[]{:S(2)}) collective-permute-start(bf16[128,1024]{1,0:T(8,128)(2,1)S(1)} %get-tuple-element.70), channel_id=1, source_target_pairs={{0,8},{4,12},{8,0},{12,4},{16,24},{20,28},{24,16},{28,20},{1,9},{5... | collective-permute-start | bytes 786440 | tf_op jit(solution)/shard_map/ppermute | solution.py:388
  66.0 12.4 %collective-permute-start.26 = (bf16[128,1024]{1,0:T(8,128)(2,1)S(1)}, bf16[128,1024]{1,0:T(8,128)(2,1)S(1)}, u32[]{:S(2)}, u32[]{:S(2)}) collective-permute-start(bf16[128,1024]{1,0:T(8,128)(2,1)S(1)} %fold.6), channel_id=1, source_target_pairs={{0,4},{4,0},{8,12},{12,8},{16,20},{20,16},{24,28},{28,24},{1,5},{5... | collective-permute-start | bytes 786440 | tf_op jit(solution)/shard_map/ppermute | solution.py:388
  67.0 12.6 %collective-permute-start.22 = (bf16[256,1024]{1,0:T(8,128)(2,1)S(1)}, bf16[256,1024]{1,0:T(8,128)(2,1)S(1)}, u32[]{:S(2)}, u32[]{:S(2)}) collective-permute-start(bf16[256,1024]{1,0:T(8,128)(2,1)S(1)} %get-tuple-element.64.refs_2_), channel_id=1, source_target_pairs={{0,1},{1,0},{2,3},{3,2},{4,5},{5,4},{6,7},{7,6},{8,9},{9,8},{10,11... | collective-permute-start | bytes 1572872 | tf_op jit(solution)/shard_map/ppermute | solution.py:388
  73.1 6.4 %collective-permute-start.25 = (bf16[256,1024]{1,0:T(8,128)(2,1)S(1)}, bf16[256,1024]{1,0:T(8,128)(2,1)S(1)}, u32[]{:S(2)}, u32[]{:S(2)}) collective-permute-start(bf16[256,1024]{1,0:T(8,128)(2,1)S(1)} %hold.11), channel_id=1, source_target_pairs={{0,1},{1,0},{2,3},{3,2},{4,5},{5,4},{6,7},{7,6},{8,9},{9,8},{10,11... | collective-permute-start | bytes 1572872 | tf_op jit(solution)/shard_map/ppermute | solution.py:388
  76.7 5.3 %collective-permute-start.21 = (f32[8,128]{1,0:T(8,128)S(1)}, f32[8,128]{1,0:T(8,128)S(1)}, u32[]{:S(2)}, u32[]{:S(2)}) collective-permute-start(f32[8,128]{1,0:T(8,128)S(1)} %ride_end.1.refs_0_), channel_id=1, source_target_pairs={{0,3},{1,2},{2,1},{3,0},{4,7},{5,6},{6,5},{7,4},{8,11},{9,10},{10,... | collective-permute-start | bytes 12296 | tf_op jit(solution)/shard_map/ppermute | solution.py:388
  77.3 4.8 %collective-permute-start.20 = (f32[8,128]{1,0:T(8,128)S(1)}, f32[8,128]{1,0:T(8,128)S(1)}, u32[]{:S(2)}, u32[]{:S(2)}) collective-permute-start(f32[8,128]{1,0:T(8,128)S(1)} %ride_end.1.refs_0_), channel_id=1, source_target_pairs={{0,2},{1,3},{2,0},{3,1},{4,6},{5,7},{6,4},{7,5},{8,10},{9,11},{10,... | collective-permute-start | bytes 12296 | tf_op jit(solution)/shard_map/ppermute | solution.py:388
  78.3 3.8 %collective-permute-start.19 = (f32[8,128]{1,0:T(8,128)S(1)}, f32[8,128]{1,0:T(8,128)S(1)}, u32[]{:S(2)}, u32[]{:S(2)}) collective-permute-start(f32[8,128]{1,0:T(8,128)S(1)} %ride_end.1.refs_0_), channel_id=1, source_target_pairs={{0,1},{1,0},{2,3},{3,2},{4,5},{5,4},{6,7},{7,6},{8,9},{9,8},{10,11... | collective-permute-start | bytes 12296 | tf_op jit(solution)/shard_map/ppermute | solution.py:388
  (2 other events, 7.1 us)

commit v10 on v9

--- a/solution.py
+++ b/solution.py
@@ -467,7 +467,11 @@
 
     grad_head = fold([parts[0], across[0], *came[0]], None, (), [], last=True)[0]
 
-    parts = [loss] + [swap(loss, "fsdp", j) for j in range(1, n_fsdp)]
+    bit = n_fsdp // 2
+    while bit > 1:
+        loss = loss + swap(loss, "fsdp", bit)
+        bit //= 2
+    parts = [loss, swap(loss, "fsdp", bit)]
     return finish(parts, [packed])[0, 0], grad_hidden, grad_head[None]
 
 

time: 82.8 us -> 84.6 us (1.022)
  waiting for transfers between devices: 36.8 us -> 38.9 us
    ppermute x28 -> x27, waiting for transfers between devices: 36.8 us -> 38.9 us  [swap(): return lax.ppermute(value, axis, [(i, i ^ offset) for i in range(size)])]
    ppermute x28 -> x27, starting transfers between devices: 24.9 us -> 24.5 us  [swap(): return lax.ppermute(value, axis, [(i, i ^ offset) for i in range(size)])]
  transfers between devices with their start and end apart: 28 -> 27, of which waited for: 14 -> 15; matrix products, arithmetic and copies ran while one was open for 0% -> 0% of each run, Pallas kernels for 17% -> 17%
where the time goes in v10:
time: 84.6 us; the launch traced here: 84.4 us
  waiting for transfers between devices  38.9 us (46%)
  starting transfers between devices  24.5 us (29%)
  Pallas kernels  19.5 us (23%)
    ppermute x27, waiting for transfers between devices, swap(): return lax.ppermute(value, axis, [(i, i ^ offset) for i in range(size)])  38.9 us
    ppermute x27, starting transfers between devices, swap(): return lax.ppermute(value, axis, [(i, i ^ offset) for i in range(size)])  24.5 us
    pallas_call x1, Pallas kernels, forward_far(): pl.pallas_call(body, in_specs=[SMEM] + [VMEM] * (6 + n), out_specs=[VMEM]...  4.92 us
    pallas_call x1, Pallas kernels, unpack(): pl.pallas_call(body, in_specs=[ANY], out_specs=[VMEM] * (positions + 1),...  3.61 us
    pallas_call x1, Pallas kernels, forward_near(): pl.pallas_call(body, in_specs=[SMEM] + [VMEM] * (1 + n_gain + n) + [ANY]...  3.48 us
    pallas_call x2, Pallas kernels, backward(): pl.pallas_call(body, in_specs=[VMEM] * (3 + n) + [ANY] * (len(after) + le...  3.18 us
    pallas_call x1, Pallas kernels, pack(): pl.pallas_call(body, grid=(frames // chunk,), in_specs=[pl.BlockSpec((chu...  2.53 us
  transfers between devices with their start and end apart: 27, of which 15 were waited for; matrix products, arithmetic and copies ran while one was open for 0% of the time, Pallas kernels for 17%

profile of v10, /device:TPU:0, one launch (start us, length us, event | category | flops | bytes accessed | tf_op | source)
XLA Modules:
  0.0 84.4 jit_solution(5969079895543396751)
XLA Ops:
  0.6 3.0 %collective-permute-start.2 = (bf16[128,1024]{1,0:T(8,128)(2,1)}, bf16[128,1024]{1,0:T(8,128)(2,1)S(1)}, u32[]{:S(2)}, u32[]{:S(2)}) collective-permute-start(bf16[128,1024]{1,0:T(8,128)(2,1)} %bitcast.6), channel_id=1, source_target_pairs={{0,4},{4,0},{8,12},{12,8},{16,20},{20,16},{24,28},{28,24},{1,5},{5... | collective-permute-start | bytes 786440 | tf_op jit(solution)/shard_map/ppermute | solution.py:388
  3.6 1.6 %collective-permute-start.1 = (bf16[128,1024]{1,0:T(8,128)(2,1)}, bf16[128,1024]{1,0:T(8,128)(2,1)S(1)}, u32[]{:S(2)}, u32[]{:S(2)}) collective-permute-start(bf16[128,1024]{1,0:T(8,128)(2,1)} %bitcast.7), channel_id=1, source_target_pairs={{0,8},{4,12},{8,0},{12,4},{16,24},{20,28},{24,16},{28,20},{1,9},{5... | collective-permute-start | bytes 786440 | tf_op jit(solution)/shard_map/ppermute | solution.py:388
  5.2 2.6 %collective-permute-start.4 = (bf16[128,1024]{1,0:T(8,128)(2,1)}, bf16[128,1024]{1,0:T(8,128)(2,1)S(1)}, u32[]{:S(2)}, u32[]{:S(2)}) collective-permute-start(bf16[128,1024]{1,0:T(8,128)(2,1)} %bitcast.8), channel_id=1, source_target_pairs={{0,16},{4,20},{8,24},{12,28},{16,0},{20,4},{24,8},{28,12},{1,17},{... | collective-permute-start | bytes 786440 | tf_op jit(solution)/shard_map/ppermute | solution.py:388
  8.3 3.6 %unpack.1 = (bf16[256,1024]{1,0:T(8,128)(2,1)}, bf16[256,1024]{1,0:T(8,128)(2,1)}, bf16[256,1024]{1,0:T(8,128)(2,1)}, bf16[256,1024]{1,0:T(8,128)(2,1)}, f32[8,128]{1,0:T(8,128)}) custom-call(bf16[256,4,1024]{2,1,0:T(4,128)(2,1)} %hidden_ref.1), custom_call_target="tpu_custom_call" | custom-call | flops 10000000 | tf_op jit(solution)/shard_map/unpack/pallas_call | solution.py:60
  12.0 1.6 %collective-permute-start.11 = (bf16[256,1024]{1,0:T(8,128)(2,1)}, bf16[256,1024]{1,0:T(8,128)(2,1)S(1)}, u32[]{:S(2)}, u32[]{:S(2)}) collective-permute-start(bf16[256,1024]{1,0:T(8,128)(2,1)} %get-tuple-element.46), channel_id=1, source_target_pairs={{0,2},{1,3},{2,0},{3,1},{4,6},{5,7},{6,4},{7,5},{8,10},{9,11},{10,... | collective-permute-start | bytes 1572872 | tf_op jit(solution)/shard_map/ppermute | solution.py:388
  14.1 3.0 %collective-permute-done.1.refs_2_ = bf16[128,1024]{1,0:T(8,128)(2,1)S(1)} collective-permute-done((bf16[128,1024]{1,0:T(8,128)(2,1)}, bf16[128,1024]{1,0:T(8,128)(2,1)S(1)}, u32[]{:S(2)}, u32[]{:S(2)}) %collective-permute-start.1) | collective-permute-done | bytes 262176 | tf_op jit(solution)/shard_map/ppermute | solution.py:388
  17.6 1.9 %collective-permute-done.4.refs_0_ = bf16[128,1024]{1,0:T(8,128)(2,1)S(1)} collective-permute-done((bf16[128,1024]{1,0:T(8,128)(2,1)}, bf16[128,1024]{1,0:T(8,128)(2,1)S(1)}, u32[]{:S(2)}, u32[]{:S(2)}) %collective-permute-start.4) | collective-permute-done | bytes 262176 | tf_op jit(solution)/shard_map/ppermute | solution.py:388
  19.5 0.7 copy-done.2
  21.1 1.7 %collective-permute-start.8 = (bf16[128,1024]{1,0:T(8,128)(2,1)S(1)}, bf16[128,1024]{1,0:T(8,128)(2,1)S(1)}, u32[]{:S(2)}, u32[]{:S(2)}) collective-permute-start(bf16[128,1024]{1,0:T(8,128)(2,1)S(1)} %hold.7.refs_3_.refs_10_), channel_id=1, source_target_pairs={{0,4},{4,0},{8,12},{12,8},{16,20},{20,16},{24,28},{28,24},{1,5},{5... | collective-permute-start | bytes 786440 | tf_op jit(solution)/shard_map/ppermute | solution.py:388
  22.8 3.6 %collective-permute-done.7.refs_1_.refs_9_ = bf16[128,1024]{1,0:T(8,128)(2,1)S(1)} collective-permute-done((bf16[128,1024]{1,0:T(8,128)(2,1)S(1)}, bf16[128,1024]{1,0:T(8,128)(2,1)S(1)}, u32[]{:S(2)}, u32[]{:S(2)}) %collective-permute-start.7) | collective-permute-done | bytes 262176 | tf_op jit(solution)/shard_map/ppermute | solution.py:388
  26.5 1.5 %collective-permute-start.5 = (bf16[4,128]{1,0:T(4,128)(2,1)S(1)}, bf16[4,128]{1,0:T(4,128)(2,1)S(1)}, u32[]{:S(2)}, u32[]{:S(2)}) collective-permute-start(bf16[4,128]{1,0:T(4,128)(2,1)S(1)} %get-tuple-element.40.refs_2_), channel_id=1, source_target_pairs={{0,16},{4,20},{8,24},{12,28},{16,0},{20,4},{24,8},{28,12},{1,17},{... | collective-permute-start | bytes 3080 | tf_op jit(solution)/shard_map/ppermute | solution.py:388
  28.0 1.7 %collective-permute-done.8.refs_2_.refs_11_ = bf16[128,1024]{1,0:T(8,128)(2,1)S(1)} collective-permute-done((bf16[128,1024]{1,0:T(8,128)(2,1)S(1)}, bf16[128,1024]{1,0:T(8,128)(2,1)S(1)}, u32[]{:S(2)}, u32[]{:S(2)}) %collective-permute-start.8) | collective-permute-done | bytes 262176 | tf_op jit(solution)/shard_map/ppermute | solution.py:388
  29.7 0.8 collective-permute-start.10
  31.0 5.0 %collective-permute-done.12.refs_0_ = bf16[256,1024]{1,0:T(8,128)(2,1)S(1)} collective-permute-done((bf16[256,1024]{1,0:T(8,128)(2,1)}, bf16[256,1024]{1,0:T(8,128)(2,1)S(1)}, u32[]{:S(2)}, u32[]{:S(2)}) %collective-permute-start.12) | collective-permute-done | bytes 524320 | tf_op jit(solution)/shard_map/ppermute | solution.py:388
  36.1 3.5 %forward_near.1 = (f32[8,128]{1,0:T(8,128)S(1)}, f32[1,1024]{1,0:T(1,128)S(1)}, bf16[1024,1024]{1,0:T(8,128)(2,1)S(1)}, bf16[2,256,1024]{2,1,0:T(8,128)(2,1)S(1)}, bf16[2,256,1024]{2,1,0:T(8,128)(2,1)S(1)}) custom-call(s32[8]{0:T(128)S(1)} %copy-done.3, s32[1,1024]{1,0:T(1,128)S(1)} %bitcast.4, bf16[4,128]{1,0:T(4,128)(2,1)S(1)} %get-tuple-element.40.refs_2_, ...), custom_call_target="tpu_custom_call" | custom-call | flops 3000000000 | tf_op jit(solution)/shard_map/forward_near/pallas_call | solution.py:177
  39.6 4.9 %forward_far.1 = (f32[8,1024]{1,0:T(8,128)S(1)}, bf16[2,256,1024]{2,1,0:T(8,128)(2,1)S(1)}, bf16[128,1024]{1,0:T(8,128)(2,1)S(1)}, bf16[128,1024]{1,0:T(8,128)(2...) custom-call(s32[8]{0:T(128)S(1)} %copy-done.3, ...), custom_call_target="tpu_custom_call" | custom-call | flops 10000000 | tf_op jit(solution)/shard_map/forward_far/pallas_call | solution.py:240
  44.6 1.5 %collective-permute-start.15 = (bf16[136,1024]{1,0:T(8,128)(2,1)S(1)}, bf16[136,1024]{1,0:T(8,128)(2,1)S(1)}, u32[]{:S(2)}, u32[]{:S(2)}) collective-permute-start(bf16[136,1024]{1,0:T(8,128)(2,1)S(1)} %get-tuple-element.54), channel_id=1, source_target_pairs={{0,4},{4,0},{8,12},{12,8},{16,20},{20,16},{24,28},{28,24},{1,5},{5... | collective-permute-start | bytes 835592 | tf_op jit(solution)/shard_map/ppermute | solution.py:388
  46.0 0.8 collective-permute-start.16
  46.8 1.6 %backward.2 = (bf16[256,1024]{1,0:T(8,128)(2,1)S(1)}, bf16[256,1024]{1,0:T(8,128)(2,1)S(1)}) custom-call(f32[1,1024]{1,0:T(1,128)S(1)} %get-tuple-element.44.refs_2_.gain_ref, bf16[1024,1024]{1,0:T(8,128)(2,1)S(1)} %get-tuple-element.45.refs_3_.weight_ref, bf16[2,256,1024]{2,1,0:T(8,128)(2,1)S(1)} %get-tuple-element.56.slope_ref, ...), custom_call_target="tpu_custom_call" | custom-call | flops 10000000 | tf_op jit(solution)/shard_map/backward/pallas_call | solution.py:278
  48.4 1.6 %collective-permute-start.22 = (bf16[256,1024]{1,0:T(8,128)(2,1)S(1)}, bf16[256,1024]{1,0:T(8,128)(2,1)S(1)}, u32[]{:S(2)}, u32[]{:S(2)}) collective-permute-start(bf16[256,1024]{1,0:T(8,128)(2,1)S(1)} %get-tuple-element.65), channel_id=1, source_target_pairs={{0,2},{1,3},{2,0},{3,1},{4,6},{5,7},{6,4},{7,5},{8,10},{9,11},{10,... | collective-permute-start | bytes 1572872 | tf_op jit(solution)/shard_map/ppermute | solution.py:388
  50.5 3.9 %collective-permute-done.16.refs_4_.refs_1_ = bf16[128,1024]{1,0:T(8,128)(2,1)S(1)} collective-permute-done((bf16[128,1024]{1,0:T(8,128)(2,1)S(1)}, bf16[128,1024]{1,0:T(8,128)(2,1)S(1)}, u32[]{:S(2)}, u32[]{:S(2)}) %collective-permute-start.16) | collective-permute-done | bytes 262176 | tf_op jit(solution)/shard_map/ppermute | solution.py:388
  55.1 0.9 %collective-permute-start.14 = (bf16[128,1024]{1,0:T(8,128)(2,1)S(1)}, bf16[128,1024]{1,0:T(8,128)(2,1)S(1)}, u32[]{:S(2)}, u32[]{:S(2)}) collective-permute-start(bf16[128,1024]{1,0:T(8,128)(2,1)S(1)} %get-tuple-element.52), channel_id=1, source_target_pairs={{0,4},{4,0},{8,12},{12,8},{16,20},{20,16},{24,28},{28,24},{1,5},{5... | collective-permute-start | bytes 786440 | tf_op jit(solution)/shard_map/ppermute | solution.py:388
  56.1 6.3 %collective-permute-done.14.refs_1_ = bf16[128,1024]{1,0:T(8,128)(2,1)S(1)} collective-permute-done((bf16[128,1024]{1,0:T(8,128)(2,1)S(1)}, bf16[128,1024]{1,0:T(8,128)(2,1)S(1)}, u32[]{:S(2)}, u32[]{:S(2)}) %collective-permute-start.14) | collective-permute-done | bytes 262176 | tf_op jit(solution)/shard_map/ppermute | solution.py:388
  62.8 1.5 %collective-permute-start.26 = (bf16[128,1024]{1,0:T(8,128)(2,1)S(1)}, bf16[128,1024]{1,0:T(8,128)(2,1)S(1)}, u32[]{:S(2)}, u32[]{:S(2)}) collective-permute-start(bf16[128,1024]{1,0:T(8,128)(2,1)S(1)} %get-tuple-element.70), channel_id=1, source_target_pairs={{0,8},{4,12},{8,0},{12,4},{16,24},{20,28},{24,16},{28,20},{1,9},{5... | collective-permute-start | bytes 786440 | tf_op jit(solution)/shard_map/ppermute | solution.py:388
  64.3 1.6 %backward.3 = (bf16[256,1024]{1,0:T(8,128)(2,1)S(1)}, bf16[256,1024]{1,0:T(8,128)(2,1)S(1)}) custom-call(f32[1,1024]{1,0:T(1,128)S(1)} %get-tuple-element.44.refs_2_.gain_ref, bf16[1024,1024]{1,0:T(8,128)(2,1)S(1)} %get-tuple-element.45.refs_3_.weight_ref, bf16[2,256,1024]{2,1,0:T(8,128)(2,1)S(1)} %get-tuple-element.49.refs_7_.slope_ref, ...), custom_call_target="tpu_custom_call" | custom-call | flops 10000000 | tf_op jit(solution)/shard_map/backward/pallas_call | solution.py:278
  66.0 1.0 %collective-permute-start.25 = (bf16[128,1024]{1,0:T(8,128)(2,1)S(1)}, bf16[128,1024]{1,0:T(8,128)(2,1)S(1)}, u32[]{:S(2)}, u32[]{:S(2)}) collective-permute-start(bf16[128,1024]{1,0:T(8,128)(2,1)S(1)} %fold.6), channel_id=1, source_target_pairs={{0,4},{4,0},{8,12},{12,8},{16,20},{20,16},{24,28},{28,24},{1,5},{5... | collective-permute-start | bytes 786440 | tf_op jit(solution)/shard_map/ppermute | solution.py:388
  67.0 6.2 %collective-permute-done.23.refs_0_ = bf16[256,1024]{1,0:T(8,128)(2,1)S(1)} collective-permute-done((bf16[256,1024]{1,0:T(8,128)(2,1)S(1)}, bf16[256,1024]{1,0:T(8,128)(2,1)S(1)}, u32[]{:S(2)}, u32[]{:S(2)}) %collective-permute-start.23) | collective-permute-done | bytes 524320 | tf_op jit(solution)/shard_map/ppermute | solution.py:388
  73.2 3.6 %collective-permute-done.18.piece_ref.refs_3_ = bf16[136,1024]{1,0:T(8,128)(2,1)S(1)} collective-permute-done((bf16[136,1024]{1,0:T(8,128)(2,1)S(1)}, bf16[136,1024]{1,0:T(8,128)(2,1)S(1)}, u32[]{:S(2)}, u32[]{:S(2)}) %collective-permute-start.18) | collective-permute-done | bytes 278560 | tf_op jit(solution)/shard_map/ppermute | solution.py:388
  76.7 1.5 %collective-permute-start.19 = (f32[8,128]{1,0:T(8,128)S(1)}, f32[8,128]{1,0:T(8,128)S(1)}, u32[]{:S(2)}, u32[]{:S(2)}) collective-permute-start(f32[8,128]{1,0:T(8,128)S(1)} %ride_end.1), channel_id=1, source_target_pairs={{0,2},{1,3},{2,0},{3,1},{4,6},{5,7},{6,4},{7,5},{8,10},{9,11},{10,... | collective-permute-start | bytes 12296 | tf_op jit(solution)/shard_map/ppermute | solution.py:388
  78.3 2.1 %collective-permute-done.19 = f32[8,128]{1,0:T(8,128)S(1)} collective-permute-done((f32[8,128]{1,0:T(8,128)S(1)}, f32[8,128]{1,0:T(8,128)S(1)}, u32[]{:S(2)}, u32[]{:S(2)}) %collective-permute-start.19) | collective-permute-done | bytes 4128 | tf_op jit(solution)/shard_map/ppermute | solution.py:388
  80.4 0.9 %fold.7 = f32[128,1024]{1,0:T(8,128)} custom-call(bf16[128,1024]{1,0:T(8,128)(2,1)S(1)} %get-tuple-element.68.refs_0_, bf16[128,1024]{1,0:T(8,128)(2,1)S(1)} %collective-permute-done.25.refs_1_, bf16[128,1024]{1,0:T(8,128)(2,1)S(1)} %collective-permute-done.26.refs_2_, bf16[136,1024]{1,0:T(8,128)(2,1)S(1)} %collective-permute-done.18.piece_ref.refs_3_), custom_call_target="tpu_custom_call" | custom-call | flops 3000000000 | tf_op jit(solution)/shard_map/fold/pallas_call | solution.py:314
  81.3 2.5 %pack.1 = (bf16[256,4,1024]{2,1,0:T(4,128)(2,1)}, f32[8,128]{1,0:T(8,128)S(1)}) custom-call(bf16[256,1024]{1,0:T(8,128)(2,1)S(1)} %get-tuple-element.63.refs_0_, bf16[256,1024]{1,0:T(8,128)(2,1)S(1)} %collective-permute-done.21.refs_1_, bf16[256,1024]{1,0:T(8,128)(2,1)S(1)} %collective-permute-done.22.refs_1_.refs_2_, ...), custom_call_target="tpu_custom_call" | custom-call | flops 10000000 | tf_op jit(solution)/shard_map/pack/pallas_call | solution.py:91
  (53 shorter events, 5.5 us)
Async XLA Ops:
  0.6 16.5 %copy-start.4 = (bf16[1,128]{1,0:T(2,128)(2,1)S(1)}, bf16[1,128]{1,0:T(2,128)(2,1)}, u32[]{:S(2)}) copy-start(bf16[1,128]{1,0:T(2,128)(2,1)} %refs_0_.3) | copy-start | bytes 772
  0.6 13.4 %collective-permute-start.2 = (bf16[128,1024]{1,0:T(8,128)(2,1)}, bf16[128,1024]{1,0:T(8,128)(2,1)S(1)}, u32[]{:S(2)}, u32[]{:S(2)}) collective-permute-start(bf16[128,1024]{1,0:T(8,128)(2,1)} %bitcast.6), channel_id=1, source_target_pairs={{0,4},{4,0},{8,12},{12,8},{16,20},{20,16},{24,28},{28,24},{1,5},{5... | collective-permute-start | bytes 786440 | tf_op jit(solution)/shard_map/ppermute | solution.py:388
  3.6 13.5 %collective-permute-start.1 = (bf16[128,1024]{1,0:T(8,128)(2,1)}, bf16[128,1024]{1,0:T(8,128)(2,1)S(1)}, u32[]{:S(2)}, u32[]{:S(2)}) collective-permute-start(bf16[128,1024]{1,0:T(8,128)(2,1)} %bitcast.7), channel_id=1, source_target_pairs={{0,8},{4,12},{8,0},{12,4},{16,24},{20,28},{24,16},{28,20},{1,9},{5... | collective-permute-start | bytes 786440 | tf_op jit(solution)/shard_map/ppermute | solution.py:388
  5.2 14.3 %collective-permute-start.4 = (bf16[128,1024]{1,0:T(8,128)(2,1)}, bf16[128,1024]{1,0:T(8,128)(2,1)S(1)}, u32[]{:S(2)}, u32[]{:S(2)}) collective-permute-start(bf16[128,1024]{1,0:T(8,128)(2,1)} %bitcast.8), channel_id=1, source_target_pairs={{0,16},{4,20},{8,24},{12,28},{16,0},{20,4},{24,8},{28,12},{1,17},{... | collective-permute-start | bytes 786440 | tf_op jit(solution)/shard_map/ppermute | solution.py:388
  7.8 5.7 %collective-permute-start = (bf16[1,128]{1,0:T(2,128)(2,1)}, bf16[1,128]{1,0:T(2,128)(2,1)S(1)}, u32[]{:S(2)}, u32[]{:S(2)}) collective-permute-start(bf16[1,128]{1,0:T(2,128)(2,1)} %refs_0_.3), channel_id=1, source_target_pairs={{0,4},{4,0},{8,12},{12,8},{16,20},{20,16},{24,28},{28,24},{1,5},{5... | collective-permute-start | bytes 776 | tf_op jit(solution)/shard_map/ppermute | solution.py:388
  12.0 19.1 %collective-permute-start.11 = (bf16[256,1024]{1,0:T(8,128)(2,1)}, bf16[256,1024]{1,0:T(8,128)(2,1)S(1)}, u32[]{:S(2)}, u32[]{:S(2)}) collective-permute-start(bf16[256,1024]{1,0:T(8,128)(2,1)} %get-tuple-element.46), channel_id=1, source_target_pairs={{0,2},{1,3},{2,0},{3,1},{4,6},{5,7},{6,4},{7,5},{8,10},{9,11},{10,... | collective-permute-start | bytes 1572872 | tf_op jit(solution)/shard_map/ppermute | solution.py:388
  13.5 22.5 %collective-permute-start.12 = (bf16[256,1024]{1,0:T(8,128)(2,1)}, bf16[256,1024]{1,0:T(8,128)(2,1)S(1)}, u32[]{:S(2)}, u32[]{:S(2)}) collective-permute-start(bf16[256,1024]{1,0:T(8,128)(2,1)} %get-tuple-element.47), channel_id=1, source_target_pairs={{0,2},{1,3},{2,0},{3,1},{4,6},{5,7},{6,4},{7,5},{8,10},{9,11},{10,... | collective-permute-start | bytes 1572872 | tf_op jit(solution)/shard_map/ppermute | solution.py:388
  17.1 9.3 %collective-permute-start.7 = (bf16[128,1024]{1,0:T(8,128)(2,1)S(1)}, bf16[128,1024]{1,0:T(8,128)(2,1)S(1)}, u32[]{:S(2)}, u32[]{:S(2)}) collective-permute-start(bf16[128,1024]{1,0:T(8,128)(2,1)S(1)} %get-tuple-element.43.refs_8_), channel_id=1, source_target_pairs={{0,4},{4,0},{8,12},{12,8},{16,20},{20,16},{24,28},{28,24},{1,5},{5... | collective-permute-start | bytes 786440 | tf_op jit(solution)/shard_map/ppermute | solution.py:388
  17.6 3.6 %collective-permute-start.3 = (bf16[2,128]{1,0:T(2,128)(2,1)S(1)}, bf16[2,128]{1,0:T(2,128)(2,1)S(1)}, u32[]{:S(2)}, u32[]{:S(2)}) collective-permute-start(bf16[2,128]{1,0:T(2,128)(2,1)S(1)} %get-tuple-element.37.refs_0_), channel_id=1, source_target_pairs={{0,8},{4,12},{8,0},{12,4},{16,24},{20,28},{24,16},{28,20},{1,9},{5... | collective-permute-start | bytes 1544 | tf_op jit(solution)/shard_map/ppermute | solution.py:388
  20.2 6.4 %collective-permute-start.9 = (bf16[128,1024]{1,0:T(8,128)(2,1)S(1)}, bf16[128,1024]{1,0:T(8,128)(2,1)S(1)}, u32[]{:S(2)}, u32[]{:S(2)}) collective-permute-start(bf16[128,1024]{1,0:T(8,128)(2,1)S(1)} %hold.7.refs_3_.refs_10_), channel_id=1, source_target_pairs={{0,8},{4,12},{8,0},{12,4},{16,24},{20,28},{24,16},{28,20},{1,9},{5... | collective-permute-start | bytes 786440 | tf_op jit(solution)/shard_map/ppermute | solution.py:388
  21.1 8.5 %collective-permute-start.8 = (bf16[128,1024]{1,0:T(8,128)(2,1)S(1)}, bf16[128,1024]{1,0:T(8,128)(2,1)S(1)}, u32[]{:S(2)}, u32[]{:S(2)}) collective-permute-start(bf16[128,1024]{1,0:T(8,128)(2,1)S(1)} %hold.7.refs_3_.refs_10_), channel_id=1, source_target_pairs={{0,4},{4,0},{8,12},{12,8},{16,20},{20,16},{24,28},{28,24},{1,5},{5... | collective-permute-start | bytes 786440 | tf_op jit(solution)/shard_map/ppermute | solution.py:388
  26.4 9.7 %collective-permute-start.6 = (bf16[256,1024]{1,0:T(8,128)(2,1)}, bf16[256,1024]{1,0:T(8,128)(2,1)S(1)}, u32[]{:S(2)}, u32[]{:S(2)}) collective-permute-start(bf16[256,1024]{1,0:T(8,128)(2,1)} %get-tuple-element.42), channel_id=1, source_target_pairs={{0,1},{1,0},{2,3},{3,2},{4,5},{5,4},{6,7},{7,6},{8,9},{9,8},{10,11... | collective-permute-start | bytes 1572872 | tf_op jit(solution)/shard_map/ppermute | solution.py:388
  26.5 4.5 %collective-permute-start.5 = (bf16[4,128]{1,0:T(4,128)(2,1)S(1)}, bf16[4,128]{1,0:T(4,128)(2,1)S(1)}, u32[]{:S(2)}, u32[]{:S(2)}) collective-permute-start(bf16[4,128]{1,0:T(4,128)(2,1)S(1)} %get-tuple-element.40.refs_2_), channel_id=1, source_target_pairs={{0,16},{4,20},{8,24},{12,28},{16,0},{20,4},{24,8},{28,12},{1,17},{... | collective-permute-start | bytes 3080 | tf_op jit(solution)/shard_map/ppermute | solution.py:388
  29.7 6.5 %copy-start = (bf16[256,1024]{1,0:T(8,128)(2,1)S(1)}, bf16[256,1024]{1,0:T(8,128)(2,1)}, u32[]{:S(2)}) copy-start(bf16[256,1024]{1,0:T(8,128)(2,1)} %get-tuple-element.41.refs_4_.refs_0_) | copy-start | bytes 1572868
  29.7 6.5 %copy-start.1 = (s32[1024,1]{0,1:T(1,128)S(1)}, s32[1024,1]{0,1:T(1,128)}, u32[]{:S(2)}) copy-start(s32[1024,1]{0,1:T(1,128)} %param.8) | copy-start | bytes 12292
  29.7 6.5 %copy-start.3 = (s32[8]{0:T(128)S(1)}, s32[8]{0:T(128)}, u32[]{:S(2)}) copy-start(s32[8]{0:T(128)} %refs_0_.5) | copy-start | bytes 100
  29.7 6.5 %copy-start.5 = (bf16[1,128,1024]{2,1,0:T(8,128)(2,1)S(1)}, bf16[1,128,1024]{2,1,0:T(8,128)(2,1)}, u32[]{:S(2)}) copy-start(bf16[1,128,1024]{2,1,0:T(8,128)(2,1)} %param.6) | copy-start | bytes 786436
  29.7 6.4 %collective-permute-start.10 = (bf16[128,1024]{1,0:T(8,128)(2,1)S(1)}, bf16[128,1024]{1,0:T(8,128)(2,1)S(1)}, u32[]{:S(2)}, u32[]{:S(2)}) collective-permute-start(bf16[128,1024]{1,0:T(8,128)(2,1)S(1)} %hold.9.refs_12_), channel_id=1, source_target_pairs={{0,4},{4,0},{8,12},{12,8},{16,20},{20,16},{24,28},{28,24},{1,5},{5... | collective-permute-start | bytes 786440 | tf_op jit(solution)/shard_map/ppermute | solution.py:388
  36.0 3.6 %collective-permute-start.13 = (bf16[256,1024]{1,0:T(8,128)(2,1)S(1)}, bf16[256,1024]{1,0:T(8,128)(2,1)S(1)}, u32[]{:S(2)}, u32[]{:S(2)}) collective-permute-start(bf16[256,1024]{1,0:T(8,128)(2,1)S(1)} %hold.10), channel_id=1, source_target_pairs={{0,1},{1,0},{2,3},{3,2},{4,5},{5,4},{6,7},{7,6},{8,9},{9,8},{10,11... | collective-permute-start | bytes 1572872 | tf_op jit(solution)/shard_map/ppermute | solution.py:388
  44.6 9.9 %collective-permute-start.15 = (bf16[136,1024]{1,0:T(8,128)(2,1)S(1)}, bf16[136,1024]{1,0:T(8,128)(2,1)S(1)}, u32[]{:S(2)}, u32[]{:S(2)}) collective-permute-start(bf16[136,1024]{1,0:T(8,128)(2,1)S(1)} %get-tuple-element.54), channel_id=1, source_target_pairs={{0,4},{4,0},{8,12},{12,8},{16,20},{20,16},{24,28},{28,24},{1,5},{5... | collective-permute-start | bytes 835592 | tf_op jit(solution)/shard_map/ppermute | solution.py:388
  46.0 8.4 %collective-permute-start.16 = (bf16[128,1024]{1,0:T(8,128)(2,1)S(1)}, bf16[128,1024]{1,0:T(8,128)(2,1)S(1)}, u32[]{:S(2)}, u32[]{:S(2)}) collective-permute-start(bf16[128,1024]{1,0:T(8,128)(2,1)S(1)} %get-tuple-element.58), channel_id=1, source_target_pairs={{0,8},{4,12},{8,0},{12,4},{16,24},{20,28},{24,16},{28,20},{1,9},{5... | collective-permute-start | bytes 786440 | tf_op jit(solution)/shard_map/ppermute | solution.py:388
  48.4 18.6 %collective-permute-start.22 = (bf16[256,1024]{1,0:T(8,128)(2,1)S(1)}, bf16[256,1024]{1,0:T(8,128)(2,1)S(1)}, u32[]{:S(2)}, u32[]{:S(2)}) collective-permute-start(bf16[256,1024]{1,0:T(8,128)(2,1)S(1)} %get-tuple-element.65), channel_id=1, source_target_pairs={{0,2},{1,3},{2,0},{3,1},{4,6},{5,7},{6,4},{7,5},{8,10},{9,11},{10,... | collective-permute-start | bytes 1572872 | tf_op jit(solution)/shard_map/ppermute | solution.py:388
  50.0 23.1 %collective-permute-start.23 = (bf16[256,1024]{1,0:T(8,128)(2,1)S(1)}, bf16[256,1024]{1,0:T(8,128)(2,1)S(1)}, u32[]{:S(2)}, u32[]{:S(2)}) collective-permute-start(bf16[256,1024]{1,0:T(8,128)(2,1)S(1)} %get-tuple-element.57.refs_3_), channel_id=1, source_target_pairs={{0,2},{1,3},{2,0},{3,1},{4,6},{5,7},{6,4},{7,5},{8,10},{9,11},{10,... | collective-permute-start | bytes 1572872 | tf_op jit(solution)/shard_map/ppermute | solution.py:388
  54.6 8.0 %collective-permute-start.17 = (bf16[136,1024]{1,0:T(8,128)(2,1)S(1)}, bf16[136,1024]{1,0:T(8,128)(2,1)S(1)}, u32[]{:S(2)}, u32[]{:S(2)}) collective-permute-start(bf16[136,1024]{1,0:T(8,128)(2,1)S(1)} %get-tuple-element.59.refs_4_), channel_id=1, source_target_pairs={{0,8},{4,12},{8,0},{12,4},{16,24},{20,28},{24,16},{28,20},{1,9},{5... | collective-permute-start | bytes 835592 | tf_op jit(solution)/shard_map/ppermute | solution.py:388
  55.1 7.2 %collective-permute-start.14 = (bf16[128,1024]{1,0:T(8,128)(2,1)S(1)}, bf16[128,1024]{1,0:T(8,128)(2,1)S(1)}, u32[]{:S(2)}, u32[]{:S(2)}) collective-permute-start(bf16[128,1024]{1,0:T(8,128)(2,1)S(1)} %get-tuple-element.52), channel_id=1, source_target_pairs={{0,4},{4,0},{8,12},{12,8},{16,20},{20,16},{24,28},{28,24},{1,5},{5... | collective-permute-start | bytes 786440 | tf_op jit(solution)/shard_map/ppermute | solution.py:388
  62.8 14.0 %collective-permute-start.18 = (bf16[136,1024]{1,0:T(8,128)(2,1)S(1)}, bf16[136,1024]{1,0:T(8,128)(2,1)S(1)}, u32[]{:S(2)}, u32[]{:S(2)}) collective-permute-start(bf16[136,1024]{1,0:T(8,128)(2,1)S(1)} %get-tuple-element.62.refs_2_), channel_id=1, source_target_pairs={{0,16},{4,20},{8,24},{12,28},{16,0},{20,4},{24,8},{28,12},{1,17},{... | collective-permute-start | bytes 835592 | tf_op jit(solution)/shard_map/ppermute | solution.py:388
  62.8 17.5 %collective-permute-start.26 = (bf16[128,1024]{1,0:T(8,128)(2,1)S(1)}, bf16[128,1024]{1,0:T(8,128)(2,1)S(1)}, u32[]{:S(2)}, u32[]{:S(2)}) collective-permute-start(bf16[128,1024]{1,0:T(8,128)(2,1)S(1)} %get-tuple-element.70), channel_id=1, source_target_pairs={{0,8},{4,12},{8,0},{12,4},{16,24},{20,28},{24,16},{28,20},{1,9},{5... | collective-permute-start | bytes 786440 | tf_op jit(solution)/shard_map/ppermute | solution.py:388
  66.0 14.4 %collective-permute-start.25 = (bf16[128,1024]{1,0:T(8,128)(2,1)S(1)}, bf16[128,1024]{1,0:T(8,128)(2,1)S(1)}, u32[]{:S(2)}, u32[]{:S(2)}) collective-permute-start(bf16[128,1024]{1,0:T(8,128)(2,1)S(1)} %fold.6), channel_id=1, source_target_pairs={{0,4},{4,0},{8,12},{12,8},{16,20},{20,16},{24,28},{28,24},{1,5},{5... | collective-permute-start | bytes 786440 | tf_op jit(solution)/shard_map/ppermute | solution.py:388
  67.0 14.3 %collective-permute-start.21 = (bf16[256,1024]{1,0:T(8,128)(2,1)S(1)}, bf16[256,1024]{1,0:T(8,128)(2,1)S(1)}, u32[]{:S(2)}, u32[]{:S(2)}) collective-permute-start(bf16[256,1024]{1,0:T(8,128)(2,1)S(1)} %get-tuple-element.64.refs_2_), channel_id=1, source_target_pairs={{0,1},{1,0},{2,3},{3,2},{4,5},{5,4},{6,7},{7,6},{8,9},{9,8},{10,11... | collective-permute-start | bytes 1572872 | tf_op jit(solution)/shard_map/ppermute | solution.py:388
  73.2 8.2 %collective-permute-start.24 = (bf16[256,1024]{1,0:T(8,128)(2,1)S(1)}, bf16[256,1024]{1,0:T(8,128)(2,1)S(1)}, u32[]{:S(2)}, u32[]{:S(2)}) collective-permute-start(bf16[256,1024]{1,0:T(8,128)(2,1)S(1)} %hold.11), channel_id=1, source_target_pairs={{0,1},{1,0},{2,3},{3,2},{4,5},{5,4},{6,7},{7,6},{8,9},{9,8},{10,11... | collective-permute-start | bytes 1572872 | tf_op jit(solution)/shard_map/ppermute | solution.py:388
  76.7 3.6 %collective-permute-start.19 = (f32[8,128]{1,0:T(8,128)S(1)}, f32[8,128]{1,0:T(8,128)S(1)}, u32[]{:S(2)}, u32[]{:S(2)}) collective-permute-start(f32[8,128]{1,0:T(8,128)S(1)} %ride_end.1), channel_id=1, source_target_pairs={{0,2},{1,3},{2,0},{3,1},{4,6},{5,7},{6,4},{7,5},{8,10},{9,11},{10,... | collective-permute-start | bytes 12296 | tf_op jit(solution)/shard_map/ppermute | solution.py:388
  80.4 3.5 %collective-permute-start.20 = (f32[8,128]{1,0:T(8,128)S(1)}, f32[8,128]{1,0:T(8,128)S(1)}, u32[]{:S(2)}, u32[]{:S(2)}) collective-permute-start(f32[8,128]{1,0:T(8,128)S(1)} %add.3.refs_0_), channel_id=1, source_target_pairs={{0,1},{1,0},{2,3},{3,2},{4,5},{5,4},{6,7},{7,6},{8,9},{9,8},{10,11... | collective-permute-start | bytes 12296 | tf_op jit(solution)/shard_map/ppermute | solution.py:388
  (1 other events, 0.7 us)
